TPU v7x, 32 devices: a whole 2x2x4 slice. The times are simulated.
32 devices in a mesh: groups: 2 (over y), store: 4 (over x, core), tensor: 4 (over z).
Axes of the slice: x: 2, y: 2, z: 4, core: 2. Of those that a mesh axis runs over, the one named last changes fastest.
Arguments:
- hidden: bfloat16 [2, 1024, 8192], P(None, ('groups', 'store'), 'tensor'), parts along dimension 1, may hold values from -6 to 6
- input_norm_scale: float32 [8192], replicated, may hold values from 0.1 to 1.9
- query_key_value_weight: bfloat16 [8192, 5120], P(None, 'tensor'), may hold values from -0.0625 to 0.0625
- output_weight: bfloat16 [4096, 8192], P(None, 'tensor'), may hold values from -0.09375 to 0.09375
- adapter_down_weight: bfloat16 [256, 8192, 64], P(('groups', 'store'), 'tensor'), parts along dimension 0, may hold values from -0.0625 to 0.0625
- adapter_up_weight: bfloat16 [256, 64, 5120], P(('groups', 'store'), None, 'tensor'), parts along dimension 0, may hold values from -0.75 to 0.75
- row_adapter_index: int32 [1024], P(('groups', 'store')), parts along dimension 0, may hold values from 0 to 127, as said below
- adapter_store_slot: int32 [256], P('groups'), parts along dimension 0, may hold values from 0 to 127, each once
- lengths: int32 [1024], P(('groups', 'store', 'tensor')), parts along dimension 0, may hold values from 1 to 512, 131072 in all
- key_value_cache: bfloat16 [1024, 4, 512, 256], P(('groups', 'store', 'tensor')), parts along dimension 0
Outputs:
- attended: bfloat16 [2, 1024, 8192], P(None, ('groups', 'store'), 'tensor'), parts along dimension 1
There are 2 independent parts, one for each index of `groups`. A program takes and returns all parts, laid end to end along the dimension named above; an argument that names none is the same for every part. Nothing has to cross between parts.
Inputs may be any that keep to these rules, and one draw needn't show every extreme that they name: `row_adapter_index`: ids never decrease along the rows of a part and change only between aligned runs of 8 rows. `adapter_store_slot`: slot k lies with store index k // 32.
All inputs are finite; a program needn't handle non-finite values. No bound on the sum of `lengths` on one device may be relied on, other than what follows from the above.
Results may differ from a plain program's by a relative error of at most 0.0055.
The roundings to bfloat16 on the way count: a program that leaves them out, or rounds other values in their place, can miss the bound.
Values may be sent and summed in bfloat16 or wider, within the bound.
No kernel may reach another device: no remote copies, remote signals or barrier semaphores. Data moves between devices by JAX's collectives and lax.ppermute only.
A program may use at most 320 MiB of HBM per device.

v0:
```python
import jax
import jax.numpy as jnp
from jax import lax
from jax.sharding import PartitionSpec as P

HEADS = 32
KVH = 4
HD = 128


eps_norm = 1e-05
rope_base = 500000.0
masked = -1e30


def rotate(values, angles):
    half = values.shape[-1] // 2
    cosine = jnp.cos(angles)[..., None, :]
    sine = jnp.sin(angles)[..., None, :]
    first = values[..., :half]
    second = values[..., half:]
    return jnp.concatenate(
        [first * cosine - second * sine, second * cosine + first * sine], axis=-1
    )


def angles_for(lengths, head_dim):
    position = (lengths[None, :] + jnp.arange(2, dtype=jnp.int32)[:, None]).astype(jnp.float32)
    freq = rope_base ** (-(jnp.arange(head_dim // 2, dtype=jnp.float32) * 2.0 / head_dim))
    return position[..., None] * freq


def lookup(identity, table):
    hits = identity[:, None] == jnp.arange(table.shape[0], dtype=jnp.int32)[None, :]
    return jnp.sum(jnp.where(hits, table[None, :], 0), axis=1)


def run_down(features, tiles):
    steps_count, rows, width = features.shape
    grouped = features.reshape(steps_count, rows // 8, 8, width)
    result = jnp.einsum("sngd,ndk->sngk", grouped, tiles, preferred_element_type=jnp.float32)
    return result.reshape(steps_count, rows, tiles.shape[2])


def run_up(shrink, tiles):
    steps_count, rows, rank_width = shrink.shape
    grouped = shrink.reshape(steps_count, rows // 8, 8, rank_width)
    result = jnp.einsum("sngk,nkc->sngc", grouped, tiles, preferred_element_type=jnp.float32)
    return result.reshape(steps_count, rows, tiles.shape[2])


def attend(query, key_new, value_new, key_value_cache, lengths):
    rows = query.shape[1]
    heads = query.shape[2]
    head_dim = query.shape[3]
    kv_heads = key_value_cache.shape[1]
    group = heads // kv_heads
    grouped = query.reshape(2, rows, kv_heads, group, head_dim)
    keys = key_value_cache[..., :head_dim]
    vals = key_value_cache[..., head_dim:]
    scale = head_dim ** (-0.5)
    older = (
        jnp.einsum("srhgd,rhcd->srhgc", grouped, keys, preferred_element_type=jnp.float32) * scale
    )
    live = jnp.arange(key_value_cache.shape[2], dtype=jnp.int32)[None, :] < lengths[:, None]
    older = jnp.where(live[None, :, None, None, :], older, masked)
    fresh = (
        jnp.einsum("srhgd,trhd->srhgt", grouped, key_new, preferred_element_type=jnp.float32)
        * scale
    )
    valid = jnp.arange(2, dtype=jnp.int32)[None, :] <= jnp.arange(2, dtype=jnp.int32)[:, None]
    fresh = jnp.where(valid[:, None, None, None, :], fresh, masked)
    peak = jnp.maximum(
        jnp.max(older, axis=-1, keepdims=True), jnp.max(fresh, axis=-1, keepdims=True)
    )
    p_old = jnp.exp(older - peak)
    p_new = jnp.exp(fresh - peak)
    total = jnp.sum(p_old, axis=-1, keepdims=True) + jnp.sum(p_new, axis=-1, keepdims=True)
    w_old = p_old.astype(jnp.bfloat16)
    w_new = p_new.astype(jnp.bfloat16)
    mixed = jnp.einsum("srhgc,rhcd->srhgd", w_old, vals, preferred_element_type=jnp.float32)
    mixed = mixed + jnp.einsum(
        "srhgt,trhd->srhgd", w_new, value_new, preferred_element_type=jnp.float32
    )
    return (mixed / total).astype(jnp.bfloat16).reshape(2, rows, heads * head_dim)


def on_device(
    hidden,
    input_norm_scale,
    query_key_value_weight,
    output_weight,
    adapter_down_weight,
    adapter_up_weight,
    row_adapter_index,
    adapter_store_slot,
    lengths,
    key_value_cache,
):
    tensor_count = lax.axis_size("tensor")
    tensor_pos = lax.axis_index("tensor")
    whole = lax.all_gather(hidden, "tensor", axis=2, tiled=True)
    values = whole.astype(jnp.float32)
    scale = lax.rsqrt(jnp.mean(values * values, axis=-1, keepdims=True) + eps_norm)
    normed = (values * scale * input_norm_scale).astype(jnp.bfloat16)
    column_span = adapter_down_weight.shape[1]
    own_cols = lax.dynamic_slice_in_dim(normed, tensor_pos * column_span, column_span, 2)
    base = jnp.einsum(
        "srd,dc->src", normed, query_key_value_weight, preferred_element_type=jnp.float32
    )
    down_all, up_all = (
        lax.all_gather(adapter_down_weight, "store", axis=0, tiled=True),
        lax.all_gather(adapter_up_weight, "store", axis=0, tiled=True),
    )
    run_slots = lookup(row_adapter_index[::8], adapter_store_slot)
    partial_rank = run_down(own_cols, jnp.take(down_all, run_slots, axis=0))
    shrink = lax.psum(partial_rank, "tensor").astype(jnp.bfloat16)
    adapter_delta = run_up(shrink, jnp.take(up_all, run_slots, axis=0))
    qkv = (base + adapter_delta).astype(jnp.bfloat16)
    moved = lax.all_to_all(qkv, "tensor", split_axis=1, concat_axis=2, tiled=True)
    rows_here = moved.shape[1]
    grid = moved.reshape(2, rows_here, tensor_count, qkv.shape[2])
    q_cols = HEADS * HD // tensor_count
    query = grid[..., :q_cols].reshape(2, rows_here, HEADS, HD)
    pairs = grid[..., q_cols:].reshape(2, rows_here, 2, KVH, HD)
    angles = angles_for(lengths, HD)
    query_rot = rotate(query.astype(jnp.float32), angles).astype(jnp.bfloat16)
    key_rot = rotate(pairs[:, :, 0].astype(jnp.float32), angles).astype(jnp.bfloat16)
    context = attend(query_rot, key_rot, pairs[:, :, 1], key_value_cache, lengths)
    output = jnp.einsum(
        "srq,qc->src",
        lax.all_gather(context, "tensor", axis=1, tiled=True),
        output_weight,
        preferred_element_type=jnp.float32,
    )
    return output.astype(jnp.bfloat16)


def solution(mesh):
    in_specs = (
        P(None, ("groups", "store"), "tensor"),
        P(),
        P(None, "tensor"),
        P(None, "tensor"),
        P(("groups", "store"), "tensor", None),
        P(("groups", "store"), None, "tensor"),
        P(("groups", "store")),
        P("groups"),
        P(("groups", "store", "tensor")),
        P(("groups", "store", "tensor"), None, None, None),
    )
    out_specs = P(None, ("groups", "store"), "tensor")
    return jax.shard_map(
        on_device, mesh=mesh, in_specs=in_specs, out_specs=out_specs, check_vma=False
    )
```

profile of v0, /device:TPU:0, one launch (start us, length us, event | category | flops | bytes accessed | tf_op | source)
XLA Modules:
  0.0 581.7 jit_solution(11568611612419370934)
XLA Ops:
  6.5 0.7 all-gather.5.cloned.1.call-update
  7.3 0.7 all-gather.7.cloned.1.call-update
  8.1 0.7 all-gather.9.cloned.1.call-update
  9.1 83.3 %all-gather.5.cloned.1.call-done = bf16[2,128,8192]{2,1,0:T(8,128)(2,1)} async-done(((bf16[2,128,2048]{2,1,0:T(8,128)(2,1)}), bf16[2,128,8192]{2,1,0:T(8,128)(2,1)}) %all-gather.5.cloned.1.call-update) | async-done | bytes 4194320 | tf_op jit(solution)/shard_map/all_gather | solution.py:102
  92.4 3.3 fusion.10
  95.9 3.2 fusion.12
  99.1 125.0 %all-gather.7.cloned.1.call-done = bf16[128,64,1280]{2,1,0:T(8,128)(2,1)} async-done(((bf16[32,64,1280]{2,1,0:T(8,128)(2,1)}), bf16[128,64,1280]{2,1,0:T(8,128)(2,1)}) %all-gather.7.cloned.1.call-update) | async-done | bytes 20971536 | tf_op jit(solution)/shard_map/all_gather | solution.py:113
  224.2 7.7 %gather_fusion = bf16[16,64,1280]{2,1,0:T(8,128)(2,1)S(1)} fusion(bf16[128,64,1280]{2,1,0:T(8,128)(2,1)} %all-gather.7.cloned.1.call-done, s32[1024]{0:T(1024)S(1)} %pad_clamp_fusion), kind=kCustom, calls=%fused_computation | custom fusion | bytes 5242944 | tf_op jit(solution)/shard_map/jit(_take)/gather | solution.py:118
  231.8 195.4 %all-gather.9.cloned.1.call-done = bf16[128,2048,64]{1,2,0:T(8,128)(2,1)} async-done(((bf16[32,2048,64]{1,2,0:T(8,128)(2,1)}), bf16[128,2048,64]{1,2,0:T(8,128)(2,1)}) %all-gather.9.cloned.1.call-update) | async-done | bytes 33554448 | tf_op jit(solution)/shard_map/all_gather | solution.py:112
  427.3 5.0 gather_fusion.1
  432.3 3.7 fusion.49
  436.1 21.1 %psum.7 = bf16[2,128,64]{2,1,0:T(8,128)(2,1)S(1)} all-reduce(f32[2,128,64]{2,1,0:T(8,128)S(1)} %bitcast.120), channel_id=1, replica_groups=mesh['groups'=2,'store'=4,'tensor'=4] {'tensor'}, use_global_device_ids=true, to_apply=%region_2.3 | all-reduce | flops 16384 | bytes 98304 | tf_op jit(solution)/shard_map/psum | solution.py:117
  457.8 1.6 copy-done.2
  459.3 10.0 %fusion.26 = bf16[2,128,1280]{2,1,0:T(8,128)(2,1)S(1)} fusion(bf16[2,128,8192]{2,1,0:T(8,128)(2,1)S(1)} %copy-done.2, bf16[8192,1280]{1,0:T(8,128)(2,1)} %param.12, f32[2,16,8,1280]{3,2,0,1:T(8,128)S(1)} %convolution_bitcast_fusion), kind=kOutput, calls=%fused_computation.32 | convolution fusion | flops 5369364480 | bytes 27131904 | tf_op jit(solution)/shard_map/srd,dc->src/dot_general | solution.py:108
  469.4 1.5 copy.56
  470.9 3.5 all-to-all-start
  475.0 13.4 %all-to-all-done = bf16[2,128,1280]{2,0,1:T(2,128)(2,1)S(1)} async-done(((bf16[2,128,1280]{2,0,1:T(2,128)(2,1)}), bf16[2,128,1280]{2,0,1:T(2,128)(2,1)S(1)}, u32[]{:S(2)}, u32[]{:S(2)}) %all-to-all-start) | async-done | bytes 655392 | tf_op jit(solution)/shard_map/all_to_all | solution.py:120
  490.5 12.3 %bitcast_reduce_fusion = (f32[2,32,4,8]{3,0,2,1:T(2,128)S(1)}, f32[32,4,2,8,512]{4,3,2,1,0:T(8,128)}) fusion(pred[32,512]{1,0:T(8,128)(4,1)S(1)} %iota_compare_fusion, bf16[32,4,512,256]{3,2,1,0:T(8,128)(2,1)} %param.19, bf16[2,32,4,8,64]{4,3,2,1,0:T(8,128)(2,1)S(1)} %get-tuple-element.6, bf16[2,32,4,8,64]{4,3,2,1,0:T(8,128)(2,1)S(1)} %get-tuple-element.5), kind=kOutput, calls=%fused_computation.20 | convolution fusion | flops 272627712 | bytes 21520384 | tf_op jit(solution)/shard_map/srhgd,rhcd->srhgc/dot_general | solution.py:63
  502.8 2.7 fusion.72
  505.5 3.5 fusion.18
  509.1 7.5 %fusion.38 = f32[2,32,4,8,128]{4,3,0,2,1:T(8,128)S(1)} fusion(bf16[32,4,512,256]{3,2,1,0:T(8,128)(2,1)} %param.19, f32[32,4,2,8,512]{4,3,2,1,0:T(8,128)S(1)} %copy-done.1, f32[2,32,4,8]{3,0,2,1:T(2,128)S(1)} %max.8, pred[32,512]{1,0:T(8,128)(4,1)S(1)} %iota_compare_fusion), kind=kOutput, calls=%fused_computation.39 | convolution fusion | flops 272629760 | bytes 22044672 | tf_op jit(solution)/shard_map/srhgc,rhcd->srhgd/dot_general | solution.py:81
  517.9 1.0 reshape.133
  519.0 44.3 %all-gather.11.cloned.1.call-done = bf16[2,128,4096]{2,1,0:T(8,128)(2,1)} async-done(((bf16[2,32,4096]{2,1,0:T(8,128)(2,1)}), bf16[2,128,4096]{2,1,0:T(8,128)(2,1)}) %all-gather.11.cloned.1.call-update) | async-done | bytes 2097168 | tf_op jit(solution)/shard_map/all_gather | solution.py:132
  563.3 11.9 %fusion.29 = bf16[2,128,2048]{2,1,0:T(8,128)(2,1)} fusion(bf16[2,128,4096]{2,1,0:T(8,128)(2,1)} %all-gather.11.cloned.1.call-done, bf16[4096,2048]{1,0:T(8,128)(2,1)} %param.13), kind=kOutput, calls=%fused_computation.33 | convolution fusion | flops 4295491584 | bytes 19922944 | tf_op jit(solution)/shard_map/srq,qc->src/dot_general | solution.py:130
  (47 shorter events, 5.2 us)
Async XLA Ops:
  6.5 85.9 %all-gather.5.cloned.1.call-start = ((), (), s32[]{:S(2)}) async-start(), calls=%async_computation.1 | async-start | bytes 5242880 | tf_op jit(solution)/shard_map/all_gather | solution.py:102
  7.3 216.9 %all-gather.7.cloned.1.call-start = ((), (), s32[]{:S(2)}) async-start(), calls=%async_computation.2 | async-start | bytes 26214400 | tf_op jit(solution)/shard_map/all_gather | solution.py:113
  8.0 0.8 copy-start.5
  8.0 0.9 copy-start.6
  8.0 419.3 %all-gather.9.cloned.1.call-start = ((), (), s32[]{:S(2)}) async-start(), calls=%async_computation.3 | async-start | bytes 41943040 | tf_op jit(solution)/shard_map/all_gather | solution.py:112
  8.1 87.6 %copy-start.3 = (f32[8192]{0:T(1024)S(1)}, f32[8192]{0:T(1024)}, u32[]{:S(2)}) copy-start(f32[8192]{0:T(1024)} %param.11) | copy-start | bytes 98308
  92.4 3.4 copy-start
  457.1 2.2 copy-start.2
  459.3 15.3 %copy-start.4 = (s32[32]{0:T(128)S(1)}, s32[32]{0:T(128)}, u32[]{:S(2)}) copy-start(s32[32]{0:T(128)} %param.18) | copy-start | bytes 388
  470.9 17.5 %all-to-all-start = ((bf16[2,128,1280]{2,0,1:T(2,128)(2,1)}), bf16[2,128,1280]{2,0,1:T(2,128)(2,1)S(1)}, u32[]{:S(2)}, u32[]{:S(2)}) async-start(bf16[2,128,1280]{2,0,1:T(2,128)(2,1)} %copy.56), calls=%async_computation | async-start | bytes 1310720 | tf_op jit(solution)/shard_map/all_to_all | solution.py:120
  474.4 88.9 %all-gather.11.cloned.1.call-start = ((), (), s32[]{:S(2)}) async-start(), calls=%async_computation.4 | async-start | bytes 2621440 | tf_op jit(solution)/shard_map/all_gather | solution.py:132
  502.8 6.3 %copy-start.1 = (f32[32,4,2,8,512]{4,3,2,1,0:T(8,128)S(1)}, f32[32,4,2,8,512]{4,3,2,1,0:T(8,128)}, u32[]{:S(2)}) copy-start(f32[32,4,2,8,512]{4,3,2,1,0:T(8,128)} %get-tuple-element.14) | copy-start | bytes 12582916
Sparse Core Ops, SparseCore 0:
  8.9 83.4 all-gather.4
  94.0 130.1 all-gather.6
  225.7 201.5 all-gather.8
  519.1 44.1 all-gather.10
where the time goes:
time: 582 us
  waiting for transfers between devices  464 us (80%)
  matrix products  49.4 us (8%)
  blocking collectives  21.1 us (4%)
  local copies, waits for them, and re-layouts  18.3 us (3%)
  between operations  13.4 us (2%)
  other arithmetic  12.1 us (2%)
    all_gather x1, waiting for transfers between devices, on_device(): lax.all_gather(adapter_down_weight, 'store', axis=0, tiled=True)  195 us
    all_gather x1, waiting for transfers between devices, on_device(): lax.all_gather(adapter_up_weight, 'store', axis=0, tiled=True)  125 us
    all_gather x1, waiting for transfers between devices, on_device(): whole = lax.all_gather(hidden, 'tensor', axis=2, tiled=True)  83.3 us
    all_gather x1, waiting for transfers between devices, on_device(): lax.all_gather(context, 'tensor', axis=1, tiled=True)  44.3 us
    psum x1, blocking collectives, on_device(): shrink = lax.psum(partial_rank, 'tensor').astype(jnp.bfloat16)  21.1 us
    all_to_all x1, waiting for transfers between devices, on_device(): lax.all_to_all(qkv, 'tensor', split_axis=1, concat_axis=2, tiled=True)  13.4 us
    dot_general x1, matrix products, attend(): jnp.einsum('srhgd,rhcd->srhgc', grouped, keys, preferred_element_type=jnp...  12.3 us
    dot_general x1, matrix products, on_device(): jnp.einsum('srq,qc->src', lax.all_gather(context, 'tensor', axis=1, tiled...  11.9 us
  transfers between devices with their start and end apart: 5, of which 5 were waited for; matrix products, arithmetic and copies ran while one was open for 3% of the time, Pallas kernels for 0%

commit v1 on v0

v1 whole, which is shorter than its diff:
```python
import functools

import jax
import jax.numpy as jnp
from jax import lax
from jax.experimental import pallas as pl
from jax.experimental.pallas import tpu as pltpu
from jax.sharding import PartitionSpec as P

HEADS = 32
KVH = 4
HD = 128
GROUP = HEADS // KVH
RUN = 8
STEPS = 2
LANES = 128
HALVES = 2

eps_norm = 1e-05
rope_base = 500000.0
masked = -1e30

MIB = 1 << 20
F32 = jnp.float32
BF16 = jnp.bfloat16
VMEM = pl.BlockSpec(memory_space=pltpu.VMEM)
SMEM = pl.BlockSpec(memory_space=pltpu.SMEM)
HBM = pl.BlockSpec(memory_space=pltpu.HBM)


def swap(values, axis, distance):
    count = lax.axis_size(axis)
    return lax.ppermute(values, axis, [(i, i ^ distance) for i in range(count)])


def summed_over(values, axis):
    distance = 1
    while distance < lax.axis_size(axis):
        values = values + swap(values, axis, distance)
        distance *= 2
    return values


def base_kernel(x_ref, scale_ref, gain_ref, w_ref, out_ref, held, sems):
    owners, _, span = x_ref.shape
    tiles, depth, _ = held.shape
    copies = [
        pltpu.make_async_copy(w_ref.at[pl.ds(k * depth, depth), :], held.at[k], sems.at[k])
        for k in range(tiles)
    ]
    for copy in copies:
        copy.start()
    scale = scale_ref[...]
    for k, copy in enumerate(copies):
        owner, first = divmod(k * depth, span)
        gain = gain_ref[:, k * depth : (k + 1) * depth]
        rows = x_ref[owner, :, first : first + depth].astype(F32)
        normed = (rows * scale * gain).astype(BF16)
        copy.wait()
        product = jnp.dot(normed, held[k], preferred_element_type=F32)
        if k > 0:
            out_ref[...] += product
        else:
            out_ref[...] = product


def base_rows(x, scale, gain, weight):
    owners, rows, span = x.shape
    depth, columns = weight.shape
    tile = min(512, span)
    tiles = depth // tile
    return pl.pallas_call(
        base_kernel,
        out_shape=jax.ShapeDtypeStruct((rows, columns), F32),
        in_specs=[VMEM] * 3 + [HBM],
        out_specs=VMEM,
        scratch_shapes=[
            pltpu.VMEM((tiles, tile, columns), BF16),
            pltpu.SemaphoreType.DMA((tiles,)),
        ],
        compiler_params=pltpu.CompilerParams(vmem_limit_bytes=48 * MIB),
        cost_estimate=pl.CostEstimate(
            flops=2 * rows * depth * columns,
            bytes_accessed=2 * depth * (rows + columns) + 4 * rows * columns,
            transcendentals=0,
        ),
        name="base_rows",
    )(x, scale, gain, weight)


def shrink_kernel(place_ref, slots, x0, x1, x2, x3, scale_ref, gain_ref, down_ref, out_ref, held, sems):
    runs = held.shape[0] // 4
    pairs = runs // 2

    def fetch(n, carry):
        @pl.when(slots[n] >= 0)
        def _():
            pltpu.make_async_copy(down_ref.at[slots[n]], held.at[n], sems.at[n]).start()

        return carry

    lax.fori_loop(0, 4 * runs, fetch, 0)
    out_ref[...] = jnp.zeros_like(out_ref)
    rank = down_ref.shape[1]
    for slab, (d, x_ref) in enumerate(((0, x0), (2, x2), (1, x1), (3, x3))):
        owner = place_ref[0] ^ d
        for half in range(2):

            def one(i, carry):
                run = half * pairs + i
                n = owner * runs + run

                @pl.when(slots[n] >= 0)
                def _():
                    pltpu.make_async_copy(
                        down_ref.at[slots[n]], held.at[n], sems.at[n]
                    ).wait()
                    place = pl.ds(pl.multiple_of(run * 16, 16), 16)
                    rows = x_ref[place, :].astype(F32) * scale_ref[owner, place, :] * gain_ref[...]
                    rows = rows.astype(BF16)
                    part = lax.dot_general(
                        rows, held[n], (((1,), (1,)), ((), ())), preferred_element_type=F32
                    )
                    out_ref[
                        slab, pl.ds(pl.multiple_of(i * 16, 16), 16), half * rank : (half + 1) * rank
                    ] = part

                return carry

            lax.fori_loop(0, pairs, one, 0)


def shrink_rows(place, slots, blocks, scales, gain, down):
    rows, depth = blocks[0].shape
    rank = down.shape[1]
    runs = rows // 16
    return pl.pallas_call(
        shrink_kernel,
        out_shape=jax.ShapeDtypeStruct((4, rows // 2, 2 * rank), F32),
        in_specs=[SMEM] * 2 + [VMEM] * 6 + [HBM],
        out_specs=VMEM,
        scratch_shapes=[
            pltpu.VMEM((4 * runs, rank, depth), BF16),
            pltpu.SemaphoreType.DMA((4 * runs,)),
        ],
        compiler_params=pltpu.CompilerParams(vmem_limit_bytes=56 * MIB),
        cost_estimate=pl.CostEstimate(
            flops=2 * rows * depth * rank,
            bytes_accessed=8 * rows * depth + down.size,
            transcendentals=0,
        ),
        name="shrink_rows",
    )(place, slots, *blocks, scales, gain, down)


def grow_kernel(place_ref, slots, s_ref, up_ref, out_ref, held, sems):
    runs = held.shape[0] // 4
    pairs = runs // 2
    rank = up_ref.shape[1]

    def fetch(n, carry):
        @pl.when(slots[n] >= 0)
        def _():
            pltpu.make_async_copy(up_ref.at[slots[n]], held.at[n], sems.at[n]).start()

        return carry

    lax.fori_loop(0, 4 * runs, fetch, 0)
    for slab, d in enumerate((0, 2, 1, 3)):
        owner = place_ref[0] ^ d
        for half in range(2):

            def one(i, carry):
                run = half * pairs + i
                n = owner * runs + run
                place = pl.ds(pl.multiple_of(run * 16, 16), 16)

                @pl.when(slots[n] >= 0)
                def _():
                    pltpu.make_async_copy(up_ref.at[slots[n]], held.at[n], sems.at[n]).wait()
                    rows = s_ref[
                        slab, pl.ds(pl.multiple_of(i * 16, 16), 16), half * rank : (half + 1) * rank
                    ]
                    out_ref[slab, place, :] = jnp.dot(
                        rows, held[n], preferred_element_type=F32
                    )

                @pl.when(slots[n] < 0)
                def _():
                    out_ref[slab, place, :] = jnp.zeros((16, out_ref.shape[2]), F32)

                return carry

            lax.fori_loop(0, pairs, one, 0)


def grow_rows(place, slots, shrunk, up):
    _, pair_rows, _ = shrunk.shape
    rows = 2 * pair_rows
    rank, columns = up.shape[1:]
    runs = rows // 16
    return pl.pallas_call(
        grow_kernel,
        out_shape=jax.ShapeDtypeStruct((4, rows, columns), F32),
        in_specs=[SMEM, SMEM, VMEM, HBM],
        out_specs=VMEM,
        scratch_shapes=[
            pltpu.VMEM((4 * runs, rank, columns), BF16),
            pltpu.SemaphoreType.DMA((4 * runs,)),
        ],
        compiler_params=pltpu.CompilerParams(vmem_limit_bytes=60 * MIB),
        cost_estimate=pl.CostEstimate(
            flops=2 * rows * rank * columns,
            bytes_accessed=8 * rows * columns + up.size,
            transcendentals=0,
        ),
        name="grow_rows",
    )(place, slots, shrunk, up)


def attend_kernel(
    unit,
    first_row,
    lengths,
    order,
    qkv_ref,
    cos_ref,
    sin_ref,
    cache_ref,
    out_ref,
    queries,
    keys,
    values,
    context,
    held,
    sems,
):
    rows, _, cached, _ = held.shape
    local = STEPS * rows
    q_columns = GROUP * HD
    part = cached // 2
    scale = HD ** (-0.5)
    team = min(4, rows)

    def copy(r, b):
        span = pl.ds(b * part, part)
        return pltpu.make_async_copy(
            cache_ref.at[first_row + r, :, span, :], held.at[r, :, span, :], sems.at[r, b]
        )

    def longest(group):
        return lengths[order[group * team + team - 1]]

    def fetch(i, carry):
        r = order[i]
        copy(r, 0).start()

        @pl.when(longest(i // team) > part)
        def _():
            copy(r, 1).start()

        return carry

    lax.fori_loop(0, rows, fetch, 0)

    cosine = cos_ref[...]
    sine = sin_ref[...]

    def rotated(x):
        x = x.astype(F32)
        turned = x * cosine + pltpu.roll(x, HD // 2, 1) * sine
        return turned.astype(BF16).astype(F32)

    for k in range(KVH):
        for g in range(GROUP):
            queries[k, g * local : (g + 1) * local, :] = rotated(
                qkv_ref[k, :, g * HD : (g + 1) * HD]
            )
        place = q_columns + (k % 2) * HD
        keys[k] = rotated(qkv_ref[k // 2, :, place : place + HD])
        values[k] = qkv_ref[2 + k // 2, :, place : place + HD].astype(F32)

    early = lax.broadcasted_iota(jnp.int32, (4 * GROUP, 1), 0) % (2 * GROUP) < GROUP

    def scores(r, at, pair, span, live):
        heads = (2 * pair, 2 * pair + 1)
        query = [
            jnp.concatenate(
                [queries[k, pl.ds(at[s], GROUP, stride=local), :] for s in range(STEPS)], axis=0
            )
            for k in heads
        ]
        blank = jnp.zeros((2 * GROUP, HD), F32)
        spread = jnp.concatenate(
            [
                jnp.concatenate([query[0], blank], axis=1),
                jnp.concatenate([blank, query[1]], axis=1),
            ],
            axis=0,
        ).astype(BF16)
        old_keys = jnp.concatenate([held[r, k, :span, :HD] for k in heads], axis=1)
        old = lax.dot_general(
            spread, old_keys, (((1,), (1,)), ((), ())), preferred_element_type=F32
        )
        old = jnp.where(live, old * scale, masked)
        fresh = []
        for t in range(STEPS):
            both = jnp.concatenate(
                [
                    jnp.sum(query[i] * keys[k, pl.ds(at[t], 1), :], axis=1, keepdims=True)
                    for i, k in enumerate(heads)
                ],
                axis=0,
            )
            fresh.append(both * scale)
        fresh[1] = jnp.where(early, masked, fresh[1])
        return old, fresh

    def soften(old, fresh):
        peak = jnp.maximum(jnp.max(old, axis=1, keepdims=True), jnp.maximum(fresh[0], fresh[1]))
        p_old = jnp.exp(old - peak)
        p_new = [jnp.exp(f - peak) for f in fresh]
        total = jnp.sum(p_old, axis=1, keepdims=True) + (p_new[0] + p_new[1])
        return p_old.astype(BF16), [p.astype(BF16).astype(F32) for p in p_new], total

    def mix(r, at, pair, span, w_old, w_new, total):
        heads = (2 * pair, 2 * pair + 1)
        old_values = jnp.concatenate([held[r, k, :span, HD:] for k in heads], axis=1)
        mixed = jnp.dot(w_old, old_values, preferred_element_type=F32)
        for i, k in enumerate(heads):
            own = slice(i * 2 * GROUP, (i + 1) * 2 * GROUP)
            result = mixed[own, i * HD : (i + 1) * HD]
            for t in range(STEPS):
                result = result + w_new[t][own] * values[k, pl.ds(at[t], 1), :]
            result = result / total[own]
            for s in range(STEPS):
                context[k, pl.ds(at[s], GROUP, stride=local), :] = result[
                    s * GROUP : (s + 1) * GROUP
                ]

    def attend_team(members, span):
        jobs = []
        for r in members:
            at = [(r // unit) * (STEPS * unit) + s * unit + r % unit for s in range(STEPS)]
            live = lax.broadcasted_iota(jnp.int32, (4 * GROUP, span), 1) < lengths[r]
            for pair in range(KVH // 2):
                jobs.append((r, at, pair, scores(r, at, pair, span, live)))
        softened = [soften(*job[3]) for job in jobs]
        for (r, at, pair, _), weights in zip(jobs, softened):
            mix(r, at, pair, span, *weights)

    def each(group, carry):
        members = [order[group * team + i] for i in range(team)]
        wide = longest(group) > part
        for r in members:
            copy(r, 0).wait()

        @pl.when(wide)
        def _():
            for r in members:
                copy(r, 1).wait()
            attend_team(members, cached)

        @pl.when(jnp.logical_not(wide))
        def _():
            attend_team(members, part)

        return carry

    lax.fori_loop(0, rows // team, each, 0)
    for k in range(KVH):
        for g in range(GROUP):
            place = (k * GROUP + g) * HD
            out_ref[:, place : place + HD] = context[k, g * local : (g + 1) * local, :].astype(BF16)


def attend(lengths, order, qkv, cosine, sine, cache, first_row, unit):
    rows = lengths.shape[0]
    local = STEPS * rows
    _, kv_heads, cached, width = cache.shape
    return pl.pallas_call(
        functools.partial(attend_kernel, unit, first_row),
        out_shape=jax.ShapeDtypeStruct((local, HEADS * HD), BF16),
        in_specs=[SMEM, SMEM, VMEM, VMEM, VMEM, HBM],
        out_specs=VMEM,
        scratch_shapes=[
            pltpu.VMEM((KVH, GROUP * local, HD), F32),
            pltpu.VMEM((KVH, local, HD), F32),
            pltpu.VMEM((KVH, local, HD), F32),
            pltpu.VMEM((KVH, GROUP * local, HD), F32),
            pltpu.VMEM((rows, kv_heads, cached, width), BF16),
            pltpu.SemaphoreType.DMA((rows, 2)),
        ],
        compiler_params=pltpu.CompilerParams(vmem_limit_bytes=48 * MIB),
        cost_estimate=pl.CostEstimate(
            flops=4 * local * HEADS * HD * cached,
            bytes_accessed=2 * rows * kv_heads * cached * width,
            transcendentals=local * HEADS * cached,
        ),
        name="attend",
    )(lengths, order, qkv, cosine, sine, cache)


def out_kernel(context_ref, w_ref, out_ref, total, held, sems):
    owners, local, _ = context_ref.shape
    rows = local // STEPS
    unit = min(RUN, rows)
    tiles, depth, columns = held.shape
    copies = [
        pltpu.make_async_copy(w_ref.at[pl.ds(k * depth, depth), :], held.at[k], sems.at[k])
        for k in range(tiles)
    ]
    for copy in copies:
        copy.start()
    width = min(512, columns)
    for k, copy in enumerate(copies):
        lhs = context_ref[:, :, k * depth : (k + 1) * depth].reshape(owners * local, depth)
        copy.wait()
        for j in range(columns // width):
            span = slice(j * width, (j + 1) * width)
            product = jnp.dot(lhs, held[k, :, span], preferred_element_type=F32)
            if k > 0:
                product = total[:, span] + product
            if k < tiles - 1:
                total[:, span] = product
                continue
            block = product.reshape(owners, rows // unit, STEPS, unit, width)
            for s in range(STEPS):
                piece = block[:, :, s].reshape(owners, rows, width)
                out_ref[s, :, :, span] = piece.astype(BF16)


def project(context, weight):
    owners, local, depth = context.shape
    columns = weight.shape[1]
    tile = min(512, depth)
    rows = local // STEPS
    return pl.pallas_call(
        out_kernel,
        out_shape=jax.ShapeDtypeStruct((STEPS, owners, rows, columns), BF16),
        in_specs=[VMEM, HBM],
        out_specs=VMEM,
        scratch_shapes=[
            pltpu.VMEM((owners * local, columns), F32),
            pltpu.VMEM((depth // tile, tile, columns), BF16),
            pltpu.SemaphoreType.DMA((depth // tile,)),
        ],
        compiler_params=pltpu.CompilerParams(vmem_limit_bytes=52 * MIB),
        cost_estimate=pl.CostEstimate(
            flops=2 * owners * local * depth * columns,
            bytes_accessed=2 * depth * columns + 2 * owners * local * (depth + columns),
            transcendentals=0,
        ),
        name="project",
    )(context, weight)


def lookup(identity, table):
    hits = identity[:, None] == jnp.arange(table.shape[0], dtype=jnp.int32)[None, :]
    return jnp.sum(jnp.where(hits, table[None, :], 0), axis=1)


def ascending(lengths):
    count = lengths.shape[0]
    rows = jnp.arange(count, dtype=jnp.int32)
    keyed = lengths * count + rows
    rank = jnp.sum((keyed[None, :] < keyed[:, None]).astype(jnp.int32), axis=1)
    return jnp.sum(jnp.where(rank[:, None] == rows[None, :], rows[:, None], 0), axis=0)


def angle_tables(lengths, unit):
    steps = jnp.arange(STEPS, dtype=jnp.int32)
    position = lengths.reshape(-1, 1, unit) + steps[None, :, None]
    freq = rope_base ** (-(jnp.arange(HD // 2, dtype=F32) * 2.0 / HD))
    angles = position.reshape(-1).astype(F32)[:, None] * freq
    cosine = jnp.cos(angles)
    sine = jnp.sin(angles)
    return jnp.concatenate([cosine, cosine], 1), jnp.concatenate([-sine, sine], 1)


def on_device(
    hidden,
    input_norm_scale,
    query_key_value_weight,
    output_weight,
    adapter_down_weight,
    adapter_up_weight,
    row_adapter_index,
    adapter_store_slot,
    lengths,
    key_value_cache,
):
    tensor_count = lax.axis_size("tensor")
    tensor_pos = lax.axis_index("tensor")
    store_pos = lax.axis_index("store")
    _, rows, span = hidden.shape
    model_width = input_norm_scale.shape[0]
    rows_here = lengths.shape[0]
    unit = min(RUN, rows_here)
    halves = HALVES if rows_here % (HALVES * RUN) == 0 else 1
    part_rows = rows_here // halves
    local = STEPS * part_rows
    held_slots = adapter_down_weight.shape[0]
    rank = adapter_down_weight.shape[2]

    raw = hidden.reshape(STEPS, rows // unit, unit, span).transpose(1, 0, 2, 3)
    raw = raw.reshape(STEPS * rows, span)
    values = raw.astype(F32)
    squares = jnp.sum(values * values, axis=1)
    squares = summed_over(squares, "tensor")
    told = jnp.concatenate([squares, row_adapter_index[::RUN].astype(F32)])
    told = told.reshape(1, -1)
    told = jnp.concatenate([told, swap(told, "store", 2)], axis=0)
    told = jnp.concatenate([told, swap(told, "store", 1)], axis=0)
    told = jnp.stack([told[d] for d in (0, 2, 1, 3)])
    told = lax.dynamic_index_in_dim(
        jnp.stack([jnp.stack([told[p ^ q] for q in range(4)]) for p in range(4)]),
        store_pos,
        0,
        keepdims=False,
    )
    scales = lax.rsqrt(told[:, : STEPS * rows] / model_width + eps_norm)
    runs = told[:, STEPS * rows :].astype(jnp.int32)
    slots = lookup(runs.reshape(-1), adapter_store_slot).reshape(runs.shape)
    slots = jnp.where(slots // held_slots == store_pos, slots % held_slots, -1)
    place = store_pos.reshape(1).astype(jnp.int32)
    gains = input_norm_scale.reshape(1, -1)
    gain = lax.dynamic_slice_in_dim(gains, tensor_pos * span, span, 1)
    scales = scales.reshape(-1, tensor_count, halves, local)
    raw = raw.reshape(tensor_count, halves, local, span)

    down = jnp.swapaxes(adapter_down_weight, 1, 2)
    results = []
    context = None
    for h in range(halves):
        own = raw[:, h].reshape(tensor_count * local, span)
        count = own.shape[0]
        part_scales = scales[:, :, h].reshape(-1, count, 1)
        own_scale = lax.dynamic_index_in_dim(part_scales, store_pos, 0, keepdims=False)

        across = swap(own, "store", 2)
        beside = swap(own, "store", 1)
        diagonal = swap(across, "store", 1)

        everything = lax.all_gather(own, "tensor", axis=0, tiled=False)
        if context is not None:
            everything, context = lax.optimization_barrier((everything, context))
        total = base_rows(everything, own_scale, gains, query_key_value_weight)

        mine = slots.reshape(4, -1, halves, max(1, part_rows // RUN))[:, :, h].reshape(-1)
        partial = shrink_rows(
            place, mine, (own, beside, across, diagonal), part_scales, gain, down
        )
        pair = partial[:2] + swap(partial[2:], "store", 1)
        shrunk = pair[0] + swap(pair[1], "store", 2)
        shrunk = summed_over(shrunk, "tensor")
        shrunk = shrunk.astype(BF16)
        pair = jnp.stack([shrunk, swap(shrunk, "store", 2)])
        shrunk = jnp.concatenate([pair, swap(pair, "store", 1)], axis=0)
        grown = grow_rows(place, mine, shrunk, adapter_up_weight)
        pair = grown[:2] + swap(grown[2:], "store", 1)
        delta = pair[0] + swap(pair[1], "store", 2)

        qkv = (total + delta).astype(BF16)
        qkv = qkv.reshape(tensor_count, local, -1)
        moved = lax.all_to_all(qkv, "tensor", split_axis=0, concat_axis=0, tiled=True)
        if tensor_count != 4:
            q_columns = HEADS * HD // tensor_count
            parts = []
            for piece in (moved[..., :q_columns], moved[..., q_columns:]):
                joined = piece.transpose(1, 0, 2).reshape(local, 4, -1)
                parts.append(joined.transpose(1, 0, 2))
            moved = jnp.concatenate(parts, axis=2)

        here = lengths[h * part_rows : (h + 1) * part_rows]
        cosine, sine = angle_tables(here, unit)
        context = attend(
            here, ascending(here), moved, cosine, sine, key_value_cache, h * part_rows, unit
        )

        everything = lax.all_gather(context, "tensor", axis=0, tiled=False)
        if part_rows % RUN == 0:
            result = project(everything, output_weight)
        else:
            everything = everything.reshape(-1, HEADS * HD)
            result = jnp.dot(everything, output_weight, preferred_element_type=F32).astype(BF16)
            result = result.reshape(tensor_count, part_rows // unit, STEPS, unit, -1)
            result = result.transpose(2, 0, 1, 3, 4).reshape(STEPS, tensor_count, part_rows, -1)
        results.append(result)
    output = results[0] if halves == 1 else jnp.concatenate(results, axis=2)
    return output.reshape(STEPS, rows, -1)


def solution(mesh):
    in_specs = (
        P(None, ("groups", "store"), "tensor"),
        P(),
        P(None, "tensor"),
        P(None, "tensor"),
        P(("groups", "store"), "tensor", None),
        P(("groups", "store"), None, "tensor"),
        P(("groups", "store")),
        P("groups"),
        P(("groups", "store", "tensor")),
        P(("groups", "store", "tensor"), None, None, None),
    )
    out_specs = P(None, ("groups", "store"), "tensor")
    return jax.shard_map(
        on_device, mesh=mesh, in_specs=in_specs, out_specs=out_specs, check_vma=False
    )
```

time: 582 us -> 236 us (0.41)
  waiting for transfers between devices: 464 us -> 83.3 us
  Pallas kernels: 0 us -> 63.5 us
  matrix products: 49.4 us -> 0 us
  starting transfers between devices: 3.78 us -> 40.9 us
  blocking collectives: 21.1 us -> 0 us
    all_gather x4, waiting for transfers between devices: 448 us -> 19.6 us  [the longest x2 19.5 us: on_device(): everything = lax.all_gather(context, 'tensor', axis=0, tiled=False)]
    pallas_call x0 -> x10, Pallas kernels: none -> 63.5 us  [the longest x2 15.4 us: base_rows(): pl.pallas_call(base_kernel, out_shape=jax.ShapeDtypeStruct((rows, columns...]
    dot_general x8 -> x0, matrix products: 49.4 us -> none  [the longest x1 12.3 us: attend(): jnp.einsum('srhgd,rhcd->srhgc', grouped, keys, preferred_element_type=jnp...]
    ppermute x0 -> x26, waiting for transfers between devices: none -> 36.7 us  [swap(): return lax.ppermute(values, axis, [(i, i ^ distance) for i in range(count)])]
    ppermute x0 -> x26, starting transfers between devices: none -> 31.8 us  [swap(): return lax.ppermute(values, axis, [(i, i ^ distance) for i in range(count)])]
    psum x1 -> x0, blocking collectives: 21.1 us -> none  [on_device(): shrink = lax.psum(partial_rank, 'tensor').astype(jnp.bfloat16)]
    all_to_all x1 -> x2, waiting for transfers between devices: 13.4 us -> 27 us  [on_device(): lax.all_to_all(qkv, 'tensor', split_axis=0, concat_axis=0, tiled=True)]
    gather x2 -> x0, local copies, waits for them, and re-layouts: 12.7 us -> none  [the longest x1 7.68 us: on_device(): adapter_delta = run_up(shrink, jnp.take(up_all, run_slots, axis=0))]
  transfers between devices with their start and end apart: 5 -> 32, of which waited for: 5 -> 16; matrix products, arithmetic and copies ran while one was open for 3% -> 9% of each run, Pallas kernels for 0% -> 24%
where the time goes in v1:
time: 236 us; the launch traced here: 234 us
  waiting for transfers between devices  83.3 us (35%)
  Pallas kernels  63.5 us (27%)
  starting transfers between devices  40.9 us (17%)
  local copies, waits for them, and re-layouts  22.4 us (9%)
  between operations  13.5 us (6%)
  other arithmetic  10.5 us (4%)
    ppermute x26, waiting for transfers between devices, swap(): return lax.ppermute(values, axis, [(i, i ^ distance) for i in range(count)])  36.7 us
    ppermute x26, starting transfers between devices, swap(): return lax.ppermute(values, axis, [(i, i ^ distance) for i in range(count)])  31.8 us
    all_to_all x2, waiting for transfers between devices, on_device(): lax.all_to_all(qkv, 'tensor', split_axis=0, concat_axis=0, tiled=True)  27 us
    all_gather x2, waiting for transfers between devices, on_device(): everything = lax.all_gather(context, 'tensor', axis=0, tiled=False)  19.5 us
    pallas_call x2, Pallas kernels, base_rows(): pl.pallas_call(base_kernel, out_shape=jax.ShapeDtypeStruct((rows, columns...  15.4 us
    pallas_call x2, Pallas kernels, attend(): pl.pallas_call(functools.partial(attend_kernel, unit, first_row), out_sha...  14.2 us
    pallas_call x2, Pallas kernels, project(): pl.pallas_call(out_kernel, out_shape=jax.ShapeDtypeStruct((STEPS, owners,...  12.9 us
    pallas_call x2, Pallas kernels, shrink_rows(): pl.pallas_call(shrink_kernel, out_shape=jax.ShapeDtypeStruct((4, rows //...  10.6 us
  transfers between devices with their start and end apart: 32, of which 16 were waited for; matrix products, arithmetic and copies ran while one was open for 9% of the time, Pallas kernels for 24%

profile of v1, /device:TPU:0, one launch (start us, length us, event | category | flops | bytes accessed | tf_op | source)
XLA Modules:
  0.0 234.2 jit_solution(16434726594201987338)
XLA Ops:
  9.3 3.1 %collective-permute-start = (f32[256]{0:T(256)S(1)}, f32[256]{0:T(256)S(1)}, u32[]{:S(2)}, u32[]{:S(2)}) collective-permute-start(f32[256]{0:T(256)S(1)} %reduce_sum.59), channel_id=1, source_target_pairs={{0,1},{1,0},{2,3},{3,2},{4,5},{5,4},{6,7},{7,6},{8,9},{9,8},{10,11... | collective-permute-start | bytes 3080 | tf_op jit(solution)/shard_map/ppermute | solution.py:33
  14.0 3.0 %collective-permute-start.1 = (f32[256]{0:T(256)S(1)}, f32[256]{0:T(256)S(1)}, u32[]{:S(2)}, u32[]{:S(2)}) collective-permute-start(f32[256]{0:T(256)S(1)} %add.122), channel_id=1, source_target_pairs={{0,2},{1,3},{2,0},{3,1},{4,6},{5,7},{6,4},{7,5},{8,10},{9,11},{10,... | collective-permute-start | bytes 3080 | tf_op jit(solution)/shard_map/ppermute | solution.py:33
  25.4 11.9 %collective-permute-done.5.x2 = bf16[128,2048]{1,0:T(8,128)(2,1)S(1)} collective-permute-done((bf16[128,2048]{1,0:T(8,128)(2,1)}, bf16[128,2048]{1,0:T(8,128)(2,1)S(1)}, u32[]{:S(2)}, u32[]{:S(2)}) %collective-permute-start.5) | collective-permute-done | bytes 524320 | tf_op jit(solution)/shard_map/ppermute | solution.py:33
  40.5 5.6 %shrink_rows.2 = f32[4,64,128]{2,1,0:T(8,128)} custom-call(s32[1]{0:T(128)} %bitcast.12.place_ref, s32[32]{0:T(128)} %reshape_squeeze.19.slots, bf16[128,2048]{1,0:T(8,128)(2,1)} %bitcast.81, bf16[128,2048]{1,0:T(8,128)(2,1)} %copy-done.13, bf16[128,2048]{1,0:T(8,128)(2,1)} %copy-done.12, bf16[128,2048]{1,0:T(8,128)(2,1)} %copy-done.16, ...), custom_call_target="tpu_custom_call" | custom-call | flops 33554432 | bytes 6291456 | tf_op jit(solution)/shard_map/shrink_rows/pallas_call | solution.py:137
  55.4 5.0 %shrink_rows.3 = f32[4,64,128]{2,1,0:T(8,128)} custom-call(s32[1]{0:T(128)} %bitcast.12.place_ref, s32[32]{0:T(128)} %reshape_squeeze.22.slots, bf16[128,2048]{1,0:T(8,128)(2,1)} %bitcast.77, bf16[128,2048]{1,0:T(8,128)(2,1)} %copy-done.14, bf16[128,2048]{1,0:T(8,128)(2,1)} %copy-done.11, bf16[128,2048]{1,0:T(8,128)(2,1)} %copy-done.15, ...), custom_call_target="tpu_custom_call" | custom-call | flops 33554432 | bytes 6291456 | tf_op jit(solution)/shard_map/shrink_rows/pallas_call | solution.py:137
  66.8 2.6 %collective-permute-start.10 = (f32[64,128]{1,0:T(8,128)S(1)}, f32[64,128]{1,0:T(8,128)S(1)}, u32[]{:S(2)}, u32[]{:S(2)}) collective-permute-start(f32[64,128]{1,0:T(8,128)S(1)} %add.131), channel_id=1, source_target_pairs={{0,2},{1,3},{2,0},{3,1},{4,6},{5,7},{6,4},{7,5},{8,10},{9,11},{10,... | collective-permute-start | bytes 98312 | tf_op jit(solution)/shard_map/ppermute | solution.py:33
  70.2 3.0 %collective-permute-done.10 = f32[64,128]{1,0:T(8,128)S(1)} collective-permute-done((f32[64,128]{1,0:T(8,128)S(1)}, f32[64,128]{1,0:T(8,128)S(1)}, u32[]{:S(2)}, u32[]{:S(2)}) %collective-permute-start.10) | collective-permute-done | bytes 32800 | tf_op jit(solution)/shard_map/ppermute | solution.py:33
  79.6 5.4 %grow_rows.2 = f32[4,128,1280]{2,1,0:T(8,128)} custom-call(s32[1]{0:T(128)} %bitcast.12.place_ref, s32[32]{0:T(128)} %reshape_squeeze.19.slots, bf16[4,64,128]{2,1,0:T(8,128)(2,1)} %pad_maximum_fusion.1.s_ref, bf16[32,64,1280]{2,1,0:T(8,128)(2,1)} %up_ref.3), custom_call_target="tpu_custom_call" | custom-call | flops 20971520 | bytes 3932160 | tf_op jit(solution)/shard_map/grow_rows/pallas_call | solution.py:202
  87.8 3.7 %collective-permute-start.21 = (f32[64,128]{1,0:T(8,128)S(1)}, f32[64,128]{1,0:T(8,128)S(1)}, u32[]{:S(2)}, u32[]{:S(2)}) collective-permute-start(f32[64,128]{1,0:T(8,128)S(1)} %add.143), channel_id=1, source_target_pairs={{0,2},{1,3},{2,0},{3,1},{4,6},{5,7},{6,4},{7,5},{8,10},{9,11},{10,... | collective-permute-start | bytes 98312 | tf_op jit(solution)/shard_map/ppermute | solution.py:33
  91.6 3.5 %collective-permute-done.21 = f32[64,128]{1,0:T(8,128)S(1)} collective-permute-done((f32[64,128]{1,0:T(8,128)S(1)}, f32[64,128]{1,0:T(8,128)S(1)}, u32[]{:S(2)}, u32[]{:S(2)}) %collective-permute-start.21) | collective-permute-done | bytes 32800 | tf_op jit(solution)/shard_map/ppermute | solution.py:33
  100.7 5.1 %grow_rows.3 = f32[4,128,1280]{2,1,0:T(8,128)} custom-call(s32[1]{0:T(128)} %bitcast.12.place_ref, s32[32]{0:T(128)} %reshape_squeeze.22.slots, bf16[4,64,128]{2,1,0:T(8,128)(2,1)} %pad_maximum_fusion.2.s_ref, bf16[32,64,1280]{2,1,0:T(8,128)(2,1)} %up_ref.3), custom_call_target="tpu_custom_call" | custom-call | flops 20971520 | bytes 3932160 | tf_op jit(solution)/shard_map/grow_rows/pallas_call | solution.py:202
  105.8 2.6 %slice.155 = f32[2,128,1280]{2,1,0:T(8,128)} slice(f32[4,128,1280]{2,1,0:T(8,128)} %grow_rows.3), slice={[2:4], [0:128], [0:1280]} | slice | bytes 2621440 | tf_op jit(solution)/shard_map/slice | solution.py:561
  116.4 7.6 %base_rows.2 = f32[128,1280]{1,0:T(8,128)S(1)} custom-call(bf16[4,128,2048]{2,1,0:T(8,128)(2,1)S(1)} %copy-done, f32[128,1]{1,0:T(8,128)S(1)} %copy.32.scale_ref, f32[1,8192]{1,0:T(1,128)S(1)} %bitcast.70, bf16[8192,1280]{1,0:T(8,128)(2,1)} %w_ref.6), custom_call_target="tpu_custom_call" | custom-call | flops 2684354560 | bytes 23724032 | tf_op jit(solution)/shard_map/base_rows/pallas_call | solution.py:72
  124.0 4.7 %collective-permute-done.14 = f32[128,1280]{1,0:T(8,128)S(1)} collective-permute-done((f32[128,1280]{1,0:T(8,128)S(1)}, f32[128,1280]{1,0:T(8,128)S(1)}, u32[]{:S(2)}, u32[]{:S(2)}) %collective-permute-start.14) | collective-permute-done | bytes 655392 | tf_op jit(solution)/shard_map/ppermute | solution.py:33
  129.5 5.3 %all-to-all-start = ((bf16[4,32,1280]{2,1,0:T(8,128)(2,1)}), bf16[4,32,1280]{2,1,0:T(8,128)(2,1)S(1)}, u32[]{:S(2)}, u32[]{:S(2)}) async-start(bf16[4,32,1280]{2,1,0:T(8,128)(2,1)} %bitcast.22), calls=%async_computation | async-start | bytes 655360 | tf_op jit(solution)/shard_map/all_to_all | solution.py:566
  136.0 8.5 %all-to-all-done.qkv_ref = bf16[4,32,1280]{2,1,0:T(8,128)(2,1)S(1)} async-done(((bf16[4,32,1280]{2,1,0:T(8,128)(2,1)}), bf16[4,32,1280]{2,1,0:T(8,128)(2,1)S(1)}, u32[]{:S(2)}, u32[]{:S(2)}) %all-to-all-start) | async-done | bytes 327712 | tf_op jit(solution)/shard_map/all_to_all | solution.py:566
  144.5 6.8 %attend.2 = bf16[32,4096]{1,0:T(8,128)(2,1)} custom-call(s32[16]{0:T(128)S(1)} %get-tuple-element.31.lengths, s32[16]{0:T(128)S(1)} %select_reduce_fusion.2.order, bf16[4,32,1280]{2,1,0:T(8,128)(2,1)S(1)} %all-to-all-done.qkv_ref, f32[32,128]{1,0:T(8,128)S(1)} %get-tuple-element.32.cos_ref, f32[32,128]{1,0:T(8,128)S(1)} %get-tuple-element.33.sin_ref, ...), custom_call_target="tpu_custom_call" | custom-call | flops 268435456 | bytes 16777216 | tf_op jit(solution)/shard_map/attend/pallas_call | solution.py:381
  153.0 7.8 %base_rows.3 = f32[128,1280]{1,0:T(8,128)S(1)} custom-call(bf16[4,128,2048]{2,1,0:T(8,128)(2,1)S(1)} %copy-done.1, f32[128,1]{1,0:T(8,128)S(1)} %copy.34.scale_ref, f32[1,8192]{1,0:T(1,128)S(1)} %bitcast.71, bf16[8192,1280]{1,0:T(8,128)(2,1)} %w_ref.6), custom_call_target="tpu_custom_call" | custom-call | flops 2684354560 | bytes 23724032 | tf_op jit(solution)/shard_map/base_rows/pallas_call | solution.py:72
  161.7 3.5 %all-to-all-start.1 = ((bf16[4,32,1280]{2,1,0:T(8,128)(2,1)}), bf16[4,32,1280]{2,1,0:T(8,128)(2,1)S(1)}, u32[]{:S(2)}, u32[]{:S(2)}) async-start(bf16[4,32,1280]{2,1,0:T(8,128)(2,1)} %bitcast.33), calls=%async_computation.1 | async-start | bytes 655360 | tf_op jit(solution)/shard_map/all_to_all | solution.py:566
  165.8 18.5 %all-to-all-done.1.qkv_ref = bf16[4,32,1280]{2,1,0:T(8,128)(2,1)S(1)} async-done(((bf16[4,32,1280]{2,1,0:T(8,128)(2,1)}), bf16[4,32,1280]{2,1,0:T(8,128)(2,1)S(1)}, u32[]{:S(2)}, u32[]{:S(2)}) %all-to-all-start.1) | async-done | bytes 327712 | tf_op jit(solution)/shard_map/all_to_all | solution.py:566
  184.2 7.4 %attend.3 = bf16[32,4096]{1,0:T(8,128)(2,1)} custom-call(s32[16]{0:T(128)S(1)} %get-tuple-element.30.lengths, s32[16]{0:T(128)S(1)} %select_reduce_fusion.1.order, bf16[4,32,1280]{2,1,0:T(8,128)(2,1)S(1)} %all-to-all-done.1.qkv_ref, f32[32,128]{1,0:T(8,128)S(1)} %get-tuple-element.34.cos_ref, f32[32,128]{1,0:T(8,128)S(1)} %get-tuple-element.35.sin_ref, ...), custom_call_target="tpu_custom_call" | custom-call | flops 268435456 | bytes 16777216 | tf_op jit(solution)/shard_map/attend/pallas_call | solution.py:381
  192.9 6.5 %project.2 = bf16[2,4,16,2048]{3,2,1,0:T(8,128)(2,1)S(1)} custom-call(bf16[4,32,4096]{2,1,0:T(8,128)(2,1)S(1)} %bitcast.68, bf16[4096,2048]{1,0:T(8,128)(2,1)} %w_ref.7), custom_call_target="tpu_custom_call" | custom-call | flops 2147483648 | bytes 18350080 | tf_op jit(solution)/shard_map/project/pallas_call | solution.py:438
  199.5 19.5 %all-gather.13.cloned.1.call-done = bf16[128,4096]{1,0:T(8,128)(2,1)} async-done(((bf16[32,4096]{1,0:T(8,128)(2,1)}), bf16[128,4096]{1,0:T(8,128)(2,1)}) %all-gather.13.cloned.1.call-update) | async-done | bytes 1048592 | tf_op jit(solution)/shard_map/all_gather | solution.py:581
  220.2 6.4 %project.3 = bf16[2,4,16,2048]{3,2,1,0:T(8,128)(2,1)S(1)} custom-call(bf16[4,32,4096]{2,1,0:T(8,128)(2,1)S(1)} %bitcast.69, bf16[4096,2048]{1,0:T(8,128)(2,1)} %w_ref.7), custom_call_target="tpu_custom_call" | custom-call | flops 2147483648 | bytes 18350080 | tf_op jit(solution)/shard_map/project/pallas_call | solution.py:438
  (169 shorter events, 63.6 us)
Async XLA Ops:
  6.5 108.3 %all-gather.7.cloned.1.call-start = ((), (), s32[]{:S(2)}) async-start(), calls=%async_computation.2 | async-start | bytes 2621440 | tf_op jit(solution)/shard_map/all_gather | solution.py:545
  8.9 142.6 %all-gather.9.cloned.1.call-start = ((), (), s32[]{:S(2)}) async-start(), calls=%async_computation.3 | async-start | bytes 2621440 | tf_op jit(solution)/shard_map/all_gather | solution.py:545
  9.3 4.6 %collective-permute-start = (f32[256]{0:T(256)S(1)}, f32[256]{0:T(256)S(1)}, u32[]{:S(2)}, u32[]{:S(2)}) collective-permute-start(f32[256]{0:T(256)S(1)} %reduce_sum.59), channel_id=1, source_target_pairs={{0,1},{1,0},{2,3},{3,2},{4,5},{5,4},{6,7},{7,6},{8,9},{9,8},{10,11... | collective-permute-start | bytes 3080 | tf_op jit(solution)/shard_map/ppermute | solution.py:33
  14.0 4.6 %collective-permute-start.1 = (f32[256]{0:T(256)S(1)}, f32[256]{0:T(256)S(1)}, u32[]{:S(2)}, u32[]{:S(2)}) collective-permute-start(f32[256]{0:T(256)S(1)} %add.122), channel_id=1, source_target_pairs={{0,2},{1,3},{2,0},{3,1},{4,6},{5,7},{6,4},{7,5},{8,10},{9,11},{10,... | collective-permute-start | bytes 3080 | tf_op jit(solution)/shard_map/ppermute | solution.py:33
  22.3 15.0 %collective-permute-start.5 = (bf16[128,2048]{1,0:T(8,128)(2,1)}, bf16[128,2048]{1,0:T(8,128)(2,1)S(1)}, u32[]{:S(2)}, u32[]{:S(2)}) collective-permute-start(bf16[128,2048]{1,0:T(8,128)(2,1)} %bitcast.79), channel_id=1, source_target_pairs={{0,8},{4,12},{8,0},{12,4},{1,9},{5,13},{9,1},{13,5},{2,10},{6,14},... | collective-permute-start | bytes 1572872 | tf_op jit(solution)/shard_map/ppermute | solution.py:33
  24.2 15.3 %collective-permute-start.4 = (bf16[128,2048]{1,0:T(8,128)(2,1)}, bf16[128,2048]{1,0:T(8,128)(2,1)S(1)}, u32[]{:S(2)}, u32[]{:S(2)}) collective-permute-start(bf16[128,2048]{1,0:T(8,128)(2,1)} %bitcast.80), channel_id=1, source_target_pairs={{0,4},{4,0},{8,12},{12,8},{1,5},{5,1},{9,13},{13,9},{2,6},{6,2},{1... | collective-permute-start | bytes 1572872 | tf_op jit(solution)/shard_map/ppermute | solution.py:33
  24.3 24.3 %collective-permute-start.16 = (bf16[128,2048]{1,0:T(8,128)(2,1)S(1)}, bf16[128,2048]{1,0:T(8,128)(2,1)S(1)}, u32[]{:S(2)}, u32[]{:S(2)}) collective-permute-start(bf16[128,2048]{1,0:T(8,128)(2,1)S(1)} %bitcast.74), channel_id=1, source_target_pairs={{0,8},{4,12},{8,0},{12,4},{1,9},{5,13},{9,1},{13,5},{2,10},{6,14},... | collective-permute-start | bytes 1572872 | tf_op jit(solution)/shard_map/ppermute | solution.py:33
  48.6 5.2 %collective-permute-start.15 = (bf16[128,2048]{1,0:T(8,128)(2,1)S(1)}, bf16[128,2048]{1,0:T(8,128)(2,1)S(1)}, u32[]{:S(2)}, u32[]{:S(2)}) collective-permute-start(bf16[128,2048]{1,0:T(8,128)(2,1)S(1)} %bitcast.75), channel_id=1, source_target_pairs={{0,4},{4,0},{8,12},{12,8},{1,5},{5,1},{9,13},{13,9},{2,6},{6,2},{1... | collective-permute-start | bytes 1572872 | tf_op jit(solution)/shard_map/ppermute | solution.py:33
  48.7 5.2 %collective-permute-start.17 = (bf16[128,2048]{1,0:T(8,128)(2,1)S(1)}, bf16[128,2048]{1,0:T(8,128)(2,1)S(1)}, u32[]{:S(2)}, u32[]{:S(2)}) collective-permute-start(bf16[128,2048]{1,0:T(8,128)(2,1)S(1)} %collective-permute-done.16.x2), channel_id=1, source_target_pairs={{0,4},{4,0},{8,12},{12,8},{1,5},{5,1},{9,13},{13,9},{2,6},{6,2},{1... | collective-permute-start | bytes 1572872 | tf_op jit(solution)/shard_map/ppermute | solution.py:33
  50.3 12.4 %collective-permute-start.8 = (f32[64,128]{1,0:T(8,128)S(1)}, f32[64,128]{1,0:T(8,128)S(1)}, u32[]{:S(2)}, u32[]{:S(2)}) collective-permute-start(f32[64,128]{1,0:T(8,128)S(1)} %slice_bitcast_fusion.6), channel_id=1, source_target_pairs={{0,8},{4,12},{8,0},{12,4},{1,9},{5,13},{9,1},{13,5},{2,10},{6,14},... | collective-permute-start | bytes 98312 | tf_op jit(solution)/shard_map/ppermute | solution.py:33
  61.2 8.1 %collective-permute-start.18 = (f32[2,64,128]{2,1,0:T(8,128)S(1)}, f32[2,64,128]{2,1,0:T(8,128)S(1)}, u32[]{:S(2)}, u32[]{:S(2)}) collective-permute-start(f32[2,64,128]{2,1,0:T(8,128)S(1)} %slice.151), channel_id=1, source_target_pairs={{0,4},{4,0},{8,12},{12,8},{1,5},{5,1},{9,13},{13,9},{2,6},{6,2},{1... | collective-permute-start | bytes 196616 | tf_op jit(solution)/shard_map/ppermute | solution.py:33
  62.8 4.0 %collective-permute-start.9 = (f32[64,128]{1,0:T(8,128)S(1)}, f32[64,128]{1,0:T(8,128)S(1)}, u32[]{:S(2)}, u32[]{:S(2)}) collective-permute-start(f32[64,128]{1,0:T(8,128)S(1)} %fusion.7), channel_id=1, source_target_pairs={{0,1},{1,0},{2,3},{3,2},{4,5},{5,4},{6,7},{7,6},{8,9},{9,8},{10,11... | collective-permute-start | bytes 98312 | tf_op jit(solution)/shard_map/ppermute | solution.py:33
  66.8 6.5 %collective-permute-start.10 = (f32[64,128]{1,0:T(8,128)S(1)}, f32[64,128]{1,0:T(8,128)S(1)}, u32[]{:S(2)}, u32[]{:S(2)}) collective-permute-start(f32[64,128]{1,0:T(8,128)S(1)} %add.131), channel_id=1, source_target_pairs={{0,2},{1,3},{2,0},{3,1},{4,6},{5,7},{6,4},{7,5},{8,10},{9,11},{10,... | collective-permute-start | bytes 98312 | tf_op jit(solution)/shard_map/ppermute | solution.py:33
  74.7 3.9 %collective-permute-start.19 = (f32[64,128]{1,0:T(8,128)S(1)}, f32[64,128]{1,0:T(8,128)S(1)}, u32[]{:S(2)}, u32[]{:S(2)}) collective-permute-start(f32[64,128]{1,0:T(8,128)S(1)} %slice_bitcast_fusion.4), channel_id=1, source_target_pairs={{0,8},{4,12},{8,0},{12,4},{1,9},{5,13},{9,1},{13,5},{2,10},{6,14},... | collective-permute-start | bytes 98312 | tf_op jit(solution)/shard_map/ppermute | solution.py:33
  78.6 9.2 %collective-permute-start.20 = (f32[64,128]{1,0:T(8,128)S(1)}, f32[64,128]{1,0:T(8,128)S(1)}, u32[]{:S(2)}, u32[]{:S(2)}) collective-permute-start(f32[64,128]{1,0:T(8,128)S(1)} %fusion.6), channel_id=1, source_target_pairs={{0,1},{1,0},{2,3},{3,2},{4,5},{5,4},{6,7},{7,6},{8,9},{9,8},{10,11... | collective-permute-start | bytes 98312 | tf_op jit(solution)/shard_map/ppermute | solution.py:33
  87.5 22.3 %collective-permute-start.13 = (f32[2,128,1280]{2,1,0:T(8,128)}, f32[2,128,1280]{2,1,0:T(8,128)}, u32[]{:S(2)}, u32[]{:S(2)}) collective-permute-start(f32[2,128,1280]{2,1,0:T(8,128)} %slice.144), channel_id=1, source_target_pairs={{0,4},{4,0},{8,12},{12,8},{1,5},{5,1},{9,13},{13,9},{2,6},{6,2},{1... | collective-permute-start | bytes 3932168 | tf_op jit(solution)/shard_map/ppermute | solution.py:33
  87.8 7.3 %collective-permute-start.21 = (f32[64,128]{1,0:T(8,128)S(1)}, f32[64,128]{1,0:T(8,128)S(1)}, u32[]{:S(2)}, u32[]{:S(2)}) collective-permute-start(f32[64,128]{1,0:T(8,128)S(1)} %add.143), channel_id=1, source_target_pairs={{0,2},{1,3},{2,0},{3,1},{4,6},{5,7},{6,4},{7,5},{8,10},{9,11},{10,... | collective-permute-start | bytes 98312 | tf_op jit(solution)/shard_map/ppermute | solution.py:33
  108.4 4.8 %collective-permute-start.24 = (f32[2,128,1280]{2,1,0:T(8,128)}, f32[2,128,1280]{2,1,0:T(8,128)}, u32[]{:S(2)}, u32[]{:S(2)}) collective-permute-start(f32[2,128,1280]{2,1,0:T(8,128)} %slice.155), channel_id=1, source_target_pairs={{0,4},{4,0},{8,12},{12,8},{1,5},{5,1},{9,13},{13,9},{2,6},{6,2},{1... | collective-permute-start | bytes 3932168 | tf_op jit(solution)/shard_map/ppermute | solution.py:33
  111.6 17.1 %collective-permute-start.14 = (f32[128,1280]{1,0:T(8,128)S(1)}, f32[128,1280]{1,0:T(8,128)S(1)}, u32[]{:S(2)}, u32[]{:S(2)}) collective-permute-start(f32[128,1280]{1,0:T(8,128)S(1)} %slice_bitcast_fusion.2), channel_id=1, source_target_pairs={{0,8},{4,12},{8,0},{12,4},{1,9},{5,13},{9,1},{13,5},{2,10},{6,14},... | collective-permute-start | bytes 1966088 | tf_op jit(solution)/shard_map/ppermute | solution.py:33
  129.5 14.9 %all-to-all-start = ((bf16[4,32,1280]{2,1,0:T(8,128)(2,1)}), bf16[4,32,1280]{2,1,0:T(8,128)(2,1)S(1)}, u32[]{:S(2)}, u32[]{:S(2)}) async-start(bf16[4,32,1280]{2,1,0:T(8,128)(2,1)} %bitcast.22), calls=%async_computation | async-start | bytes 655360 | tf_op jit(solution)/shard_map/all_to_all | solution.py:566
  134.9 56.8 %all-gather.11.cloned.1.call-start = ((), (), s32[]{:S(2)}) async-start(), calls=%async_computation.4 | async-start | bytes 1310720 | tf_op jit(solution)/shard_map/all_gather | solution.py:581
  134.9 25.9 %collective-permute-start.25 = (f32[128,1280]{1,0:T(8,128)S(1)}, f32[128,1280]{1,0:T(8,128)S(1)}, u32[]{:S(2)}, u32[]{:S(2)}) collective-permute-start(f32[128,1280]{1,0:T(8,128)S(1)} %slice_bitcast_fusion), channel_id=1, source_target_pairs={{0,8},{4,12},{8,0},{12,4},{1,9},{5,13},{9,1},{13,5},{2,10},{6,14},... | collective-permute-start | bytes 1966088 | tf_op jit(solution)/shard_map/ppermute | solution.py:33
  161.7 22.6 %all-to-all-start.1 = ((bf16[4,32,1280]{2,1,0:T(8,128)(2,1)}), bf16[4,32,1280]{2,1,0:T(8,128)(2,1)S(1)}, u32[]{:S(2)}, u32[]{:S(2)}) async-start(bf16[4,32,1280]{2,1,0:T(8,128)(2,1)} %bitcast.33), calls=%async_computation.1 | async-start | bytes 655360 | tf_op jit(solution)/shard_map/all_to_all | solution.py:566
  165.1 53.8 %all-gather.13.cloned.1.call-start = ((), (), s32[]{:S(2)}) async-start(), calls=%async_computation.5 | async-start | bytes 1310720 | tf_op jit(solution)/shard_map/all_gather | solution.py:581
  (28 other events, 168.1 us)
Sparse Core Ops, SparseCore 0:
  9.0 48.6 all-gather.6
  59.2 47.2 all-gather.8
  151.4 34.6 all-gather.10
  191.8 27.1 all-gather.12

commit v2 on v1

--- a/solution.py
+++ b/solution.py
@@ -33,12 +33,81 @@
     return lax.ppermute(values, axis, [(i, i ^ distance) for i in range(count)])
 
 
-def summed_over(values, axis):
-    distance = 1
-    while distance < lax.axis_size(axis):
-        values = values + swap(values, axis, distance)
-        distance *= 2
-    return values
+def line_gather(block, axis):
+    up = down = block
+    hops = []
+    for hop in range(1, 4):
+        up = lax.ppermute(up, axis, [(i, i + 1) for i in range(hop - 1, 3)])
+        down = lax.ppermute(down, axis, [(i, i - 1) for i in range(4 - hop, 0, -1)])
+        hops.append((up, down))
+    return hops
+
+
+def hop_owners(position, hop):
+    below = position - hop
+    above = position + hop
+    return jnp.stack([jnp.where(below >= 0, below, -1), jnp.where(above < 4, above, -1)])
+
+
+def block_kernel(count, has_total, owners, *refs):
+    x_refs = refs[:count]
+    scale_ref, gain_ref, w_ref = refs[count : count + 3]
+    out_ref, held, sems = refs[-3:]
+    _, tiles, depth, _ = held.shape
+
+    def copy(j, k):
+        first = pl.multiple_of((owners[j] * tiles + k) * depth, depth)
+        return pltpu.make_async_copy(
+            w_ref.at[pl.ds(first, depth), :], held.at[j, k], sems.at[j, k]
+        )
+
+    for j in range(count):
+
+        @pl.when(owners[j] >= 0)
+        def _():
+            for k in range(tiles):
+                copy(j, k).start()
+
+    out_ref[...] = refs[count + 3][...] if has_total else jnp.zeros_like(out_ref)
+    for j, x_ref in enumerate(x_refs):
+
+        @pl.when(owners[j] >= 0)
+        def _():
+            scale = scale_ref[...]
+            for k in range(tiles):
+                span = slice(k * depth, (k + 1) * depth)
+                first = pl.multiple_of((owners[j] * tiles + k) * depth, depth)
+                gain = gain_ref[:, pl.ds(first, depth)]
+                normed = (x_ref[:, span].astype(F32) * scale * gain).astype(BF16)
+                copy(j, k).wait()
+                out_ref[...] += jnp.dot(normed, held[j, k], preferred_element_type=F32)
+
+
+def base_block(blocks, scale, gain, weight, owners, total):
+    rows, depth = blocks[0].shape
+    columns = weight.shape[1]
+    tile = min(512, depth)
+    count = len(blocks)
+    operands = [owners, *blocks, scale, gain, weight]
+    if total is not None:
+        operands.append(total)
+    return pl.pallas_call(
+        functools.partial(block_kernel, count, total is not None),
+        out_shape=jax.ShapeDtypeStruct((rows, columns), F32),
+        in_specs=[SMEM] + [VMEM] * (count + 2) + [HBM] + [VMEM] * (total is not None),
+        out_specs=VMEM,
+        scratch_shapes=[
+            pltpu.VMEM((count, depth // tile, tile, columns), BF16),
+            pltpu.SemaphoreType.DMA((count, depth // tile)),
+        ],
+        compiler_params=pltpu.CompilerParams(vmem_limit_bytes=48 * MIB),
+        cost_estimate=pl.CostEstimate(
+            flops=2 * count * rows * depth * columns,
+            bytes_accessed=2 * depth * (rows + columns) + 8 * rows * columns,
+            transcendentals=0,
+        ),
+        name="base_block",
+    )(*operands)
 
 
 def base_kernel(x_ref, scale_ref, gain_ref, w_ref, out_ref, held, sems):
@@ -88,46 +157,105 @@
     )(x, scale, gain, weight)
 
 
-def shrink_kernel(place_ref, slots, x0, x1, x2, x3, scale_ref, gain_ref, down_ref, out_ref, held, sems):
+TEAM = 4
+SLABS = (0, 2, 1, 3)
+
+
+def list_runs(place_ref, slots, runs, jobs, start):
+    def look(run, carry, slab, d):
+        slot = slots[(place_ref[0] ^ d) * runs + run]
+
+        @pl.when(slot >= 0)
+        def _():
+            jobs[carry] = slab * runs + run
+            start(carry, d, run, slot)
+
+        return carry + (slot >= 0).astype(jnp.int32)
+
+    count = jnp.int32(0)
+    for slab, d in enumerate(SLABS):
+        count = lax.fori_loop(0, runs, functools.partial(look, slab=slab, d=d), count)
+    return count
+
+
+def work_in_teams(count, wait, work):
+    def team(g, carry):
+        for u in range(TEAM):
+
+            @pl.when(g * TEAM + u < count)
+            def _():
+                wait(g * TEAM + u)
+
+        work([jnp.minimum(g * TEAM + u, count - 1) for u in range(TEAM)])
+        return carry
+
+    lax.fori_loop(0, (count + TEAM - 1) // TEAM, team, 0)
+
+
+def shrink_kernel(
+    place_ref,
+    slots,
+    x0,
+    x1,
+    x2,
+    x3,
+    scale_ref,
+    gain_ref,
+    down_ref,
+    keep_ref,
+    send_ref,
+    jobs,
+    parts,
+    held_x,
+    held,
+    x_sems,
+    sems,
+):
     runs = held.shape[0] // 4
-    pairs = runs // 2
-
-    def fetch(n, carry):
-        @pl.when(slots[n] >= 0)
-        def _():
-            pltpu.make_async_copy(down_ref.at[slots[n]], held.at[n], sems.at[n]).start()
-
-        return carry
-
-    lax.fori_loop(0, 4 * runs, fetch, 0)
-    out_ref[...] = jnp.zeros_like(out_ref)
-    rank = down_ref.shape[1]
-    for slab, (d, x_ref) in enumerate(((0, x0), (2, x2), (1, x1), (3, x3))):
-        owner = place_ref[0] ^ d
-        for half in range(2):
-
-            def one(i, carry):
-                run = half * pairs + i
-                n = owner * runs + run
-
-                @pl.when(slots[n] >= 0)
-                def _():
-                    pltpu.make_async_copy(
-                        down_ref.at[slots[n]], held.at[n], sems.at[n]
-                    ).wait()
-                    place = pl.ds(pl.multiple_of(run * 16, 16), 16)
-                    rows = x_ref[place, :].astype(F32) * scale_ref[owner, place, :] * gain_ref[...]
-                    rows = rows.astype(BF16)
-                    part = lax.dot_general(
-                        rows, held[n], (((1,), (1,)), ((), ())), preferred_element_type=F32
-                    )
-                    out_ref[
-                        slab, pl.ds(pl.multiple_of(i * 16, 16), 16), half * rank : (half + 1) * rank
-                    ] = part
-
-                return carry
-
-            lax.fori_loop(0, pairs, one, 0)
+    rank = held.shape[1]
+    x_refs = (x0, x1, x2, x3)
+
+    def x_copy(i, d, run):
+        rows = pl.ds(pl.multiple_of(run * 16, 16), 16)
+        return pltpu.make_async_copy(x_refs[d].at[rows, :], held_x.at[i], x_sems.at[i])
+
+    def copy(i, slot):
+        return pltpu.make_async_copy(down_ref.at[slot], held.at[i], sems.at[i])
+
+    def start(i, d, run, slot):
+        copy(i, slot).start()
+        x_copy(i, d, run).start()
+
+    def wait(i):
+        copy(i, 0).wait()
+        x_copy(i, 0, 0).wait()
+
+    def work(members):
+        results = []
+        for i in members:
+            job = jobs[i]
+            slab = job // runs
+            d = jnp.where(slab == 1, 2, jnp.where(slab == 2, 1, slab))
+            rows = pl.ds(pl.multiple_of((job % runs) * 16, 16), 16)
+            scale = scale_ref[place_ref[0] ^ d, rows, :]
+            normed = (held_x[i].astype(F32) * scale * gain_ref[...]).astype(BF16)
+            part = lax.dot_general(
+                normed, held[i], (((1,), (1,)), ((), ())), preferred_element_type=F32
+            )
+            results.append((job, part))
+        for job, part in results:
+            parts[job] = part
+
+    count = list_runs(place_ref, slots, runs, jobs, start)
+    parts[...] = jnp.zeros_like(parts)
+    work_in_teams(count, wait, work)
+    for slab in range(4):
+        for i in range(runs // 2):
+            low = slab * runs + i
+            out_ref = (keep_ref, send_ref)[slab // 2]
+            out_ref[slab % 2, i * 16 : (i + 1) * 16, :] = jnp.concatenate(
+                [parts[low], parts[low + runs // 2]], axis=1
+            )
 
 
 def shrink_rows(place, slots, blocks, scales, gain, down):
@@ -136,14 +264,18 @@
     runs = rows // 16
     return pl.pallas_call(
         shrink_kernel,
-        out_shape=jax.ShapeDtypeStruct((4, rows // 2, 2 * rank), F32),
-        in_specs=[SMEM] * 2 + [VMEM] * 6 + [HBM],
-        out_specs=VMEM,
+        out_shape=[jax.ShapeDtypeStruct((2, rows // 2, 2 * rank), F32)] * 2,
+        in_specs=[SMEM] * 2 + [HBM] * 4 + [VMEM] * 2 + [HBM],
+        out_specs=[VMEM] * 2,
         scratch_shapes=[
+            pltpu.SMEM((4 * runs,), jnp.int32),
+            pltpu.VMEM((4 * runs, 16, rank), F32),
+            pltpu.VMEM((4 * runs, 16, depth), BF16),
             pltpu.VMEM((4 * runs, rank, depth), BF16),
             pltpu.SemaphoreType.DMA((4 * runs,)),
+            pltpu.SemaphoreType.DMA((4 * runs,)),
         ],
-        compiler_params=pltpu.CompilerParams(vmem_limit_bytes=56 * MIB),
+        compiler_params=pltpu.CompilerParams(vmem_limit_bytes=54 * MIB),
         cost_estimate=pl.CostEstimate(
             flops=2 * rows * depth * rank,
             bytes_accessed=8 * rows * depth + down.size,
@@ -153,58 +285,64 @@
     )(place, slots, *blocks, scales, gain, down)
 
 
-def grow_kernel(place_ref, slots, s_ref, up_ref, out_ref, held, sems):
+def grow_kernel(
+    place_ref, slots, s0, s1, up_ref, keep_ref, send_ref, jobs, parts, held, sems
+):
     runs = held.shape[0] // 4
-    pairs = runs // 2
-    rank = up_ref.shape[1]
-
-    def fetch(n, carry):
-        @pl.when(slots[n] >= 0)
-        def _():
-            pltpu.make_async_copy(up_ref.at[slots[n]], held.at[n], sems.at[n]).start()
-
-        return carry
-
-    lax.fori_loop(0, 4 * runs, fetch, 0)
-    for slab, d in enumerate((0, 2, 1, 3)):
-        owner = place_ref[0] ^ d
-        for half in range(2):
-
-            def one(i, carry):
-                run = half * pairs + i
-                n = owner * runs + run
-                place = pl.ds(pl.multiple_of(run * 16, 16), 16)
-
-                @pl.when(slots[n] >= 0)
-                def _():
-                    pltpu.make_async_copy(up_ref.at[slots[n]], held.at[n], sems.at[n]).wait()
-                    rows = s_ref[
-                        slab, pl.ds(pl.multiple_of(i * 16, 16), 16), half * rank : (half + 1) * rank
-                    ]
-                    out_ref[slab, place, :] = jnp.dot(
-                        rows, held[n], preferred_element_type=F32
-                    )
-
-                @pl.when(slots[n] < 0)
-                def _():
-                    out_ref[slab, place, :] = jnp.zeros((16, out_ref.shape[2]), F32)
-
-                return carry
-
-            lax.fori_loop(0, pairs, one, 0)
-
-
-def grow_rows(place, slots, shrunk, up):
-    _, pair_rows, _ = shrunk.shape
+    rank = held.shape[1]
+
+    def copy(i, slot):
+        return pltpu.make_async_copy(up_ref.at[slot], held.at[i], sems.at[i])
+
+    def start(i, d, run, slot):
+        copy(i, slot).start()
+
+    def wait(i):
+        copy(i, 0).wait()
+
+    def work(members):
+        results = []
+        for i in members:
+            job = jobs[i]
+            grown = jnp.dot(parts[job], held[i], preferred_element_type=F32)
+            results.append((job, grown))
+        for job, grown in results:
+            rows = pl.ds(pl.multiple_of((job % runs) * 16, 16), 16)
+            slab = job // runs
+
+            @pl.when(slab < 2)
+            def _():
+                keep_ref[slab, rows, :] = grown
+
+            @pl.when(slab >= 2)
+            def _():
+                send_ref[slab - 2, rows, :] = grown
+
+    count = list_runs(place_ref, slots, runs, jobs, start)
+    for slab in range(4):
+        for i in range(runs // 2):
+            low = slab * runs + i
+            both = (s0, s1)[slab // 2][slab % 2, i * 16 : (i + 1) * 16, :]
+            parts[low] = both[:, :rank]
+            parts[low + runs // 2] = both[:, rank:]
+    keep_ref[...] = jnp.zeros_like(keep_ref)
+    send_ref[...] = jnp.zeros_like(send_ref)
+    work_in_teams(count, wait, work)
+
+
+def grow_rows(place, slots, kept, passed, up):
+    _, pair_rows, _ = kept.shape
     rows = 2 * pair_rows
     rank, columns = up.shape[1:]
     runs = rows // 16
     return pl.pallas_call(
         grow_kernel,
-        out_shape=jax.ShapeDtypeStruct((4, rows, columns), F32),
-        in_specs=[SMEM, SMEM, VMEM, HBM],
-        out_specs=VMEM,
+        out_shape=[jax.ShapeDtypeStruct((2, rows, columns), F32)] * 2,
+        in_specs=[SMEM, SMEM, VMEM, VMEM, HBM],
+        out_specs=[VMEM] * 2,
         scratch_shapes=[
+            pltpu.SMEM((4 * runs,), jnp.int32),
+            pltpu.VMEM((4 * runs, 16, rank), BF16),
             pltpu.VMEM((4 * runs, rank, columns), BF16),
             pltpu.SemaphoreType.DMA((4 * runs,)),
         ],
@@ -215,7 +353,7 @@
             transcendentals=0,
         ),
         name="grow_rows",
-    )(place, slots, shrunk, up)
+    )(place, slots, kept, passed, up)
 
 
 def attend_kernel(
@@ -503,65 +641,69 @@
     held_slots = adapter_down_weight.shape[0]
     rank = adapter_down_weight.shape[2]
 
-    raw = hidden.reshape(STEPS, rows // unit, unit, span).transpose(1, 0, 2, 3)
-    raw = raw.reshape(STEPS * rows, span)
+    raw = hidden.reshape(STEPS, tensor_count, halves, part_rows // unit, unit, span)
+    raw = raw.transpose(2, 1, 3, 0, 4, 5).reshape(STEPS * rows, span)
     values = raw.astype(F32)
     squares = jnp.sum(values * values, axis=1)
-    squares = summed_over(squares, "tensor")
-    told = jnp.concatenate([squares, row_adapter_index[::RUN].astype(F32)])
-    told = told.reshape(1, -1)
-    told = jnp.concatenate([told, swap(told, "store", 2)], axis=0)
-    told = jnp.concatenate([told, swap(told, "store", 1)], axis=0)
-    told = jnp.stack([told[d] for d in (0, 2, 1, 3)])
-    told = lax.dynamic_index_in_dim(
-        jnp.stack([jnp.stack([told[p ^ q] for q in range(4)]) for p in range(4)]),
-        store_pos,
-        0,
-        keepdims=False,
-    )
-    scales = lax.rsqrt(told[:, : STEPS * rows] / model_width + eps_norm)
-    runs = told[:, STEPS * rows :].astype(jnp.int32)
+    own_runs = row_adapter_index[::RUN]
+    if halves > 1:
+        own_runs = own_runs.reshape(tensor_count, halves, -1).swapaxes(0, 1).reshape(-1)
+    told = jnp.concatenate([squares, own_runs.astype(F32)])
+    told = lax.all_gather(told, ("store", "tensor"), axis=0, tiled=False)
+    told = told.reshape(-1, tensor_count, told.shape[-1])
+    runs = told[:, 0, STEPS * rows :].astype(jnp.int32)
+    told = jnp.sum(told[:, :, : STEPS * rows], axis=1)
+    scales = lax.rsqrt(told / model_width + eps_norm)
     slots = lookup(runs.reshape(-1), adapter_store_slot).reshape(runs.shape)
     slots = jnp.where(slots // held_slots == store_pos, slots % held_slots, -1)
     place = store_pos.reshape(1).astype(jnp.int32)
     gains = input_norm_scale.reshape(1, -1)
     gain = lax.dynamic_slice_in_dim(gains, tensor_pos * span, span, 1)
-    scales = scales.reshape(-1, tensor_count, halves, local)
-    raw = raw.reshape(tensor_count, halves, local, span)
-
+    scales = scales[:, :, None]
+    own_scale = lax.dynamic_index_in_dim(scales, store_pos, 0, keepdims=False)
+
+    line = tensor_count == 4
+    owners = [tensor_pos.reshape(1).astype(jnp.int32)]
+    owners += [hop_owners(tensor_pos, hop) for hop in (1, 2, 3)]
+    hops = line_gather(raw, "tensor") if line else None
+
+    across = swap(raw, "store", 2)
+    beside = swap(raw, "store", 1)
+    diagonal = swap(across, "store", 1)
+    mine = slots.reshape(-1)
     down = jnp.swapaxes(adapter_down_weight, 1, 2)
-    results = []
+    if line:
+        diagonal, hops[0] = lax.optimization_barrier((diagonal, hops[0]))
+    kept, passed = shrink_rows(place, mine, (raw, beside, across, diagonal), scales, gain, down)
+    kept = kept + swap(passed, "store", 1)
+    shrunk = kept[0] + swap(kept[1], "store", 2)
+    shrunk = lax.all_gather(shrunk, "tensor", axis=0, tiled=False)
+    if line:
+        shrunk, hops[1] = lax.optimization_barrier((shrunk, hops[1]))
+    shrunk = jnp.sum(shrunk, axis=0).astype(BF16)
+    shrunk = jnp.stack([shrunk, swap(shrunk, "store", 2)])
+    kept, passed = grow_rows(place, mine, shrunk, swap(shrunk, "store", 1), adapter_up_weight)
+
+    weight = query_key_value_weight
+    if line:
+        raw, passed = lax.optimization_barrier((raw, passed))
+        blocks = (raw,) + hops[0] + hops[1]
+        near = jnp.concatenate(owners[:3])
+        total = base_block(blocks, own_scale, gains, weight, near, None)
+        total = base_block(hops[2], own_scale, gains, weight, owners[3], total)
+    else:
+        everything = lax.all_gather(raw, "tensor", axis=0, tiled=False)
+        total = base_rows(everything, own_scale, gains, weight)
+    passed = swap(passed, "store", 1)
+
+    count = tensor_count * local
+    gathered = []
     context = None
     for h in range(halves):
-        own = raw[:, h].reshape(tensor_count * local, span)
-        count = own.shape[0]
-        part_scales = scales[:, :, h].reshape(-1, count, 1)
-        own_scale = lax.dynamic_index_in_dim(part_scales, store_pos, 0, keepdims=False)
-
-        across = swap(own, "store", 2)
-        beside = swap(own, "store", 1)
-        diagonal = swap(across, "store", 1)
-
-        everything = lax.all_gather(own, "tensor", axis=0, tiled=False)
-        if context is not None:
-            everything, context = lax.optimization_barrier((everything, context))
-        total = base_rows(everything, own_scale, gains, query_key_value_weight)
-
-        mine = slots.reshape(4, -1, halves, max(1, part_rows // RUN))[:, :, h].reshape(-1)
-        partial = shrink_rows(
-            place, mine, (own, beside, across, diagonal), part_scales, gain, down
-        )
-        pair = partial[:2] + swap(partial[2:], "store", 1)
-        shrunk = pair[0] + swap(pair[1], "store", 2)
-        shrunk = summed_over(shrunk, "tensor")
-        shrunk = shrunk.astype(BF16)
-        pair = jnp.stack([shrunk, swap(shrunk, "store", 2)])
-        shrunk = jnp.concatenate([pair, swap(pair, "store", 1)], axis=0)
-        grown = grow_rows(place, mine, shrunk, adapter_up_weight)
-        pair = grown[:2] + swap(grown[2:], "store", 1)
-        delta = pair[0] + swap(pair[1], "store", 2)
-
-        qkv = (total + delta).astype(BF16)
+        part = slice(h * count, (h + 1) * count)
+        delta = swap(kept[1, part] + passed[1, part], "store", 2)
+        delta = (kept[0, part] + passed[0, part]) + delta
+        qkv = (total[part] + delta).astype(BF16)
         qkv = qkv.reshape(tensor_count, local, -1)
         moved = lax.all_to_all(qkv, "tensor", split_axis=0, concat_axis=0, tiled=True)
         if tensor_count != 4:
@@ -578,7 +720,12 @@
             here, ascending(here), moved, cosine, sine, key_value_cache, h * part_rows, unit
         )
 
-        everything = lax.all_gather(context, "tensor", axis=0, tiled=False)
+        gathered.append(lax.all_gather(context, "tensor", axis=0, tiled=False))
+
+    previous = context
+    results = []
+    for everything in gathered:
+        everything, previous = lax.optimization_barrier((everything, previous))
         if part_rows % RUN == 0:
             result = project(everything, output_weight)
         else:
@@ -587,6 +734,7 @@
             result = result.reshape(tensor_count, part_rows // unit, STEPS, unit, -1)
             result = result.transpose(2, 0, 1, 3, 4).reshape(STEPS, tensor_count, part_rows, -1)
         results.append(result)
+        previous = result
     output = results[0] if halves == 1 else jnp.concatenate(results, axis=2)
     return output.reshape(STEPS, rows, -1)
 

time: 236 us -> 286 us (1.21)
  blocking collectives: 0 us -> 80.8 us
  starting transfers between devices: 40.9 us -> 22 us
  local copies, waits for them, and re-layouts: 22.4 us -> 11.1 us
  waiting for transfers between devices: 83.3 us -> 91.8 us
  Pallas kernels: 63.5 us -> 55.8 us
    unnamed x0 -> x1, blocking collectives: none -> 62.7 us
    ppermute x26 -> x10, starting transfers between devices: 31.8 us -> 5.79 us  [swap(): return lax.ppermute(values, axis, [(i, i ^ distance) for i in range(count)])]
    all_gather x0 -> x1, blocking collectives: none -> 18.1 us  [on_device(): shrunk = lax.all_gather(shrunk, 'tensor', axis=0, tiled=False)]
    ppermute x0 -> x6, waiting for transfers between devices: none -> 9.69 us  [the longest x3 9.68 us: line_gather(): down = lax.ppermute(down, axis, [(i, i - 1) for i in range(4 - hop, 0, -1)])]
    ppermute x0 -> x6, starting transfers between devices: none -> 8.98 us  [the longest x3 5.1 us: line_gather(): up = lax.ppermute(up, axis, [(i, i + 1) for i in range(hop - 1, 3)])]
    pallas_call x6 -> x4, Pallas kernels: 36.4 us -> 27.6 us  [the longest x2 14.6 us: base_block(): pl.pallas_call(functools.partial(block_kernel, count, total is not None),...]
    slice x9 -> x1, local copies, waits for them, and re-layouts: 7.9 us -> 0.1 us  [on_device(): own_runs = row_adapter_index[::RUN]]
    all_gather x4 -> x2, waiting for transfers between devices: 19.6 us -> 25 us  [on_device(): gathered.append(lax.all_gather(context, 'tensor', axis=0, tiled=False))]
  transfers between devices with their start and end apart: 32 -> 20, of which waited for: 16 -> 12; matrix products, arithmetic and copies ran while one was open for 9% -> 3% of each run, Pallas kernels for 24% -> 12%
where the time goes in v2:
time: 286 us
  waiting for transfers between devices  91.8 us (32%)
  blocking collectives  80.8 us (28%)
  Pallas kernels  55.8 us (20%)
  starting transfers between devices  22 us (8%)
  between operations  14.4 us (5%)
  local copies, waits for them, and re-layouts  11.1 us (4%)
  other arithmetic  9.84 us (3%)
    unnamed x1, blocking collectives  62.7 us
    ppermute x10, waiting for transfers between devices, swap(): return lax.ppermute(values, axis, [(i, i ^ distance) for i in range(count)])  34.5 us
    all_gather x2, waiting for transfers between devices, on_device(): gathered.append(lax.all_gather(context, 'tensor', axis=0, tiled=False))  25 us
    all_to_all x2, waiting for transfers between devices, on_device(): lax.all_to_all(qkv, 'tensor', split_axis=0, concat_axis=0, tiled=True)  22.6 us
    all_gather x1, blocking collectives, on_device(): shrunk = lax.all_gather(shrunk, 'tensor', axis=0, tiled=False)  18.1 us
    pallas_call x2, Pallas kernels, attend(): pl.pallas_call(functools.partial(attend_kernel, unit, first_row), out_sha...  15.4 us
    pallas_call x2, Pallas kernels, base_block(): pl.pallas_call(functools.partial(block_kernel, count, total is not None),...  14.6 us
    pallas_call x2, Pallas kernels, project(): pl.pallas_call(out_kernel, out_shape=jax.ShapeDtypeStruct((STEPS, owners,...  12.8 us
  transfers between devices with their start and end apart: 20, of which 12 were waited for; matrix products, arithmetic and copies ran while one was open for 3% of the time, Pallas kernels for 12%

profile of v2, /device:TPU:0, one launch (start us, length us, event | category | flops | bytes accessed | tf_op | source)
XLA Modules:
  0.0 285.8 jit_solution(15090081186835308908)
XLA Ops:
  7.9 3.0 %collective-permute-start.7 = (bf16[256,2048]{1,0:T(8,128)(2,1)S(1)}, bf16[256,2048]{1,0:T(8,128)(2,1)}, u32[]{:S(2)}, u32[]{:S(2)}) collective-permute-start(bf16[256,2048]{1,0:T(8,128)(2,1)S(1)} %bitcast.56), channel_id=1, source_target_pairs={{0,8},{4,12},{8,0},{12,4},{1,9},{5,13},{9,1},{13,5},{2,10},{6,14},... | collective-permute-start | bytes 3145736 | tf_op jit(solution)/shard_map/ppermute | solution.py:33
  10.9 3.5 %collective-permute-start = (bf16[256,2048]{1,0:T(8,128)(2,1)S(1)}, bf16[256,2048]{1,0:T(8,128)(2,1)S(1)}, u32[]{:S(2)}, u32[]{:S(2)}) collective-permute-start(bf16[256,2048]{1,0:T(8,128)(2,1)S(1)} %bitcast.57), channel_id=1, source_target_pairs={{0,1},{1,2},{2,3},{4,5},{5,6},{6,7},{8,9},{9,10},{10,11},{12,13},{... | collective-permute-start | bytes 3145736 | tf_op jit(solution)/shard_map/ppermute | solution.py:40
  15.8 18.3 %collective-permute-done.7.x2 = bf16[256,2048]{1,0:T(8,128)(2,1)} collective-permute-done((bf16[256,2048]{1,0:T(8,128)(2,1)S(1)}, bf16[256,2048]{1,0:T(8,128)(2,1)}, u32[]{:S(2)}, u32[]{:S(2)}) %collective-permute-start.7) | collective-permute-done | bytes 1048608 | tf_op jit(solution)/shard_map/ppermute | solution.py:33
  37.5 62.7 %all-reduce = f32[4352]{0:T(1024)S(1)} all-reduce(f32[4352]{0:T(1024)S(1)} %maximum_dynamic-update-slice_fusion), channel_id=2, replica_groups=mesh['groups'=2,'store'=4,'tensor'=4] {'store','tensor'}, use_global_device_ids=true, to_apply=%add | all-reduce | flops 4352 | bytes 34816
  104.8 6.7 %shrink_rows.1 = (f32[2,128,128]{2,1,0:T(8,128)}, f32[2,128,128]{2,1,0:T(8,128)}) custom-call(s32[1]{0:T(128)} %bitcast.15.place_ref, s32[64]{0:T(128)} %compare_select_fusion.slots, bf16[256,2048]{1,0:T(8,128)(2,1)} %bitcast.60, bf16[256,2048]{1,0:T(8,128)(2,1)} %collective-permute-done.6.x1, bf16[256,2048]{1,0:T(8,128)(2,1)} %collective-permute-done.7.x2, ...), custom_call_target="tpu_custom_call" | custom-call | flops 67108864 | bytes 8388608 | tf_op jit(solution)/shard_map/shrink_rows/pallas_call | solution.py:265
  114.3 4.1 %collective-permute-done.10 = f32[128,128]{1,0:T(8,128)S(1)} collective-permute-done((f32[128,128]{1,0:T(8,128)S(1)}, f32[128,128]{1,0:T(8,128)S(1)}, u32[]{:S(2)}, u32[]{:S(2)}) %collective-permute-start.10) | collective-permute-done | bytes 65568 | tf_op jit(solution)/shard_map/ppermute | solution.py:33
  118.4 18.1 %all-gather.1 = f32[512,128]{1,0:T(8,128)S(1)} all-gather(f32[128,128]{1,0:T(8,128)S(1)} %fusion.10), channel_id=3, replica_groups=mesh['groups'=2,'store'=4,'tensor'=4] {'tensor'}, dimensions={0}, use_global_device_ids=true | all-gather | bytes 327680 | tf_op jit(solution)/shard_map/all_gather | solution.py:680
  138.6 3.9 %collective-permute-done.11 = bf16[128,128]{1,0:T(8,128)(2,1)S(1)} collective-permute-done((bf16[128,128]{1,0:T(8,128)(2,1)S(1)}, bf16[128,128]{1,0:T(8,128)(2,1)S(1)}, u32[]{:S(2)}, u32[]{:S(2)}) %collective-permute-start.11) | collective-permute-done | bytes 32800 | tf_op jit(solution)/shard_map/ppermute | solution.py:33
  144.5 6.4 %grow_rows.1 = (f32[2,256,1280]{2,1,0:T(8,128)}, f32[2,256,1280]{2,1,0:T(8,128)}) custom-call(s32[1]{0:T(128)} %bitcast.15.place_ref, s32[64]{0:T(128)} %compare_select_fusion.slots, bf16[2,128,128]{2,1,0:T(8,128)(2,1)} %copy-done.11, bf16[2,128,128]{2,1,0:T(8,128)(2,1)} %copy-done.12, bf16[32,64,1280]{2,1,0:T(8,128)(2,1)} %up_ref.1), custom_call_target="tpu_custom_call" | custom-call | flops 41943040 | bytes 5242880 | tf_op jit(solution)/shard_map/grow_rows/pallas_call | solution.py:338
  160.1 10.4 %base_block.2.refs_5_ = f32[256,1280]{1,0:T(8,128)} custom-call(s32[5]{0:T(128)S(1)} %concatenate.22.owners, bf16[256,2048]{1,0:T(8,128)(2,1)S(1)} %bitcast.61, bf16[256,2048]{1,0:T(8,128)(2,1)S(1)} %collective-permute-done.refs_1_, bf16[256,2048]{1,0:T(8,128)(2,1)S(1)} %collective-permute-done.3.refs_2_, bf16[256,2048]{1,0:T(8,128)(2,1)S(1)} %copy-done.4, ...), custom_call_target="tpu_custom_call" | custom-call | flops 6710886400 | bytes 8912896 | tf_op jit(solution)/shard_map/base_block/pallas_call | solution.py:94
  170.6 9.7 %collective-permute-done.5.refs_1_ = bf16[256,2048]{1,0:T(8,128)(2,1)S(1)} collective-permute-done((bf16[256,2048]{1,0:T(8,128)(2,1)}, bf16[256,2048]{1,0:T(8,128)(2,1)S(1)}, u32[]{:S(2)}, u32[]{:S(2)}) %collective-permute-start.5) | collective-permute-done | bytes 1048608 | tf_op jit(solution)/shard_map/ppermute | solution.py:41
  181.6 4.1 %base_block.3 = f32[256,1280]{1,0:T(8,128)S(1)} custom-call(s32[2]{0:T(128)S(1)} %pad_add_fusion.owners, bf16[256,2048]{1,0:T(8,128)(2,1)S(1)} %collective-permute-done.2.refs_0_, bf16[256,2048]{1,0:T(8,128)(2,1)S(1)} %collective-permute-done.5.refs_1_, f32[256,1]{1,0:T(8,128)S(1)} %copy.22.refs_5_.refs_2_, f32[1,8192]{1,0:T(1,128)S(1)} %bitcast.65, ...), custom_call_target="tpu_custom_call" | custom-call | flops 2684354560 | bytes 8912896 | tf_op jit(solution)/shard_map/base_block/pallas_call | solution.py:94
  185.8 3.2 %collective-permute-done.15 = f32[128,1280]{1,0:T(8,128)S(1)} collective-permute-done((f32[128,1280]{1,0:T(8,128)S(1)}, f32[128,1280]{1,0:T(8,128)S(1)}, u32[]{:S(2)}, u32[]{:S(2)}) %collective-permute-start.15) | collective-permute-done | bytes 655392 | tf_op jit(solution)/shard_map/ppermute | solution.py:33
  189.0 2.5 fusion.9
  191.4 3.5 %all-to-all-start = ((bf16[4,32,1280]{2,1,0:T(8,128)(2,1)}), bf16[4,32,1280]{2,1,0:T(8,128)(2,1)S(1)}, u32[]{:S(2)}, u32[]{:S(2)}) async-start(bf16[4,32,1280]{2,1,0:T(8,128)(2,1)} %bitcast.26), calls=%async_computation | async-start | bytes 655360 | tf_op jit(solution)/shard_map/all_to_all | solution.py:708
  195.5 9.5 %all-to-all-done.qkv_ref = bf16[4,32,1280]{2,1,0:T(8,128)(2,1)S(1)} async-done(((bf16[4,32,1280]{2,1,0:T(8,128)(2,1)}), bf16[4,32,1280]{2,1,0:T(8,128)(2,1)S(1)}, u32[]{:S(2)}, u32[]{:S(2)}) %all-to-all-start) | async-done | bytes 327712 | tf_op jit(solution)/shard_map/all_to_all | solution.py:708
  205.0 7.4 %attend.2 = bf16[32,4096]{1,0:T(8,128)(2,1)} custom-call(s32[16]{0:T(128)S(1)} %get-tuple-element.51.lengths, s32[16]{0:T(128)S(1)} %select_reduce_fusion.2.order, bf16[4,32,1280]{2,1,0:T(8,128)(2,1)S(1)} %all-to-all-done.qkv_ref, f32[32,128]{1,0:T(8,128)S(1)} %get-tuple-element.52.cos_ref, f32[32,128]{1,0:T(8,128)S(1)} %get-tuple-element.53.sin_ref, ...), custom_call_target="tpu_custom_call" | custom-call | flops 268435456 | bytes 16777216 | tf_op jit(solution)/shard_map/attend/pallas_call | solution.py:519
  212.4 3.5 %all-to-all-start.1 = ((bf16[4,32,1280]{2,1,0:T(8,128)(2,1)}), bf16[4,32,1280]{2,1,0:T(8,128)(2,1)S(1)}, u32[]{:S(2)}, u32[]{:S(2)}) async-start(bf16[4,32,1280]{2,1,0:T(8,128)(2,1)} %bitcast.30), calls=%async_computation.1 | async-start | bytes 655360 | tf_op jit(solution)/shard_map/all_to_all | solution.py:708
  216.5 13.1 %all-to-all-done.1.qkv_ref = bf16[4,32,1280]{2,1,0:T(8,128)(2,1)S(1)} async-done(((bf16[4,32,1280]{2,1,0:T(8,128)(2,1)}), bf16[4,32,1280]{2,1,0:T(8,128)(2,1)S(1)}, u32[]{:S(2)}, u32[]{:S(2)}) %all-to-all-start.1) | async-done | bytes 327712 | tf_op jit(solution)/shard_map/all_to_all | solution.py:708
  229.6 8.0 %attend.3 = bf16[32,4096]{1,0:T(8,128)(2,1)} custom-call(s32[16]{0:T(128)S(1)} %get-tuple-element.50.lengths, s32[16]{0:T(128)S(1)} %select_reduce_fusion.1.order, bf16[4,32,1280]{2,1,0:T(8,128)(2,1)S(1)} %all-to-all-done.1.qkv_ref, f32[32,128]{1,0:T(8,128)S(1)} %get-tuple-element.54.cos_ref, f32[32,128]{1,0:T(8,128)S(1)} %get-tuple-element.55.sin_ref, ...), custom_call_target="tpu_custom_call" | custom-call | flops 268435456 | bytes 16777216 | tf_op jit(solution)/shard_map/attend/pallas_call | solution.py:519
  237.7 4.0 %all-gather.7.cloned.1.call-done = bf16[128,4096]{1,0:T(8,128)(2,1)} async-done(((bf16[32,4096]{1,0:T(8,128)(2,1)}), bf16[128,4096]{1,0:T(8,128)(2,1)}) %all-gather.7.cloned.1.call-update) | async-done | bytes 1048592 | tf_op jit(solution)/shard_map/all_gather | solution.py:723
  242.9 6.4 %project.2 = bf16[2,4,16,2048]{3,2,1,0:T(8,128)(2,1)S(1)} custom-call(bf16[4,32,4096]{2,1,0:T(8,128)(2,1)S(1)} %bitcast.62, bf16[4096,2048]{1,0:T(8,128)(2,1)} %w_ref.3), custom_call_target="tpu_custom_call" | custom-call | flops 2147483648 | bytes 18350080 | tf_op jit(solution)/shard_map/project/pallas_call | solution.py:576
  249.3 21.0 %all-gather.9.cloned.1.call-done = bf16[128,4096]{1,0:T(8,128)(2,1)} async-done(((bf16[32,4096]{1,0:T(8,128)(2,1)}), bf16[128,4096]{1,0:T(8,128)(2,1)}) %all-gather.9.cloned.1.call-update) | async-done | bytes 1048592 | tf_op jit(solution)/shard_map/all_gather | solution.py:723
  271.5 6.4 %project.3 = bf16[2,4,16,2048]{3,2,1,0:T(8,128)(2,1)S(1)} custom-call(bf16[4,32,4096]{2,1,0:T(8,128)(2,1)S(1)} %bitcast.63, bf16[4096,2048]{1,0:T(8,128)(2,1)} %w_ref.3), custom_call_target="tpu_custom_call" | custom-call | flops 2147483648 | bytes 18350080 | tf_op jit(solution)/shard_map/project/pallas_call | solution.py:576
  (109 shorter events, 32.0 us)
Async XLA Ops:
  6.5 29.5 %copy-start.16 = (u32[32]{0:T(128)S(1)}, u32[32]{0:T(128)}, u32[]{:S(2)}) copy-start(u32[32]{0:T(128)} %constant.75) | copy-start | bytes 388
  6.5 94.9 %copy-start.9 = (f32[8192]{0:T(1024)S(1)}, f32[8192]{0:T(1024)}, u32[]{:S(2)}) copy-start(f32[8192]{0:T(1024)} %param.11) | copy-start | bytes 98308
  6.5 97.5 %copy-start.15 = (s32[128]{0:T(128)S(1)}, s32[128]{0:T(128)}, u32[]{:S(2)}) copy-start(s32[128]{0:T(128)} %param.17) | copy-start | bytes 1540
  7.9 96.9 %copy-start = (bf16[2,4,2,2,8,2048]{5,4,0,3,1,2:T(8,128)(2,1)}, bf16[2,4,2,2,8,2048]{5,4,0,3,1,2:T(8,128)(2,1)S(1)}, u32[]{:S(2)}) copy-start(bf16[2,4,2,2,8,2048]{5,4,0,3,1,2:T(8,128)(2,1)S(1)} %copy.18) | copy-start | bytes 3145732
  7.9 26.3 %collective-permute-start.7 = (bf16[256,2048]{1,0:T(8,128)(2,1)S(1)}, bf16[256,2048]{1,0:T(8,128)(2,1)}, u32[]{:S(2)}, u32[]{:S(2)}) collective-permute-start(bf16[256,2048]{1,0:T(8,128)(2,1)S(1)} %bitcast.56), channel_id=1, source_target_pairs={{0,8},{4,12},{8,0},{12,4},{1,9},{5,13},{9,1},{13,5},{2,10},{6,14},... | collective-permute-start | bytes 3145736 | tf_op jit(solution)/shard_map/ppermute | solution.py:33
  10.9 91.1 %collective-permute-start = (bf16[256,2048]{1,0:T(8,128)(2,1)S(1)}, bf16[256,2048]{1,0:T(8,128)(2,1)S(1)}, u32[]{:S(2)}, u32[]{:S(2)}) collective-permute-start(bf16[256,2048]{1,0:T(8,128)(2,1)S(1)} %bitcast.57), channel_id=1, source_target_pairs={{0,1},{1,2},{2,3},{4,5},{5,6},{6,7},{8,9},{9,10},{10,11},{12,13},{... | collective-permute-start | bytes 3145736 | tf_op jit(solution)/shard_map/ppermute | solution.py:40
  14.4 88.3 %collective-permute-start.3 = (bf16[256,2048]{1,0:T(8,128)(2,1)S(1)}, bf16[256,2048]{1,0:T(8,128)(2,1)S(1)}, u32[]{:S(2)}, u32[]{:S(2)}) collective-permute-start(bf16[256,2048]{1,0:T(8,128)(2,1)S(1)} %bitcast.58), channel_id=1, source_target_pairs={{3,2},{2,1},{1,0},{7,6},{6,5},{5,4},{11,10},{10,9},{9,8},{15,14},{... | collective-permute-start | bytes 3145736 | tf_op jit(solution)/shard_map/ppermute | solution.py:41
  15.7 89.1 %collective-permute-start.6 = (bf16[256,2048]{1,0:T(8,128)(2,1)S(1)}, bf16[256,2048]{1,0:T(8,128)(2,1)}, u32[]{:S(2)}, u32[]{:S(2)}) collective-permute-start(bf16[256,2048]{1,0:T(8,128)(2,1)S(1)} %bitcast.59), channel_id=1, source_target_pairs={{0,4},{4,0},{8,12},{12,8},{1,5},{5,1},{9,13},{13,9},{2,6},{6,2},{1... | collective-permute-start | bytes 3145736 | tf_op jit(solution)/shard_map/ppermute | solution.py:33
  34.2 70.6 %collective-permute-start.8 = (bf16[256,2048]{1,0:T(8,128)(2,1)}, bf16[256,2048]{1,0:T(8,128)(2,1)}, u32[]{:S(2)}, u32[]{:S(2)}) collective-permute-start(bf16[256,2048]{1,0:T(8,128)(2,1)} %collective-permute-done.7.x2), channel_id=1, source_target_pairs={{0,4},{4,0},{8,12},{12,8},{1,5},{5,1},{9,13},{13,9},{2,6},{6,2},{1... | collective-permute-start | bytes 3145736 | tf_op jit(solution)/shard_map/ppermute | solution.py:33
  102.0 34.5 %collective-permute-start.1 = (bf16[256,2048]{1,0:T(8,128)(2,1)S(1)}, bf16[256,2048]{1,0:T(8,128)(2,1)S(1)}, u32[]{:S(2)}, u32[]{:S(2)}) collective-permute-start(bf16[256,2048]{1,0:T(8,128)(2,1)S(1)} %collective-permute-done.refs_1_), channel_id=1, source_target_pairs={{1,2},{2,3},{5,6},{6,7},{9,10},{10,11},{13,14},{14,15},{17,18},{18... | collective-permute-start | bytes 3145736 | tf_op jit(solution)/shard_map/ppermute | solution.py:40
  102.7 33.8 %collective-permute-start.4 = (bf16[256,2048]{1,0:T(8,128)(2,1)S(1)}, bf16[256,2048]{1,0:T(8,128)(2,1)S(1)}, u32[]{:S(2)}, u32[]{:S(2)}) collective-permute-start(bf16[256,2048]{1,0:T(8,128)(2,1)S(1)} %collective-permute-done.3.refs_2_), channel_id=1, source_target_pairs={{2,1},{1,0},{6,5},{5,4},{10,9},{9,8},{14,13},{13,12},{18,17},{17,1... | collective-permute-start | bytes 3145736 | tf_op jit(solution)/shard_map/ppermute | solution.py:41
  111.5 1.6 collective-permute-start.9
  114.1 4.3 %collective-permute-start.10 = (f32[128,128]{1,0:T(8,128)S(1)}, f32[128,128]{1,0:T(8,128)S(1)}, u32[]{:S(2)}, u32[]{:S(2)}) collective-permute-start(f32[128,128]{1,0:T(8,128)S(1)} %slice_bitcast_fusion), channel_id=1, source_target_pairs={{0,8},{4,12},{8,0},{12,4},{1,9},{5,13},{9,1},{13,5},{2,10},{6,14},... | collective-permute-start | bytes 196616 | tf_op jit(solution)/shard_map/ppermute | solution.py:33
  138.6 4.0 %collective-permute-start.11 = (bf16[128,128]{1,0:T(8,128)(2,1)S(1)}, bf16[128,128]{1,0:T(8,128)(2,1)S(1)}, u32[]{:S(2)}, u32[]{:S(2)}) collective-permute-start(bf16[128,128]{1,0:T(8,128)(2,1)S(1)} %reduce_sum.80), channel_id=1, source_target_pairs={{0,8},{4,12},{8,0},{12,4},{1,9},{5,13},{9,1},{13,5},{2,10},{6,14},... | collective-permute-start | bytes 98312 | tf_op jit(solution)/shard_map/ppermute | solution.py:33
  142.6 1.3 collective-permute-start.12
  150.9 5.3 %collective-permute-start.13 = (f32[2,256,1280]{2,1,0:T(8,128)}, f32[2,256,1280]{2,1,0:T(8,128)}, u32[]{:S(2)}, u32[]{:S(2)}) collective-permute-start(f32[2,256,1280]{2,1,0:T(8,128)} %get-tuple-element.30), channel_id=1, source_target_pairs={{0,4},{4,0},{8,12},{12,8},{1,5},{5,1},{9,13},{13,9},{2,6},{6,2},{1... | collective-permute-start | bytes 7864328 | tf_op jit(solution)/shard_map/ppermute | solution.py:33
  151.9 18.7 %collective-permute-start.2 = (bf16[256,2048]{1,0:T(8,128)(2,1)}, bf16[256,2048]{1,0:T(8,128)(2,1)S(1)}, u32[]{:S(2)}, u32[]{:S(2)}) collective-permute-start(bf16[256,2048]{1,0:T(8,128)(2,1)} %copy-done.3), channel_id=1, source_target_pairs={{2,3},{6,7},{10,11},{14,15},{18,19},{22,23},{26,27},{30,31}} | collective-permute-start | bytes 3145736 | tf_op jit(solution)/shard_map/ppermute | solution.py:40
  152.8 27.5 %collective-permute-start.5 = (bf16[256,2048]{1,0:T(8,128)(2,1)}, bf16[256,2048]{1,0:T(8,128)(2,1)S(1)}, u32[]{:S(2)}, u32[]{:S(2)}) collective-permute-start(bf16[256,2048]{1,0:T(8,128)(2,1)} %copy-done.5), channel_id=1, source_target_pairs={{1,0},{5,4},{9,8},{13,12},{17,16},{21,20},{25,24},{29,28}} | collective-permute-start | bytes 3145736 | tf_op jit(solution)/shard_map/ppermute | solution.py:41
  158.0 27.7 %collective-permute-start.14 = (f32[128,1280]{1,0:T(8,128)S(1)}, f32[128,1280]{1,0:T(8,128)S(1)}, u32[]{:S(2)}, u32[]{:S(2)}) collective-permute-start(f32[128,1280]{1,0:T(8,128)S(1)} %get-tuple-element.35), channel_id=1, source_target_pairs={{0,8},{4,12},{8,0},{12,4},{1,9},{5,13},{9,1},{13,5},{2,10},{6,14},... | collective-permute-start | bytes 1966088 | tf_op jit(solution)/shard_map/ppermute | solution.py:33
  158.1 30.8 %collective-permute-start.15 = (f32[128,1280]{1,0:T(8,128)S(1)}, f32[128,1280]{1,0:T(8,128)S(1)}, u32[]{:S(2)}, u32[]{:S(2)}) collective-permute-start(f32[128,1280]{1,0:T(8,128)S(1)} %get-tuple-element.36), channel_id=1, source_target_pairs={{0,8},{4,12},{8,0},{12,4},{1,9},{5,13},{9,1},{13,5},{2,10},{6,14},... | collective-permute-start | bytes 1966088 | tf_op jit(solution)/shard_map/ppermute | solution.py:33
  191.4 13.5 %all-to-all-start = ((bf16[4,32,1280]{2,1,0:T(8,128)(2,1)}), bf16[4,32,1280]{2,1,0:T(8,128)(2,1)S(1)}, u32[]{:S(2)}, u32[]{:S(2)}) async-start(bf16[4,32,1280]{2,1,0:T(8,128)(2,1)} %bitcast.26), calls=%async_computation | async-start | bytes 655360 | tf_op jit(solution)/shard_map/all_to_all | solution.py:708
  194.9 46.8 %all-gather.7.cloned.1.call-start = ((), (), s32[]{:S(2)}) async-start(), calls=%async_computation.2 | async-start | bytes 1310720 | tf_op jit(solution)/shard_map/all_gather | solution.py:723
  212.4 17.2 %all-to-all-start.1 = ((bf16[4,32,1280]{2,1,0:T(8,128)(2,1)}), bf16[4,32,1280]{2,1,0:T(8,128)(2,1)S(1)}, u32[]{:S(2)}, u32[]{:S(2)}) async-start(bf16[4,32,1280]{2,1,0:T(8,128)(2,1)} %bitcast.30), calls=%async_computation.1 | async-start | bytes 655360 | tf_op jit(solution)/shard_map/all_to_all | solution.py:708
  215.8 54.4 %all-gather.9.cloned.1.call-start = ((), (), s32[]{:S(2)}) async-start(), calls=%async_computation.3 | async-start | bytes 1310720 | tf_op jit(solution)/shard_map/all_gather | solution.py:723
  (13 other events, 100.4 us)
Sparse Core Ops, SparseCore 0:
  212.5 29.1 all-gather.6
  243.2 26.9 all-gather.8

commit v3 on v2

--- a/solution.py
+++ b/solution.py
@@ -31,6 +31,14 @@
 def swap(values, axis, distance):
     count = lax.axis_size(axis)
     return lax.ppermute(values, axis, [(i, i ^ distance) for i in range(count)])
+
+
+def summed_over(values, axis):
+    distance = 1
+    while distance < lax.axis_size(axis):
+        values = values + swap(values, axis, distance)
+        distance *= 2
+    return values
 
 
 def line_gather(block, axis):
@@ -110,38 +118,44 @@
     )(*operands)
 
 
-def base_kernel(x_ref, scale_ref, gain_ref, w_ref, out_ref, held, sems):
+def base_kernel(first_row, place_ref, x_ref, scale_ref, gain_ref, own_ref, w_ref, out_ref, held, sems):
     owners, _, span = x_ref.shape
+    rows = scale_ref.shape[0]
     tiles, depth, _ = held.shape
+    tiles_each = span // depth
+
+    def spot(k):
+        owner = lax.rem(place_ref[0] + 1 + k // tiles_each, owners)
+        return owner, pl.multiple_of((owner * tiles_each + k % tiles_each) * depth, depth)
+
     copies = [
-        pltpu.make_async_copy(w_ref.at[pl.ds(k * depth, depth), :], held.at[k], sems.at[k])
+        pltpu.make_async_copy(w_ref.at[pl.ds(spot(k)[1], depth), :], held.at[k], sems.at[k])
         for k in range(tiles)
     ]
     for copy in copies:
         copy.start()
     scale = scale_ref[...]
+    out_ref[...] = own_ref[first_row : first_row + rows, :]
     for k, copy in enumerate(copies):
-        owner, first = divmod(k * depth, span)
-        gain = gain_ref[:, k * depth : (k + 1) * depth]
-        rows = x_ref[owner, :, first : first + depth].astype(F32)
-        normed = (rows * scale * gain).astype(BF16)
+        owner, first = spot(k)
+        inner = (k % tiles_each) * depth
+        gain = gain_ref[:, pl.ds(first, depth)]
+        part = x_ref[owner, first_row : first_row + rows, inner : inner + depth].astype(F32)
+        normed = (part * scale * gain).astype(BF16)
         copy.wait()
-        product = jnp.dot(normed, held[k], preferred_element_type=F32)
-        if k > 0:
-            out_ref[...] += product
-        else:
-            out_ref[...] = product
-
-
-def base_rows(x, scale, gain, weight):
-    owners, rows, span = x.shape
-    depth, columns = weight.shape
+        out_ref[...] += jnp.dot(normed, held[k], preferred_element_type=F32)
+
+
+def base_rows(place, x, scale, gain, own, weight, first_row):
+    owners, _, span = x.shape
+    rows = scale.shape[0]
+    columns = weight.shape[1]
     tile = min(512, span)
-    tiles = depth // tile
+    tiles = (owners - 1) * span // tile
     return pl.pallas_call(
-        base_kernel,
+        functools.partial(base_kernel, first_row),
         out_shape=jax.ShapeDtypeStruct((rows, columns), F32),
-        in_specs=[VMEM] * 3 + [HBM],
+        in_specs=[SMEM] + [VMEM] * 4 + [HBM],
         out_specs=VMEM,
         scratch_shapes=[
             pltpu.VMEM((tiles, tile, columns), BF16),
@@ -149,12 +163,12 @@
         ],
         compiler_params=pltpu.CompilerParams(vmem_limit_bytes=48 * MIB),
         cost_estimate=pl.CostEstimate(
-            flops=2 * rows * depth * columns,
-            bytes_accessed=2 * depth * (rows + columns) + 4 * rows * columns,
+            flops=2 * rows * tiles * tile * columns,
+            bytes_accessed=2 * tiles * tile * (rows + columns) + 8 * rows * columns,
             transcendentals=0,
         ),
         name="base_rows",
-    )(x, scale, gain, weight)
+    )(place, x, scale, gain, own, weight)
 
 
 TEAM = 4
@@ -539,10 +553,11 @@
     )(lengths, order, qkv, cosine, sine, cache)
 
 
-def out_kernel(context_ref, w_ref, out_ref, total, held, sems):
-    owners, local, _ = context_ref.shape
+def out_kernel(owners, *refs):
+    blocks = refs[:7]
+    w_ref, out_ref, lhs, total, held, sems = refs[7:]
+    local = blocks[0].shape[0]
     rows = local // STEPS
-    unit = min(RUN, rows)
     tiles, depth, columns = held.shape
     copies = [
         pltpu.make_async_copy(w_ref.at[pl.ds(k * depth, depth), :], held.at[k], sems.at[k])
@@ -550,47 +565,55 @@
     ]
     for copy in copies:
         copy.start()
+    for j, ref in enumerate(blocks):
+
+        @pl.when(owners[j] >= 0)
+        def _():
+            lhs[pl.ds(pl.multiple_of(owners[j] * local, local), local), :] = ref[...]
+
     width = min(512, columns)
     for k, copy in enumerate(copies):
-        lhs = context_ref[:, :, k * depth : (k + 1) * depth].reshape(owners * local, depth)
         copy.wait()
         for j in range(columns // width):
             span = slice(j * width, (j + 1) * width)
-            product = jnp.dot(lhs, held[k, :, span], preferred_element_type=F32)
+            product = jnp.dot(
+                lhs[:, k * depth : (k + 1) * depth], held[k, :, span], preferred_element_type=F32
+            )
             if k > 0:
                 product = total[:, span] + product
             if k < tiles - 1:
                 total[:, span] = product
                 continue
-            block = product.reshape(owners, rows // unit, STEPS, unit, width)
+            block = product.reshape(4, rows // RUN, STEPS, RUN, width)
             for s in range(STEPS):
-                piece = block[:, :, s].reshape(owners, rows, width)
+                piece = block[:, :, s].reshape(4, rows, width)
                 out_ref[s, :, :, span] = piece.astype(BF16)
 
 
-def project(context, weight):
-    owners, local, depth = context.shape
+def project(owners, blocks, weight):
+    local, depth = blocks[0].shape
     columns = weight.shape[1]
     tile = min(512, depth)
     rows = local // STEPS
     return pl.pallas_call(
         out_kernel,
-        out_shape=jax.ShapeDtypeStruct((STEPS, owners, rows, columns), BF16),
-        in_specs=[VMEM, HBM],
+        out_shape=jax.ShapeDtypeStruct((STEPS, 4, rows, columns), BF16),
+        in_specs=[SMEM] + [VMEM] * 7 + [HBM],
         out_specs=VMEM,
         scratch_shapes=[
-            pltpu.VMEM((owners * local, columns), F32),
+            pltpu.VMEM((4 * local, depth), BF16),
+            pltpu.VMEM((4 * local, columns), F32),
             pltpu.VMEM((depth // tile, tile, columns), BF16),
             pltpu.SemaphoreType.DMA((depth // tile,)),
         ],
         compiler_params=pltpu.CompilerParams(vmem_limit_bytes=52 * MIB),
         cost_estimate=pl.CostEstimate(
-            flops=2 * owners * local * depth * columns,
-            bytes_accessed=2 * depth * columns + 2 * owners * local * (depth + columns),
+            flops=8 * local * depth * columns,
+            bytes_accessed=2 * depth * columns + 8 * local * (depth + columns),
             transcendentals=0,
         ),
         name="project",
-    )(context, weight)
+    )(owners, *blocks, weight)
 
 
 def lookup(identity, table):
@@ -645,14 +668,18 @@
     raw = raw.transpose(2, 1, 3, 0, 4, 5).reshape(STEPS * rows, span)
     values = raw.astype(F32)
     squares = jnp.sum(values * values, axis=1)
+    squares = summed_over(squares, "tensor")
     own_runs = row_adapter_index[::RUN]
     if halves > 1:
         own_runs = own_runs.reshape(tensor_count, halves, -1).swapaxes(0, 1).reshape(-1)
-    told = jnp.concatenate([squares, own_runs.astype(F32)])
-    told = lax.all_gather(told, ("store", "tensor"), axis=0, tiled=False)
-    told = told.reshape(-1, tensor_count, told.shape[-1])
-    runs = told[:, 0, STEPS * rows :].astype(jnp.int32)
-    told = jnp.sum(told[:, :, : STEPS * rows], axis=1)
+    told = jnp.concatenate([squares, own_runs.astype(F32)]).reshape(1, -1)
+    told = jnp.concatenate([told, swap(told, "store", 2)], axis=0)
+    told = jnp.concatenate([told, swap(told, "store", 1)], axis=0)
+    told = jnp.stack([told[d] for d in (0, 2, 1, 3)])
+    told = jnp.stack([jnp.stack([told[p ^ q] for q in range(4)]) for p in range(4)])
+    told = lax.dynamic_index_in_dim(told, store_pos, 0, keepdims=False)
+    runs = told[:, STEPS * rows :].astype(jnp.int32)
+    told = told[:, : STEPS * rows]
     scales = lax.rsqrt(told / model_width + eps_norm)
     slots = lookup(runs.reshape(-1), adapter_store_slot).reshape(runs.shape)
     slots = jnp.where(slots // held_slots == store_pos, slots % held_slots, -1)
@@ -662,79 +689,73 @@
     scales = scales[:, :, None]
     own_scale = lax.dynamic_index_in_dim(scales, store_pos, 0, keepdims=False)
 
-    line = tensor_count == 4
-    owners = [tensor_pos.reshape(1).astype(jnp.int32)]
-    owners += [hop_owners(tensor_pos, hop) for hop in (1, 2, 3)]
-    hops = line_gather(raw, "tensor") if line else None
+    line = tensor_count == 4 and part_rows % RUN == 0
+    own_index = tensor_pos.reshape(1).astype(jnp.int32)
+    everything = lax.all_gather(raw, "tensor", axis=0, tiled=False)
 
     across = swap(raw, "store", 2)
     beside = swap(raw, "store", 1)
     diagonal = swap(across, "store", 1)
     mine = slots.reshape(-1)
     down = jnp.swapaxes(adapter_down_weight, 1, 2)
-    if line:
-        diagonal, hops[0] = lax.optimization_barrier((diagonal, hops[0]))
     kept, passed = shrink_rows(place, mine, (raw, beside, across, diagonal), scales, gain, down)
     kept = kept + swap(passed, "store", 1)
     shrunk = kept[0] + swap(kept[1], "store", 2)
-    shrunk = lax.all_gather(shrunk, "tensor", axis=0, tiled=False)
-    if line:
-        shrunk, hops[1] = lax.optimization_barrier((shrunk, hops[1]))
-    shrunk = jnp.sum(shrunk, axis=0).astype(BF16)
+    shrunk = summed_over(shrunk, "tensor").astype(BF16)
     shrunk = jnp.stack([shrunk, swap(shrunk, "store", 2)])
     kept, passed = grow_rows(place, mine, shrunk, swap(shrunk, "store", 1), adapter_up_weight)
-
-    weight = query_key_value_weight
-    if line:
-        raw, passed = lax.optimization_barrier((raw, passed))
-        blocks = (raw,) + hops[0] + hops[1]
-        near = jnp.concatenate(owners[:3])
-        total = base_block(blocks, own_scale, gains, weight, near, None)
-        total = base_block(hops[2], own_scale, gains, weight, owners[3], total)
-    else:
-        everything = lax.all_gather(raw, "tensor", axis=0, tiled=False)
-        total = base_rows(everything, own_scale, gains, weight)
+    raw, passed = lax.optimization_barrier((raw, passed))
+    own = base_block((raw,), own_scale, gains, query_key_value_weight, own_index, None)
     passed = swap(passed, "store", 1)
 
     count = tensor_count * local
-    gathered = []
-    context = None
+    parts = []
     for h in range(halves):
         part = slice(h * count, (h + 1) * count)
         delta = swap(kept[1, part] + passed[1, part], "store", 2)
         delta = (kept[0, part] + passed[0, part]) + delta
-        qkv = (total[part] + delta).astype(BF16)
-        qkv = qkv.reshape(tensor_count, local, -1)
-        moved = lax.all_to_all(qkv, "tensor", split_axis=0, concat_axis=0, tiled=True)
+        if parts:
+            everything, parts[-1] = lax.optimization_barrier((everything, parts[-1]))
+        total = base_rows(
+            own_index, everything, own_scale[part], gains, own, query_key_value_weight, h * count
+        )
+        parts.append((total + delta).astype(BF16).reshape(tensor_count, local, -1))
+
+    contexts = []
+    exchanged = [lax.all_to_all(qkv, "tensor", 0, 0, tiled=True) for qkv in parts]
+    for h, moved in enumerate(exchanged):
+        if h + 1 < halves:
+            moved, parts[-1] = lax.optimization_barrier((moved, parts[-1]))
         if tensor_count != 4:
             q_columns = HEADS * HD // tensor_count
-            parts = []
+            pieces = []
             for piece in (moved[..., :q_columns], moved[..., q_columns:]):
                 joined = piece.transpose(1, 0, 2).reshape(local, 4, -1)
-                parts.append(joined.transpose(1, 0, 2))
-            moved = jnp.concatenate(parts, axis=2)
-
+                pieces.append(joined.transpose(1, 0, 2))
+            moved = jnp.concatenate(pieces, axis=2)
         here = lengths[h * part_rows : (h + 1) * part_rows]
         cosine, sine = angle_tables(here, unit)
-        context = attend(
-            here, ascending(here), moved, cosine, sine, key_value_cache, h * part_rows, unit
+        contexts.append(
+            attend(here, ascending(here), moved, cosine, sine, key_value_cache, h * part_rows, unit)
         )
 
-        gathered.append(lax.all_gather(context, "tensor", axis=0, tiled=False))
-
-    previous = context
     results = []
-    for everything in gathered:
-        everything, previous = lax.optimization_barrier((everything, previous))
-        if part_rows % RUN == 0:
-            result = project(everything, output_weight)
-        else:
-            everything = everything.reshape(-1, HEADS * HD)
-            result = jnp.dot(everything, output_weight, preferred_element_type=F32).astype(BF16)
+    if line:
+        owners = [own_index] + [hop_owners(tensor_pos, hop) for hop in (1, 2, 3)]
+        owners = jnp.concatenate(owners)
+        hops = [line_gather(context, "tensor") for context in contexts]
+        for h in range(halves):
+            if h + 1 < halves:
+                hops[h], hops[h + 1][1] = lax.optimization_barrier((hops[h], hops[h + 1][1]))
+            blocks = (contexts[h],) + hops[h][0] + hops[h][1] + hops[h][2]
+            results.append(project(owners, blocks, output_weight))
+    else:
+        for context in contexts:
+            context = lax.all_gather(context, "tensor", axis=0, tiled=True)
+            result = jnp.dot(context, output_weight, preferred_element_type=F32).astype(BF16)
             result = result.reshape(tensor_count, part_rows // unit, STEPS, unit, -1)
             result = result.transpose(2, 0, 1, 3, 4).reshape(STEPS, tensor_count, part_rows, -1)
-        results.append(result)
-        previous = result
+            results.append(result)
     output = results[0] if halves == 1 else jnp.concatenate(results, axis=2)
     return output.reshape(STEPS, rows, -1)
 

time: 286 us -> 227 us (0.79)
  blocking collectives: 80.8 us -> 0 us
  starting transfers between devices: 22 us -> 41.3 us
  Pallas kernels: 55.8 us -> 64.2 us
  local copies, waits for them, and re-layouts: 11.1 us -> 5.09 us
    unnamed x1 -> x0, blocking collectives: 62.7 us -> none
    all_to_all x2, waiting for transfers between devices: 22.6 us -> 0.01 us  [on_device(): lax.all_to_all(qkv, 'tensor', 0, 0, tiled=True)]
    pallas_call x2 -> x4, Pallas kernels: 12.8 us -> 32.4 us  [the longest x2 16.4 us: base_rows(): pl.pallas_call(functools.partial(base_kernel, first_row), out_shape=jax.S...]
    all_gather x1 -> x0, blocking collectives: 18.1 us -> none  [on_device(): shrunk = lax.all_gather(shrunk, 'tensor', axis=0, tiled=False)]
    ppermute x10 -> x16, waiting for transfers between devices: 34.5 us -> 52 us  [swap(): return lax.ppermute(values, axis, [(i, i ^ distance) for i in range(count)])]
    pallas_call x2 -> x1, Pallas kernels: 14.6 us -> 3.58 us  [base_block(): pl.pallas_call(functools.partial(block_kernel, count, total is not None),...]
    ppermute x3 -> x6, waiting for transfers between devices: 9.68 us -> 18.3 us  [line_gather(): down = lax.ppermute(down, axis, [(i, i - 1) for i in range(4 - hop, 0, -1)])]
    ppermute x10 -> x16, starting transfers between devices: 5.79 us -> 13.8 us  [swap(): return lax.ppermute(values, axis, [(i, i ^ distance) for i in range(count)])]
  transfers between devices with their start and end apart: 20 -> 31, of which waited for: 12 -> 17; matrix products, arithmetic and copies ran while one was open for 3% -> 6% of each run, Pallas kernels for 12% -> 25%
where the time goes in v3:
time: 227 us; the launch traced here: 226 us
  waiting for transfers between devices  89.2 us (39%)
  Pallas kernels  64.2 us (28%)
  starting transfers between devices  41.3 us (18%)
  between operations  13.9 us (6%)
  other arithmetic  12.7 us (6%)
  local copies, waits for them, and re-layouts  5.09 us (2%)
    ppermute x16, waiting for transfers between devices, swap(): return lax.ppermute(values, axis, [(i, i ^ distance) for i in range(count)])  52 us
    all_gather x1, waiting for transfers between devices, on_device(): everything = lax.all_gather(raw, 'tensor', axis=0, tiled=False)  18.4 us
    ppermute x6, waiting for transfers between devices, line_gather(): down = lax.ppermute(down, axis, [(i, i - 1) for i in range(4 - hop, 0, -1)])  18.3 us
    pallas_call x2, Pallas kernels, base_rows(): pl.pallas_call(functools.partial(base_kernel, first_row), out_shape=jax.S...  16.4 us
    pallas_call x2, Pallas kernels, project(): pl.pallas_call(out_kernel, out_shape=jax.ShapeDtypeStruct((STEPS, 4, rows...  15.9 us
    ppermute x16, starting transfers between devices, swap(): return lax.ppermute(values, axis, [(i, i ^ distance) for i in range(count)])  13.8 us
    pallas_call x2, Pallas kernels, attend(): pl.pallas_call(functools.partial(attend_kernel, unit, first_row), out_sha...  13.4 us
    ppermute x6, starting transfers between devices, line_gather(): up = lax.ppermute(up, axis, [(i, i + 1) for i in range(hop - 1, 3)])  11.2 us
  transfers between devices with their start and end apart: 31, of which 17 were waited for; matrix products, arithmetic and copies ran while one was open for 6% of the time, Pallas kernels for 25%

profile of v3, /device:TPU:0, one launch (start us, length us, event | category | flops | bytes accessed | tf_op | source)
XLA Modules:
  0.0 226.4 jit_solution(11689715157466171111)
XLA Ops:
  8.0 3.0 %collective-permute-start.5 = (bf16[256,2048]{1,0:T(8,128)(2,1)S(1)}, bf16[256,2048]{1,0:T(8,128)(2,1)S(1)}, u32[]{:S(2)}, u32[]{:S(2)}) collective-permute-start(bf16[256,2048]{1,0:T(8,128)(2,1)S(1)} %bitcast.68), channel_id=1, source_target_pairs={{0,8},{4,12},{8,0},{12,4},{1,9},{5,13},{9,1},{13,5},{2,10},{6,14},... | collective-permute-start | bytes 3145736 | tf_op jit(solution)/shard_map/ppermute | solution.py:33
  19.8 14.4 %collective-permute-done.2 = f32[1,272]{1,0:T(1,128)S(1)} collective-permute-done((f32[1,272]{1,0:T(1,128)S(1)}, f32[1,272]{1,0:T(1,128)S(1)}, u32[]{:S(2)}, u32[]{:S(2)}) %collective-permute-start.2) | collective-permute-done | bytes 1120 | tf_op jit(solution)/shard_map/ppermute | solution.py:33
  38.7 8.0 %shrink_rows.1 = (f32[2,128,128]{2,1,0:T(8,128)}, f32[2,128,128]{2,1,0:T(8,128)}) custom-call(s32[1]{0:T(128)} %bitcast.19.place_ref, s32[64]{0:T(128)} %compare_select_fusion.slots, bf16[256,2048]{1,0:T(8,128)(2,1)} %bitcast.71, bf16[256,2048]{1,0:T(8,128)(2,1)} %copy-done.6, bf16[256,2048]{1,0:T(8,128)(2,1)} %copy-done.5, ...), custom_call_target="tpu_custom_call" | custom-call | flops 67108864 | bytes 8388608 | tf_op jit(solution)/shard_map/shrink_rows/pallas_call | solution.py:279
  49.7 4.0 %collective-permute-done.8 = f32[128,128]{1,0:T(8,128)S(1)} collective-permute-done((f32[128,128]{1,0:T(8,128)S(1)}, f32[128,128]{1,0:T(8,128)S(1)}, u32[]{:S(2)}, u32[]{:S(2)}) %collective-permute-start.8) | collective-permute-done | bytes 65568 | tf_op jit(solution)/shard_map/ppermute | solution.py:33
  55.5 8.2 %collective-permute-done.9 = f32[128,128]{1,0:T(8,128)S(1)} collective-permute-done((f32[128,128]{1,0:T(8,128)S(1)}, f32[128,128]{1,0:T(8,128)S(1)}, u32[]{:S(2)}, u32[]{:S(2)}) %collective-permute-start.9) | collective-permute-done | bytes 65568 | tf_op jit(solution)/shard_map/ppermute | solution.py:33
  63.9 10.1 %collective-permute-done.10 = f32[128,128]{1,0:T(8,128)S(1)} collective-permute-done((f32[128,128]{1,0:T(8,128)S(1)}, f32[128,128]{1,0:T(8,128)S(1)}, u32[]{:S(2)}, u32[]{:S(2)}) %collective-permute-start.10) | collective-permute-done | bytes 65568 | tf_op jit(solution)/shard_map/ppermute | solution.py:33
  80.0 6.9 %grow_rows.1 = (f32[2,256,1280]{2,1,0:T(8,128)}, f32[2,256,1280]{2,1,0:T(8,128)}) custom-call(s32[1]{0:T(128)} %bitcast.19.place_ref, s32[64]{0:T(128)} %compare_select_fusion.slots, bf16[2,128,128]{2,1,0:T(8,128)(2,1)} %copy-done.7, bf16[2,128,128]{2,1,0:T(8,128)(2,1)} %copy-done.8, bf16[32,64,1280]{2,1,0:T(8,128)(2,1)} %up_ref.1), custom_call_target="tpu_custom_call" | custom-call | flops 41943040 | bytes 5242880 | tf_op jit(solution)/shard_map/grow_rows/pallas_call | solution.py:352
  87.4 4.8 %collective-permute-done.13 = f32[2,256,1280]{2,1,0:T(8,128)} collective-permute-done((f32[2,256,1280]{2,1,0:T(8,128)}, f32[2,256,1280]{2,1,0:T(8,128)}, u32[]{:S(2)}, u32[]{:S(2)}) %collective-permute-start.13) | collective-permute-done | bytes 2621472 | tf_op jit(solution)/shard_map/ppermute | solution.py:33
  96.2 3.6 %base_block.1.own_ref = f32[256,1280]{1,0:T(8,128)S(1)} custom-call(s32[1]{0:T(128)} %bitcast.owners.place_ref, bf16[256,2048]{1,0:T(8,128)(2,1)S(1)} %bitcast.72, f32[256,1]{1,0:T(8,128)S(1)} %copy.30.refs_1_, f32[1,8192]{1,0:T(1,128)S(1)} %bitcast.73, bf16[8192,1280]{1,0:T(8,128)(2,1)} %w_ref.3), custom_call_target="tpu_custom_call" | custom-call | flops 1342177280 | bytes 8912896 | tf_op jit(solution)/shard_map/base_block/pallas_call | solution.py:102
  101.6 18.4 %all-gather.2.cloned.1.call-done.x_ref = bf16[4,256,2048]{2,1,0:T(8,128)(2,1)} async-done(((bf16[1,256,2048]{2,1,0:T(8,128)(2,1)}), bf16[4,256,2048]{2,1,0:T(8,128)(2,1)}) %all-gather.2.cloned.1.call-update) | async-done | bytes 4194320 | tf_op jit(solution)/shard_map/all_gather | solution.py:694
  120.0 8.2 %base_rows.2 = f32[128,1280]{1,0:T(8,128)S(1)} custom-call(s32[1]{0:T(128)} %bitcast.owners.place_ref, bf16[4,256,2048]{2,1,0:T(8,128)(2,1)} %all-gather.2.cloned.1.call-done.x_ref, f32[128,1]{1,0:T(8,128)S(1)} %copy.31.scale_ref, f32[1,8192]{1,0:T(1,128)S(1)} %bitcast.74, f32[256,1280]{1,0:T(8,128)S(1)} %base_block.1.own_ref, bf16[8192,1280]{1,0:T(8,128)(2,1)} %w_ref.3), custom_call_target="tpu_custom_call" | custom-call | flops 2013265920 | bytes 18612224 | tf_op jit(solution)/shard_map/base_rows/pallas_call | solution.py:155
  130.4 3.6 %all-to-all-start = ((bf16[4,32,1280]{2,1,0:T(8,128)(2,1)}), bf16[4,32,1280]{2,1,0:T(8,128)(2,1)S(1)}, u32[]{:S(2)}, u32[]{:S(2)}) async-start(bf16[4,32,1280]{2,1,0:T(8,128)(2,1)} %bitcast.31), calls=%async_computation | async-start | bytes 655360 | tf_op jit(solution)/shard_map/all_to_all | solution.py:725
  134.1 8.2 %base_rows.3 = f32[128,1280]{1,0:T(8,128)S(1)} custom-call(s32[1]{0:T(128)} %bitcast.owners.place_ref, bf16[4,256,2048]{2,1,0:T(8,128)(2,1)} %all-gather.2.cloned.1.call-done.x_ref, f32[128,1]{1,0:T(8,128)S(1)} %copy.32.scale_ref, f32[1,8192]{1,0:T(1,128)S(1)} %bitcast.75, f32[256,1280]{1,0:T(8,128)S(1)} %base_block.1.own_ref, bf16[8192,1280]{1,0:T(8,128)(2,1)} %w_ref.3), custom_call_target="tpu_custom_call" | custom-call | flops 2013265920 | bytes 18612224 | tf_op jit(solution)/shard_map/base_rows/pallas_call | solution.py:155
  144.7 4.9 %all-to-all-start.1 = ((bf16[4,32,1280]{2,1,0:T(8,128)(2,1)}), bf16[4,32,1280]{2,1,0:T(8,128)(2,1)S(1)}, u32[]{:S(2)}, u32[]{:S(2)}) async-start(bf16[4,32,1280]{2,1,0:T(8,128)(2,1)} %bitcast.35), calls=%async_computation.1 | async-start | bytes 655360 | tf_op jit(solution)/shard_map/all_to_all | solution.py:725
  149.9 6.7 %attend.2.refs_0_ = bf16[32,4096]{1,0:T(8,128)(2,1)S(1)} custom-call(s32[16]{0:T(128)S(1)} %get-tuple-element.63.lengths, s32[16]{0:T(128)S(1)} %select_reduce_fusion.2.order, bf16[4,32,1280]{2,1,0:T(8,128)(2,1)S(1)} %all-to-all-done.qkv_ref, f32[32,128]{1,0:T(8,128)S(1)} %get-tuple-element.64.cos_ref, f32[32,128]{1,0:T(8,128)S(1)} %get-tuple-element.65.sin_ref, ...), custom_call_target="tpu_custom_call" | custom-call | flops 268435456 | bytes 16777216 | tf_op jit(solution)/shard_map/attend/pallas_call | solution.py:533
  156.6 3.9 %collective-permute-start.16 = (bf16[32,4096]{1,0:T(8,128)(2,1)S(1)}, bf16[32,4096]{1,0:T(8,128)(2,1)S(1)}, u32[]{:S(2)}, u32[]{:S(2)}) collective-permute-start(bf16[32,4096]{1,0:T(8,128)(2,1)S(1)} %attend.2.refs_0_), channel_id=1, source_target_pairs={{0,1},{1,2},{2,3},{4,5},{5,6},{6,7},{8,9},{9,10},{10,11},{12,13},{... | collective-permute-start | bytes 786440 | tf_op jit(solution)/shard_map/ppermute | solution.py:48
  162.0 6.7 %attend.3.refs_0_ = bf16[32,4096]{1,0:T(8,128)(2,1)S(1)} custom-call(s32[16]{0:T(128)S(1)} %get-tuple-element.62.lengths, s32[16]{0:T(128)S(1)} %select_reduce_fusion.1.order, bf16[4,32,1280]{2,1,0:T(8,128)(2,1)S(1)} %all-to-all-done.1.qkv_ref, f32[32,128]{1,0:T(8,128)S(1)} %get-tuple-element.66.cos_ref, f32[32,128]{1,0:T(8,128)S(1)} %get-tuple-element.67.sin_ref, ...), custom_call_target="tpu_custom_call" | custom-call | flops 268435456 | bytes 16777216 | tf_op jit(solution)/shard_map/attend/pallas_call | solution.py:533
  168.7 4.6 %collective-permute-start.22 = (bf16[32,4096]{1,0:T(8,128)(2,1)S(1)}, bf16[32,4096]{1,0:T(8,128)(2,1)S(1)}, u32[]{:S(2)}, u32[]{:S(2)}) collective-permute-start(bf16[32,4096]{1,0:T(8,128)(2,1)S(1)} %attend.3.refs_0_), channel_id=1, source_target_pairs={{0,1},{1,2},{2,3},{4,5},{5,6},{6,7},{8,9},{9,10},{10,11},{12,13},{... | collective-permute-start | bytes 786440 | tf_op jit(solution)/shard_map/ppermute | solution.py:48
  177.9 4.3 %collective-permute-done.24.refs_2_ = bf16[32,4096]{1,0:T(8,128)(2,1)S(1)} collective-permute-done((bf16[32,4096]{1,0:T(8,128)(2,1)S(1)}, bf16[32,4096]{1,0:T(8,128)(2,1)S(1)}, u32[]{:S(2)}, u32[]{:S(2)}) %collective-permute-start.24) | collective-permute-done | bytes 262176 | tf_op jit(solution)/shard_map/ppermute | solution.py:49
  184.1 4.4 %collective-permute-done.19.refs_4_ = bf16[32,4096]{1,0:T(8,128)(2,1)S(1)} collective-permute-done((bf16[32,4096]{1,0:T(8,128)(2,1)S(1)}, bf16[32,4096]{1,0:T(8,128)(2,1)S(1)}, u32[]{:S(2)}, u32[]{:S(2)}) %collective-permute-start.19) | collective-permute-done | bytes 262176 | tf_op jit(solution)/shard_map/ppermute | solution.py:49
  190.5 5.7 %collective-permute-done.25.refs_4_ = bf16[32,4096]{1,0:T(8,128)(2,1)S(1)} collective-permute-done((bf16[32,4096]{1,0:T(8,128)(2,1)S(1)}, bf16[32,4096]{1,0:T(8,128)(2,1)S(1)}, u32[]{:S(2)}, u32[]{:S(2)}) %collective-permute-start.25) | collective-permute-done | bytes 262176 | tf_op jit(solution)/shard_map/ppermute | solution.py:49
  197.6 3.9 %collective-permute-done.21.refs_6_ = bf16[32,4096]{1,0:T(8,128)(2,1)S(1)} collective-permute-done((bf16[32,4096]{1,0:T(8,128)(2,1)S(1)}, bf16[32,4096]{1,0:T(8,128)(2,1)S(1)}, u32[]{:S(2)}, u32[]{:S(2)}) %collective-permute-start.21) | collective-permute-done | bytes 262176 | tf_op jit(solution)/shard_map/ppermute | solution.py:49
  201.5 7.7 %project.2 = bf16[2,4,16,2048]{3,2,1,0:T(8,128)(2,1)} custom-call(s32[7]{0:T(128)S(1)} %concatenate.24.owners, bf16[32,4096]{1,0:T(8,128)(2,1)S(1)} %attend.2.refs_0_, bf16[32,4096]{1,0:T(8,128)(2,1)S(1)} %collective-permute-done.16.refs_1_, bf16[32,4096]{1,0:T(8,128)(2,1)S(1)} %collective-permute-done.17.refs_2_, ...), custom_call_target="tpu_custom_call" | custom-call | flops 2147483648 | bytes 18350080 | tf_op jit(solution)/shard_map/project/pallas_call | solution.py:598
  209.3 8.2 %project.3 = bf16[2,4,16,2048]{3,2,1,0:T(8,128)(2,1)} custom-call(s32[7]{0:T(128)S(1)} %concatenate.24.owners, bf16[32,4096]{1,0:T(8,128)(2,1)S(1)} %attend.3.refs_0_, bf16[32,4096]{1,0:T(8,128)(2,1)S(1)} %collective-permute-done.22.refs_1_, bf16[32,4096]{1,0:T(8,128)(2,1)S(1)} %collective-permute-done.24.refs_2_, ...), custom_call_target="tpu_custom_call" | custom-call | flops 2147483648 | bytes 18350080 | tf_op jit(solution)/shard_map/project/pallas_call | solution.py:598
  (126 shorter events, 50.1 us)
Async XLA Ops:
  6.5 113.5 %all-gather.2.cloned.1.call-start = ((), (), s32[]{:S(2)}) async-start(), calls=%async_computation.2 | async-start | bytes 5242880 | tf_op jit(solution)/shard_map/all_gather | solution.py:694
  8.0 27.5 %collective-permute-start.5 = (bf16[256,2048]{1,0:T(8,128)(2,1)S(1)}, bf16[256,2048]{1,0:T(8,128)(2,1)S(1)}, u32[]{:S(2)}, u32[]{:S(2)}) collective-permute-start(bf16[256,2048]{1,0:T(8,128)(2,1)S(1)} %bitcast.68), channel_id=1, source_target_pairs={{0,8},{4,12},{8,0},{12,4},{1,9},{5,13},{9,1},{13,5},{2,10},{6,14},... | collective-permute-start | bytes 3145736 | tf_op jit(solution)/shard_map/ppermute | solution.py:33
  15.0 4.5 %collective-permute-start.1 = (f32[256]{0:T(256)S(1)}, f32[256]{0:T(256)S(1)}, u32[]{:S(2)}, u32[]{:S(2)}) collective-permute-start(f32[256]{0:T(256)S(1)} %add.142), channel_id=1, source_target_pairs={{0,2},{1,3},{2,0},{3,1},{4,6},{5,7},{6,4},{7,5},{8,10},{9,11},{10,... | collective-permute-start | bytes 3080 | tf_op jit(solution)/shard_map/ppermute | solution.py:33
  19.5 14.7 %collective-permute-start.2 = (f32[1,272]{1,0:T(1,128)S(1)}, f32[1,272]{1,0:T(1,128)S(1)}, u32[]{:S(2)}, u32[]{:S(2)}) collective-permute-start(f32[1,272]{1,0:T(1,128)S(1)} %reshape.109), channel_id=1, source_target_pairs={{0,8},{4,12},{8,0},{12,4},{1,9},{5,13},{9,1},{13,5},{2,10},{6,14},... | collective-permute-start | bytes 3272 | tf_op jit(solution)/shard_map/ppermute | solution.py:33
  49.3 4.3 %collective-permute-start.8 = (f32[128,128]{1,0:T(8,128)S(1)}, f32[128,128]{1,0:T(8,128)S(1)}, u32[]{:S(2)}, u32[]{:S(2)}) collective-permute-start(f32[128,128]{1,0:T(8,128)S(1)} %slice_bitcast_fusion), channel_id=1, source_target_pairs={{0,8},{4,12},{8,0},{12,4},{1,9},{5,13},{9,1},{13,5},{2,10},{6,14},... | collective-permute-start | bytes 196616 | tf_op jit(solution)/shard_map/ppermute | solution.py:33
  53.7 10.1 %collective-permute-start.9 = (f32[128,128]{1,0:T(8,128)S(1)}, f32[128,128]{1,0:T(8,128)S(1)}, u32[]{:S(2)}, u32[]{:S(2)}) collective-permute-start(f32[128,128]{1,0:T(8,128)S(1)} %fusion.10), channel_id=1, source_target_pairs={{0,1},{1,0},{2,3},{3,2},{4,5},{5,4},{6,7},{7,6},{8,9},{9,8},{10,11... | collective-permute-start | bytes 196616 | tf_op jit(solution)/shard_map/ppermute | solution.py:33
  63.8 10.2 %collective-permute-start.10 = (f32[128,128]{1,0:T(8,128)S(1)}, f32[128,128]{1,0:T(8,128)S(1)}, u32[]{:S(2)}, u32[]{:S(2)}) collective-permute-start(f32[128,128]{1,0:T(8,128)S(1)} %add.151), channel_id=1, source_target_pairs={{0,2},{1,3},{2,0},{3,1},{4,6},{5,7},{6,4},{7,5},{8,10},{9,11},{10,... | collective-permute-start | bytes 196616 | tf_op jit(solution)/shard_map/ppermute | solution.py:33
  86.9 5.3 %collective-permute-start.13 = (f32[2,256,1280]{2,1,0:T(8,128)}, f32[2,256,1280]{2,1,0:T(8,128)}, u32[]{:S(2)}, u32[]{:S(2)}) collective-permute-start(f32[2,256,1280]{2,1,0:T(8,128)} %get-tuple-element.27), channel_id=1, source_target_pairs={{0,4},{4,0},{8,12},{12,8},{1,5},{5,1},{9,13},{13,9},{2,6},{6,2},{1... | collective-permute-start | bytes 7864328 | tf_op jit(solution)/shard_map/ppermute | solution.py:33
  95.1 33.1 %collective-permute-start.14 = (f32[128,1280]{1,0:T(8,128)}, f32[128,1280]{1,0:T(8,128)S(1)}, u32[]{:S(2)}, u32[]{:S(2)}) collective-permute-start(f32[128,1280]{1,0:T(8,128)} %get-tuple-element.40), channel_id=1, source_target_pairs={{0,8},{4,12},{8,0},{12,4},{1,9},{5,13},{9,1},{13,5},{2,10},{6,14},... | collective-permute-start | bytes 1966088 | tf_op jit(solution)/shard_map/ppermute | solution.py:33
  99.8 42.5 %collective-permute-start.15 = (f32[128,1280]{1,0:T(8,128)}, f32[128,1280]{1,0:T(8,128)}, u32[]{:S(2)}, u32[]{:S(2)}) collective-permute-start(f32[128,1280]{1,0:T(8,128)} %get-tuple-element.39), channel_id=1, source_target_pairs={{0,8},{4,12},{8,0},{12,4},{1,9},{5,13},{9,1},{13,5},{2,10},{6,14},... | collective-permute-start | bytes 1966088 | tf_op jit(solution)/shard_map/ppermute | solution.py:33
  130.4 14.3 %all-to-all-start = ((bf16[4,32,1280]{2,1,0:T(8,128)(2,1)}), bf16[4,32,1280]{2,1,0:T(8,128)(2,1)S(1)}, u32[]{:S(2)}, u32[]{:S(2)}) async-start(bf16[4,32,1280]{2,1,0:T(8,128)(2,1)} %bitcast.31), calls=%async_computation | async-start | bytes 655360 | tf_op jit(solution)/shard_map/all_to_all | solution.py:725
  144.7 17.3 %all-to-all-start.1 = ((bf16[4,32,1280]{2,1,0:T(8,128)(2,1)}), bf16[4,32,1280]{2,1,0:T(8,128)(2,1)S(1)}, u32[]{:S(2)}, u32[]{:S(2)}) async-start(bf16[4,32,1280]{2,1,0:T(8,128)(2,1)} %bitcast.35), calls=%async_computation.1 | async-start | bytes 655360 | tf_op jit(solution)/shard_map/all_to_all | solution.py:725
  156.6 18.0 %collective-permute-start.16 = (bf16[32,4096]{1,0:T(8,128)(2,1)S(1)}, bf16[32,4096]{1,0:T(8,128)(2,1)S(1)}, u32[]{:S(2)}, u32[]{:S(2)}) collective-permute-start(bf16[32,4096]{1,0:T(8,128)(2,1)S(1)} %attend.2.refs_0_), channel_id=1, source_target_pairs={{0,1},{1,2},{2,3},{4,5},{5,6},{6,7},{8,9},{9,10},{10,11},{12,13},{... | collective-permute-start | bytes 786440 | tf_op jit(solution)/shard_map/ppermute | solution.py:48
  160.6 14.8 %collective-permute-start.17 = (bf16[32,4096]{1,0:T(8,128)(2,1)S(1)}, bf16[32,4096]{1,0:T(8,128)(2,1)S(1)}, u32[]{:S(2)}, u32[]{:S(2)}) collective-permute-start(bf16[32,4096]{1,0:T(8,128)(2,1)S(1)} %attend.2.refs_0_), channel_id=1, source_target_pairs={{3,2},{2,1},{1,0},{7,6},{6,5},{5,4},{11,10},{10,9},{9,8},{15,14},{... | collective-permute-start | bytes 786440 | tf_op jit(solution)/shard_map/ppermute | solution.py:49
  168.7 8.5 %collective-permute-start.22 = (bf16[32,4096]{1,0:T(8,128)(2,1)S(1)}, bf16[32,4096]{1,0:T(8,128)(2,1)S(1)}, u32[]{:S(2)}, u32[]{:S(2)}) collective-permute-start(bf16[32,4096]{1,0:T(8,128)(2,1)S(1)} %attend.3.refs_0_), channel_id=1, source_target_pairs={{0,1},{1,2},{2,3},{4,5},{5,6},{6,7},{8,9},{9,10},{10,11},{12,13},{... | collective-permute-start | bytes 786440 | tf_op jit(solution)/shard_map/ppermute | solution.py:48
  173.3 8.8 %collective-permute-start.24 = (bf16[32,4096]{1,0:T(8,128)(2,1)S(1)}, bf16[32,4096]{1,0:T(8,128)(2,1)S(1)}, u32[]{:S(2)}, u32[]{:S(2)}) collective-permute-start(bf16[32,4096]{1,0:T(8,128)(2,1)S(1)} %attend.3.refs_0_), channel_id=1, source_target_pairs={{3,2},{2,1},{1,0},{7,6},{6,5},{5,4},{11,10},{10,9},{9,8},{15,14},{... | collective-permute-start | bytes 786440 | tf_op jit(solution)/shard_map/ppermute | solution.py:49
  174.6 8.8 %collective-permute-start.18 = (bf16[32,4096]{1,0:T(8,128)(2,1)S(1)}, bf16[32,4096]{1,0:T(8,128)(2,1)S(1)}, u32[]{:S(2)}, u32[]{:S(2)}) collective-permute-start(bf16[32,4096]{1,0:T(8,128)(2,1)S(1)} %collective-permute-done.16.refs_1_), channel_id=1, source_target_pairs={{1,2},{2,3},{5,6},{6,7},{9,10},{10,11},{13,14},{14,15},{17,18},{18... | collective-permute-start | bytes 786440 | tf_op jit(solution)/shard_map/ppermute | solution.py:48
  175.3 13.2 %collective-permute-start.19 = (bf16[32,4096]{1,0:T(8,128)(2,1)S(1)}, bf16[32,4096]{1,0:T(8,128)(2,1)S(1)}, u32[]{:S(2)}, u32[]{:S(2)}) collective-permute-start(bf16[32,4096]{1,0:T(8,128)(2,1)S(1)} %collective-permute-done.17.refs_2_), channel_id=1, source_target_pairs={{2,1},{1,0},{6,5},{5,4},{10,9},{9,8},{14,13},{13,12},{18,17},{17,1... | collective-permute-start | bytes 786440 | tf_op jit(solution)/shard_map/ppermute | solution.py:49
  177.2 12.7 %collective-permute-start.23 = (bf16[32,4096]{1,0:T(8,128)(2,1)S(1)}, bf16[32,4096]{1,0:T(8,128)(2,1)S(1)}, u32[]{:S(2)}, u32[]{:S(2)}) collective-permute-start(bf16[32,4096]{1,0:T(8,128)(2,1)S(1)} %collective-permute-done.22.refs_1_), channel_id=1, source_target_pairs={{1,2},{2,3},{5,6},{6,7},{9,10},{10,11},{13,14},{14,15},{17,18},{18... | collective-permute-start | bytes 786440 | tf_op jit(solution)/shard_map/ppermute | solution.py:48
  182.1 14.1 %collective-permute-start.25 = (bf16[32,4096]{1,0:T(8,128)(2,1)S(1)}, bf16[32,4096]{1,0:T(8,128)(2,1)S(1)}, u32[]{:S(2)}, u32[]{:S(2)}) collective-permute-start(bf16[32,4096]{1,0:T(8,128)(2,1)S(1)} %collective-permute-done.24.refs_2_), channel_id=1, source_target_pairs={{2,1},{1,0},{6,5},{5,4},{10,9},{9,8},{14,13},{13,12},{18,17},{17,1... | collective-permute-start | bytes 786440 | tf_op jit(solution)/shard_map/ppermute | solution.py:49
  183.4 14.2 %collective-permute-start.20 = (bf16[32,4096]{1,0:T(8,128)(2,1)S(1)}, bf16[32,4096]{1,0:T(8,128)(2,1)S(1)}, u32[]{:S(2)}, u32[]{:S(2)}) collective-permute-start(bf16[32,4096]{1,0:T(8,128)(2,1)S(1)} %collective-permute-done.18.refs_3_), channel_id=1, source_target_pairs={{2,3},{6,7},{10,11},{14,15},{18,19},{22,23},{26,27},{30,31}} | collective-permute-start | bytes 786440 | tf_op jit(solution)/shard_map/ppermute | solution.py:48
  188.5 13.0 %collective-permute-start.21 = (bf16[32,4096]{1,0:T(8,128)(2,1)S(1)}, bf16[32,4096]{1,0:T(8,128)(2,1)S(1)}, u32[]{:S(2)}, u32[]{:S(2)}) collective-permute-start(bf16[32,4096]{1,0:T(8,128)(2,1)S(1)} %collective-permute-done.19.refs_4_), channel_id=1, source_target_pairs={{1,0},{5,4},{9,8},{13,12},{17,16},{21,20},{25,24},{29,28}} | collective-permute-start | bytes 786440 | tf_op jit(solution)/shard_map/ppermute | solution.py:49
  189.8 19.4 %collective-permute-start.26 = (bf16[32,4096]{1,0:T(8,128)(2,1)S(1)}, bf16[32,4096]{1,0:T(8,128)(2,1)S(1)}, u32[]{:S(2)}, u32[]{:S(2)}) collective-permute-start(bf16[32,4096]{1,0:T(8,128)(2,1)S(1)} %collective-permute-done.23.refs_3_), channel_id=1, source_target_pairs={{2,3},{6,7},{10,11},{14,15},{18,19},{22,23},{26,27},{30,31}} | collective-permute-start | bytes 786440 | tf_op jit(solution)/shard_map/ppermute | solution.py:48
  196.2 13.0 %collective-permute-start.27 = (bf16[32,4096]{1,0:T(8,128)(2,1)S(1)}, bf16[32,4096]{1,0:T(8,128)(2,1)}, u32[]{:S(2)}, u32[]{:S(2)}) collective-permute-start(bf16[32,4096]{1,0:T(8,128)(2,1)S(1)} %collective-permute-done.25.refs_4_), channel_id=1, source_target_pairs={{1,0},{5,4},{9,8},{13,12},{17,16},{21,20},{25,24},{29,28}} | collective-permute-start | bytes 786440 | tf_op jit(solution)/shard_map/ppermute | solution.py:49
  (19 other events, 152.2 us)
Sparse Core Ops, SparseCore 0:
  34.9 85.0 all-gather.1

commit v4 on v3

--- a/solution.py
+++ b/solution.py
@@ -23,6 +23,7 @@
 MIB = 1 << 20
 F32 = jnp.float32
 BF16 = jnp.bfloat16
+F16 = jnp.float16
 VMEM = pl.BlockSpec(memory_space=pltpu.VMEM)
 SMEM = pl.BlockSpec(memory_space=pltpu.SMEM)
 HBM = pl.BlockSpec(memory_space=pltpu.HBM)
@@ -553,24 +554,37 @@
     )(lengths, order, qkv, cosine, sine, cache)
 
 
-def out_kernel(owners, *refs):
-    blocks = refs[:7]
-    w_ref, out_ref, lhs, total, held, sems = refs[7:]
+def out_kernel(count, has_earlier, owners, *refs):
+    blocks = refs[:count]
+    w_ref = refs[count]
+    out_ref, lhs, total, held, sems = refs[-5:]
     local = blocks[0].shape[0]
     rows = local // STEPS
     tiles, depth, columns = held.shape
+    halves = out_ref.shape[2]
     copies = [
         pltpu.make_async_copy(w_ref.at[pl.ds(k * depth, depth), :], held.at[k], sems.at[k])
         for k in range(tiles)
     ]
     for copy in copies:
         copy.start()
+    slots = count // halves
+
+    def place(j):
+        used = jnp.int32(0)
+        for i in range(j % slots):
+            used = used + (owners[i] >= 0).astype(jnp.int32)
+        return (j // slots) * (lhs.shape[0] // halves) + used * local
+
+    lhs[...] = jnp.zeros_like(lhs)
     for j, ref in enumerate(blocks):
 
-        @pl.when(owners[j] >= 0)
+        @pl.when(owners[j % slots] >= 0)
         def _():
-            lhs[pl.ds(pl.multiple_of(owners[j] * local, local), local), :] = ref[...]
-
+            lhs[pl.ds(pl.multiple_of(place(j), local), local), :] = ref[...]
+
+    if has_earlier:
+        out_ref[...] = refs[count + 1][...]
     width = min(512, columns)
     for k, copy in enumerate(copies):
         copy.wait()
@@ -581,39 +595,46 @@
             )
             if k > 0:
                 product = total[:, span] + product
-            if k < tiles - 1:
-                total[:, span] = product
-                continue
-            block = product.reshape(4, rows // RUN, STEPS, RUN, width)
+            total[:, span] = product
+    for j in range(count):
+
+        @pl.when(owners[j % slots] >= 0)
+        def _():
+            block = total[pl.ds(pl.multiple_of(place(j), local), local), :]
+            block = block.reshape(rows // RUN, STEPS, RUN, columns)
             for s in range(STEPS):
-                piece = block[:, :, s].reshape(4, rows, width)
-                out_ref[s, :, :, span] = piece.astype(BF16)
-
-
-def project(owners, blocks, weight):
-    local, depth = blocks[0].shape
+                piece = block[:, s].reshape(rows, columns).astype(BF16)
+                out_ref[s, owners[j % slots], j // slots] = piece
+
+
+def project(owners, blocks, weight, present, earlier=None):
+    halves = len(blocks)
+    flat = [block for part in blocks for block in part]
+    local, depth = flat[0].shape
     columns = weight.shape[1]
     tile = min(512, depth)
     rows = local // STEPS
+    count = len(flat)
+    more = [] if earlier is None else [earlier]
     return pl.pallas_call(
-        out_kernel,
-        out_shape=jax.ShapeDtypeStruct((STEPS, 4, rows, columns), BF16),
-        in_specs=[SMEM] + [VMEM] * 7 + [HBM],
+        functools.partial(out_kernel, count, earlier is not None),
+        out_shape=jax.ShapeDtypeStruct((STEPS, 4, halves, rows, columns), BF16),
+        in_specs=[SMEM] + [VMEM] * count + [HBM] + [VMEM] * len(more),
         out_specs=VMEM,
         scratch_shapes=[
-            pltpu.VMEM((4 * local, depth), BF16),
-            pltpu.VMEM((4 * local, columns), F32),
+            pltpu.VMEM((present * halves * local, depth), BF16),
+            pltpu.VMEM((present * halves * local, columns), F32),
             pltpu.VMEM((depth // tile, tile, columns), BF16),
             pltpu.SemaphoreType.DMA((depth // tile,)),
         ],
         compiler_params=pltpu.CompilerParams(vmem_limit_bytes=52 * MIB),
         cost_estimate=pl.CostEstimate(
-            flops=8 * local * depth * columns,
-            bytes_accessed=2 * depth * columns + 8 * local * (depth + columns),
+            flops=2 * present * halves * local * depth * columns,
+            bytes_accessed=2 * depth * columns + 4 * present * local * (depth + columns),
             transcendentals=0,
         ),
         name="project",
-    )(owners, *blocks, weight)
+    )(owners, *flat, weight, *more)
 
 
 def lookup(identity, table):
@@ -658,7 +679,8 @@
     model_width = input_norm_scale.shape[0]
     rows_here = lengths.shape[0]
     unit = min(RUN, rows_here)
-    halves = HALVES if rows_here % (HALVES * RUN) == 0 else 1
+    line = tensor_count == 4 and rows_here % (HALVES * RUN) == 0
+    halves = HALVES if line else 1
     part_rows = rows_here // halves
     local = STEPS * part_rows
     held_slots = adapter_down_weight.shape[0]
@@ -666,6 +688,16 @@
 
     raw = hidden.reshape(STEPS, tensor_count, halves, part_rows // unit, unit, span)
     raw = raw.transpose(2, 1, 3, 0, 4, 5).reshape(STEPS * rows, span)
+    own_index = tensor_pos.reshape(1).astype(jnp.int32)
+    owners = [own_index] + [hop_owners(tensor_pos, hop) for hop in (1, 2, 3)]
+    count = tensor_count * local
+    parts = [slice(h * count, (h + 1) * count) for h in range(halves)]
+    everything = [None] * halves
+    hops = None
+    everything[0] = lax.all_gather(raw[parts[0]], "tensor", axis=0, tiled=False)
+    if halves > 1:
+        hops = line_gather(raw[parts[1]], "tensor")
+
     values = raw.astype(F32)
     squares = jnp.sum(values * values, axis=1)
     squares = summed_over(squares, "tensor")
@@ -674,6 +706,8 @@
         own_runs = own_runs.reshape(tensor_count, halves, -1).swapaxes(0, 1).reshape(-1)
     told = jnp.concatenate([squares, own_runs.astype(F32)]).reshape(1, -1)
     told = jnp.concatenate([told, swap(told, "store", 2)], axis=0)
+    if halves > 1:
+        told, hops[0] = lax.optimization_barrier((told, hops[0]))
     told = jnp.concatenate([told, swap(told, "store", 1)], axis=0)
     told = jnp.stack([told[d] for d in (0, 2, 1, 3)])
     told = jnp.stack([jnp.stack([told[p ^ q] for q in range(4)]) for p in range(4)])
@@ -689,10 +723,6 @@
     scales = scales[:, :, None]
     own_scale = lax.dynamic_index_in_dim(scales, store_pos, 0, keepdims=False)
 
-    line = tensor_count == 4 and part_rows % RUN == 0
-    own_index = tensor_pos.reshape(1).astype(jnp.int32)
-    everything = lax.all_gather(raw, "tensor", axis=0, tiled=False)
-
     across = swap(raw, "store", 2)
     beside = swap(raw, "store", 1)
     diagonal = swap(across, "store", 1)
@@ -701,31 +731,38 @@
     kept, passed = shrink_rows(place, mine, (raw, beside, across, diagonal), scales, gain, down)
     kept = kept + swap(passed, "store", 1)
     shrunk = kept[0] + swap(kept[1], "store", 2)
+    if halves > 1:
+        shrunk, hops[1] = lax.optimization_barrier((shrunk, hops[1]))
     shrunk = summed_over(shrunk, "tensor").astype(BF16)
     shrunk = jnp.stack([shrunk, swap(shrunk, "store", 2)])
     kept, passed = grow_rows(place, mine, shrunk, swap(shrunk, "store", 1), adapter_up_weight)
+    passed = swap(passed.astype(F16), "store", 1).astype(F32)
+    deltas = []
+    for part in parts:
+        delta = swap((kept[1, part] + passed[1, part]).astype(F16), "store", 2).astype(F32)
+        deltas.append((kept[0, part] + passed[0, part]) + delta)
+
+    weight = query_key_value_weight
     raw, passed = lax.optimization_barrier((raw, passed))
-    own = base_block((raw,), own_scale, gains, query_key_value_weight, own_index, None)
-    passed = swap(passed, "store", 1)
-
-    count = tensor_count * local
-    parts = []
-    for h in range(halves):
-        part = slice(h * count, (h + 1) * count)
-        delta = swap(kept[1, part] + passed[1, part], "store", 2)
-        delta = (kept[0, part] + passed[0, part]) + delta
-        if parts:
-            everything, parts[-1] = lax.optimization_barrier((everything, parts[-1]))
-        total = base_rows(
-            own_index, everything, own_scale[part], gains, own, query_key_value_weight, h * count
-        )
-        parts.append((total + delta).astype(BF16).reshape(tensor_count, local, -1))
+    own = base_block((raw[parts[0]],), own_scale[parts[0]], gains, weight, own_index, None)
+    total = base_rows(own_index, everything[0], own_scale[parts[0]], gains, own, weight, 0)
+    mixed = [(total + deltas[0]).astype(BF16)]
+    if halves > 1:
+        blocks = (raw[parts[1]],) + hops[0] + hops[1]
+        near = jnp.concatenate(owners[:3])
+        total = base_block(blocks, own_scale[parts[1]], gains, weight, near, None)
+        hops[2], mixed[0] = lax.optimization_barrier((hops[2], mixed[0]))
+        total = base_block(hops[2], own_scale[parts[1]], gains, weight, owners[3], total)
+        mixed.append((total + deltas[1]).astype(BF16))
+    mixed = [qkv.reshape(tensor_count, local, -1) for qkv in mixed]
 
     contexts = []
-    exchanged = [lax.all_to_all(qkv, "tensor", 0, 0, tiled=True) for qkv in parts]
+    exchanged = []
+    for qkv in mixed:
+        if exchanged:
+            qkv, exchanged[-1] = lax.optimization_barrier((qkv, exchanged[-1]))
+        exchanged.append(lax.all_to_all(qkv, "tensor", 0, 0, tiled=True))
     for h, moved in enumerate(exchanged):
-        if h + 1 < halves:
-            moved, parts[-1] = lax.optimization_barrier((moved, parts[-1]))
         if tensor_count != 4:
             q_columns = HEADS * HD // tensor_count
             pieces = []
@@ -739,24 +776,21 @@
             attend(here, ascending(here), moved, cosine, sine, key_value_cache, h * part_rows, unit)
         )
 
-    results = []
     if line:
-        owners = [own_index] + [hop_owners(tensor_pos, hop) for hop in (1, 2, 3)]
-        owners = jnp.concatenate(owners)
         hops = [line_gather(context, "tensor") for context in contexts]
-        for h in range(halves):
-            if h + 1 < halves:
-                hops[h], hops[h + 1][1] = lax.optimization_barrier((hops[h], hops[h + 1][1]))
-            blocks = (contexts[h],) + hops[h][0] + hops[h][1] + hops[h][2]
-            results.append(project(owners, blocks, output_weight))
+        first = [(context,) + hop[0] for context, hop in zip(contexts, hops)]
+        last = [hop[1] + hop[2] for hop in hops]
+        output = project(jnp.concatenate(owners[:2]), first, output_weight, 3)
+        output = project(jnp.concatenate(owners[2:]), last, output_weight, 2, output)
     else:
+        results = []
         for context in contexts:
             context = lax.all_gather(context, "tensor", axis=0, tiled=True)
             result = jnp.dot(context, output_weight, preferred_element_type=F32).astype(BF16)
             result = result.reshape(tensor_count, part_rows // unit, STEPS, unit, -1)
             result = result.transpose(2, 0, 1, 3, 4).reshape(STEPS, tensor_count, part_rows, -1)
             results.append(result)
-    output = results[0] if halves == 1 else jnp.concatenate(results, axis=2)
+        output = jnp.stack(results, axis=2)
     return output.reshape(STEPS, rows, -1)
 
 

time: 227 us -> 226 us (level)
  waiting for transfers between devices: 89.2 us -> 74.2 us
  starting transfers between devices: 41.3 us -> 51 us
  local copies, waits for them, and re-layouts: 5.09 us -> 9.34 us
    all_gather x1, waiting for transfers between devices: 18.4 us -> 0.02 us  [on_device(): everything[0] = lax.all_gather(raw[parts[0]], 'tensor', axis=0, tiled=False)]
    pallas_call x2 -> x1, Pallas kernels: 16.4 us -> 6 us  [base_rows(): pl.pallas_call(functools.partial(base_kernel, first_row), out_shape=jax.S...]
    pallas_call x1 -> x3, Pallas kernels: 3.58 us -> 13.7 us  [base_block(): pl.pallas_call(functools.partial(block_kernel, count, total is not None),...]
    ppermute x16, waiting for transfers between devices: 52 us -> 42.9 us  [swap(): return lax.ppermute(values, axis, [(i, i ^ distance) for i in range(count)])]
    ppermute x6 -> x9, waiting for transfers between devices: 18.3 us -> 26.2 us  [line_gather(): down = lax.ppermute(down, axis, [(i, i - 1) for i in range(4 - hop, 0, -1)])]
    ppermute x6 -> x9, starting transfers between devices: 11.2 us -> 16.9 us  [line_gather(): up = lax.ppermute(up, axis, [(i, i + 1) for i in range(hop - 1, 3)])]
    convert_element_type x2 -> x5, other arithmetic: 4.55 us -> 10.1 us  [the longest x2 4.53 us: on_device(): passed = swap(passed.astype(F16), 'store', 1).astype(F32)]
    all_to_all x2, waiting for transfers between devices: 0.01 us -> 4.38 us  [on_device(): exchanged.append(lax.all_to_all(qkv, 'tensor', 0, 0, tiled=True))]
  transfers between devices with their start and end apart: 31 -> 37, of which waited for: 17 -> 15; matrix products, arithmetic and copies ran while one was open for 6% -> 8% of each run, Pallas kernels for 25% -> 21%
where the time goes in v4:
time: 226 us
  waiting for transfers between devices  74.2 us (33%)
  Pallas kernels  63.5 us (28%)
  starting transfers between devices  51 us (23%)
  between operations  14.1 us (6%)
  other arithmetic  13.5 us (6%)
  local copies, waits for them, and re-layouts  9.34 us (4%)
    ppermute x16, waiting for transfers between devices, swap(): return lax.ppermute(values, axis, [(i, i ^ distance) for i in range(count)])  42.9 us
    ppermute x9, waiting for transfers between devices, line_gather(): down = lax.ppermute(down, axis, [(i, i - 1) for i in range(4 - hop, 0, -1)])  26.2 us
    pallas_call x2, Pallas kernels, project(): pl.pallas_call(functools.partial(out_kernel, count, earlier is not None),...  16.9 us
    ppermute x9, starting transfers between devices, line_gather(): up = lax.ppermute(up, axis, [(i, i + 1) for i in range(hop - 1, 3)])  16.9 us
    pallas_call x3, Pallas kernels, base_block(): pl.pallas_call(functools.partial(block_kernel, count, total is not None),...  13.7 us
    ppermute x16, starting transfers between devices, swap(): return lax.ppermute(values, axis, [(i, i ^ distance) for i in range(count)])  13.7 us
    pallas_call x2, Pallas kernels, attend(): pl.pallas_call(functools.partial(attend_kernel, unit, first_row), out_sha...  13.4 us
    ppermute x9, starting transfers between devices, line_gather(): down = lax.ppermute(down, axis, [(i, i - 1) for i in range(4 - hop, 0, -1)])  11.6 us
  transfers between devices with their start and end apart: 37, of which 15 were waited for; matrix products, arithmetic and copies ran while one was open for 8% of the time, Pallas kernels for 21%

profile of v4, /device:TPU:0, one launch (start us, length us, event | category | flops | bytes accessed | tf_op | source)
XLA Modules:
  0.0 225.7 jit_solution(9504370643493741425)
XLA Ops:
  12.1 3.5 %collective-permute-start = (bf16[128,2048]{1,0:T(8,128)(2,1)}, bf16[128,2048]{1,0:T(8,128)(2,1)S(1)}, u32[]{:S(2)}, u32[]{:S(2)}) collective-permute-start(bf16[128,2048]{1,0:T(8,128)(2,1)} %bitcast.6), channel_id=1, source_target_pairs={{0,1},{1,2},{2,3},{4,5},{5,6},{6,7},{8,9},{9,10},{10,11},{12,13},{... | collective-permute-start | bytes 1572872 | tf_op jit(solution)/shard_map/ppermute | solution.py:49
  20.0 10.9 %collective-permute-done.6 = f32[256]{0:T(256)S(1)} collective-permute-done((f32[256]{0:T(256)S(1)}, f32[256]{0:T(256)S(1)}, u32[]{:S(2)}, u32[]{:S(2)}) %collective-permute-start.6) | collective-permute-done | bytes 1056 | tf_op jit(solution)/shard_map/ppermute | solution.py:34
  43.2 7.1 %shrink_rows.1 = (f32[2,128,128]{2,1,0:T(8,128)}, f32[2,128,128]{2,1,0:T(8,128)}) custom-call(s32[1]{0:T(128)} %bitcast.18.place_ref, s32[64]{0:T(128)} %compare_select_fusion.slots, bf16[256,2048]{1,0:T(8,128)(2,1)} %bitcast.75, bf16[256,2048]{1,0:T(8,128)(2,1)} %copy-done.7, bf16[256,2048]{1,0:T(8,128)(2,1)} %collective-permute-done.11.x2, ...), custom_call_target="tpu_custom_call" | custom-call | flops 67108864 | bytes 8388608 | tf_op jit(solution)/shard_map/shrink_rows/pallas_call | solution.py:280
  54.3 4.3 %collective-permute-done.14 = f32[128,128]{1,0:T(8,128)S(1)} collective-permute-done((f32[128,128]{1,0:T(8,128)S(1)}, f32[128,128]{1,0:T(8,128)S(1)}, u32[]{:S(2)}, u32[]{:S(2)}) %collective-permute-start.14) | collective-permute-done | bytes 65568 | tf_op jit(solution)/shard_map/ppermute | solution.py:34
  58.7 12.0 %collective-permute-done.4.refs_4_ = bf16[128,2048]{1,0:T(8,128)(2,1)} collective-permute-done((bf16[128,2048]{1,0:T(8,128)(2,1)S(1)}, bf16[128,2048]{1,0:T(8,128)(2,1)}, u32[]{:S(2)}, u32[]{:S(2)}) %collective-permute-start.4) | collective-permute-done | bytes 524320 | tf_op jit(solution)/shard_map/ppermute | solution.py:50
  72.3 7.8 %collective-permute-done.15 = f32[128,128]{1,0:T(8,128)S(1)} collective-permute-done((f32[128,128]{1,0:T(8,128)S(1)}, f32[128,128]{1,0:T(8,128)S(1)}, u32[]{:S(2)}, u32[]{:S(2)}) %collective-permute-start.15) | collective-permute-done | bytes 65568 | tf_op jit(solution)/shard_map/ppermute | solution.py:34
  80.2 10.1 %collective-permute-done.16 = f32[128,128]{1,0:T(8,128)S(1)} collective-permute-done((f32[128,128]{1,0:T(8,128)S(1)}, f32[128,128]{1,0:T(8,128)S(1)}, u32[]{:S(2)}, u32[]{:S(2)}) %collective-permute-start.16) | collective-permute-done | bytes 65568 | tf_op jit(solution)/shard_map/ppermute | solution.py:34
  90.4 3.9 %collective-permute-done.17 = bf16[128,128]{1,0:T(8,128)(2,1)S(1)} collective-permute-done((bf16[128,128]{1,0:T(8,128)(2,1)S(1)}, bf16[128,128]{1,0:T(8,128)(2,1)S(1)}, u32[]{:S(2)}, u32[]{:S(2)}) %collective-permute-start.17) | collective-permute-done | bytes 32800 | tf_op jit(solution)/shard_map/ppermute | solution.py:34
  96.3 6.4 %grow_rows.1 = (f32[2,256,1280]{2,1,0:T(8,128)}, f32[2,256,1280]{2,1,0:T(8,128)}) custom-call(s32[1]{0:T(128)} %bitcast.18.place_ref, s32[64]{0:T(128)} %compare_select_fusion.slots, bf16[2,128,128]{2,1,0:T(8,128)(2,1)} %copy-done.9, bf16[2,128,128]{2,1,0:T(8,128)(2,1)} %copy-done.10, bf16[32,64,1280]{2,1,0:T(8,128)(2,1)} %up_ref.1), custom_call_target="tpu_custom_call" | custom-call | flops 41943040 | bytes 5242880 | tf_op jit(solution)/shard_map/grow_rows/pallas_call | solution.py:353
  118.5 6.0 %base_rows.1 = f32[128,1280]{1,0:T(8,128)S(1)} custom-call(s32[1]{0:T(128)} %bitcast.7.owners.place_ref, bf16[4,128,2048]{2,1,0:T(8,128)(2,1)S(1)} %copy-done, f32[128,1]{1,0:T(8,128)S(1)} %copy.35.refs_1_.scale_ref, f32[1,8192]{1,0:T(1,128)S(1)} %bitcast.70, f32[128,1280]{1,0:T(8,128)S(1)} %base_block.3.own_ref, bf16[8192,1280]{1,0:T(8,128)(2,1)} %refs_4_.1), custom_call_target="tpu_custom_call" | custom-call | flops 2013265920 | bytes 18612224 | tf_op jit(solution)/shard_map/base_rows/pallas_call | solution.py:156
  124.5 7.3 %base_block.4.refs_5_ = f32[128,1280]{1,0:T(8,128)S(1)} custom-call(s32[5]{0:T(128)S(1)} %concatenate.33.owners, bf16[128,2048]{1,0:T(8,128)(2,1)S(1)} %get-tuple-element.39.refs_0_, bf16[128,2048]{1,0:T(8,128)(2,1)S(1)} %collective-permute-done.refs_1_, bf16[128,2048]{1,0:T(8,128)(2,1)S(1)} %collective-permute-done.3.refs_2_, ...), custom_call_target="tpu_custom_call" | custom-call | flops 3355443200 | bytes 7077888 | tf_op jit(solution)/shard_map/base_block/pallas_call | solution.py:103
  134.0 5.4 %all-to-all-start = ((bf16[4,32,1280]{2,1,0:T(8,128)(2,1)}), bf16[4,32,1280]{2,1,0:T(8,128)(2,1)S(1)}, u32[]{:S(2)}, u32[]{:S(2)}) async-start(bf16[4,32,1280]{2,1,0:T(8,128)(2,1)} %bitcast.35), calls=%async_computation | async-start | bytes 655360 | tf_op jit(solution)/shard_map/all_to_all | solution.py:764
  139.4 3.5 %base_block.5 = f32[128,1280]{1,0:T(8,128)S(1)} custom-call(s32[2]{0:T(128)S(1)} %pad_add_fusion.1.owners, bf16[128,2048]{1,0:T(8,128)(2,1)S(1)} %collective-permute-done.2.refs_0_, bf16[128,2048]{1,0:T(8,128)(2,1)S(1)} %collective-permute-done.5.refs_1_, f32[128,1]{1,0:T(8,128)S(1)} %copy.37.refs_5_.refs_2_, f32[1,8192]{1,0:T(1,128)S(1)} %bitcast.72, ...), custom_call_target="tpu_custom_call" | custom-call | flops 1342177280 | bytes 7077888 | tf_op jit(solution)/shard_map/base_block/pallas_call | solution.py:103
  145.2 4.4 %all-to-all-done.qkv_ref = bf16[4,32,1280]{2,1,0:T(8,128)(2,1)S(1)} async-done(((bf16[4,32,1280]{2,1,0:T(8,128)(2,1)}), bf16[4,32,1280]{2,1,0:T(8,128)(2,1)S(1)}, u32[]{:S(2)}, u32[]{:S(2)}) %all-to-all-start) | async-done | bytes 327712 | tf_op jit(solution)/shard_map/all_to_all | solution.py:764
  149.6 3.5 %all-to-all-start.1 = ((bf16[4,32,1280]{2,1,0:T(8,128)(2,1)}), bf16[4,32,1280]{2,1,0:T(8,128)(2,1)S(1)}, u32[]{:S(2)}, u32[]{:S(2)}) async-start(bf16[4,32,1280]{2,1,0:T(8,128)(2,1)} %bitcast.34), calls=%async_computation.1 | async-start | bytes 655360 | tf_op jit(solution)/shard_map/all_to_all | solution.py:764
  153.7 6.7 %attend.2.refs_0_ = bf16[32,4096]{1,0:T(8,128)(2,1)S(1)} custom-call(s32[16]{0:T(128)S(1)} %get-tuple-element.69.lengths, s32[16]{0:T(128)S(1)} %select_reduce_fusion.2.order, bf16[4,32,1280]{2,1,0:T(8,128)(2,1)S(1)} %all-to-all-done.qkv_ref, f32[32,128]{1,0:T(8,128)S(1)} %get-tuple-element.70.cos_ref, f32[32,128]{1,0:T(8,128)S(1)} %get-tuple-element.71.sin_ref, ...), custom_call_target="tpu_custom_call" | custom-call | flops 268435456 | bytes 16777216 | tf_op jit(solution)/shard_map/attend/pallas_call | solution.py:534
  160.4 3.9 %collective-permute-start.22 = (bf16[32,4096]{1,0:T(8,128)(2,1)S(1)}, bf16[32,4096]{1,0:T(8,128)(2,1)S(1)}, u32[]{:S(2)}, u32[]{:S(2)}) collective-permute-start(bf16[32,4096]{1,0:T(8,128)(2,1)S(1)} %attend.2.refs_0_), channel_id=1, source_target_pairs={{0,1},{1,2},{2,3},{4,5},{5,6},{6,7},{8,9},{9,10},{10,11},{12,13},{... | collective-permute-start | bytes 786440 | tf_op jit(solution)/shard_map/ppermute | solution.py:49
  165.6 6.7 %attend.3.refs_3_ = bf16[32,4096]{1,0:T(8,128)(2,1)S(1)} custom-call(s32[16]{0:T(128)S(1)} %get-tuple-element.68.lengths, s32[16]{0:T(128)S(1)} %select_reduce_fusion.1.order, bf16[4,32,1280]{2,1,0:T(8,128)(2,1)S(1)} %all-to-all-done.1.qkv_ref, f32[32,128]{1,0:T(8,128)S(1)} %get-tuple-element.72.cos_ref, f32[32,128]{1,0:T(8,128)S(1)} %get-tuple-element.73.sin_ref, ...), custom_call_target="tpu_custom_call" | custom-call | flops 268435456 | bytes 16777216 | tf_op jit(solution)/shard_map/attend/pallas_call | solution.py:534
  172.3 4.6 %collective-permute-start.28 = (bf16[32,4096]{1,0:T(8,128)(2,1)S(1)}, bf16[32,4096]{1,0:T(8,128)(2,1)S(1)}, u32[]{:S(2)}, u32[]{:S(2)}) collective-permute-start(bf16[32,4096]{1,0:T(8,128)(2,1)S(1)} %attend.3.refs_3_), channel_id=1, source_target_pairs={{0,1},{1,2},{2,3},{4,5},{5,6},{6,7},{8,9},{9,10},{10,11},{12,13},{... | collective-permute-start | bytes 786440 | tf_op jit(solution)/shard_map/ppermute | solution.py:49
  181.5 4.3 %collective-permute-done.30.refs_5_ = bf16[32,4096]{1,0:T(8,128)(2,1)S(1)} collective-permute-done((bf16[32,4096]{1,0:T(8,128)(2,1)S(1)}, bf16[32,4096]{1,0:T(8,128)(2,1)S(1)}, u32[]{:S(2)}, u32[]{:S(2)}) %collective-permute-start.30) | collective-permute-done | bytes 262176 | tf_op jit(solution)/shard_map/ppermute | solution.py:50
  187.9 3.8 %collective-permute-done.25.refs_1_ = bf16[32,4096]{1,0:T(8,128)(2,1)S(1)} collective-permute-done((bf16[32,4096]{1,0:T(8,128)(2,1)S(1)}, bf16[32,4096]{1,0:T(8,128)(2,1)S(1)}, u32[]{:S(2)}, u32[]{:S(2)}) %collective-permute-start.25) | collective-permute-done | bytes 262176 | tf_op jit(solution)/shard_map/ppermute | solution.py:50
  193.6 6.2 %collective-permute-done.31.refs_5_ = bf16[32,4096]{1,0:T(8,128)(2,1)S(1)} collective-permute-done((bf16[32,4096]{1,0:T(8,128)(2,1)S(1)}, bf16[32,4096]{1,0:T(8,128)(2,1)S(1)}, u32[]{:S(2)}, u32[]{:S(2)}) %collective-permute-start.31) | collective-permute-done | bytes 262176 | tf_op jit(solution)/shard_map/ppermute | solution.py:50
  201.1 8.1 %project.2.refs_9_ = bf16[2,4,2,16,2048]{4,3,2,1,0:T(8,128)(2,1)} custom-call(s32[3]{0:T(128)S(1)} %pad_add_fusion.2.owners, bf16[32,4096]{1,0:T(8,128)(2,1)S(1)} %attend.2.refs_0_, bf16[32,4096]{1,0:T(8,128)(2,1)S(1)} %collective-permute-done.22.refs_1_, bf16[32,4096]{1,0:T(8,128)(2,1)S(1)} %collective-permute-done.24.refs_2_, ...), custom_call_target="tpu_custom_call" | custom-call | flops 3221225472 | bytes 19136512 | tf_op jit(solution)/shard_map/project/pallas_call | solution.py:619
  210.0 8.8 %project.3 = bf16[2,4,2,16,2048]{4,3,2,1,0:T(8,128)(2,1)} custom-call(s32[4]{0:T(128)S(1)} %pad_add_fusion.owners, bf16[32,4096]{1,0:T(8,128)(2,1)S(1)} %collective-permute-done.23.refs_0_, bf16[32,4096]{1,0:T(8,128)(2,1)S(1)} %collective-permute-done.25.refs_1_, bf16[32,4096]{1,0:T(8,128)(2,1)S(1)} %collective-permute-done.26.refs_2_, ...), custom_call_target="tpu_custom_call" | custom-call | flops 2147483648 | bytes 18350080 | tf_op jit(solution)/shard_map/project/pallas_call | solution.py:619
  (148 shorter events, 62.6 us)
Async XLA Ops:
  6.5 110.3 %all-gather.2.cloned.1.call-start = ((), (), s32[]{:S(2)}) async-start(), calls=%async_computation.2 | async-start | bytes 2621440 | tf_op jit(solution)/shard_map/all_gather | solution.py:697
  8.0 31.1 %collective-permute-start.11 = (bf16[256,2048]{1,0:T(8,128)(2,1)S(1)}, bf16[256,2048]{1,0:T(8,128)(2,1)}, u32[]{:S(2)}, u32[]{:S(2)}) collective-permute-start(bf16[256,2048]{1,0:T(8,128)(2,1)S(1)} %bitcast.73), channel_id=1, source_target_pairs={{0,8},{4,12},{8,0},{12,4},{1,9},{5,13},{9,1},{13,5},{2,10},{6,14},... | collective-permute-start | bytes 3145736 | tf_op jit(solution)/shard_map/ppermute | solution.py:34
  12.1 26.9 %collective-permute-start = (bf16[128,2048]{1,0:T(8,128)(2,1)}, bf16[128,2048]{1,0:T(8,128)(2,1)S(1)}, u32[]{:S(2)}, u32[]{:S(2)}) collective-permute-start(bf16[128,2048]{1,0:T(8,128)(2,1)} %bitcast.6), channel_id=1, source_target_pairs={{0,1},{1,2},{2,3},{4,5},{5,6},{6,7},{8,9},{9,10},{10,11},{12,13},{... | collective-permute-start | bytes 1572872 | tf_op jit(solution)/shard_map/ppermute | solution.py:49
  15.6 23.4 %collective-permute-start.3 = (bf16[128,2048]{1,0:T(8,128)(2,1)}, bf16[128,2048]{1,0:T(8,128)(2,1)S(1)}, u32[]{:S(2)}, u32[]{:S(2)}) collective-permute-start(bf16[128,2048]{1,0:T(8,128)(2,1)} %bitcast.6), channel_id=1, source_target_pairs={{3,2},{2,1},{1,0},{7,6},{6,5},{5,4},{11,10},{10,9},{9,8},{15,14},{... | collective-permute-start | bytes 1572872 | tf_op jit(solution)/shard_map/ppermute | solution.py:50
  17.3 13.6 %collective-permute-start.6 = (f32[256]{0:T(256)S(1)}, f32[256]{0:T(256)S(1)}, u32[]{:S(2)}, u32[]{:S(2)}) collective-permute-start(f32[256]{0:T(256)S(1)} %reduce_sum.59), channel_id=1, source_target_pairs={{0,1},{1,0},{2,3},{3,2},{4,5},{5,4},{6,7},{7,6},{8,9},{9,8},{10,11... | collective-permute-start | bytes 3080 | tf_op jit(solution)/shard_map/ppermute | solution.py:34
  51.8 18.8 %collective-permute-start.4 = (bf16[128,2048]{1,0:T(8,128)(2,1)S(1)}, bf16[128,2048]{1,0:T(8,128)(2,1)}, u32[]{:S(2)}, u32[]{:S(2)}) collective-permute-start(bf16[128,2048]{1,0:T(8,128)(2,1)S(1)} %collective-permute-done.3.refs_2_), channel_id=1, source_target_pairs={{2,1},{1,0},{6,5},{5,4},{10,9},{9,8},{14,13},{13,12},{18,17},{17,1... | collective-permute-start | bytes 1572872 | tf_op jit(solution)/shard_map/ppermute | solution.py:50
  70.6 9.5 %collective-permute-start.15 = (f32[128,128]{1,0:T(8,128)S(1)}, f32[128,128]{1,0:T(8,128)S(1)}, u32[]{:S(2)}, u32[]{:S(2)}) collective-permute-start(f32[128,128]{1,0:T(8,128)S(1)} %fusion.12), channel_id=1, source_target_pairs={{0,1},{1,0},{2,3},{3,2},{4,5},{5,4},{6,7},{7,6},{8,9},{9,8},{10,11... | collective-permute-start | bytes 196616 | tf_op jit(solution)/shard_map/ppermute | solution.py:34
  80.2 10.2 %collective-permute-start.16 = (f32[128,128]{1,0:T(8,128)S(1)}, f32[128,128]{1,0:T(8,128)S(1)}, u32[]{:S(2)}, u32[]{:S(2)}) collective-permute-start(f32[128,128]{1,0:T(8,128)S(1)} %add.146), channel_id=1, source_target_pairs={{0,2},{1,3},{2,0},{3,1},{4,6},{5,7},{6,4},{7,5},{8,10},{9,11},{10,... | collective-permute-start | bytes 196616 | tf_op jit(solution)/shard_map/ppermute | solution.py:34
  107.0 27.0 %collective-permute-start.2 = (bf16[128,2048]{1,0:T(8,128)(2,1)}, bf16[128,2048]{1,0:T(8,128)(2,1)S(1)}, u32[]{:S(2)}, u32[]{:S(2)}) collective-permute-start(bf16[128,2048]{1,0:T(8,128)(2,1)} %collective-permute-done.1.refs_3_), channel_id=1, source_target_pairs={{2,3},{6,7},{10,11},{14,15},{18,19},{22,23},{26,27},{30,31}} | collective-permute-start | bytes 1572872 | tf_op jit(solution)/shard_map/ppermute | solution.py:49
  107.8 26.2 %collective-permute-start.5 = (bf16[128,2048]{1,0:T(8,128)(2,1)}, bf16[128,2048]{1,0:T(8,128)(2,1)S(1)}, u32[]{:S(2)}, u32[]{:S(2)}) collective-permute-start(bf16[128,2048]{1,0:T(8,128)(2,1)} %collective-permute-done.4.refs_4_), channel_id=1, source_target_pairs={{1,0},{5,4},{9,8},{13,12},{17,16},{21,20},{25,24},{29,28}} | collective-permute-start | bytes 1572872 | tf_op jit(solution)/shard_map/ppermute | solution.py:50
  111.8 20.0 %collective-permute-start.20 = (f16[128,1280]{1,0:T(8,128)(2,1)}, f16[128,1280]{1,0:T(8,128)(2,1)}, u32[]{:S(2)}, u32[]{:S(2)}) collective-permute-start(f16[128,1280]{1,0:T(8,128)(2,1)} %get-tuple-element.38), channel_id=1, source_target_pairs={{0,8},{4,12},{8,0},{12,4},{1,9},{5,13},{9,1},{13,5},{2,10},{6,14},... | collective-permute-start | bytes 983048 | tf_op jit(solution)/shard_map/ppermute | solution.py:34
  111.8 31.1 %collective-permute-start.21 = (f16[128,1280]{1,0:T(8,128)(2,1)}, f16[128,1280]{1,0:T(8,128)(2,1)}, u32[]{:S(2)}, u32[]{:S(2)}) collective-permute-start(f16[128,1280]{1,0:T(8,128)(2,1)} %get-tuple-element.37), channel_id=1, source_target_pairs={{0,8},{4,12},{8,0},{12,4},{1,9},{5,13},{9,1},{13,5},{2,10},{6,14},... | collective-permute-start | bytes 983048 | tf_op jit(solution)/shard_map/ppermute | solution.py:34
  134.0 15.6 %all-to-all-start = ((bf16[4,32,1280]{2,1,0:T(8,128)(2,1)}), bf16[4,32,1280]{2,1,0:T(8,128)(2,1)S(1)}, u32[]{:S(2)}, u32[]{:S(2)}) async-start(bf16[4,32,1280]{2,1,0:T(8,128)(2,1)} %bitcast.35), calls=%async_computation | async-start | bytes 655360 | tf_op jit(solution)/shard_map/all_to_all | solution.py:764
  149.6 16.0 %all-to-all-start.1 = ((bf16[4,32,1280]{2,1,0:T(8,128)(2,1)}), bf16[4,32,1280]{2,1,0:T(8,128)(2,1)S(1)}, u32[]{:S(2)}, u32[]{:S(2)}) async-start(bf16[4,32,1280]{2,1,0:T(8,128)(2,1)} %bitcast.34), calls=%async_computation.1 | async-start | bytes 655360 | tf_op jit(solution)/shard_map/all_to_all | solution.py:764
  160.4 17.8 %collective-permute-start.22 = (bf16[32,4096]{1,0:T(8,128)(2,1)S(1)}, bf16[32,4096]{1,0:T(8,128)(2,1)S(1)}, u32[]{:S(2)}, u32[]{:S(2)}) collective-permute-start(bf16[32,4096]{1,0:T(8,128)(2,1)S(1)} %attend.2.refs_0_), channel_id=1, source_target_pairs={{0,1},{1,2},{2,3},{4,5},{5,6},{6,7},{8,9},{9,10},{10,11},{12,13},{... | collective-permute-start | bytes 786440 | tf_op jit(solution)/shard_map/ppermute | solution.py:49
  164.3 14.6 %collective-permute-start.24 = (bf16[32,4096]{1,0:T(8,128)(2,1)S(1)}, bf16[32,4096]{1,0:T(8,128)(2,1)S(1)}, u32[]{:S(2)}, u32[]{:S(2)}) collective-permute-start(bf16[32,4096]{1,0:T(8,128)(2,1)S(1)} %attend.2.refs_0_), channel_id=1, source_target_pairs={{3,2},{2,1},{1,0},{7,6},{6,5},{5,4},{11,10},{10,9},{9,8},{15,14},{... | collective-permute-start | bytes 786440 | tf_op jit(solution)/shard_map/ppermute | solution.py:50
  178.2 9.0 %collective-permute-start.23 = (bf16[32,4096]{1,0:T(8,128)(2,1)S(1)}, bf16[32,4096]{1,0:T(8,128)(2,1)S(1)}, u32[]{:S(2)}, u32[]{:S(2)}) collective-permute-start(bf16[32,4096]{1,0:T(8,128)(2,1)S(1)} %collective-permute-done.22.refs_1_), channel_id=1, source_target_pairs={{1,2},{2,3},{5,6},{6,7},{9,10},{10,11},{13,14},{14,15},{17,18},{18... | collective-permute-start | bytes 786440 | tf_op jit(solution)/shard_map/ppermute | solution.py:49
  178.8 12.8 %collective-permute-start.25 = (bf16[32,4096]{1,0:T(8,128)(2,1)S(1)}, bf16[32,4096]{1,0:T(8,128)(2,1)S(1)}, u32[]{:S(2)}, u32[]{:S(2)}) collective-permute-start(bf16[32,4096]{1,0:T(8,128)(2,1)S(1)} %collective-permute-done.24.refs_2_), channel_id=1, source_target_pairs={{2,1},{1,0},{6,5},{5,4},{10,9},{9,8},{14,13},{13,12},{18,17},{17,1... | collective-permute-start | bytes 786440 | tf_op jit(solution)/shard_map/ppermute | solution.py:50
  180.8 12.1 %collective-permute-start.29 = (bf16[32,4096]{1,0:T(8,128)(2,1)S(1)}, bf16[32,4096]{1,0:T(8,128)(2,1)S(1)}, u32[]{:S(2)}, u32[]{:S(2)}) collective-permute-start(bf16[32,4096]{1,0:T(8,128)(2,1)S(1)} %collective-permute-done.28.refs_4_), channel_id=1, source_target_pairs={{1,2},{2,3},{5,6},{6,7},{9,10},{10,11},{13,14},{14,15},{17,18},{18... | collective-permute-start | bytes 786440 | tf_op jit(solution)/shard_map/ppermute | solution.py:49
  185.7 14.1 %collective-permute-start.31 = (bf16[32,4096]{1,0:T(8,128)(2,1)S(1)}, bf16[32,4096]{1,0:T(8,128)(2,1)S(1)}, u32[]{:S(2)}, u32[]{:S(2)}) collective-permute-start(bf16[32,4096]{1,0:T(8,128)(2,1)S(1)} %collective-permute-done.30.refs_5_), channel_id=1, source_target_pairs={{2,1},{1,0},{6,5},{5,4},{10,9},{9,8},{14,13},{13,12},{18,17},{17,1... | collective-permute-start | bytes 786440 | tf_op jit(solution)/shard_map/ppermute | solution.py:50
  187.2 22.1 %collective-permute-start.26 = (bf16[32,4096]{1,0:T(8,128)(2,1)S(1)}, bf16[32,4096]{1,0:T(8,128)(2,1)S(1)}, u32[]{:S(2)}, u32[]{:S(2)}) collective-permute-start(bf16[32,4096]{1,0:T(8,128)(2,1)S(1)} %collective-permute-done.23.refs_0_), channel_id=1, source_target_pairs={{2,3},{6,7},{10,11},{14,15},{18,19},{22,23},{26,27},{30,31}} | collective-permute-start | bytes 786440 | tf_op jit(solution)/shard_map/ppermute | solution.py:49
  191.6 17.6 %collective-permute-start.27 = (bf16[32,4096]{1,0:T(8,128)(2,1)S(1)}, bf16[32,4096]{1,0:T(8,128)(2,1)S(1)}, u32[]{:S(2)}, u32[]{:S(2)}) collective-permute-start(bf16[32,4096]{1,0:T(8,128)(2,1)S(1)} %collective-permute-done.25.refs_1_), channel_id=1, source_target_pairs={{1,0},{5,4},{9,8},{13,12},{17,16},{21,20},{25,24},{29,28}} | collective-permute-start | bytes 786440 | tf_op jit(solution)/shard_map/ppermute | solution.py:50
  192.9 16.4 %collective-permute-start.32 = (bf16[32,4096]{1,0:T(8,128)(2,1)S(1)}, bf16[32,4096]{1,0:T(8,128)(2,1)S(1)}, u32[]{:S(2)}, u32[]{:S(2)}) collective-permute-start(bf16[32,4096]{1,0:T(8,128)(2,1)S(1)} %collective-permute-done.29.refs_4_), channel_id=1, source_target_pairs={{2,3},{6,7},{10,11},{14,15},{18,19},{22,23},{26,27},{30,31}} | collective-permute-start | bytes 786440 | tf_op jit(solution)/shard_map/ppermute | solution.py:49
  199.8 9.5 %collective-permute-start.33 = (bf16[32,4096]{1,0:T(8,128)(2,1)S(1)}, bf16[32,4096]{1,0:T(8,128)(2,1)S(1)}, u32[]{:S(2)}, u32[]{:S(2)}) collective-permute-start(bf16[32,4096]{1,0:T(8,128)(2,1)S(1)} %collective-permute-done.31.refs_5_), channel_id=1, source_target_pairs={{1,0},{5,4},{9,8},{13,12},{17,16},{21,20},{25,24},{29,28}} | collective-permute-start | bytes 786440 | tf_op jit(solution)/shard_map/ppermute | solution.py:50
  (27 other events, 213.1 us)
Sparse Core Ops, SparseCore 0:
  54.4 54.1 all-gather.1

commit v5 on v4

--- a/solution.py
+++ b/solution.py
@@ -692,11 +692,7 @@
     owners = [own_index] + [hop_owners(tensor_pos, hop) for hop in (1, 2, 3)]
     count = tensor_count * local
     parts = [slice(h * count, (h + 1) * count) for h in range(halves)]
-    everything = [None] * halves
-    hops = None
-    everything[0] = lax.all_gather(raw[parts[0]], "tensor", axis=0, tiled=False)
-    if halves > 1:
-        hops = line_gather(raw[parts[1]], "tensor")
+    everything = [lax.all_gather(raw[part], "tensor", axis=0, tiled=False) for part in parts]
 
     values = raw.astype(F32)
     squares = jnp.sum(values * values, axis=1)
@@ -706,8 +702,6 @@
         own_runs = own_runs.reshape(tensor_count, halves, -1).swapaxes(0, 1).reshape(-1)
     told = jnp.concatenate([squares, own_runs.astype(F32)]).reshape(1, -1)
     told = jnp.concatenate([told, swap(told, "store", 2)], axis=0)
-    if halves > 1:
-        told, hops[0] = lax.optimization_barrier((told, hops[0]))
     told = jnp.concatenate([told, swap(told, "store", 1)], axis=0)
     told = jnp.stack([told[d] for d in (0, 2, 1, 3)])
     told = jnp.stack([jnp.stack([told[p ^ q] for q in range(4)]) for p in range(4)])
@@ -731,12 +725,10 @@
     kept, passed = shrink_rows(place, mine, (raw, beside, across, diagonal), scales, gain, down)
     kept = kept + swap(passed, "store", 1)
     shrunk = kept[0] + swap(kept[1], "store", 2)
-    if halves > 1:
-        shrunk, hops[1] = lax.optimization_barrier((shrunk, hops[1]))
     shrunk = summed_over(shrunk, "tensor").astype(BF16)
     shrunk = jnp.stack([shrunk, swap(shrunk, "store", 2)])
     kept, passed = grow_rows(place, mine, shrunk, swap(shrunk, "store", 1), adapter_up_weight)
-    passed = swap(passed.astype(F16), "store", 1).astype(F32)
+    passed = swap(passed, "store", 1)
     deltas = []
     for part in parts:
         delta = swap((kept[1, part] + passed[1, part]).astype(F16), "store", 2).astype(F32)
@@ -744,16 +736,13 @@
 
     weight = query_key_value_weight
     raw, passed = lax.optimization_barrier((raw, passed))
-    own = base_block((raw[parts[0]],), own_scale[parts[0]], gains, weight, own_index, None)
-    total = base_rows(own_index, everything[0], own_scale[parts[0]], gains, own, weight, 0)
-    mixed = [(total + deltas[0]).astype(BF16)]
-    if halves > 1:
-        blocks = (raw[parts[1]],) + hops[0] + hops[1]
-        near = jnp.concatenate(owners[:3])
-        total = base_block(blocks, own_scale[parts[1]], gains, weight, near, None)
-        hops[2], mixed[0] = lax.optimization_barrier((hops[2], mixed[0]))
-        total = base_block(hops[2], own_scale[parts[1]], gains, weight, owners[3], total)
-        mixed.append((total + deltas[1]).astype(BF16))
+    mixed = []
+    for h, part in enumerate(parts):
+        if mixed:
+            everything[h], mixed[-1] = lax.optimization_barrier((everything[h], mixed[-1]))
+        own = base_block((raw[part],), own_scale[part], gains, weight, own_index, None)
+        total = base_rows(own_index, everything[h], own_scale[part], gains, own, weight, 0)
+        mixed.append((total + deltas[h]).astype(BF16))
     mixed = [qkv.reshape(tensor_count, local, -1) for qkv in mixed]
 
     contexts = []

time: 226 us -> 225 us (level)
  waiting for transfers between devices: 74.2 us -> 85.9 us
  starting transfers between devices: 51 us -> 42 us
  other arithmetic: 13.5 us -> 9.53 us
    all_gather x1 -> x2, waiting for transfers between devices: 0.02 us -> 20.8 us  [on_device(): lax.all_gather(raw[part], 'tensor', axis=0, tiled=False)]
    ppermute x9 -> x6, waiting for transfers between devices: 26.2 us -> 12.8 us  [line_gather(): down = lax.ppermute(down, axis, [(i, i - 1) for i in range(4 - hop, 0, -1)])]
    pallas_call x3 -> x2, Pallas kernels: 13.7 us -> 5.85 us  [base_block(): pl.pallas_call(functools.partial(block_kernel, count, total is not None),...]
    ppermute x16, waiting for transfers between devices: 42.9 us -> 50.2 us  [swap(): return lax.ppermute(values, axis, [(i, i ^ distance) for i in range(count)])]
    pallas_call x1 -> x2, Pallas kernels: 6 us -> 12.1 us  [base_rows(): pl.pallas_call(functools.partial(base_kernel, first_row), out_shape=jax.S...]
    ppermute x9 -> x6, starting transfers between devices: 16.9 us -> 11.2 us  [line_gather(): up = lax.ppermute(up, axis, [(i, i + 1) for i in range(hop - 1, 3)])]
    convert_element_type x4 -> x2, other arithmetic: 9.06 us -> 4.31 us  [on_device(): mixed.append((total + deltas[h]).astype(BF16))]
    ppermute x9 -> x6, starting transfers between devices: 11.6 us -> 7.72 us  [line_gather(): down = lax.ppermute(down, axis, [(i, i - 1) for i in range(4 - hop, 0, -1)])]
  transfers between devices with their start and end apart: 37 -> 32, of which waited for: 15 -> 17; matrix products, arithmetic and copies ran while one was open for 8% -> 6% of each run, Pallas kernels for 21% -> 24%
where the time goes in v5:
time: 225 us; the launch traced here: 224 us
  waiting for transfers between devices  85.9 us (38%)
  Pallas kernels  61.5 us (27%)
  starting transfers between devices  42 us (19%)
  between operations  13.9 us (6%)
  local copies, waits for them, and re-layouts  11 us (5%)
  other arithmetic  9.53 us (4%)
    ppermute x16, waiting for transfers between devices, swap(): return lax.ppermute(values, axis, [(i, i ^ distance) for i in range(count)])  50.2 us
    all_gather x2, waiting for transfers between devices, on_device(): lax.all_gather(raw[part], 'tensor', axis=0, tiled=False)  20.8 us
    pallas_call x2, Pallas kernels, project(): pl.pallas_call(functools.partial(out_kernel, count, earlier is not None),...  16.9 us
    ppermute x16, starting transfers between devices, swap(): return lax.ppermute(values, axis, [(i, i ^ distance) for i in range(count)])  15.1 us
    pallas_call x2, Pallas kernels, attend(): pl.pallas_call(functools.partial(attend_kernel, unit, first_row), out_sha...  13.4 us
    ppermute x6, waiting for transfers between devices, line_gather(): down = lax.ppermute(down, axis, [(i, i - 1) for i in range(4 - hop, 0, -1)])  12.8 us
    pallas_call x2, Pallas kernels, base_rows(): pl.pallas_call(functools.partial(base_kernel, first_row), out_shape=jax.S...  12.1 us
    ppermute x6, starting transfers between devices, line_gather(): up = lax.ppermute(up, axis, [(i, i + 1) for i in range(hop - 1, 3)])  11.2 us
  transfers between devices with their start and end apart: 32, of which 17 were waited for; matrix products, arithmetic and copies ran while one was open for 6% of the time, Pallas kernels for 24%

profile of v5, /device:TPU:0, one launch (start us, length us, event | category | flops | bytes accessed | tf_op | source)
XLA Modules:
  0.0 223.9 jit_solution(9649599554457810109)
XLA Ops:
  8.1 3.0 %collective-permute-start.5 = (bf16[256,2048]{1,0:T(8,128)(2,1)S(1)}, bf16[256,2048]{1,0:T(8,128)(2,1)}, u32[]{:S(2)}, u32[]{:S(2)}) collective-permute-start(bf16[256,2048]{1,0:T(8,128)(2,1)S(1)} %bitcast.73), channel_id=1, source_target_pairs={{0,8},{4,12},{8,0},{12,4},{1,9},{5,13},{9,1},{13,5},{2,10},{6,14},... | collective-permute-start | bytes 3145736 | tf_op jit(solution)/shard_map/ppermute | solution.py:34
  19.9 14.5 %collective-permute-done.2 = f32[1,272]{1,0:T(1,128)S(1)} collective-permute-done((f32[1,272]{1,0:T(1,128)S(1)}, f32[1,272]{1,0:T(1,128)S(1)}, u32[]{:S(2)}, u32[]{:S(2)}) %collective-permute-start.2) | collective-permute-done | bytes 1120 | tf_op jit(solution)/shard_map/ppermute | solution.py:34
  40.3 7.0 %shrink_rows.1 = (f32[2,128,128]{2,1,0:T(8,128)}, f32[2,128,128]{2,1,0:T(8,128)}) custom-call(s32[1]{0:T(128)} %bitcast.18.place_ref, s32[64]{0:T(128)} %compare_select_fusion.slots, bf16[256,2048]{1,0:T(8,128)(2,1)} %bitcast.75, bf16[256,2048]{1,0:T(8,128)(2,1)} %copy-done.6, bf16[256,2048]{1,0:T(8,128)(2,1)} %collective-permute-done.5.x2, ...), custom_call_target="tpu_custom_call" | custom-call | flops 67108864 | bytes 8388608 | tf_op jit(solution)/shard_map/shrink_rows/pallas_call | solution.py:280
  50.5 4.2 %collective-permute-done.8 = f32[128,128]{1,0:T(8,128)S(1)} collective-permute-done((f32[128,128]{1,0:T(8,128)S(1)}, f32[128,128]{1,0:T(8,128)S(1)}, u32[]{:S(2)}, u32[]{:S(2)}) %collective-permute-start.8) | collective-permute-done | bytes 65568 | tf_op jit(solution)/shard_map/ppermute | solution.py:34
  56.7 8.6 %collective-permute-done.9 = f32[128,128]{1,0:T(8,128)S(1)} collective-permute-done((f32[128,128]{1,0:T(8,128)S(1)}, f32[128,128]{1,0:T(8,128)S(1)}, u32[]{:S(2)}, u32[]{:S(2)}) %collective-permute-start.9) | collective-permute-done | bytes 65568 | tf_op jit(solution)/shard_map/ppermute | solution.py:34
  65.5 9.7 %collective-permute-done.10 = f32[128,128]{1,0:T(8,128)S(1)} collective-permute-done((f32[128,128]{1,0:T(8,128)S(1)}, f32[128,128]{1,0:T(8,128)S(1)}, u32[]{:S(2)}, u32[]{:S(2)}) %collective-permute-start.10) | collective-permute-done | bytes 65568 | tf_op jit(solution)/shard_map/ppermute | solution.py:34
  81.1 6.4 %grow_rows.1 = (f32[2,256,1280]{2,1,0:T(8,128)}, f32[2,256,1280]{2,1,0:T(8,128)}) custom-call(s32[1]{0:T(128)} %bitcast.18.place_ref, s32[64]{0:T(128)} %compare_select_fusion.slots, bf16[2,128,128]{2,1,0:T(8,128)(2,1)} %copy-done.9, bf16[2,128,128]{2,1,0:T(8,128)(2,1)} %copy-done.10, bf16[32,64,1280]{2,1,0:T(8,128)(2,1)} %up_ref.1), custom_call_target="tpu_custom_call" | custom-call | flops 41943040 | bytes 5242880 | tf_op jit(solution)/shard_map/grow_rows/pallas_call | solution.py:353
  89.1 3.8 %collective-permute-done.13 = f32[2,256,1280]{2,1,0:T(8,128)} collective-permute-done((f32[2,256,1280]{2,1,0:T(8,128)}, f32[2,256,1280]{2,1,0:T(8,128)}, u32[]{:S(2)}, u32[]{:S(2)}) %collective-permute-start.13) | collective-permute-done | bytes 2621472 | tf_op jit(solution)/shard_map/ppermute | solution.py:34
  97.1 2.9 %base_block.3.own_ref = f32[128,1280]{1,0:T(8,128)S(1)} custom-call(s32[1]{0:T(128)} %bitcast.4.owners.place_ref, bf16[128,2048]{1,0:T(8,128)(2,1)S(1)} %get-tuple-element.25.refs_0_, f32[128,1]{1,0:T(8,128)S(1)} %copy.37.refs_1_.scale_ref, f32[1,8192]{1,0:T(1,128)S(1)} %bitcast.69, bf16[8192,1280]{1,0:T(8,128)(2,1)} %w_ref.3), custom_call_target="tpu_custom_call" | custom-call | flops 671088640 | bytes 7077888 | tf_op jit(solution)/shard_map/base_block/pallas_call | solution.py:103
  100.0 2.9 %base_block.2.own_ref = f32[128,1280]{1,0:T(8,128)S(1)} custom-call(s32[1]{0:T(128)} %bitcast.4.owners.place_ref, bf16[128,2048]{1,0:T(8,128)(2,1)S(1)} %get-tuple-element.26.refs_0_, f32[128,1]{1,0:T(8,128)S(1)} %copy.35.refs_1_.scale_ref, f32[1,8192]{1,0:T(1,128)S(1)} %bitcast.70, bf16[8192,1280]{1,0:T(8,128)(2,1)} %w_ref.3), custom_call_target="tpu_custom_call" | custom-call | flops 671088640 | bytes 7077888 | tf_op jit(solution)/shard_map/base_block/pallas_call | solution.py:103
  104.6 6.1 %base_rows.2 = f32[128,1280]{1,0:T(8,128)S(1)} custom-call(s32[1]{0:T(128)} %bitcast.4.owners.place_ref, bf16[4,128,2048]{2,1,0:T(8,128)(2,1)S(1)} %copy-done, f32[128,1]{1,0:T(8,128)S(1)} %copy.35.refs_1_.scale_ref, f32[1,8192]{1,0:T(1,128)S(1)} %bitcast.71, f32[128,1280]{1,0:T(8,128)S(1)} %base_block.2.own_ref, bf16[8192,1280]{1,0:T(8,128)(2,1)} %w_ref.3), custom_call_target="tpu_custom_call" | custom-call | flops 2013265920 | bytes 18612224 | tf_op jit(solution)/shard_map/base_rows/pallas_call | solution.py:156
  112.8 20.8 %all-gather.3.cloned.1.call-done.x_ref = bf16[4,128,2048]{2,1,0:T(8,128)(2,1)} async-done(((bf16[1,128,2048]{2,1,0:T(8,128)(2,1)}), bf16[4,128,2048]{2,1,0:T(8,128)(2,1)}) %all-gather.3.cloned.1.call-update) | async-done | bytes 2097168 | tf_op jit(solution)/shard_map/all_gather | solution.py:695
  133.6 3.6 %all-to-all-start = ((bf16[4,32,1280]{2,1,0:T(8,128)(2,1)}), bf16[4,32,1280]{2,1,0:T(8,128)(2,1)S(1)}, u32[]{:S(2)}, u32[]{:S(2)}) async-start(bf16[4,32,1280]{2,1,0:T(8,128)(2,1)} %bitcast.33), calls=%async_computation | async-start | bytes 655360 | tf_op jit(solution)/shard_map/all_to_all | solution.py:753
  138.9 6.0 %base_rows.3 = f32[128,1280]{1,0:T(8,128)S(1)} custom-call(s32[1]{0:T(128)} %bitcast.4.owners.place_ref, bf16[4,128,2048]{2,1,0:T(8,128)(2,1)S(1)} %copy-done.1, f32[128,1]{1,0:T(8,128)S(1)} %copy.37.refs_1_.scale_ref, f32[1,8192]{1,0:T(1,128)S(1)} %bitcast.72, f32[128,1280]{1,0:T(8,128)S(1)} %base_block.3.own_ref, bf16[8192,1280]{1,0:T(8,128)(2,1)} %w_ref.3), custom_call_target="tpu_custom_call" | custom-call | flops 2013265920 | bytes 18612224 | tf_op jit(solution)/shard_map/base_rows/pallas_call | solution.py:156
  147.6 4.2 %all-to-all-start.1 = ((bf16[4,32,1280]{2,1,0:T(8,128)(2,1)}), bf16[4,32,1280]{2,1,0:T(8,128)(2,1)S(1)}, u32[]{:S(2)}, u32[]{:S(2)}) async-start(bf16[4,32,1280]{2,1,0:T(8,128)(2,1)} %bitcast.32), calls=%async_computation.1 | async-start | bytes 655360 | tf_op jit(solution)/shard_map/all_to_all | solution.py:753
  152.5 6.7 %attend.2.refs_0_ = bf16[32,4096]{1,0:T(8,128)(2,1)S(1)} custom-call(s32[16]{0:T(128)S(1)} %get-tuple-element.53.lengths, s32[16]{0:T(128)S(1)} %select_reduce_fusion.2.order, bf16[4,32,1280]{2,1,0:T(8,128)(2,1)S(1)} %all-to-all-done.qkv_ref, f32[32,128]{1,0:T(8,128)S(1)} %get-tuple-element.54.cos_ref, f32[32,128]{1,0:T(8,128)S(1)} %get-tuple-element.55.sin_ref, ...), custom_call_target="tpu_custom_call" | custom-call | flops 268435456 | bytes 16777216 | tf_op jit(solution)/shard_map/attend/pallas_call | solution.py:534
  159.2 3.9 %collective-permute-start.16 = (bf16[32,4096]{1,0:T(8,128)(2,1)S(1)}, bf16[32,4096]{1,0:T(8,128)(2,1)S(1)}, u32[]{:S(2)}, u32[]{:S(2)}) collective-permute-start(bf16[32,4096]{1,0:T(8,128)(2,1)S(1)} %attend.2.refs_0_), channel_id=1, source_target_pairs={{0,1},{1,2},{2,3},{4,5},{5,6},{6,7},{8,9},{9,10},{10,11},{12,13},{... | collective-permute-start | bytes 786440 | tf_op jit(solution)/shard_map/ppermute | solution.py:49
  164.5 6.7 %attend.3.refs_3_ = bf16[32,4096]{1,0:T(8,128)(2,1)S(1)} custom-call(s32[16]{0:T(128)S(1)} %get-tuple-element.52.lengths, s32[16]{0:T(128)S(1)} %select_reduce_fusion.1.order, bf16[4,32,1280]{2,1,0:T(8,128)(2,1)S(1)} %all-to-all-done.1.qkv_ref, f32[32,128]{1,0:T(8,128)S(1)} %get-tuple-element.56.cos_ref, f32[32,128]{1,0:T(8,128)S(1)} %get-tuple-element.57.sin_ref, ...), custom_call_target="tpu_custom_call" | custom-call | flops 268435456 | bytes 16777216 | tf_op jit(solution)/shard_map/attend/pallas_call | solution.py:534
  171.1 4.6 %collective-permute-start.22 = (bf16[32,4096]{1,0:T(8,128)(2,1)S(1)}, bf16[32,4096]{1,0:T(8,128)(2,1)S(1)}, u32[]{:S(2)}, u32[]{:S(2)}) collective-permute-start(bf16[32,4096]{1,0:T(8,128)(2,1)S(1)} %attend.3.refs_3_), channel_id=1, source_target_pairs={{0,1},{1,2},{2,3},{4,5},{5,6},{6,7},{8,9},{9,10},{10,11},{12,13},{... | collective-permute-start | bytes 786440 | tf_op jit(solution)/shard_map/ppermute | solution.py:49
  181.1 4.6 %collective-permute-done.24.refs_5_ = bf16[32,4096]{1,0:T(8,128)(2,1)S(1)} collective-permute-done((bf16[32,4096]{1,0:T(8,128)(2,1)S(1)}, bf16[32,4096]{1,0:T(8,128)(2,1)S(1)}, u32[]{:S(2)}, u32[]{:S(2)}) %collective-permute-start.24) | collective-permute-done | bytes 262176 | tf_op jit(solution)/shard_map/ppermute | solution.py:50
  187.8 3.7 %collective-permute-done.19.refs_1_ = bf16[32,4096]{1,0:T(8,128)(2,1)S(1)} collective-permute-done((bf16[32,4096]{1,0:T(8,128)(2,1)S(1)}, bf16[32,4096]{1,0:T(8,128)(2,1)S(1)}, u32[]{:S(2)}, u32[]{:S(2)}) %collective-permute-start.19) | collective-permute-done | bytes 262176 | tf_op jit(solution)/shard_map/ppermute | solution.py:50
  193.5 4.5 %collective-permute-done.25.refs_5_ = bf16[32,4096]{1,0:T(8,128)(2,1)S(1)} collective-permute-done((bf16[32,4096]{1,0:T(8,128)(2,1)S(1)}, bf16[32,4096]{1,0:T(8,128)(2,1)S(1)}, u32[]{:S(2)}, u32[]{:S(2)}) %collective-permute-start.25) | collective-permute-done | bytes 262176 | tf_op jit(solution)/shard_map/ppermute | solution.py:50
  199.3 8.1 %project.2.refs_9_ = bf16[2,4,2,16,2048]{4,3,2,1,0:T(8,128)(2,1)} custom-call(s32[3]{0:T(128)S(1)} %pad_add_fusion.1.owners, bf16[32,4096]{1,0:T(8,128)(2,1)S(1)} %attend.2.refs_0_, bf16[32,4096]{1,0:T(8,128)(2,1)S(1)} %collective-permute-done.16.refs_1_, bf16[32,4096]{1,0:T(8,128)(2,1)S(1)} %collective-permute-done.18.refs_2_, ...), custom_call_target="tpu_custom_call" | custom-call | flops 3221225472 | bytes 19136512 | tf_op jit(solution)/shard_map/project/pallas_call | solution.py:619
  208.3 8.8 %project.3 = bf16[2,4,2,16,2048]{4,3,2,1,0:T(8,128)(2,1)} custom-call(s32[4]{0:T(128)S(1)} %pad_add_fusion.owners, bf16[32,4096]{1,0:T(8,128)(2,1)S(1)} %collective-permute-done.17.refs_0_, bf16[32,4096]{1,0:T(8,128)(2,1)S(1)} %collective-permute-done.19.refs_1_, bf16[32,4096]{1,0:T(8,128)(2,1)S(1)} %collective-permute-done.20.refs_2_, ...), custom_call_target="tpu_custom_call" | custom-call | flops 2147483648 | bytes 18350080 | tf_op jit(solution)/shard_map/project/pallas_call | solution.py:619
  (134 shorter events, 54.7 us)
Async XLA Ops:
  6.5 96.4 %all-gather.5.cloned.1.call-start = ((), (), s32[]{:S(2)}) async-start(), calls=%async_computation.3 | async-start | bytes 2621440 | tf_op jit(solution)/shard_map/all_gather | solution.py:695
  8.1 28.2 %collective-permute-start.5 = (bf16[256,2048]{1,0:T(8,128)(2,1)S(1)}, bf16[256,2048]{1,0:T(8,128)(2,1)}, u32[]{:S(2)}, u32[]{:S(2)}) collective-permute-start(bf16[256,2048]{1,0:T(8,128)(2,1)S(1)} %bitcast.73), channel_id=1, source_target_pairs={{0,8},{4,12},{8,0},{12,4},{1,9},{5,13},{9,1},{13,5},{2,10},{6,14},... | collective-permute-start | bytes 3145736 | tf_op jit(solution)/shard_map/ppermute | solution.py:34
  19.7 14.8 %collective-permute-start.2 = (f32[1,272]{1,0:T(1,128)S(1)}, f32[1,272]{1,0:T(1,128)S(1)}, u32[]{:S(2)}, u32[]{:S(2)}) collective-permute-start(f32[1,272]{1,0:T(1,128)S(1)} %reshape.115), channel_id=1, source_target_pairs={{0,8},{4,12},{8,0},{12,4},{1,9},{5,13},{9,1},{13,5},{2,10},{6,14},... | collective-permute-start | bytes 3272 | tf_op jit(solution)/shard_map/ppermute | solution.py:34
  19.9 18.9 %collective-permute-start.4 = (bf16[256,2048]{1,0:T(8,128)(2,1)S(1)}, bf16[256,2048]{1,0:T(8,128)(2,1)S(1)}, u32[]{:S(2)}, u32[]{:S(2)}) collective-permute-start(bf16[256,2048]{1,0:T(8,128)(2,1)S(1)} %bitcast.74), channel_id=1, source_target_pairs={{0,4},{4,0},{8,12},{12,8},{1,5},{5,1},{9,13},{13,9},{2,6},{6,2},{1... | collective-permute-start | bytes 3145736 | tf_op jit(solution)/shard_map/ppermute | solution.py:34
  35.7 97.9 %all-gather.3.cloned.1.call-start = ((), (), s32[]{:S(2)}) async-start(), calls=%async_computation.2 | async-start | bytes 2621440 | tf_op jit(solution)/shard_map/all_gather | solution.py:695
  54.8 10.5 %collective-permute-start.9 = (f32[128,128]{1,0:T(8,128)S(1)}, f32[128,128]{1,0:T(8,128)S(1)}, u32[]{:S(2)}, u32[]{:S(2)}) collective-permute-start(f32[128,128]{1,0:T(8,128)S(1)} %fusion.12), channel_id=1, source_target_pairs={{0,1},{1,0},{2,3},{3,2},{4,5},{5,4},{6,7},{7,6},{8,9},{9,8},{10,11... | collective-permute-start | bytes 196616 | tf_op jit(solution)/shard_map/ppermute | solution.py:34
  65.2 9.9 %collective-permute-start.10 = (f32[128,128]{1,0:T(8,128)S(1)}, f32[128,128]{1,0:T(8,128)S(1)}, u32[]{:S(2)}, u32[]{:S(2)}) collective-permute-start(f32[128,128]{1,0:T(8,128)S(1)} %add.146), channel_id=1, source_target_pairs={{0,2},{1,3},{2,0},{3,1},{4,6},{5,7},{6,4},{7,5},{8,10},{9,11},{10,... | collective-permute-start | bytes 196616 | tf_op jit(solution)/shard_map/ppermute | solution.py:34
  87.5 5.4 %collective-permute-start.13 = (f32[2,256,1280]{2,1,0:T(8,128)}, f32[2,256,1280]{2,1,0:T(8,128)}, u32[]{:S(2)}, u32[]{:S(2)}) collective-permute-start(f32[2,256,1280]{2,1,0:T(8,128)} %get-tuple-element.16), channel_id=1, source_target_pairs={{0,4},{4,0},{8,12},{12,8},{1,5},{5,1},{9,13},{13,9},{2,6},{6,2},{1... | collective-permute-start | bytes 7864328 | tf_op jit(solution)/shard_map/ppermute | solution.py:34
  94.8 15.8 %collective-permute-start.14 = (f16[128,1280]{1,0:T(8,128)(2,1)S(1)}, f16[128,1280]{1,0:T(8,128)(2,1)S(1)}, u32[]{:S(2)}, u32[]{:S(2)}) collective-permute-start(f16[128,1280]{1,0:T(8,128)(2,1)S(1)} %get-tuple-element.24), channel_id=1, source_target_pairs={{0,8},{4,12},{8,0},{12,4},{1,9},{5,13},{9,1},{13,5},{2,10},{6,14},... | collective-permute-start | bytes 983048 | tf_op jit(solution)/shard_map/ppermute | solution.py:34
  95.3 49.5 %collective-permute-start.15 = (f16[128,1280]{1,0:T(8,128)(2,1)S(1)}, f16[128,1280]{1,0:T(8,128)(2,1)S(1)}, u32[]{:S(2)}, u32[]{:S(2)}) collective-permute-start(f16[128,1280]{1,0:T(8,128)(2,1)S(1)} %get-tuple-element.23), channel_id=1, source_target_pairs={{0,8},{4,12},{8,0},{12,4},{1,9},{5,13},{9,1},{13,5},{2,10},{6,14},... | collective-permute-start | bytes 983048 | tf_op jit(solution)/shard_map/ppermute | solution.py:34
  133.6 14.0 %all-to-all-start = ((bf16[4,32,1280]{2,1,0:T(8,128)(2,1)}), bf16[4,32,1280]{2,1,0:T(8,128)(2,1)S(1)}, u32[]{:S(2)}, u32[]{:S(2)}) async-start(bf16[4,32,1280]{2,1,0:T(8,128)(2,1)} %bitcast.33), calls=%async_computation | async-start | bytes 655360 | tf_op jit(solution)/shard_map/all_to_all | solution.py:753
  147.6 16.8 %all-to-all-start.1 = ((bf16[4,32,1280]{2,1,0:T(8,128)(2,1)}), bf16[4,32,1280]{2,1,0:T(8,128)(2,1)S(1)}, u32[]{:S(2)}, u32[]{:S(2)}) async-start(bf16[4,32,1280]{2,1,0:T(8,128)(2,1)} %bitcast.32), calls=%async_computation.1 | async-start | bytes 655360 | tf_op jit(solution)/shard_map/all_to_all | solution.py:753
  159.2 17.8 %collective-permute-start.16 = (bf16[32,4096]{1,0:T(8,128)(2,1)S(1)}, bf16[32,4096]{1,0:T(8,128)(2,1)S(1)}, u32[]{:S(2)}, u32[]{:S(2)}) collective-permute-start(bf16[32,4096]{1,0:T(8,128)(2,1)S(1)} %attend.2.refs_0_), channel_id=1, source_target_pairs={{0,1},{1,2},{2,3},{4,5},{5,6},{6,7},{8,9},{9,10},{10,11},{12,13},{... | collective-permute-start | bytes 786440 | tf_op jit(solution)/shard_map/ppermute | solution.py:49
  163.1 14.6 %collective-permute-start.18 = (bf16[32,4096]{1,0:T(8,128)(2,1)S(1)}, bf16[32,4096]{1,0:T(8,128)(2,1)S(1)}, u32[]{:S(2)}, u32[]{:S(2)}) collective-permute-start(bf16[32,4096]{1,0:T(8,128)(2,1)S(1)} %attend.2.refs_0_), channel_id=1, source_target_pairs={{3,2},{2,1},{1,0},{7,6},{6,5},{5,4},{11,10},{10,9},{9,8},{15,14},{... | collective-permute-start | bytes 786440 | tf_op jit(solution)/shard_map/ppermute | solution.py:50
  171.1 9.3 %collective-permute-start.22 = (bf16[32,4096]{1,0:T(8,128)(2,1)S(1)}, bf16[32,4096]{1,0:T(8,128)(2,1)S(1)}, u32[]{:S(2)}, u32[]{:S(2)}) collective-permute-start(bf16[32,4096]{1,0:T(8,128)(2,1)S(1)} %attend.3.refs_3_), channel_id=1, source_target_pairs={{0,1},{1,2},{2,3},{4,5},{5,6},{6,7},{8,9},{9,10},{10,11},{12,13},{... | collective-permute-start | bytes 786440 | tf_op jit(solution)/shard_map/ppermute | solution.py:49
  175.7 9.9 %collective-permute-start.24 = (bf16[32,4096]{1,0:T(8,128)(2,1)S(1)}, bf16[32,4096]{1,0:T(8,128)(2,1)S(1)}, u32[]{:S(2)}, u32[]{:S(2)}) collective-permute-start(bf16[32,4096]{1,0:T(8,128)(2,1)S(1)} %attend.3.refs_3_), channel_id=1, source_target_pairs={{3,2},{2,1},{1,0},{7,6},{6,5},{5,4},{11,10},{10,9},{9,8},{15,14},{... | collective-permute-start | bytes 786440 | tf_op jit(solution)/shard_map/ppermute | solution.py:50
  177.1 10.1 %collective-permute-start.17 = (bf16[32,4096]{1,0:T(8,128)(2,1)S(1)}, bf16[32,4096]{1,0:T(8,128)(2,1)S(1)}, u32[]{:S(2)}, u32[]{:S(2)}) collective-permute-start(bf16[32,4096]{1,0:T(8,128)(2,1)S(1)} %collective-permute-done.16.refs_1_), channel_id=1, source_target_pairs={{1,2},{2,3},{5,6},{6,7},{9,10},{10,11},{13,14},{14,15},{17,18},{18... | collective-permute-start | bytes 786440 | tf_op jit(solution)/shard_map/ppermute | solution.py:49
  177.7 13.8 %collective-permute-start.19 = (bf16[32,4096]{1,0:T(8,128)(2,1)S(1)}, bf16[32,4096]{1,0:T(8,128)(2,1)S(1)}, u32[]{:S(2)}, u32[]{:S(2)}) collective-permute-start(bf16[32,4096]{1,0:T(8,128)(2,1)S(1)} %collective-permute-done.18.refs_2_), channel_id=1, source_target_pairs={{2,1},{1,0},{6,5},{5,4},{10,9},{9,8},{14,13},{13,12},{18,17},{17,1... | collective-permute-start | bytes 786440 | tf_op jit(solution)/shard_map/ppermute | solution.py:50
  180.4 12.4 %collective-permute-start.23 = (bf16[32,4096]{1,0:T(8,128)(2,1)S(1)}, bf16[32,4096]{1,0:T(8,128)(2,1)S(1)}, u32[]{:S(2)}, u32[]{:S(2)}) collective-permute-start(bf16[32,4096]{1,0:T(8,128)(2,1)S(1)} %collective-permute-done.22.refs_4_), channel_id=1, source_target_pairs={{1,2},{2,3},{5,6},{6,7},{9,10},{10,11},{13,14},{14,15},{17,18},{18... | collective-permute-start | bytes 786440 | tf_op jit(solution)/shard_map/ppermute | solution.py:49
  185.7 12.4 %collective-permute-start.25 = (bf16[32,4096]{1,0:T(8,128)(2,1)S(1)}, bf16[32,4096]{1,0:T(8,128)(2,1)S(1)}, u32[]{:S(2)}, u32[]{:S(2)}) collective-permute-start(bf16[32,4096]{1,0:T(8,128)(2,1)S(1)} %collective-permute-done.24.refs_5_), channel_id=1, source_target_pairs={{2,1},{1,0},{6,5},{5,4},{10,9},{9,8},{14,13},{13,12},{18,17},{17,1... | collective-permute-start | bytes 786440 | tf_op jit(solution)/shard_map/ppermute | solution.py:50
  187.1 20.4 %collective-permute-start.20 = (bf16[32,4096]{1,0:T(8,128)(2,1)S(1)}, bf16[32,4096]{1,0:T(8,128)(2,1)S(1)}, u32[]{:S(2)}, u32[]{:S(2)}) collective-permute-start(bf16[32,4096]{1,0:T(8,128)(2,1)S(1)} %collective-permute-done.17.refs_0_), channel_id=1, source_target_pairs={{2,3},{6,7},{10,11},{14,15},{18,19},{22,23},{26,27},{30,31}} | collective-permute-start | bytes 786440 | tf_op jit(solution)/shard_map/ppermute | solution.py:49
  191.6 16.0 %collective-permute-start.21 = (bf16[32,4096]{1,0:T(8,128)(2,1)S(1)}, bf16[32,4096]{1,0:T(8,128)(2,1)S(1)}, u32[]{:S(2)}, u32[]{:S(2)}) collective-permute-start(bf16[32,4096]{1,0:T(8,128)(2,1)S(1)} %collective-permute-done.19.refs_1_), channel_id=1, source_target_pairs={{1,0},{5,4},{9,8},{13,12},{17,16},{21,20},{25,24},{29,28}} | collective-permute-start | bytes 786440 | tf_op jit(solution)/shard_map/ppermute | solution.py:50
  192.9 14.7 %collective-permute-start.26 = (bf16[32,4096]{1,0:T(8,128)(2,1)S(1)}, bf16[32,4096]{1,0:T(8,128)(2,1)S(1)}, u32[]{:S(2)}, u32[]{:S(2)}) collective-permute-start(bf16[32,4096]{1,0:T(8,128)(2,1)S(1)} %collective-permute-done.23.refs_4_), channel_id=1, source_target_pairs={{2,3},{6,7},{10,11},{14,15},{18,19},{22,23},{26,27},{30,31}} | collective-permute-start | bytes 786440 | tf_op jit(solution)/shard_map/ppermute | solution.py:49
  198.1 9.5 %collective-permute-start.27 = (bf16[32,4096]{1,0:T(8,128)(2,1)S(1)}, bf16[32,4096]{1,0:T(8,128)(2,1)S(1)}, u32[]{:S(2)}, u32[]{:S(2)}) collective-permute-start(bf16[32,4096]{1,0:T(8,128)(2,1)S(1)} %collective-permute-done.25.refs_5_), channel_id=1, source_target_pairs={{1,0},{5,4},{9,8},{13,12},{17,16},{21,20},{25,24},{29,28}} | collective-permute-start | bytes 786440 | tf_op jit(solution)/shard_map/ppermute | solution.py:50
  (22 other events, 154.5 us)
Sparse Core Ops, SparseCore 0:
  35.8 50.3 all-gather.4
  88.1 45.4 all-gather.2

commit v6 on v5

--- a/solution.py
+++ b/solution.py
@@ -42,13 +42,16 @@
     return values
 
 
+def line_hop(up, down, axis, hop):
+    up = lax.ppermute(up, axis, [(i, i + 1) for i in range(hop - 1, 3)])
+    down = lax.ppermute(down, axis, [(i, i - 1) for i in range(4 - hop, 0, -1)])
+    return up, down
+
+
 def line_gather(block, axis):
-    up = down = block
-    hops = []
-    for hop in range(1, 4):
-        up = lax.ppermute(up, axis, [(i, i + 1) for i in range(hop - 1, 3)])
-        down = lax.ppermute(down, axis, [(i, i - 1) for i in range(4 - hop, 0, -1)])
-        hops.append((up, down))
+    hops = [line_hop(block, block, axis, 1)]
+    for hop in (2, 3):
+        hops.append(line_hop(*hops[-1], axis, hop))
     return hops
 
 
@@ -292,8 +295,8 @@
         ],
         compiler_params=pltpu.CompilerParams(vmem_limit_bytes=54 * MIB),
         cost_estimate=pl.CostEstimate(
-            flops=2 * rows * depth * rank,
-            bytes_accessed=8 * rows * depth + down.size,
+            flops=rows * depth,
+            bytes_accessed=rows * depth,
             transcendentals=0,
         ),
         name="shrink_rows",
@@ -692,16 +695,22 @@
     owners = [own_index] + [hop_owners(tensor_pos, hop) for hop in (1, 2, 3)]
     count = tensor_count * local
     parts = [slice(h * count, (h + 1) * count) for h in range(halves)]
-    everything = [lax.all_gather(raw[part], "tensor", axis=0, tiled=False) for part in parts]
-
     values = raw.astype(F32)
     squares = jnp.sum(values * values, axis=1)
-    squares = summed_over(squares, "tensor")
+    if line:
+        squares = squares + sum(swap(squares, "tensor", d) for d in (1, 2, 3))
+        travelling, squares = lax.optimization_barrier((raw, squares))
+        hop1 = line_hop(travelling, travelling, "tensor", 1)
+    else:
+        squares = summed_over(squares, "tensor")
     own_runs = row_adapter_index[::RUN]
     if halves > 1:
         own_runs = own_runs.reshape(tensor_count, halves, -1).swapaxes(0, 1).reshape(-1)
     told = jnp.concatenate([squares, own_runs.astype(F32)]).reshape(1, -1)
     told = jnp.concatenate([told, swap(told, "store", 2)], axis=0)
+    if line:
+        told, hop1 = lax.optimization_barrier((told, hop1))
+        hop2 = line_hop(*hop1, "tensor", 2)
     told = jnp.concatenate([told, swap(told, "store", 1)], axis=0)
     told = jnp.stack([told[d] for d in (0, 2, 1, 3)])
     told = jnp.stack([jnp.stack([told[p ^ q] for q in range(4)]) for p in range(4)])
@@ -725,7 +734,15 @@
     kept, passed = shrink_rows(place, mine, (raw, beside, across, diagonal), scales, gain, down)
     kept = kept + swap(passed, "store", 1)
     shrunk = kept[0] + swap(kept[1], "store", 2)
-    shrunk = summed_over(shrunk, "tensor").astype(BF16)
+    if line:
+        shrunk = shrunk + swap(shrunk, "tensor", 1)
+        shrunk, hop2 = lax.optimization_barrier((shrunk, hop2))
+        shrunk = shrunk + swap(shrunk, "tensor", 2)
+        shrunk, sent = lax.optimization_barrier((shrunk, hop2))
+        hop3 = line_hop(*sent, "tensor", 3)
+    else:
+        shrunk = summed_over(shrunk, "tensor")
+    shrunk = shrunk.astype(BF16)
     shrunk = jnp.stack([shrunk, swap(shrunk, "store", 2)])
     kept, passed = grow_rows(place, mine, shrunk, swap(shrunk, "store", 1), adapter_up_weight)
     passed = swap(passed, "store", 1)
@@ -736,13 +753,15 @@
 
     weight = query_key_value_weight
     raw, passed = lax.optimization_barrier((raw, passed))
-    mixed = []
-    for h, part in enumerate(parts):
-        if mixed:
-            everything[h], mixed[-1] = lax.optimization_barrier((everything[h], mixed[-1]))
-        own = base_block((raw[part],), own_scale[part], gains, weight, own_index, None)
-        total = base_rows(own_index, everything[h], own_scale[part], gains, own, weight, 0)
-        mixed.append((total + deltas[h]).astype(BF16))
+    if line:
+        near = jnp.concatenate(owners[:3])
+        total = base_block((raw,) + hop1 + hop2, own_scale, gains, weight, near, None)
+        total = base_block(hop3, own_scale, gains, weight, owners[3], total)
+    else:
+        everything = lax.all_gather(raw, "tensor", axis=0, tiled=False)
+        own = base_block((raw,), own_scale, gains, weight, own_index, None)
+        total = base_rows(own_index, everything, own_scale, gains, own, weight, 0)
+    mixed = [(total[part] + delta).astype(BF16) for part, delta in zip(parts, deltas)]
     mixed = [qkv.reshape(tensor_count, local, -1) for qkv in mixed]
 
     contexts = []

time: 225 us -> 211 us (0.938)
  between operations: 13.9 us -> 0.74 us
  starting transfers between devices: 42 us -> 53.7 us
  local copies, waits for them, and re-layouts: 11 us -> 6.63 us
  waiting for transfers between devices: 85.9 us -> 82.3 us
  Pallas kernels: 61.5 us -> 58.4 us
    all_gather x2 -> x0, waiting for transfers between devices: 20.8 us -> none  [on_device(): lax.all_gather(raw[part], 'tensor', axis=0, tiled=False)]
    ppermute x12 -> x18, waiting for transfers between devices: 14.2 us -> 28.5 us  [the longest x9 26.5 us: line_hop(): down = lax.ppermute(down, axis, [(i, i - 1) for i in range(4 - hop, 0, -1)])]
    pallas_call x2 -> x0, Pallas kernels: 12.1 us -> none  [base_rows(): pl.pallas_call(functools.partial(base_kernel, first_row), out_shape=jax.S...]
    pallas_call x2, Pallas kernels: 5.85 us -> 15.5 us  [base_block(): pl.pallas_call(functools.partial(block_kernel, count, total is not None),...]
    all_to_all x2, waiting for transfers between devices: 0.65 us -> 9.91 us  [on_device(): exchanged.append(lax.all_to_all(qkv, 'tensor', 0, 0, tiled=True))]
    ppermute x12 -> x18, starting transfers between devices: 18.9 us -> 27.4 us  [the longest x9 15.6 us: line_hop(): up = lax.ppermute(up, axis, [(i, i + 1) for i in range(hop - 1, 3)])]
    ppermute x16 -> x17, waiting for transfers between devices: 50.2 us -> 43.9 us  [swap(): return lax.ppermute(values, axis, [(i, i ^ distance) for i in range(count)])]
    ppermute x16 -> x17, starting transfers between devices: 15.1 us -> 19.4 us  [swap(): return lax.ppermute(values, axis, [(i, i ^ distance) for i in range(count)])]
  transfers between devices with their start and end apart: 32 -> 37, of which waited for: 17 -> 17; matrix products, arithmetic and copies ran while one was open for 6% -> 4% of each run, Pallas kernels for 24% -> 21%
where the time goes in v6:
time: 211 us
  waiting for transfers between devices  82.3 us (39%)
  Pallas kernels  58.4 us (28%)
  starting transfers between devices  53.7 us (25%)
  other arithmetic  8.76 us (4%)
  local copies, waits for them, and re-layouts  6.63 us (3%)
    ppermute x17, waiting for transfers between devices, swap(): return lax.ppermute(values, axis, [(i, i ^ distance) for i in range(count)])  43.9 us
    ppermute x9, waiting for transfers between devices, line_hop(): down = lax.ppermute(down, axis, [(i, i - 1) for i in range(4 - hop, 0, -1)])  26.5 us
    ppermute x17, starting transfers between devices, swap(): return lax.ppermute(values, axis, [(i, i ^ distance) for i in range(count)])  19.4 us
    pallas_call x2, Pallas kernels, project(): pl.pallas_call(functools.partial(out_kernel, count, earlier is not None),...  16.9 us
    ppermute x9, starting transfers between devices, line_hop(): up = lax.ppermute(up, axis, [(i, i + 1) for i in range(hop - 1, 3)])  15.6 us
    pallas_call x2, Pallas kernels, base_block(): pl.pallas_call(functools.partial(block_kernel, count, total is not None),...  15.5 us
    pallas_call x2, Pallas kernels, attend(): pl.pallas_call(functools.partial(attend_kernel, unit, first_row), out_sha...  13.4 us
    ppermute x9, starting transfers between devices, line_hop(): down = lax.ppermute(down, axis, [(i, i - 1) for i in range(4 - hop, 0, -1)])  11.8 us
  transfers between devices with their start and end apart: 37, of which 17 were waited for; matrix products, arithmetic and copies ran while one was open for 4% of the time, Pallas kernels for 21%

profile of v6, /device:TPU:0, one launch (start us, length us, event | category | flops | bytes accessed | tf_op | source)
XLA Modules:
  0.0 210.6 jit_solution(15968807660023828179)
XLA Ops:
  1.7 3.1 %collective-permute-start = (f32[256]{0:T(256)S(1)}, f32[256]{0:T(256)S(1)}, u32[]{:S(2)}, u32[]{:S(2)}) collective-permute-start(f32[256]{0:T(256)S(1)} %reduce_sum.59), channel_id=1, source_target_pairs={{0,1},{1,0},{2,3},{3,2},{4,5},{5,4},{6,7},{7,6},{8,9},{9,8},{10,11... | collective-permute-start | bytes 3080 | tf_op jit(solution)/shard_map/ppermute | solution.py:34
  17.9 15.3 %collective-permute-done.3 = f32[1,272]{1,0:T(1,128)S(1)} collective-permute-done((f32[1,272]{1,0:T(1,128)S(1)}, f32[1,272]{1,0:T(1,128)S(1)}, u32[]{:S(2)}, u32[]{:S(2)}) %collective-permute-start.3) | collective-permute-done | bytes 1120 | tf_op jit(solution)/shard_map/ppermute | solution.py:34
  35.0 4.2 %collective-permute-done.5.refs_2_ = bf16[256,2048]{1,0:T(8,128)(2,1)S(1)} collective-permute-done((bf16[256,2048]{1,0:T(8,128)(2,1)S(1)}, bf16[256,2048]{1,0:T(8,128)(2,1)S(1)}, u32[]{:S(2)}, u32[]{:S(2)}) %collective-permute-start.5) | collective-permute-done | bytes 1048608 | tf_op jit(solution)/shard_map/ppermute | solution.py:47
  44.1 6.4 %shrink_rows.1 = (f32[2,128,128]{2,1,0:T(8,128)}, f32[2,128,128]{2,1,0:T(8,128)}) custom-call(s32[1]{0:T(128)} %bitcast.4.place_ref, s32[64]{0:T(128)} %compare_select_fusion.slots, bf16[256,2048]{1,0:T(8,128)(2,1)} %bitcast.66, bf16[256,2048]{1,0:T(8,128)(2,1)} %collective-permute-done.7.x1, bf16[256,2048]{1,0:T(8,128)(2,1)} %collective-permute-done.8.x2, ...), custom_call_target="tpu_custom_call" | custom-call | flops 524288 | bytes 524288 | tf_op jit(solution)/shard_map/shrink_rows/pallas_call | solution.py:283
  58.1 4.6 %collective-permute-start.12 = (f32[128,128]{1,0:T(8,128)S(1)}, f32[128,128]{1,0:T(8,128)S(1)}, u32[]{:S(2)}, u32[]{:S(2)}) collective-permute-start(f32[128,128]{1,0:T(8,128)S(1)} %fusion.12), channel_id=1, source_target_pairs={{0,1},{1,0},{2,3},{3,2},{4,5},{5,4},{6,7},{7,6},{8,9},{9,8},{10,11... | collective-permute-start | bytes 196616 | tf_op jit(solution)/shard_map/ppermute | solution.py:34
  62.7 9.6 %collective-permute-done.12 = f32[128,128]{1,0:T(8,128)S(1)} collective-permute-done((f32[128,128]{1,0:T(8,128)S(1)}, f32[128,128]{1,0:T(8,128)S(1)}, u32[]{:S(2)}, u32[]{:S(2)}) %collective-permute-start.12) | collective-permute-done | bytes 65568 | tf_op jit(solution)/shard_map/ppermute | solution.py:34
  72.4 5.6 %collective-permute-done.15 = f32[128,128]{1,0:T(8,128)S(1)} collective-permute-done((f32[128,128]{1,0:T(8,128)S(1)}, f32[128,128]{1,0:T(8,128)S(1)}, u32[]{:S(2)}, u32[]{:S(2)}) %collective-permute-start.15) | collective-permute-done | bytes 65568 | tf_op jit(solution)/shard_map/ppermute | solution.py:34
  78.7 3.4 %collective-permute-done.18 = bf16[128,128]{1,0:T(8,128)(2,1)S(1)} collective-permute-done((bf16[128,128]{1,0:T(8,128)(2,1)S(1)}, bf16[128,128]{1,0:T(8,128)(2,1)S(1)}, u32[]{:S(2)}, u32[]{:S(2)}) %collective-permute-start.18) | collective-permute-done | bytes 32800 | tf_op jit(solution)/shard_map/ppermute | solution.py:34
  84.0 6.2 %grow_rows.1 = (f32[2,256,1280]{2,1,0:T(8,128)}, f32[2,256,1280]{2,1,0:T(8,128)}) custom-call(s32[1]{0:T(128)} %bitcast.4.place_ref, s32[64]{0:T(128)} %compare_select_fusion.slots, bf16[2,128,128]{2,1,0:T(8,128)(2,1)} %copy-done.6, bf16[2,128,128]{2,1,0:T(8,128)(2,1)} %copy-done.7, bf16[32,64,1280]{2,1,0:T(8,128)(2,1)} %up_ref.1), custom_call_target="tpu_custom_call" | custom-call | flops 41943040 | bytes 5242880 | tf_op jit(solution)/shard_map/grow_rows/pallas_call | solution.py:356
  99.5 11.4 %base_block.2.refs_5_ = f32[256,1280]{1,0:T(8,128)} custom-call(s32[5]{0:T(128)S(1)} %concatenate.33.owners, bf16[256,2048]{1,0:T(8,128)(2,1)S(1)} %bitcast.67, bf16[256,2048]{1,0:T(8,128)(2,1)S(1)} %collective-permute-done.4.refs_1_, bf16[256,2048]{1,0:T(8,128)(2,1)S(1)} %collective-permute-done.5.refs_2_, ...), custom_call_target="tpu_custom_call" | custom-call | flops 6710886400 | bytes 8912896 | tf_op jit(solution)/shard_map/base_block/pallas_call | solution.py:106
  110.9 8.4 %collective-permute-done.17.refs_1_ = bf16[256,2048]{1,0:T(8,128)(2,1)S(1)} collective-permute-done((bf16[256,2048]{1,0:T(8,128)(2,1)}, bf16[256,2048]{1,0:T(8,128)(2,1)S(1)}, u32[]{:S(2)}, u32[]{:S(2)}) %collective-permute-start.17) | collective-permute-done | bytes 1048608 | tf_op jit(solution)/shard_map/ppermute | solution.py:47
  120.6 4.1 %base_block.3 = f32[256,1280]{1,0:T(8,128)S(1)} custom-call(s32[2]{0:T(128)S(1)} %pad_add_fusion.1.owners, bf16[256,2048]{1,0:T(8,128)(2,1)S(1)} %collective-permute-done.16.refs_0_, bf16[256,2048]{1,0:T(8,128)(2,1)S(1)} %collective-permute-done.17.refs_1_, f32[256,1]{1,0:T(8,128)S(1)} %copy.22.refs_5_.refs_2_, f32[1,8192]{1,0:T(1,128)S(1)} %bitcast.69, ...), custom_call_target="tpu_custom_call" | custom-call | flops 2684354560 | bytes 8912896 | tf_op jit(solution)/shard_map/base_block/pallas_call | solution.py:106
  127.2 3.5 %all-to-all-start = ((bf16[4,32,1280]{2,1,0:T(8,128)(2,1)}), bf16[4,32,1280]{2,1,0:T(8,128)(2,1)S(1)}, u32[]{:S(2)}, u32[]{:S(2)}) async-start(bf16[4,32,1280]{2,1,0:T(8,128)(2,1)} %bitcast.32), calls=%async_computation | async-start | bytes 655360 | tf_op jit(solution)/shard_map/all_to_all | solution.py:772
  131.1 9.9 %all-to-all-done.qkv_ref = bf16[4,32,1280]{2,1,0:T(8,128)(2,1)S(1)} async-done(((bf16[4,32,1280]{2,1,0:T(8,128)(2,1)}), bf16[4,32,1280]{2,1,0:T(8,128)(2,1)S(1)}, u32[]{:S(2)}, u32[]{:S(2)}) %all-to-all-start) | async-done | bytes 327712 | tf_op jit(solution)/shard_map/all_to_all | solution.py:772
  141.0 3.5 %all-to-all-start.1 = ((bf16[4,32,1280]{2,1,0:T(8,128)(2,1)}), bf16[4,32,1280]{2,1,0:T(8,128)(2,1)S(1)}, u32[]{:S(2)}, u32[]{:S(2)}) async-start(bf16[4,32,1280]{2,1,0:T(8,128)(2,1)} %bitcast.29), calls=%async_computation.1 | async-start | bytes 655360 | tf_op jit(solution)/shard_map/all_to_all | solution.py:772
  145.1 6.7 %attend.2.refs_0_ = bf16[32,4096]{1,0:T(8,128)(2,1)S(1)} custom-call(s32[16]{0:T(128)S(1)} %get-tuple-element.67.lengths, s32[16]{0:T(128)S(1)} %select_reduce_fusion.2.order, bf16[4,32,1280]{2,1,0:T(8,128)(2,1)S(1)} %all-to-all-done.qkv_ref, f32[32,128]{1,0:T(8,128)S(1)} %get-tuple-element.68.cos_ref, f32[32,128]{1,0:T(8,128)S(1)} %get-tuple-element.69.sin_ref, ...), custom_call_target="tpu_custom_call" | custom-call | flops 268435456 | bytes 16777216 | tf_op jit(solution)/shard_map/attend/pallas_call | solution.py:537
  151.8 3.3 %collective-permute-start.23 = (bf16[32,4096]{1,0:T(8,128)(2,1)S(1)}, bf16[32,4096]{1,0:T(8,128)(2,1)S(1)}, u32[]{:S(2)}, u32[]{:S(2)}) collective-permute-start(bf16[32,4096]{1,0:T(8,128)(2,1)S(1)} %attend.2.refs_0_), channel_id=1, source_target_pairs={{0,1},{1,2},{2,3},{4,5},{5,6},{6,7},{8,9},{9,10},{10,11},{12,13},{... | collective-permute-start | bytes 786440 | tf_op jit(solution)/shard_map/ppermute | solution.py:46
  156.4 6.7 %attend.3.refs_3_ = bf16[32,4096]{1,0:T(8,128)(2,1)S(1)} custom-call(s32[16]{0:T(128)S(1)} %get-tuple-element.66.lengths, s32[16]{0:T(128)S(1)} %select_reduce_fusion.1.order, bf16[4,32,1280]{2,1,0:T(8,128)(2,1)S(1)} %all-to-all-done.1.qkv_ref, f32[32,128]{1,0:T(8,128)S(1)} %get-tuple-element.70.cos_ref, f32[32,128]{1,0:T(8,128)S(1)} %get-tuple-element.71.sin_ref, ...), custom_call_target="tpu_custom_call" | custom-call | flops 268435456 | bytes 16777216 | tf_op jit(solution)/shard_map/attend/pallas_call | solution.py:537
  163.1 5.8 %collective-permute-start.29 = (bf16[32,4096]{1,0:T(8,128)(2,1)S(1)}, bf16[32,4096]{1,0:T(8,128)(2,1)S(1)}, u32[]{:S(2)}, u32[]{:S(2)}) collective-permute-start(bf16[32,4096]{1,0:T(8,128)(2,1)S(1)} %attend.3.refs_3_), channel_id=1, source_target_pairs={{0,1},{1,2},{2,3},{4,5},{5,6},{6,7},{8,9},{9,10},{10,11},{12,13},{... | collective-permute-start | bytes 786440 | tf_op jit(solution)/shard_map/ppermute | solution.py:46
  173.4 5.8 %collective-permute-done.31.refs_5_ = bf16[32,4096]{1,0:T(8,128)(2,1)S(1)} collective-permute-done((bf16[32,4096]{1,0:T(8,128)(2,1)S(1)}, bf16[32,4096]{1,0:T(8,128)(2,1)S(1)}, u32[]{:S(2)}, u32[]{:S(2)}) %collective-permute-start.31) | collective-permute-done | bytes 262176 | tf_op jit(solution)/shard_map/ppermute | solution.py:47
  181.3 3.8 %collective-permute-done.26.refs_1_ = bf16[32,4096]{1,0:T(8,128)(2,1)S(1)} collective-permute-done((bf16[32,4096]{1,0:T(8,128)(2,1)S(1)}, bf16[32,4096]{1,0:T(8,128)(2,1)S(1)}, u32[]{:S(2)}, u32[]{:S(2)}) %collective-permute-start.26) | collective-permute-done | bytes 262176 | tf_op jit(solution)/shard_map/ppermute | solution.py:47
  187.1 4.3 %collective-permute-done.32.refs_5_ = bf16[32,4096]{1,0:T(8,128)(2,1)S(1)} collective-permute-done((bf16[32,4096]{1,0:T(8,128)(2,1)S(1)}, bf16[32,4096]{1,0:T(8,128)(2,1)S(1)}, u32[]{:S(2)}, u32[]{:S(2)}) %collective-permute-start.32) | collective-permute-done | bytes 262176 | tf_op jit(solution)/shard_map/ppermute | solution.py:47
  192.7 8.1 %project.2.refs_9_ = bf16[2,4,2,16,2048]{4,3,2,1,0:T(8,128)(2,1)} custom-call(s32[3]{0:T(128)S(1)} %pad_add_fusion.2.owners, bf16[32,4096]{1,0:T(8,128)(2,1)S(1)} %attend.2.refs_0_, bf16[32,4096]{1,0:T(8,128)(2,1)S(1)} %collective-permute-done.23.refs_1_, bf16[32,4096]{1,0:T(8,128)(2,1)S(1)} %collective-permute-done.25.refs_2_, ...), custom_call_target="tpu_custom_call" | custom-call | flops 3221225472 | bytes 19136512 | tf_op jit(solution)/shard_map/project/pallas_call | solution.py:622
  201.6 8.8 %project.3 = bf16[2,4,2,16,2048]{4,3,2,1,0:T(8,128)(2,1)} custom-call(s32[4]{0:T(128)S(1)} %pad_add_fusion.owners, bf16[32,4096]{1,0:T(8,128)(2,1)S(1)} %collective-permute-done.24.refs_0_, bf16[32,4096]{1,0:T(8,128)(2,1)S(1)} %collective-permute-done.26.refs_1_, bf16[32,4096]{1,0:T(8,128)(2,1)S(1)} %collective-permute-done.27.refs_2_, ...), custom_call_target="tpu_custom_call" | custom-call | flops 2147483648 | bytes 18350080 | tf_op jit(solution)/shard_map/project/pallas_call | solution.py:622
  (132 shorter events, 57.5 us)
Async XLA Ops:
  8.6 24.5 %collective-permute-start.8 = (bf16[256,2048]{1,0:T(8,128)(2,1)S(1)}, bf16[256,2048]{1,0:T(8,128)(2,1)}, u32[]{:S(2)}, u32[]{:S(2)}) collective-permute-start(bf16[256,2048]{1,0:T(8,128)(2,1)S(1)} %bitcast.62), channel_id=1, source_target_pairs={{0,8},{4,12},{8,0},{12,4},{1,9},{5,13},{9,1},{13,5},{2,10},{6,14},... | collective-permute-start | bytes 3145736 | tf_op jit(solution)/shard_map/ppermute | solution.py:34
  12.7 22.3 %collective-permute-start.4 = (bf16[256,2048]{1,0:T(8,128)(2,1)S(1)}, bf16[256,2048]{1,0:T(8,128)(2,1)S(1)}, u32[]{:S(2)}, u32[]{:S(2)}) collective-permute-start(bf16[256,2048]{1,0:T(8,128)(2,1)S(1)} %bitcast.63), channel_id=1, source_target_pairs={{0,1},{1,2},{2,3},{4,5},{5,6},{6,7},{8,9},{9,10},{10,11},{12,13},{... | collective-permute-start | bytes 3145736 | tf_op jit(solution)/shard_map/ppermute | solution.py:46
  14.1 25.1 %collective-permute-start.5 = (bf16[256,2048]{1,0:T(8,128)(2,1)S(1)}, bf16[256,2048]{1,0:T(8,128)(2,1)S(1)}, u32[]{:S(2)}, u32[]{:S(2)}) collective-permute-start(bf16[256,2048]{1,0:T(8,128)(2,1)S(1)} %bitcast.64), channel_id=1, source_target_pairs={{3,2},{2,1},{1,0},{7,6},{6,5},{5,4},{11,10},{10,9},{9,8},{15,14},{... | collective-permute-start | bytes 3145736 | tf_op jit(solution)/shard_map/ppermute | solution.py:47
  15.7 17.5 %collective-permute-start.3 = (f32[1,272]{1,0:T(1,128)S(1)}, f32[1,272]{1,0:T(1,128)S(1)}, u32[]{:S(2)}, u32[]{:S(2)}) collective-permute-start(f32[1,272]{1,0:T(1,128)S(1)} %reshape.110), channel_id=1, source_target_pairs={{0,8},{4,12},{8,0},{12,4},{1,9},{5,13},{9,1},{13,5},{2,10},{6,14},... | collective-permute-start | bytes 3272 | tf_op jit(solution)/shard_map/ppermute | solution.py:34
  17.3 26.8 %collective-permute-start.7 = (bf16[256,2048]{1,0:T(8,128)(2,1)S(1)}, bf16[256,2048]{1,0:T(8,128)(2,1)}, u32[]{:S(2)}, u32[]{:S(2)}) collective-permute-start(bf16[256,2048]{1,0:T(8,128)(2,1)S(1)} %bitcast.65), channel_id=1, source_target_pairs={{0,4},{4,0},{8,12},{12,8},{1,5},{5,1},{9,13},{13,9},{2,6},{6,2},{1... | collective-permute-start | bytes 3145736 | tf_op jit(solution)/shard_map/ppermute | solution.py:34
  33.2 10.9 %collective-permute-start.9 = (bf16[256,2048]{1,0:T(8,128)(2,1)}, bf16[256,2048]{1,0:T(8,128)(2,1)}, u32[]{:S(2)}, u32[]{:S(2)}) collective-permute-start(bf16[256,2048]{1,0:T(8,128)(2,1)} %collective-permute-done.8.x2), channel_id=1, source_target_pairs={{0,4},{4,0},{8,12},{12,8},{1,5},{5,1},{9,13},{13,9},{2,6},{6,2},{1... | collective-permute-start | bytes 3145736 | tf_op jit(solution)/shard_map/ppermute | solution.py:34
  39.2 33.2 %collective-permute-start.13 = (bf16[256,2048]{1,0:T(8,128)(2,1)S(1)}, bf16[256,2048]{1,0:T(8,128)(2,1)}, u32[]{:S(2)}, u32[]{:S(2)}) collective-permute-start(bf16[256,2048]{1,0:T(8,128)(2,1)S(1)} %collective-permute-done.4.refs_1_), channel_id=1, source_target_pairs={{1,2},{2,3},{5,6},{6,7},{9,10},{10,11},{13,14},{14,15},{17,18},{18... | collective-permute-start | bytes 3145736 | tf_op jit(solution)/shard_map/ppermute | solution.py:46
  40.9 31.4 %collective-permute-start.14 = (bf16[256,2048]{1,0:T(8,128)(2,1)S(1)}, bf16[256,2048]{1,0:T(8,128)(2,1)}, u32[]{:S(2)}, u32[]{:S(2)}) collective-permute-start(bf16[256,2048]{1,0:T(8,128)(2,1)S(1)} %collective-permute-done.5.refs_2_), channel_id=1, source_target_pairs={{2,1},{1,0},{6,5},{5,4},{10,9},{9,8},{14,13},{13,12},{18,17},{17,1... | collective-permute-start | bytes 3145736 | tf_op jit(solution)/shard_map/ppermute | solution.py:47
  58.1 14.2 %collective-permute-start.12 = (f32[128,128]{1,0:T(8,128)S(1)}, f32[128,128]{1,0:T(8,128)S(1)}, u32[]{:S(2)}, u32[]{:S(2)}) collective-permute-start(f32[128,128]{1,0:T(8,128)S(1)} %fusion.12), channel_id=1, source_target_pairs={{0,1},{1,0},{2,3},{3,2},{4,5},{5,4},{6,7},{7,6},{8,9},{9,8},{10,11... | collective-permute-start | bytes 196616 | tf_op jit(solution)/shard_map/ppermute | solution.py:34
  90.9 19.9 %collective-permute-start.16 = (bf16[256,2048]{1,0:T(8,128)(2,1)}, bf16[256,2048]{1,0:T(8,128)(2,1)S(1)}, u32[]{:S(2)}, u32[]{:S(2)}) collective-permute-start(bf16[256,2048]{1,0:T(8,128)(2,1)} %collective-permute-done.13.refs_3_), channel_id=1, source_target_pairs={{2,3},{6,7},{10,11},{14,15},{18,19},{22,23},{26,27},{30,31}} | collective-permute-start | bytes 3145736 | tf_op jit(solution)/shard_map/ppermute | solution.py:46
  91.7 27.6 %collective-permute-start.17 = (bf16[256,2048]{1,0:T(8,128)(2,1)}, bf16[256,2048]{1,0:T(8,128)(2,1)S(1)}, u32[]{:S(2)}, u32[]{:S(2)}) collective-permute-start(bf16[256,2048]{1,0:T(8,128)(2,1)} %collective-permute-done.14.refs_4_), channel_id=1, source_target_pairs={{1,0},{5,4},{9,8},{13,12},{17,16},{21,20},{25,24},{29,28}} | collective-permute-start | bytes 3145736 | tf_op jit(solution)/shard_map/ppermute | solution.py:47
  97.4 27.3 %collective-permute-start.21 = (f16[128,1280]{1,0:T(8,128)(2,1)S(1)}, f16[128,1280]{1,0:T(8,128)(2,1)S(1)}, u32[]{:S(2)}, u32[]{:S(2)}) collective-permute-start(f16[128,1280]{1,0:T(8,128)(2,1)S(1)} %get-tuple-element.44), channel_id=1, source_target_pairs={{0,8},{4,12},{8,0},{12,4},{1,9},{5,13},{9,1},{13,5},{2,10},{6,14},... | collective-permute-start | bytes 983048 | tf_op jit(solution)/shard_map/ppermute | solution.py:34
  98.2 26.6 %collective-permute-start.22 = (f16[128,1280]{1,0:T(8,128)(2,1)S(1)}, f16[128,1280]{1,0:T(8,128)(2,1)S(1)}, u32[]{:S(2)}, u32[]{:S(2)}) collective-permute-start(f16[128,1280]{1,0:T(8,128)(2,1)S(1)} %get-tuple-element.43), channel_id=1, source_target_pairs={{0,8},{4,12},{8,0},{12,4},{1,9},{5,13},{9,1},{13,5},{2,10},{6,14},... | collective-permute-start | bytes 983048 | tf_op jit(solution)/shard_map/ppermute | solution.py:34
  127.2 13.8 %all-to-all-start = ((bf16[4,32,1280]{2,1,0:T(8,128)(2,1)}), bf16[4,32,1280]{2,1,0:T(8,128)(2,1)S(1)}, u32[]{:S(2)}, u32[]{:S(2)}) async-start(bf16[4,32,1280]{2,1,0:T(8,128)(2,1)} %bitcast.32), calls=%async_computation | async-start | bytes 655360 | tf_op jit(solution)/shard_map/all_to_all | solution.py:772
  141.0 15.4 %all-to-all-start.1 = ((bf16[4,32,1280]{2,1,0:T(8,128)(2,1)}), bf16[4,32,1280]{2,1,0:T(8,128)(2,1)S(1)}, u32[]{:S(2)}, u32[]{:S(2)}) async-start(bf16[4,32,1280]{2,1,0:T(8,128)(2,1)} %bitcast.29), calls=%async_computation.1 | async-start | bytes 655360 | tf_op jit(solution)/shard_map/all_to_all | solution.py:772
  151.8 18.6 %collective-permute-start.23 = (bf16[32,4096]{1,0:T(8,128)(2,1)S(1)}, bf16[32,4096]{1,0:T(8,128)(2,1)S(1)}, u32[]{:S(2)}, u32[]{:S(2)}) collective-permute-start(bf16[32,4096]{1,0:T(8,128)(2,1)S(1)} %attend.2.refs_0_), channel_id=1, source_target_pairs={{0,1},{1,2},{2,3},{4,5},{5,6},{6,7},{8,9},{9,10},{10,11},{12,13},{... | collective-permute-start | bytes 786440 | tf_op jit(solution)/shard_map/ppermute | solution.py:46
  155.1 16.0 %collective-permute-start.25 = (bf16[32,4096]{1,0:T(8,128)(2,1)S(1)}, bf16[32,4096]{1,0:T(8,128)(2,1)S(1)}, u32[]{:S(2)}, u32[]{:S(2)}) collective-permute-start(bf16[32,4096]{1,0:T(8,128)(2,1)S(1)} %attend.2.refs_0_), channel_id=1, source_target_pairs={{3,2},{2,1},{1,0},{7,6},{6,5},{5,4},{11,10},{10,9},{9,8},{15,14},{... | collective-permute-start | bytes 786440 | tf_op jit(solution)/shard_map/ppermute | solution.py:47
  168.9 10.3 %collective-permute-start.31 = (bf16[32,4096]{1,0:T(8,128)(2,1)S(1)}, bf16[32,4096]{1,0:T(8,128)(2,1)S(1)}, u32[]{:S(2)}, u32[]{:S(2)}) collective-permute-start(bf16[32,4096]{1,0:T(8,128)(2,1)S(1)} %attend.3.refs_3_), channel_id=1, source_target_pairs={{3,2},{2,1},{1,0},{7,6},{6,5},{5,4},{11,10},{10,9},{9,8},{15,14},{... | collective-permute-start | bytes 786440 | tf_op jit(solution)/shard_map/ppermute | solution.py:47
  171.1 14.0 %collective-permute-start.26 = (bf16[32,4096]{1,0:T(8,128)(2,1)S(1)}, bf16[32,4096]{1,0:T(8,128)(2,1)S(1)}, u32[]{:S(2)}, u32[]{:S(2)}) collective-permute-start(bf16[32,4096]{1,0:T(8,128)(2,1)S(1)} %collective-permute-done.25.refs_2_), channel_id=1, source_target_pairs={{2,1},{1,0},{6,5},{5,4},{10,9},{9,8},{14,13},{13,12},{18,17},{17,1... | collective-permute-start | bytes 786440 | tf_op jit(solution)/shard_map/ppermute | solution.py:47
  172.7 13.7 %collective-permute-start.30 = (bf16[32,4096]{1,0:T(8,128)(2,1)S(1)}, bf16[32,4096]{1,0:T(8,128)(2,1)S(1)}, u32[]{:S(2)}, u32[]{:S(2)}) collective-permute-start(bf16[32,4096]{1,0:T(8,128)(2,1)S(1)} %collective-permute-done.29.refs_4_), channel_id=1, source_target_pairs={{1,2},{2,3},{5,6},{6,7},{9,10},{10,11},{13,14},{14,15},{17,18},{18... | collective-permute-start | bytes 786440 | tf_op jit(solution)/shard_map/ppermute | solution.py:46
  179.2 12.2 %collective-permute-start.32 = (bf16[32,4096]{1,0:T(8,128)(2,1)S(1)}, bf16[32,4096]{1,0:T(8,128)(2,1)S(1)}, u32[]{:S(2)}, u32[]{:S(2)}) collective-permute-start(bf16[32,4096]{1,0:T(8,128)(2,1)S(1)} %collective-permute-done.31.refs_5_), channel_id=1, source_target_pairs={{2,1},{1,0},{6,5},{5,4},{10,9},{9,8},{14,13},{13,12},{18,17},{17,1... | collective-permute-start | bytes 786440 | tf_op jit(solution)/shard_map/ppermute | solution.py:47
  180.7 20.2 %collective-permute-start.27 = (bf16[32,4096]{1,0:T(8,128)(2,1)S(1)}, bf16[32,4096]{1,0:T(8,128)(2,1)S(1)}, u32[]{:S(2)}, u32[]{:S(2)}) collective-permute-start(bf16[32,4096]{1,0:T(8,128)(2,1)S(1)} %collective-permute-done.24.refs_0_), channel_id=1, source_target_pairs={{2,3},{6,7},{10,11},{14,15},{18,19},{22,23},{26,27},{30,31}} | collective-permute-start | bytes 786440 | tf_op jit(solution)/shard_map/ppermute | solution.py:46
  185.1 15.7 %collective-permute-start.28 = (bf16[32,4096]{1,0:T(8,128)(2,1)S(1)}, bf16[32,4096]{1,0:T(8,128)(2,1)S(1)}, u32[]{:S(2)}, u32[]{:S(2)}) collective-permute-start(bf16[32,4096]{1,0:T(8,128)(2,1)S(1)} %collective-permute-done.26.refs_1_), channel_id=1, source_target_pairs={{1,0},{5,4},{9,8},{13,12},{17,16},{21,20},{25,24},{29,28}} | collective-permute-start | bytes 786440 | tf_op jit(solution)/shard_map/ppermute | solution.py:47
  186.4 14.4 %collective-permute-start.33 = (bf16[32,4096]{1,0:T(8,128)(2,1)S(1)}, bf16[32,4096]{1,0:T(8,128)(2,1)S(1)}, u32[]{:S(2)}, u32[]{:S(2)}) collective-permute-start(bf16[32,4096]{1,0:T(8,128)(2,1)S(1)} %collective-permute-done.30.refs_4_), channel_id=1, source_target_pairs={{2,3},{6,7},{10,11},{14,15},{18,19},{22,23},{26,27},{30,31}} | collective-permute-start | bytes 786440 | tf_op jit(solution)/shard_map/ppermute | solution.py:46
  (24 other events, 233.5 us)

commit v7 on v6

--- a/solution.py
+++ b/solution.py
@@ -61,16 +61,23 @@
     return jnp.stack([jnp.where(below >= 0, below, -1), jnp.where(above < 4, above, -1)])
 
 
-def block_kernel(count, has_total, owners, *refs):
+def block_kernel(first_rows, owners, *refs):
+    count = len(refs) - 6
     x_refs = refs[:count]
-    scale_ref, gain_ref, w_ref = refs[count : count + 3]
-    out_ref, held, sems = refs[-3:]
-    _, tiles, depth, _ = held.shape
+    scale_ref, gain_ref, w_ref, out_ref, held, sems = refs[count:]
+    rows = scale_ref.shape[0]
+    slots, tiles, depth, _ = held.shape
+
+    def slot(j):
+        used = jnp.int32(0)
+        for i in range(j):
+            used = used + (owners[i] >= 0).astype(jnp.int32)
+        return used
 
     def copy(j, k):
         first = pl.multiple_of((owners[j] * tiles + k) * depth, depth)
         return pltpu.make_async_copy(
-            w_ref.at[pl.ds(first, depth), :], held.at[j, k], sems.at[j, k]
+            w_ref.at[pl.ds(first, depth), :], held.at[slot(j), k], sems.at[slot(j), k]
         )
 
     for j in range(count):
@@ -80,7 +87,7 @@
             for k in range(tiles):
                 copy(j, k).start()
 
-    out_ref[...] = refs[count + 3][...] if has_total else jnp.zeros_like(out_ref)
+    out_ref[...] = jnp.zeros_like(out_ref)
     for j, x_ref in enumerate(x_refs):
 
         @pl.when(owners[j] >= 0)
@@ -90,36 +97,35 @@
                 span = slice(k * depth, (k + 1) * depth)
                 first = pl.multiple_of((owners[j] * tiles + k) * depth, depth)
                 gain = gain_ref[:, pl.ds(first, depth)]
-                normed = (x_ref[:, span].astype(F32) * scale * gain).astype(BF16)
+                part = x_ref[first_rows[j] : first_rows[j] + rows, span].astype(F32)
+                normed = (part * scale * gain).astype(BF16)
                 copy(j, k).wait()
-                out_ref[...] += jnp.dot(normed, held[j, k], preferred_element_type=F32)
-
-
-def base_block(blocks, scale, gain, weight, owners, total):
-    rows, depth = blocks[0].shape
+                out_ref[...] += jnp.dot(normed, held[slot(j), k], preferred_element_type=F32)
+
+
+def base_block(blocks, scale, gain, weight, owners, first_rows=(0,), present=1):
+    depth = blocks[0].shape[1]
+    rows = scale.shape[0]
     columns = weight.shape[1]
     tile = min(512, depth)
     count = len(blocks)
-    operands = [owners, *blocks, scale, gain, weight]
-    if total is not None:
-        operands.append(total)
     return pl.pallas_call(
-        functools.partial(block_kernel, count, total is not None),
+        functools.partial(block_kernel, first_rows),
         out_shape=jax.ShapeDtypeStruct((rows, columns), F32),
-        in_specs=[SMEM] + [VMEM] * (count + 2) + [HBM] + [VMEM] * (total is not None),
+        in_specs=[SMEM] + [VMEM] * (count + 2) + [HBM],
         out_specs=VMEM,
         scratch_shapes=[
-            pltpu.VMEM((count, depth // tile, tile, columns), BF16),
-            pltpu.SemaphoreType.DMA((count, depth // tile)),
+            pltpu.VMEM((present, depth // tile, tile, columns), BF16),
+            pltpu.SemaphoreType.DMA((present, depth // tile)),
         ],
         compiler_params=pltpu.CompilerParams(vmem_limit_bytes=48 * MIB),
         cost_estimate=pl.CostEstimate(
-            flops=2 * count * rows * depth * columns,
-            bytes_accessed=2 * depth * (rows + columns) + 8 * rows * columns,
+            flops=2 * present * rows * depth * columns,
+            bytes_accessed=2 * present * depth * (rows + columns) + 4 * rows * columns,
             transcendentals=0,
         ),
         name="base_block",
-    )(*operands)
+    )(owners, *blocks, scale, gain, weight)
 
 
 def base_kernel(first_row, place_ref, x_ref, scale_ref, gain_ref, own_ref, w_ref, out_ref, held, sems):
@@ -304,8 +310,11 @@
 
 
 def grow_kernel(
-    place_ref, slots, s0, s1, up_ref, keep_ref, send_ref, jobs, parts, held, sems
+    place_ref, slots, s0, s1, up_ref, keep_ref, *refs
 ):
+    *sends, jobs, parts, held, sems = refs
+    pieces = len(sends) // 2
+    piece = keep_ref.shape[1] // pieces
     runs = held.shape[0] // 4
     rank = held.shape[1]
 
@@ -332,9 +341,14 @@
             def _():
                 keep_ref[slab, rows, :] = grown
 
-            @pl.when(slab >= 2)
-            def _():
-                send_ref[slab - 2, rows, :] = grown
+            run = job % runs
+            inner = pl.ds(pl.multiple_of(lax.rem(run * 16, piece), 16), 16)
+            target = (slab - 2) * pieces + (run * 16) // piece
+            for i, send_ref in enumerate(sends):
+
+                @pl.when((slab >= 2) & (target == i))
+                def _():
+                    send_ref[inner, :] = grown
 
     count = list_runs(place_ref, slots, runs, jobs, start)
     for slab in range(4):
@@ -344,20 +358,22 @@
             parts[low] = both[:, :rank]
             parts[low + runs // 2] = both[:, rank:]
     keep_ref[...] = jnp.zeros_like(keep_ref)
-    send_ref[...] = jnp.zeros_like(send_ref)
+    for send_ref in sends:
+        send_ref[...] = jnp.zeros_like(send_ref)
     work_in_teams(count, wait, work)
 
 
-def grow_rows(place, slots, kept, passed, up):
+def grow_rows(place, slots, kept, passed, up, pieces):
     _, pair_rows, _ = kept.shape
     rows = 2 * pair_rows
     rank, columns = up.shape[1:]
     runs = rows // 16
     return pl.pallas_call(
         grow_kernel,
-        out_shape=[jax.ShapeDtypeStruct((2, rows, columns), F32)] * 2,
+        out_shape=[jax.ShapeDtypeStruct((2, rows, columns), F32)]
+        + [jax.ShapeDtypeStruct((rows // pieces, columns), F32)] * (2 * pieces),
         in_specs=[SMEM, SMEM, VMEM, VMEM, HBM],
-        out_specs=[VMEM] * 2,
+        out_specs=[VMEM] * (1 + 2 * pieces),
         scratch_shapes=[
             pltpu.SMEM((4 * runs,), jnp.int32),
             pltpu.VMEM((4 * runs, 16, rank), BF16),
@@ -366,8 +382,8 @@
         ],
         compiler_params=pltpu.CompilerParams(vmem_limit_bytes=60 * MIB),
         cost_estimate=pl.CostEstimate(
-            flops=2 * rows * rank * columns,
-            bytes_accessed=8 * rows * columns + up.size,
+            flops=rows * columns,
+            bytes_accessed=rows * columns,
             transcendentals=0,
         ),
         name="grow_rows",
@@ -739,29 +755,37 @@
         shrunk, hop2 = lax.optimization_barrier((shrunk, hop2))
         shrunk = shrunk + swap(shrunk, "tensor", 2)
         shrunk, sent = lax.optimization_barrier((shrunk, hop2))
-        hop3 = line_hop(*sent, "tensor", 3)
+        hop3 = [line_hop(sent[0][part], sent[1][part], "tensor", 3) for part in parts]
     else:
         shrunk = summed_over(shrunk, "tensor")
     shrunk = shrunk.astype(BF16)
     shrunk = jnp.stack([shrunk, swap(shrunk, "store", 2)])
-    kept, passed = grow_rows(place, mine, shrunk, swap(shrunk, "store", 1), adapter_up_weight)
-    passed = swap(passed, "store", 1)
-    deltas = []
-    for part in parts:
-        delta = swap((kept[1, part] + passed[1, part]).astype(F16), "store", 2).astype(F32)
-        deltas.append((kept[0, part] + passed[0, part]) + delta)
+    other = swap(shrunk, "store", 1)
+    kept, *passed = grow_rows(place, mine, shrunk, other, adapter_up_weight, 1)
+    if line:
+        passed, hop3[0] = lax.optimization_barrier((passed, hop3[0]))
+    passed = [swap(piece, "store", 1) for piece in passed]
+    leaving = [(kept[1, part] + passed[1][part]).astype(F16) for part in parts]
+    arrived = [swap(piece, "store", 2).astype(F32) for piece in leaving]
+    deltas = [(kept[0, p] + passed[0][p]) + far for p, far in zip(parts, arrived)]
 
     weight = query_key_value_weight
-    raw, passed = lax.optimization_barrier((raw, passed))
+    mixed = []
     if line:
-        near = jnp.concatenate(owners[:3])
-        total = base_block((raw,) + hop1 + hop2, own_scale, gains, weight, near, None)
-        total = base_block(hop3, own_scale, gains, weight, owners[3], total)
+        raw, leaving = lax.optimization_barrier((raw, leaving))
+        spots = jnp.concatenate(owners)
+        for h, part in enumerate(parts):
+            if mixed:
+                spots, mixed[-1] = lax.optimization_barrier((spots, mixed[-1]))
+            blocks = (raw,) + hop1 + hop2 + hop3[h]
+            first_rows = (h * count,) * 5 + (0, 0)
+            total = base_block(blocks, own_scale[part], gains, weight, spots, first_rows, 4)
+            mixed.append((total + deltas[h]).astype(BF16))
     else:
         everything = lax.all_gather(raw, "tensor", axis=0, tiled=False)
-        own = base_block((raw,), own_scale, gains, weight, own_index, None)
+        own = base_block((raw,), own_scale, gains, weight, own_index)
         total = base_rows(own_index, everything, own_scale, gains, own, weight, 0)
-    mixed = [(total[part] + delta).astype(BF16) for part, delta in zip(parts, deltas)]
+        mixed.append((total + deltas[0]).astype(BF16))
     mixed = [qkv.reshape(tensor_count, local, -1) for qkv in mixed]
 
     contexts = []

time: 211 us -> 213 us (level)
  waiting for transfers between devices: 82.3 us -> 60.9 us
  local copies, waits for them, and re-layouts: 6.63 us -> 15.7 us
  other arithmetic: 8.76 us -> 13.4 us
  starting transfers between devices: 53.7 us -> 58 us
  Pallas kernels: 58.4 us -> 61.9 us
    all_to_all x2, waiting for transfers between devices: 9.91 us -> 0.01 us  [on_device(): exchanged.append(lax.all_to_all(qkv, 'tensor', 0, 0, tiled=True))]
    ppermute x9 -> x10, waiting for transfers between devices: 26.5 us -> 17.6 us  [line_hop(): down = lax.ppermute(down, axis, [(i, i - 1) for i in range(4 - hop, 0, -1)])]
    unnamed x22 -> x54, local copies, waits for them, and re-layouts: 2.69 us -> 8.12 us
    slice x0 -> x5, local copies, waits for them, and re-layouts: none -> 3.74 us  [the longest x1 2.3 us: on_device(): sent[1][part]]
    all_to_all x2, starting transfers between devices: 6.91 us -> 10.6 us  [on_device(): exchanged.append(lax.all_to_all(qkv, 'tensor', 0, 0, tiled=True))]
    ppermute x17 -> x18, waiting for transfers between devices: 43.9 us -> 40.7 us  [swap(): return lax.ppermute(values, axis, [(i, i ^ distance) for i in range(count)])]
    convert_element_type x2 -> x3, other arithmetic: 4.22 us -> 7.15 us  [the longest x2 4.46 us: on_device(): mixed.append((total + deltas[h]).astype(BF16))]
    pallas_call x2, Pallas kernels: 15.5 us -> 18 us  [base_block(): pl.pallas_call(functools.partial(block_kernel, first_rows), out_shape=jax...]
  transfers between devices with their start and end apart: 37 -> 40, of which waited for: 17 -> 15; matrix products, arithmetic and copies ran while one was open for 4% -> 9% of each run, Pallas kernels for 21% -> 25%
where the time goes in v7:
time: 213 us; the launch traced here: 211 us
  Pallas kernels  61.9 us (29%)
  waiting for transfers between devices  60.9 us (29%)
  starting transfers between devices  58 us (27%)
  local copies, waits for them, and re-layouts  15.7 us (7%)
  other arithmetic  13.4 us (6%)
    ppermute x18, waiting for transfers between devices, swap(): return lax.ppermute(values, axis, [(i, i ^ distance) for i in range(count)])  40.7 us
    ppermute x18, starting transfers between devices, swap(): return lax.ppermute(values, axis, [(i, i ^ distance) for i in range(count)])  19.7 us
    pallas_call x2, Pallas kernels, base_block(): pl.pallas_call(functools.partial(block_kernel, first_rows), out_shape=jax...  18 us
    ppermute x10, waiting for transfers between devices, line_hop(): down = lax.ppermute(down, axis, [(i, i - 1) for i in range(4 - hop, 0, -1)])  17.6 us
    pallas_call x2, Pallas kernels, project(): pl.pallas_call(functools.partial(out_kernel, count, earlier is not None),...  17 us
    ppermute x10, starting transfers between devices, line_hop(): up = lax.ppermute(up, axis, [(i, i + 1) for i in range(hop - 1, 3)])  14.8 us
    pallas_call x2, Pallas kernels, attend(): pl.pallas_call(functools.partial(attend_kernel, unit, first_row), out_sha...  14 us
    ppermute x10, starting transfers between devices, line_hop(): down = lax.ppermute(down, axis, [(i, i - 1) for i in range(4 - hop, 0, -1)])  12.9 us
  transfers between devices with their start and end apart: 40, of which 15 were waited for; matrix products, arithmetic and copies ran while one was open for 9% of the time, Pallas kernels for 25%

profile of v7, /device:TPU:0, one launch (start us, length us, event | category | flops | bytes accessed | tf_op | source)
XLA Modules:
  0.0 210.8 jit_solution(3444446397509020585)
XLA Ops:
  1.7 3.1 %collective-permute-start = (f32[256]{0:T(256)S(1)}, f32[256]{0:T(256)S(1)}, u32[]{:S(2)}, u32[]{:S(2)}) collective-permute-start(f32[256]{0:T(256)S(1)} %reduce_sum.59), channel_id=1, source_target_pairs={{0,1},{1,0},{2,3},{3,2},{4,5},{5,4},{6,7},{7,6},{8,9},{9,8},{10,11... | collective-permute-start | bytes 3080 | tf_op jit(solution)/shard_map/ppermute | solution.py:34
  4.7 2.6 %collective-permute-start.1 = (f32[256]{0:T(256)S(1)}, f32[256]{0:T(256)S(1)}, u32[]{:S(2)}, u32[]{:S(2)}) collective-permute-start(f32[256]{0:T(256)S(1)} %reduce_sum.59), channel_id=1, source_target_pairs={{0,2},{1,3},{2,0},{3,1},{4,6},{5,7},{6,4},{7,5},{8,10},{9,11},{10,... | collective-permute-start | bytes 3080 | tf_op jit(solution)/shard_map/ppermute | solution.py:34
  17.9 15.3 %collective-permute-done.3 = f32[1,272]{1,0:T(1,128)S(1)} collective-permute-done((f32[1,272]{1,0:T(1,128)S(1)}, f32[1,272]{1,0:T(1,128)S(1)}, u32[]{:S(2)}, u32[]{:S(2)}) %collective-permute-start.3) | collective-permute-done | bytes 1120 | tf_op jit(solution)/shard_map/ppermute | solution.py:34
  35.0 4.2 %collective-permute-done.5.refs_2_ = bf16[256,2048]{1,0:T(8,128)(2,1)S(1)} collective-permute-done((bf16[256,2048]{1,0:T(8,128)(2,1)S(1)}, bf16[256,2048]{1,0:T(8,128)(2,1)S(1)}, u32[]{:S(2)}, u32[]{:S(2)}) %collective-permute-start.5) | collective-permute-done | bytes 1048608 | tf_op jit(solution)/shard_map/ppermute | solution.py:47
  44.2 6.6 %shrink_rows.1 = (f32[2,128,128]{2,1,0:T(8,128)}, f32[2,128,128]{2,1,0:T(8,128)}) custom-call(s32[1]{0:T(128)} %bitcast.10.place_ref, s32[64]{0:T(128)} %compare_select_fusion.slots, bf16[256,2048]{1,0:T(8,128)(2,1)} %bitcast.56, bf16[256,2048]{1,0:T(8,128)(2,1)} %collective-permute-done.7.x1, bf16[256,2048]{1,0:T(8,128)(2,1)} %collective-permute-done.8.x2, ...), custom_call_target="tpu_custom_call" | custom-call | flops 524288 | bytes 524288 | tf_op jit(solution)/shard_map/shrink_rows/pallas_call | solution.py:289
  58.0 4.9 %collective-permute-start.12 = (f32[128,128]{1,0:T(8,128)S(1)}, f32[128,128]{1,0:T(8,128)S(1)}, u32[]{:S(2)}, u32[]{:S(2)}) collective-permute-start(f32[128,128]{1,0:T(8,128)S(1)} %fusion.8), channel_id=1, source_target_pairs={{0,1},{1,0},{2,3},{3,2},{4,5},{5,4},{6,7},{7,6},{8,9},{9,8},{10,11... | collective-permute-start | bytes 196616 | tf_op jit(solution)/shard_map/ppermute | solution.py:34
  63.0 8.6 %collective-permute-done.12 = f32[128,128]{1,0:T(8,128)S(1)} collective-permute-done((f32[128,128]{1,0:T(8,128)S(1)}, f32[128,128]{1,0:T(8,128)S(1)}, u32[]{:S(2)}, u32[]{:S(2)}) %collective-permute-start.12) | collective-permute-done | bytes 65568 | tf_op jit(solution)/shard_map/ppermute | solution.py:34
  71.6 5.6 %collective-permute-done.15 = f32[128,128]{1,0:T(8,128)S(1)} collective-permute-done((f32[128,128]{1,0:T(8,128)S(1)}, f32[128,128]{1,0:T(8,128)S(1)}, u32[]{:S(2)}, u32[]{:S(2)}) %collective-permute-start.15) | collective-permute-done | bytes 65568 | tf_op jit(solution)/shard_map/ppermute | solution.py:34
  83.3 3.4 %collective-permute-done.16 = bf16[128,128]{1,0:T(8,128)(2,1)S(1)} collective-permute-done((bf16[128,128]{1,0:T(8,128)(2,1)S(1)}, bf16[128,128]{1,0:T(8,128)(2,1)S(1)}, u32[]{:S(2)}, u32[]{:S(2)}) %collective-permute-start.16) | collective-permute-done | bytes 32800 | tf_op jit(solution)/shard_map/ppermute | solution.py:34
  88.7 6.4 %grow_rows.1 = (f32[2,256,1280]{2,1,0:T(8,128)}, f32[256,1280]{1,0:T(8,128)}, f32[256,1280]{1,0:T(8,128)}) custom-call(s32[1]{0:T(128)} %bitcast.10.place_ref, s32[64]{0:T(128)} %compare_select_fusion.slots, bf16[2,128,128]{2,1,0:T(8,128)(2,1)} %copy-done.17, bf16[2,128,128]{2,1,0:T(8,128)(2,1)} %copy-done.18, bf16[32,64,1280]{2,1,0:T(8,128)(2,1)} %up_ref.1), custom_call_target="tpu_custom_call" | custom-call | flops 327680 | bytes 327680 | tf_op jit(solution)/shard_map/grow_rows/pallas_call | solution.py:371
  99.3 2.7 %fusion.6 = (f16[128,1280]{1,0:T(8,128)(2,1)}, f16[128,1280]{1,0:T(8,128)(2,1)}) fusion(f32[256,1280]{1,0:T(8,128)} %collective-permute-done.20, f32[2,256,1280]{2,1,0:T(8,128)} %get-tuple-element.41), kind=kLoop, calls=%fused_computation.10 | loop fusion | flops 655360 | bytes 3276800 | tf_op jit(solution)/shard_map/convert_element_type | solution.py:768
  109.4 9.0 %base_block.2 = f32[128,1280]{1,0:T(8,128)S(1)} custom-call(s32[7]{0:T(128)S(1)} %concatenate.31.owners, bf16[256,2048]{1,0:T(8,128)(2,1)S(1)} %bitcast.57, bf16[256,2048]{1,0:T(8,128)(2,1)S(1)} %collective-permute-done.4.refs_1_, bf16[256,2048]{1,0:T(8,128)(2,1)S(1)} %copy-done.3, bf16[256,2048]{1,0:T(8,128)(2,1)S(1)} %collective-permute-done.13.refs_3_, ...), custom_call_target="tpu_custom_call" | custom-call | flops 2684354560 | bytes 23724032 | tf_op jit(solution)/shard_map/base_block/pallas_call | solution.py:112
  120.7 5.5 %all-to-all-start = ((bf16[4,32,1280]{2,1,0:T(8,128)(2,1)}), bf16[4,32,1280]{2,1,0:T(8,128)(2,1)S(1)}, u32[]{:S(2)}, u32[]{:S(2)}) async-start(bf16[4,32,1280]{2,1,0:T(8,128)(2,1)} %bitcast.64), calls=%async_computation | async-start | bytes 655360 | tf_op jit(solution)/shard_map/all_to_all | solution.py:796
  128.8 9.1 %base_block.3 = f32[128,1280]{1,0:T(8,128)S(1)} custom-call(s32[7]{0:T(128)S(1)} %copy-done.11, bf16[256,2048]{1,0:T(8,128)(2,1)S(1)} %bitcast.58, bf16[256,2048]{1,0:T(8,128)(2,1)S(1)} %collective-permute-done.4.refs_1_, bf16[256,2048]{1,0:T(8,128)(2,1)S(1)} %copy-done.4, bf16[256,2048]{1,0:T(8,128)(2,1)S(1)} %collective-permute-done.13.refs_3_, ...), custom_call_target="tpu_custom_call" | custom-call | flops 2684354560 | bytes 23724032 | tf_op jit(solution)/shard_map/base_block/pallas_call | solution.py:112
  140.2 5.1 %all-to-all-start.1 = ((bf16[4,32,1280]{2,1,0:T(8,128)(2,1)}), bf16[4,32,1280]{2,1,0:T(8,128)(2,1)S(1)}, u32[]{:S(2)}, u32[]{:S(2)}) async-start(bf16[4,32,1280]{2,1,0:T(8,128)(2,1)} %bitcast.32), calls=%async_computation.1 | async-start | bytes 655360 | tf_op jit(solution)/shard_map/all_to_all | solution.py:796
  145.9 7.3 %attend.2.refs_0_ = bf16[32,4096]{1,0:T(8,128)(2,1)S(1)} custom-call(s32[16]{0:T(128)S(1)} %copy-done.15, s32[16]{0:T(128)S(1)} %select_reduce_fusion.2.order, bf16[4,32,1280]{2,1,0:T(8,128)(2,1)S(1)} %all-to-all-done.qkv_ref, f32[32,128]{1,0:T(8,128)S(1)} %get-tuple-element.86.cos_ref, f32[32,128]{1,0:T(8,128)S(1)} %get-tuple-element.87.sin_ref, ...), custom_call_target="tpu_custom_call" | custom-call | flops 268435456 | bytes 16777216 | tf_op jit(solution)/shard_map/attend/pallas_call | solution.py:553
  153.2 3.3 %collective-permute-start.26 = (bf16[32,4096]{1,0:T(8,128)(2,1)S(1)}, bf16[32,4096]{1,0:T(8,128)(2,1)S(1)}, u32[]{:S(2)}, u32[]{:S(2)}) collective-permute-start(bf16[32,4096]{1,0:T(8,128)(2,1)S(1)} %attend.2.refs_0_), channel_id=1, source_target_pairs={{0,1},{1,2},{2,3},{4,5},{5,6},{6,7},{8,9},{9,10},{10,11},{12,13},{... | collective-permute-start | bytes 786440 | tf_op jit(solution)/shard_map/ppermute | solution.py:46
  157.9 6.7 %attend.3.refs_3_ = bf16[32,4096]{1,0:T(8,128)(2,1)S(1)} custom-call(s32[16]{0:T(128)S(1)} %copy-done.13, s32[16]{0:T(128)S(1)} %select_reduce_fusion.1.order, bf16[4,32,1280]{2,1,0:T(8,128)(2,1)S(1)} %all-to-all-done.1.qkv_ref, f32[32,128]{1,0:T(8,128)S(1)} %get-tuple-element.88.cos_ref, f32[32,128]{1,0:T(8,128)S(1)} %copy-done.9, ...), custom_call_target="tpu_custom_call" | custom-call | flops 268435456 | bytes 16777216 | tf_op jit(solution)/shard_map/attend/pallas_call | solution.py:553
  164.6 4.6 %collective-permute-start.32 = (bf16[32,4096]{1,0:T(8,128)(2,1)S(1)}, bf16[32,4096]{1,0:T(8,128)(2,1)S(1)}, u32[]{:S(2)}, u32[]{:S(2)}) collective-permute-start(bf16[32,4096]{1,0:T(8,128)(2,1)S(1)} %attend.3.refs_3_), channel_id=1, source_target_pairs={{0,1},{1,2},{2,3},{4,5},{5,6},{6,7},{8,9},{9,10},{10,11},{12,13},{... | collective-permute-start | bytes 786440 | tf_op jit(solution)/shard_map/ppermute | solution.py:46
  174.0 4.0 %collective-permute-done.34.refs_5_ = bf16[32,4096]{1,0:T(8,128)(2,1)S(1)} collective-permute-done((bf16[32,4096]{1,0:T(8,128)(2,1)S(1)}, bf16[32,4096]{1,0:T(8,128)(2,1)S(1)}, u32[]{:S(2)}, u32[]{:S(2)}) %collective-permute-start.34) | collective-permute-done | bytes 262176 | tf_op jit(solution)/shard_map/ppermute | solution.py:47
  180.1 3.8 %collective-permute-done.29.refs_1_ = bf16[32,4096]{1,0:T(8,128)(2,1)S(1)} collective-permute-done((bf16[32,4096]{1,0:T(8,128)(2,1)S(1)}, bf16[32,4096]{1,0:T(8,128)(2,1)S(1)}, u32[]{:S(2)}, u32[]{:S(2)}) %collective-permute-start.29) | collective-permute-done | bytes 262176 | tf_op jit(solution)/shard_map/ppermute | solution.py:47
  185.9 5.7 %collective-permute-done.35.refs_5_ = bf16[32,4096]{1,0:T(8,128)(2,1)S(1)} collective-permute-done((bf16[32,4096]{1,0:T(8,128)(2,1)S(1)}, bf16[32,4096]{1,0:T(8,128)(2,1)S(1)}, u32[]{:S(2)}, u32[]{:S(2)}) %collective-permute-start.35) | collective-permute-done | bytes 262176 | tf_op jit(solution)/shard_map/ppermute | solution.py:47
  192.9 8.2 %project.2.refs_9_ = bf16[2,4,2,16,2048]{4,3,2,1,0:T(8,128)(2,1)} custom-call(s32[3]{0:T(128)S(1)} %pad_add_fusion.1.owners, bf16[32,4096]{1,0:T(8,128)(2,1)S(1)} %attend.2.refs_0_, bf16[32,4096]{1,0:T(8,128)(2,1)S(1)} %collective-permute-done.26.refs_1_, bf16[32,4096]{1,0:T(8,128)(2,1)S(1)} %collective-permute-done.28.refs_2_, ...), custom_call_target="tpu_custom_call" | custom-call | flops 3221225472 | bytes 19136512 | tf_op jit(solution)/shard_map/project/pallas_call | solution.py:638
  201.8 8.8 %project.3 = bf16[2,4,2,16,2048]{4,3,2,1,0:T(8,128)(2,1)} custom-call(s32[4]{0:T(128)S(1)} %pad_add_fusion.owners, bf16[32,4096]{1,0:T(8,128)(2,1)S(1)} %collective-permute-done.27.refs_0_, bf16[32,4096]{1,0:T(8,128)(2,1)S(1)} %collective-permute-done.29.refs_1_, bf16[32,4096]{1,0:T(8,128)(2,1)S(1)} %collective-permute-done.30.refs_2_, ...), custom_call_target="tpu_custom_call" | custom-call | flops 2147483648 | bytes 18350080 | tf_op jit(solution)/shard_map/project/pallas_call | solution.py:638
  (173 shorter events, 65.7 us)
Async XLA Ops:
  8.6 24.5 %collective-permute-start.8 = (bf16[256,2048]{1,0:T(8,128)(2,1)S(1)}, bf16[256,2048]{1,0:T(8,128)(2,1)}, u32[]{:S(2)}, u32[]{:S(2)}) collective-permute-start(bf16[256,2048]{1,0:T(8,128)(2,1)S(1)} %bitcast.52), channel_id=1, source_target_pairs={{0,8},{4,12},{8,0},{12,4},{1,9},{5,13},{9,1},{13,5},{2,10},{6,14},... | collective-permute-start | bytes 3145736 | tf_op jit(solution)/shard_map/ppermute | solution.py:34
  12.7 22.3 %collective-permute-start.4 = (bf16[256,2048]{1,0:T(8,128)(2,1)S(1)}, bf16[256,2048]{1,0:T(8,128)(2,1)S(1)}, u32[]{:S(2)}, u32[]{:S(2)}) collective-permute-start(bf16[256,2048]{1,0:T(8,128)(2,1)S(1)} %bitcast.53), channel_id=1, source_target_pairs={{0,1},{1,2},{2,3},{4,5},{5,6},{6,7},{8,9},{9,10},{10,11},{12,13},{... | collective-permute-start | bytes 3145736 | tf_op jit(solution)/shard_map/ppermute | solution.py:46
  14.1 25.1 %collective-permute-start.5 = (bf16[256,2048]{1,0:T(8,128)(2,1)S(1)}, bf16[256,2048]{1,0:T(8,128)(2,1)S(1)}, u32[]{:S(2)}, u32[]{:S(2)}) collective-permute-start(bf16[256,2048]{1,0:T(8,128)(2,1)S(1)} %bitcast.54), channel_id=1, source_target_pairs={{3,2},{2,1},{1,0},{7,6},{6,5},{5,4},{11,10},{10,9},{9,8},{15,14},{... | collective-permute-start | bytes 3145736 | tf_op jit(solution)/shard_map/ppermute | solution.py:47
  15.7 17.5 %collective-permute-start.3 = (f32[1,272]{1,0:T(1,128)S(1)}, f32[1,272]{1,0:T(1,128)S(1)}, u32[]{:S(2)}, u32[]{:S(2)}) collective-permute-start(f32[1,272]{1,0:T(1,128)S(1)} %reshape.107), channel_id=1, source_target_pairs={{0,8},{4,12},{8,0},{12,4},{1,9},{5,13},{9,1},{13,5},{2,10},{6,14},... | collective-permute-start | bytes 3272 | tf_op jit(solution)/shard_map/ppermute | solution.py:34
  17.3 26.9 %collective-permute-start.7 = (bf16[256,2048]{1,0:T(8,128)(2,1)S(1)}, bf16[256,2048]{1,0:T(8,128)(2,1)}, u32[]{:S(2)}, u32[]{:S(2)}) collective-permute-start(bf16[256,2048]{1,0:T(8,128)(2,1)S(1)} %bitcast.55), channel_id=1, source_target_pairs={{0,4},{4,0},{8,12},{12,8},{1,5},{5,1},{9,13},{13,9},{2,6},{6,2},{1... | collective-permute-start | bytes 3145736 | tf_op jit(solution)/shard_map/ppermute | solution.py:34
  40.2 31.4 %collective-permute-start.13 = (bf16[256,2048]{1,0:T(8,128)(2,1)S(1)}, bf16[256,2048]{1,0:T(8,128)(2,1)S(1)}, u32[]{:S(2)}, u32[]{:S(2)}) collective-permute-start(bf16[256,2048]{1,0:T(8,128)(2,1)S(1)} %collective-permute-done.4.refs_1_), channel_id=1, source_target_pairs={{1,2},{2,3},{5,6},{6,7},{9,10},{10,11},{13,14},{14,15},{17,18},{18... | collective-permute-start | bytes 3145736 | tf_op jit(solution)/shard_map/ppermute | solution.py:46
  40.9 30.7 %collective-permute-start.14 = (bf16[256,2048]{1,0:T(8,128)(2,1)}, bf16[256,2048]{1,0:T(8,128)(2,1)}, u32[]{:S(2)}, u32[]{:S(2)}) collective-permute-start(bf16[256,2048]{1,0:T(8,128)(2,1)} %copy-done.2), channel_id=1, source_target_pairs={{2,1},{1,0},{6,5},{5,4},{10,9},{9,8},{14,13},{13,12},{18,17},{17,1... | collective-permute-start | bytes 3145736 | tf_op jit(solution)/shard_map/ppermute | solution.py:47
  58.0 13.5 %collective-permute-start.12 = (f32[128,128]{1,0:T(8,128)S(1)}, f32[128,128]{1,0:T(8,128)S(1)}, u32[]{:S(2)}, u32[]{:S(2)}) collective-permute-start(f32[128,128]{1,0:T(8,128)S(1)} %fusion.8), channel_id=1, source_target_pairs={{0,1},{1,0},{2,3},{3,2},{4,5},{5,4},{6,7},{7,6},{8,9},{9,8},{10,11... | collective-permute-start | bytes 196616 | tf_op jit(solution)/shard_map/ppermute | solution.py:34
  78.4 16.7 %collective-permute-start.18 = (bf16[128,2048]{1,0:T(8,128)(2,1)}, bf16[128,2048]{1,0:T(8,128)(2,1)S(1)}, u32[]{:S(2)}, u32[]{:S(2)}) collective-permute-start(bf16[128,2048]{1,0:T(8,128)(2,1)} %get-tuple-element.60), channel_id=1, source_target_pairs={{2,3},{6,7},{10,11},{14,15},{18,19},{22,23},{26,27},{30,31}} | collective-permute-start | bytes 1572872 | tf_op jit(solution)/shard_map/ppermute | solution.py:46
  81.4 14.5 %collective-permute-start.19 = (bf16[128,2048]{1,0:T(8,128)(2,1)}, bf16[128,2048]{1,0:T(8,128)(2,1)}, u32[]{:S(2)}, u32[]{:S(2)}) collective-permute-start(bf16[128,2048]{1,0:T(8,128)(2,1)} %get-tuple-element.58), channel_id=1, source_target_pairs={{1,0},{5,4},{9,8},{13,12},{17,16},{21,20},{25,24},{29,28}} | collective-permute-start | bytes 1572872 | tf_op jit(solution)/shard_map/ppermute | solution.py:47
  97.0 21.4 %collective-permute-start.21 = (f32[256,1280]{1,0:T(8,128)}, f32[256,1280]{1,0:T(8,128)}, u32[]{:S(2)}, u32[]{:S(2)}) collective-permute-start(f32[256,1280]{1,0:T(8,128)} %get-tuple-element.50), channel_id=1, source_target_pairs={{0,4},{4,0},{8,12},{12,8},{1,5},{5,1},{9,13},{13,9},{2,6},{6,2},{1... | collective-permute-start | bytes 3932168 | tf_op jit(solution)/shard_map/ppermute | solution.py:34
  102.0 16.4 %collective-permute-start.22 = (f16[128,1280]{1,0:T(8,128)(2,1)}, f16[128,1280]{1,0:T(8,128)(2,1)}, u32[]{:S(2)}, u32[]{:S(2)}) collective-permute-start(f16[128,1280]{1,0:T(8,128)(2,1)} %get-tuple-element.56), channel_id=1, source_target_pairs={{0,8},{4,12},{8,0},{12,4},{1,9},{5,13},{9,1},{13,5},{2,10},{6,14},... | collective-permute-start | bytes 983048 | tf_op jit(solution)/shard_map/ppermute | solution.py:34
  103.1 23.0 %collective-permute-start.23 = (bf16[128,2048]{1,0:T(8,128)(2,1)}, bf16[128,2048]{1,0:T(8,128)(2,1)}, u32[]{:S(2)}, u32[]{:S(2)}) collective-permute-start(bf16[128,2048]{1,0:T(8,128)(2,1)} %get-tuple-element.59), channel_id=1, source_target_pairs={{2,3},{6,7},{10,11},{14,15},{18,19},{22,23},{26,27},{30,31}} | collective-permute-start | bytes 1572872 | tf_op jit(solution)/shard_map/ppermute | solution.py:46
  104.6 21.6 %collective-permute-start.24 = (bf16[128,2048]{1,0:T(8,128)(2,1)}, bf16[128,2048]{1,0:T(8,128)(2,1)}, u32[]{:S(2)}, u32[]{:S(2)}) collective-permute-start(bf16[128,2048]{1,0:T(8,128)(2,1)} %get-tuple-element.57), channel_id=1, source_target_pairs={{1,0},{5,4},{9,8},{13,12},{17,16},{21,20},{25,24},{29,28}} | collective-permute-start | bytes 1572872 | tf_op jit(solution)/shard_map/ppermute | solution.py:47
  105.9 32.1 %collective-permute-start.25 = (f16[128,1280]{1,0:T(8,128)(2,1)}, f16[128,1280]{1,0:T(8,128)(2,1)}, u32[]{:S(2)}, u32[]{:S(2)}) collective-permute-start(f16[128,1280]{1,0:T(8,128)(2,1)} %get-tuple-element.55), channel_id=1, source_target_pairs={{0,8},{4,12},{8,0},{12,4},{1,9},{5,13},{9,1},{13,5},{2,10},{6,14},... | collective-permute-start | bytes 983048 | tf_op jit(solution)/shard_map/ppermute | solution.py:34
  120.7 19.5 %all-to-all-start = ((bf16[4,32,1280]{2,1,0:T(8,128)(2,1)}), bf16[4,32,1280]{2,1,0:T(8,128)(2,1)S(1)}, u32[]{:S(2)}, u32[]{:S(2)}) async-start(bf16[4,32,1280]{2,1,0:T(8,128)(2,1)} %bitcast.64), calls=%async_computation | async-start | bytes 655360 | tf_op jit(solution)/shard_map/all_to_all | solution.py:796
  140.2 17.7 %all-to-all-start.1 = ((bf16[4,32,1280]{2,1,0:T(8,128)(2,1)}), bf16[4,32,1280]{2,1,0:T(8,128)(2,1)S(1)}, u32[]{:S(2)}, u32[]{:S(2)}) async-start(bf16[4,32,1280]{2,1,0:T(8,128)(2,1)} %bitcast.32), calls=%async_computation.1 | async-start | bytes 655360 | tf_op jit(solution)/shard_map/all_to_all | solution.py:796
  153.2 17.3 %collective-permute-start.26 = (bf16[32,4096]{1,0:T(8,128)(2,1)S(1)}, bf16[32,4096]{1,0:T(8,128)(2,1)S(1)}, u32[]{:S(2)}, u32[]{:S(2)}) collective-permute-start(bf16[32,4096]{1,0:T(8,128)(2,1)S(1)} %attend.2.refs_0_), channel_id=1, source_target_pairs={{0,1},{1,2},{2,3},{4,5},{5,6},{6,7},{8,9},{9,10},{10,11},{12,13},{... | collective-permute-start | bytes 786440 | tf_op jit(solution)/shard_map/ppermute | solution.py:46
  156.6 14.6 %collective-permute-start.28 = (bf16[32,4096]{1,0:T(8,128)(2,1)S(1)}, bf16[32,4096]{1,0:T(8,128)(2,1)S(1)}, u32[]{:S(2)}, u32[]{:S(2)}) collective-permute-start(bf16[32,4096]{1,0:T(8,128)(2,1)S(1)} %attend.2.refs_0_), channel_id=1, source_target_pairs={{3,2},{2,1},{1,0},{7,6},{6,5},{5,4},{11,10},{10,9},{9,8},{15,14},{... | collective-permute-start | bytes 786440 | tf_op jit(solution)/shard_map/ppermute | solution.py:47
  171.2 12.7 %collective-permute-start.29 = (bf16[32,4096]{1,0:T(8,128)(2,1)S(1)}, bf16[32,4096]{1,0:T(8,128)(2,1)S(1)}, u32[]{:S(2)}, u32[]{:S(2)}) collective-permute-start(bf16[32,4096]{1,0:T(8,128)(2,1)S(1)} %collective-permute-done.28.refs_2_), channel_id=1, source_target_pairs={{2,1},{1,0},{6,5},{5,4},{10,9},{9,8},{14,13},{13,12},{18,17},{17,1... | collective-permute-start | bytes 786440 | tf_op jit(solution)/shard_map/ppermute | solution.py:47
  178.0 13.6 %collective-permute-start.35 = (bf16[32,4096]{1,0:T(8,128)(2,1)S(1)}, bf16[32,4096]{1,0:T(8,128)(2,1)S(1)}, u32[]{:S(2)}, u32[]{:S(2)}) collective-permute-start(bf16[32,4096]{1,0:T(8,128)(2,1)S(1)} %collective-permute-done.34.refs_5_), channel_id=1, source_target_pairs={{2,1},{1,0},{6,5},{5,4},{10,9},{9,8},{14,13},{13,12},{18,17},{17,1... | collective-permute-start | bytes 786440 | tf_op jit(solution)/shard_map/ppermute | solution.py:47
  179.4 21.6 %collective-permute-start.30 = (bf16[32,4096]{1,0:T(8,128)(2,1)S(1)}, bf16[32,4096]{1,0:T(8,128)(2,1)S(1)}, u32[]{:S(2)}, u32[]{:S(2)}) collective-permute-start(bf16[32,4096]{1,0:T(8,128)(2,1)S(1)} %collective-permute-done.27.refs_0_), channel_id=1, source_target_pairs={{2,3},{6,7},{10,11},{14,15},{18,19},{22,23},{26,27},{30,31}} | collective-permute-start | bytes 786440 | tf_op jit(solution)/shard_map/ppermute | solution.py:46
  183.9 17.2 %collective-permute-start.31 = (bf16[32,4096]{1,0:T(8,128)(2,1)S(1)}, bf16[32,4096]{1,0:T(8,128)(2,1)S(1)}, u32[]{:S(2)}, u32[]{:S(2)}) collective-permute-start(bf16[32,4096]{1,0:T(8,128)(2,1)S(1)} %collective-permute-done.29.refs_1_), channel_id=1, source_target_pairs={{1,0},{5,4},{9,8},{13,12},{17,16},{21,20},{25,24},{29,28}} | collective-permute-start | bytes 786440 | tf_op jit(solution)/shard_map/ppermute | solution.py:47
  185.2 15.9 %collective-permute-start.36 = (bf16[32,4096]{1,0:T(8,128)(2,1)S(1)}, bf16[32,4096]{1,0:T(8,128)(2,1)S(1)}, u32[]{:S(2)}, u32[]{:S(2)}) collective-permute-start(bf16[32,4096]{1,0:T(8,128)(2,1)S(1)} %collective-permute-done.33.refs_4_), channel_id=1, source_target_pairs={{2,3},{6,7},{10,11},{14,15},{18,19},{22,23},{26,27},{30,31}} | collective-permute-start | bytes 786440 | tf_op jit(solution)/shard_map/ppermute | solution.py:46
  (43 other events, 347.9 us)

commit v8 on v7

--- a/solution.py
+++ b/solution.py
@@ -61,12 +61,13 @@
     return jnp.stack([jnp.where(below >= 0, below, -1), jnp.where(above < 4, above, -1)])
 
 
-def block_kernel(first_rows, owners, *refs):
-    count = len(refs) - 6
+def block_kernel(first_rows, has_total, owners, *refs):
+    count = len(first_rows)
     x_refs = refs[:count]
-    scale_ref, gain_ref, w_ref, out_ref, held, sems = refs[count:]
+    scale_ref, gain_ref, w_ref = refs[count : count + 3]
+    out_ref, held_x, held, x_sems, sems = refs[-5:]
     rows = scale_ref.shape[0]
-    slots, tiles, depth, _ = held.shape
+    _, tiles, depth, _ = held.shape
 
     def slot(j):
         used = jnp.int32(0)
@@ -80,52 +81,61 @@
             w_ref.at[pl.ds(first, depth), :], held.at[slot(j), k], sems.at[slot(j), k]
         )
 
+    def x_copy(j):
+        part = x_refs[j].at[first_rows[j] : first_rows[j] + rows, :]
+        return pltpu.make_async_copy(part, held_x.at[slot(j)], x_sems.at[slot(j)])
+
     for j in range(count):
 
         @pl.when(owners[j] >= 0)
         def _():
+            x_copy(j).start()
             for k in range(tiles):
                 copy(j, k).start()
 
-    out_ref[...] = jnp.zeros_like(out_ref)
-    for j, x_ref in enumerate(x_refs):
+    out_ref[...] = refs[count + 3][...] if has_total else jnp.zeros_like(out_ref)
+    for j in range(count):
 
         @pl.when(owners[j] >= 0)
         def _():
             scale = scale_ref[...]
+            x_copy(j).wait()
             for k in range(tiles):
                 span = slice(k * depth, (k + 1) * depth)
                 first = pl.multiple_of((owners[j] * tiles + k) * depth, depth)
                 gain = gain_ref[:, pl.ds(first, depth)]
-                part = x_ref[first_rows[j] : first_rows[j] + rows, span].astype(F32)
+                part = held_x[slot(j), :, span].astype(F32)
                 normed = (part * scale * gain).astype(BF16)
                 copy(j, k).wait()
                 out_ref[...] += jnp.dot(normed, held[slot(j), k], preferred_element_type=F32)
 
 
-def base_block(blocks, scale, gain, weight, owners, first_rows=(0,), present=1):
+def base_block(blocks, scale, gain, weight, owners, first_rows, present, total=None):
     depth = blocks[0].shape[1]
     rows = scale.shape[0]
     columns = weight.shape[1]
     tile = min(512, depth)
     count = len(blocks)
+    more = [] if total is None else [total]
     return pl.pallas_call(
-        functools.partial(block_kernel, first_rows),
+        functools.partial(block_kernel, first_rows, total is not None),
         out_shape=jax.ShapeDtypeStruct((rows, columns), F32),
-        in_specs=[SMEM] + [VMEM] * (count + 2) + [HBM],
+        in_specs=[SMEM] + [HBM] * count + [VMEM] * 2 + [HBM] + [VMEM] * len(more),
         out_specs=VMEM,
         scratch_shapes=[
+            pltpu.VMEM((present, rows, depth), BF16),
             pltpu.VMEM((present, depth // tile, tile, columns), BF16),
+            pltpu.SemaphoreType.DMA((present,)),
             pltpu.SemaphoreType.DMA((present, depth // tile)),
         ],
-        compiler_params=pltpu.CompilerParams(vmem_limit_bytes=48 * MIB),
+        compiler_params=pltpu.CompilerParams(vmem_limit_bytes=46 * MIB),
         cost_estimate=pl.CostEstimate(
-            flops=2 * present * rows * depth * columns,
-            bytes_accessed=2 * present * depth * (rows + columns) + 4 * rows * columns,
+            flops=rows * columns,
+            bytes_accessed=rows * columns,
             transcendentals=0,
         ),
         name="base_block",
-    )(owners, *blocks, scale, gain, weight)
+    )(owners, *blocks, scale, gain, weight, *more)
 
 
 def base_kernel(first_row, place_ref, x_ref, scale_ref, gain_ref, own_ref, w_ref, out_ref, held, sems):
@@ -751,11 +761,15 @@
     kept = kept + swap(passed, "store", 1)
     shrunk = kept[0] + swap(kept[1], "store", 2)
     if line:
+        shrunk, early = lax.optimization_barrier((shrunk, (raw,) + hop1))
+        near = jnp.concatenate(owners[:2])
+        total = base_block(early, own_scale, gains, query_key_value_weight, near, (0,) * 3, 3)
         shrunk = shrunk + swap(shrunk, "tensor", 1)
-        shrunk, hop2 = lax.optimization_barrier((shrunk, hop2))
+        shrunk, total, hop2 = lax.optimization_barrier((shrunk, total, hop2))
+        sent = [(hop2[0][part], hop2[1][part]) for part in parts]
         shrunk = shrunk + swap(shrunk, "tensor", 2)
-        shrunk, sent = lax.optimization_barrier((shrunk, hop2))
-        hop3 = [line_hop(sent[0][part], sent[1][part], "tensor", 3) for part in parts]
+        shrunk, sent = lax.optimization_barrier((shrunk, sent))
+        hop3 = [line_hop(up, down, "tensor", 3) for up, down in sent]
     else:
         shrunk = summed_over(shrunk, "tensor")
     shrunk = shrunk.astype(BF16)
@@ -772,18 +786,20 @@
     weight = query_key_value_weight
     mixed = []
     if line:
-        raw, leaving = lax.optimization_barrier((raw, leaving))
-        spots = jnp.concatenate(owners)
+        total, leaving = lax.optimization_barrier((total, leaving))
+        far = jnp.concatenate(owners[2:])
         for h, part in enumerate(parts):
             if mixed:
-                spots, mixed[-1] = lax.optimization_barrier((spots, mixed[-1]))
-            blocks = (raw,) + hop1 + hop2 + hop3[h]
-            first_rows = (h * count,) * 5 + (0, 0)
-            total = base_block(blocks, own_scale[part], gains, weight, spots, first_rows, 4)
-            mixed.append((total + deltas[h]).astype(BF16))
+                far, mixed[-1] = lax.optimization_barrier((far, mixed[-1]))
+            blocks = hop2 + hop3[h]
+            first_rows = (h * count, h * count, 0, 0)
+            sums = base_block(
+                blocks, own_scale[part], gains, weight, far, first_rows, 2, total[part]
+            )
+            mixed.append((sums + deltas[h]).astype(BF16))
     else:
         everything = lax.all_gather(raw, "tensor", axis=0, tiled=False)
-        own = base_block((raw,), own_scale, gains, weight, own_index)
+        own = base_block((raw,), own_scale, gains, weight, own_index, (0,), 1)
         total = base_rows(own_index, everything, own_scale, gains, own, weight, 0)
         mixed.append((total + deltas[0]).astype(BF16))
     mixed = [qkv.reshape(tensor_count, local, -1) for qkv in mixed]

time: 213 us -> 205 us (0.962)
  waiting for transfers between devices: 60.9 us -> 50.8 us
  starting transfers between devices: 58 us -> 64.8 us
  local copies, waits for them, and re-layouts: 15.7 us -> 13.3 us
    ppermute x18, waiting for transfers between devices: 40.7 us -> 26.7 us  [swap(): return lax.ppermute(values, axis, [(i, i ^ distance) for i in range(count)])]
    ppermute x18, starting transfers between devices: 19.7 us -> 23.7 us  [swap(): return lax.ppermute(values, axis, [(i, i ^ distance) for i in range(count)])]
    ppermute x10, waiting for transfers between devices: 17.6 us -> 20.9 us  [line_hop(): down = lax.ppermute(down, axis, [(i, i - 1) for i in range(4 - hop, 0, -1)])]
    ppermute x10, starting transfers between devices: 14.8 us -> 17.8 us  [line_hop(): up = lax.ppermute(up, axis, [(i, i + 1) for i in range(hop - 1, 3)])]
    unnamed x54 -> x38, local copies, waits for them, and re-layouts: 8.12 us -> 5.55 us
    pallas_call x2 -> x3, Pallas kernels: 18 us -> 17.5 us  [base_block(): pl.pallas_call(functools.partial(block_kernel, first_rows, total is not N...]
  transfers between devices with their start and end apart: 40 -> 40, of which waited for: 15 -> 16; matrix products, arithmetic and copies ran while one was open for 9% -> 10% of each run, Pallas kernels for 25% -> 25%
where the time goes in v8:
time: 205 us
  starting transfers between devices  64.8 us (32%)
  Pallas kernels  60.7 us (30%)
  waiting for transfers between devices  50.8 us (25%)
  other arithmetic  14.1 us (7%)
  local copies, waits for them, and re-layouts  13.3 us (6%)
    ppermute x18, waiting for transfers between devices, swap(): return lax.ppermute(values, axis, [(i, i ^ distance) for i in range(count)])  26.7 us
    ppermute x18, starting transfers between devices, swap(): return lax.ppermute(values, axis, [(i, i ^ distance) for i in range(count)])  23.7 us
    ppermute x10, waiting for transfers between devices, line_hop(): down = lax.ppermute(down, axis, [(i, i - 1) for i in range(4 - hop, 0, -1)])  20.9 us
    ppermute x10, starting transfers between devices, line_hop(): up = lax.ppermute(up, axis, [(i, i + 1) for i in range(hop - 1, 3)])  17.8 us
    pallas_call x3, Pallas kernels, base_block(): pl.pallas_call(functools.partial(block_kernel, first_rows, total is not N...  17.5 us
    pallas_call x2, Pallas kernels, project(): pl.pallas_call(functools.partial(out_kernel, count, earlier is not None),...  17 us
    ppermute x10, starting transfers between devices, line_hop(): down = lax.ppermute(down, axis, [(i, i - 1) for i in range(4 - hop, 0, -1)])  13.1 us
    pallas_call x2, Pallas kernels, attend(): pl.pallas_call(functools.partial(attend_kernel, unit, first_row), out_sha...  12.8 us
  transfers between devices with their start and end apart: 40, of which 16 were waited for; matrix products, arithmetic and copies ran while one was open for 10% of the time, Pallas kernels for 25%

profile of v8, /device:TPU:0, one launch (start us, length us, event | category | flops | bytes accessed | tf_op | source)
XLA Modules:
  0.0 204.6 jit_solution(18051078532996727341)
XLA Ops:
  1.6 3.1 %collective-permute-start = (f32[256]{0:T(256)S(1)}, f32[256]{0:T(256)S(1)}, u32[]{:S(2)}, u32[]{:S(2)}) collective-permute-start(f32[256]{0:T(256)S(1)} %reduce_sum.59), channel_id=1, source_target_pairs={{0,1},{1,0},{2,3},{3,2},{4,5},{5,4},{6,7},{7,6},{8,9},{9,8},{10,11... | collective-permute-start | bytes 3080 | tf_op jit(solution)/shard_map/ppermute | solution.py:34
  4.7 2.6 %collective-permute-start.1 = (f32[256]{0:T(256)S(1)}, f32[256]{0:T(256)S(1)}, u32[]{:S(2)}, u32[]{:S(2)}) collective-permute-start(f32[256]{0:T(256)S(1)} %reduce_sum.59), channel_id=1, source_target_pairs={{0,2},{1,3},{2,0},{3,1},{4,6},{5,7},{6,4},{7,5},{8,10},{9,11},{10,... | collective-permute-start | bytes 3080 | tf_op jit(solution)/shard_map/ppermute | solution.py:34
  19.5 13.7 %collective-permute-done.3 = f32[1,272]{1,0:T(1,128)S(1)} collective-permute-done((f32[1,272]{1,0:T(1,128)S(1)}, f32[1,272]{1,0:T(1,128)S(1)}, u32[]{:S(2)}, u32[]{:S(2)}) %collective-permute-start.3) | collective-permute-done | bytes 1120 | tf_op jit(solution)/shard_map/ppermute | solution.py:34
  35.0 5.1 %collective-permute-done.5.refs_2_ = bf16[256,2048]{1,0:T(8,128)(2,1)S(1)} collective-permute-done((bf16[256,2048]{1,0:T(8,128)(2,1)S(1)}, bf16[256,2048]{1,0:T(8,128)(2,1)S(1)}, u32[]{:S(2)}, u32[]{:S(2)}) %collective-permute-start.5) | collective-permute-done | bytes 1048608 | tf_op jit(solution)/shard_map/ppermute | solution.py:47
  45.1 6.9 %shrink_rows.1 = (f32[2,128,128]{2,1,0:T(8,128)}, f32[2,128,128]{2,1,0:T(8,128)}) custom-call(s32[1]{0:T(128)} %bitcast.4.place_ref, s32[64]{0:T(128)} %compare_select_fusion.slots, bf16[256,2048]{1,0:T(8,128)(2,1)} %bitcast.58, bf16[256,2048]{1,0:T(8,128)(2,1)} %collective-permute-done.7.x1, bf16[256,2048]{1,0:T(8,128)(2,1)} %collective-permute-done.8.x2, ...), custom_call_target="tpu_custom_call" | custom-call | flops 524288 | bytes 524288 | tf_op jit(solution)/shard_map/shrink_rows/pallas_call | solution.py:299
  60.0 3.8 %collective-permute-start.12 = (f32[128,128]{1,0:T(8,128)}, f32[128,128]{1,0:T(8,128)}, u32[]{:S(2)}, u32[]{:S(2)}) collective-permute-start(f32[128,128]{1,0:T(8,128)} %fusion.8), channel_id=1, source_target_pairs={{0,1},{1,0},{2,3},{3,2},{4,5},{5,4},{6,7},{7,6},{8,9},{9,8},{10,11... | collective-permute-start | bytes 196616 | tf_op jit(solution)/shard_map/ppermute | solution.py:34
  67.1 6.6 %base_block.3 = f32[256,1280]{1,0:T(8,128)S(1)} custom-call(s32[3]{0:T(128)S(1)} %pad_add_fusion.1.owners, bf16[256,2048]{1,0:T(8,128)(2,1)S(1)} %bitcast.59, bf16[256,2048]{1,0:T(8,128)(2,1)} %collective-permute-done.4.refs_1_, bf16[256,2048]{1,0:T(8,128)(2,1)S(1)} %copy-done.4, f32[256,1]{1,0:T(8,128)S(1)} %copy.24.refs_3_, f32[1,8192]{1,0:T(1,128)S(1)} %bitcast.60, ...), custom_call_target="tpu_custom_call" | custom-call | flops 327680 | bytes 327680 | tf_op jit(solution)/shard_map/base_block/pallas_call | solution.py:120
  74.7 4.3 %collective-permute-start.15 = (f32[128,128]{1,0:T(8,128)S(1)}, f32[128,128]{1,0:T(8,128)S(1)}, u32[]{:S(2)}, u32[]{:S(2)}) collective-permute-start(f32[128,128]{1,0:T(8,128)S(1)} %add.142), channel_id=1, source_target_pairs={{0,2},{1,3},{2,0},{3,1},{4,6},{5,7},{6,4},{7,5},{8,10},{9,11},{10,... | collective-permute-start | bytes 196616 | tf_op jit(solution)/shard_map/ppermute | solution.py:34
  85.5 2.6 %collective-permute-done.16 = bf16[128,128]{1,0:T(8,128)(2,1)S(1)} collective-permute-done((bf16[128,128]{1,0:T(8,128)(2,1)S(1)}, bf16[128,128]{1,0:T(8,128)(2,1)S(1)}, u32[]{:S(2)}, u32[]{:S(2)}) %collective-permute-start.16) | collective-permute-done | bytes 32800 | tf_op jit(solution)/shard_map/ppermute | solution.py:34
  90.0 6.6 %grow_rows.1 = (f32[2,256,1280]{2,1,0:T(8,128)}, f32[256,1280]{1,0:T(8,128)}, f32[256,1280]{1,0:T(8,128)}) custom-call(s32[1]{0:T(128)} %bitcast.4.place_ref, s32[64]{0:T(128)} %compare_select_fusion.slots, bf16[2,128,128]{2,1,0:T(8,128)(2,1)} %copy-done.9, bf16[2,128,128]{2,1,0:T(8,128)(2,1)} %copy-done.10, bf16[32,64,1280]{2,1,0:T(8,128)(2,1)} %up_ref.1), custom_call_target="tpu_custom_call" | custom-call | flops 327680 | bytes 327680 | tf_op jit(solution)/shard_map/grow_rows/pallas_call | solution.py:381
  104.0 2.6 %fusion.6 = (f16[128,1280]{1,0:T(8,128)(2,1)}, f16[128,1280]{1,0:T(8,128)(2,1)S(1)}) fusion(f32[256,1280]{1,0:T(8,128)} %collective-permute-done.20, f32[2,256,1280]{2,1,0:T(8,128)} %get-tuple-element.59), kind=kLoop, calls=%fused_computation.10 | loop fusion | flops 655360 | bytes 3276800 | tf_op jit(solution)/shard_map/convert_element_type | solution.py:782
  109.6 5.4 %base_block.4 = f32[128,1280]{1,0:T(8,128)S(1)} custom-call(s32[4]{0:T(128)S(1)} %pad_add_fusion.owners, bf16[256,2048]{1,0:T(8,128)(2,1)S(1)} %collective-permute-done.13.refs_0_, bf16[256,2048]{1,0:T(8,128)(2,1)S(1)} %collective-permute-done.14.refs_1_, bf16[128,2048]{1,0:T(8,128)(2,1)} %collective-permute-done.18.refs_2_, ...), custom_call_target="tpu_custom_call" | custom-call | flops 163840 | bytes 163840 | tf_op jit(solution)/shard_map/base_block/pallas_call | solution.py:120
  119.3 5.4 %all-to-all-start = ((bf16[4,32,1280]{2,1,0:T(8,128)(2,1)}), bf16[4,32,1280]{2,1,0:T(8,128)(2,1)S(1)}, u32[]{:S(2)}, u32[]{:S(2)}) async-start(bf16[4,32,1280]{2,1,0:T(8,128)(2,1)} %bitcast.66), calls=%async_computation | async-start | bytes 655360 | tf_op jit(solution)/shard_map/all_to_all | solution.py:812
  124.8 5.4 %base_block.5 = f32[128,1280]{1,0:T(8,128)S(1)} custom-call(s32[4]{0:T(128)S(1)} %pad_add_fusion.owners, bf16[256,2048]{1,0:T(8,128)(2,1)S(1)} %collective-permute-done.13.refs_0_, bf16[256,2048]{1,0:T(8,128)(2,1)S(1)} %collective-permute-done.14.refs_1_, bf16[128,2048]{1,0:T(8,128)(2,1)} %collective-permute-done.23.refs_2_, ...), custom_call_target="tpu_custom_call" | custom-call | flops 163840 | bytes 163840 | tf_op jit(solution)/shard_map/base_block/pallas_call | solution.py:120
  133.5 4.9 %all-to-all-start.1 = ((bf16[4,32,1280]{2,1,0:T(8,128)(2,1)}), bf16[4,32,1280]{2,1,0:T(8,128)(2,1)S(1)}, u32[]{:S(2)}, u32[]{:S(2)}) async-start(bf16[4,32,1280]{2,1,0:T(8,128)(2,1)} %bitcast.33), calls=%async_computation.1 | async-start | bytes 655360 | tf_op jit(solution)/shard_map/all_to_all | solution.py:812
  139.0 6.7 %attend.2.refs_0_ = bf16[32,4096]{1,0:T(8,128)(2,1)S(1)} custom-call(s32[16]{0:T(128)S(1)} %get-tuple-element.101.lengths, s32[16]{0:T(128)S(1)} %select_reduce_fusion.2.order, bf16[4,32,1280]{2,1,0:T(8,128)(2,1)S(1)} %all-to-all-done.qkv_ref, f32[32,128]{1,0:T(8,128)S(1)} %get-tuple-element.104.cos_ref, f32[32,128]{1,0:T(8,128)S(1)} %get-tuple-element.105.sin_ref, ...), custom_call_target="tpu_custom_call" | custom-call | flops 268435456 | bytes 16777216 | tf_op jit(solution)/shard_map/attend/pallas_call | solution.py:563
  145.7 3.9 %collective-permute-start.26 = (bf16[32,4096]{1,0:T(8,128)(2,1)S(1)}, bf16[32,4096]{1,0:T(8,128)(2,1)S(1)}, u32[]{:S(2)}, u32[]{:S(2)}) collective-permute-start(bf16[32,4096]{1,0:T(8,128)(2,1)S(1)} %attend.2.refs_0_), channel_id=1, source_target_pairs={{0,1},{1,2},{2,3},{4,5},{5,6},{6,7},{8,9},{9,10},{10,11},{12,13},{... | collective-permute-start | bytes 786440 | tf_op jit(solution)/shard_map/ppermute | solution.py:46
  151.2 6.1 %attend.3.refs_3_ = bf16[32,4096]{1,0:T(8,128)(2,1)S(1)} custom-call(s32[16]{0:T(128)S(1)} %get-tuple-element.100.lengths, s32[16]{0:T(128)S(1)} %select_reduce_fusion.1.order, bf16[4,32,1280]{2,1,0:T(8,128)(2,1)S(1)} %all-to-all-done.1.qkv_ref, f32[32,128]{1,0:T(8,128)S(1)} %get-tuple-element.106.cos_ref, f32[32,128]{1,0:T(8,128)S(1)} %get-tuple-element.107.sin_ref, ...), custom_call_target="tpu_custom_call" | custom-call | flops 268435456 | bytes 16777216 | tf_op jit(solution)/shard_map/attend/pallas_call | solution.py:563
  157.2 5.2 %collective-permute-start.32 = (bf16[32,4096]{1,0:T(8,128)(2,1)S(1)}, bf16[32,4096]{1,0:T(8,128)(2,1)S(1)}, u32[]{:S(2)}, u32[]{:S(2)}) collective-permute-start(bf16[32,4096]{1,0:T(8,128)(2,1)S(1)} %attend.3.refs_3_), channel_id=1, source_target_pairs={{0,1},{1,2},{2,3},{4,5},{5,6},{6,7},{8,9},{9,10},{10,11},{12,13},{... | collective-permute-start | bytes 786440 | tf_op jit(solution)/shard_map/ppermute | solution.py:46
  167.0 6.2 %collective-permute-done.34.refs_5_ = bf16[32,4096]{1,0:T(8,128)(2,1)S(1)} collective-permute-done((bf16[32,4096]{1,0:T(8,128)(2,1)S(1)}, bf16[32,4096]{1,0:T(8,128)(2,1)S(1)}, u32[]{:S(2)}, u32[]{:S(2)}) %collective-permute-start.34) | collective-permute-done | bytes 262176 | tf_op jit(solution)/shard_map/ppermute | solution.py:47
  175.2 4.2 %collective-permute-done.29.refs_1_ = bf16[32,4096]{1,0:T(8,128)(2,1)S(1)} collective-permute-done((bf16[32,4096]{1,0:T(8,128)(2,1)S(1)}, bf16[32,4096]{1,0:T(8,128)(2,1)S(1)}, u32[]{:S(2)}, u32[]{:S(2)}) %collective-permute-start.29) | collective-permute-done | bytes 262176 | tf_op jit(solution)/shard_map/ppermute | solution.py:47
  181.4 4.0 %collective-permute-done.35.refs_5_ = bf16[32,4096]{1,0:T(8,128)(2,1)S(1)} collective-permute-done((bf16[32,4096]{1,0:T(8,128)(2,1)S(1)}, bf16[32,4096]{1,0:T(8,128)(2,1)S(1)}, u32[]{:S(2)}, u32[]{:S(2)}) %collective-permute-start.35) | collective-permute-done | bytes 262176 | tf_op jit(solution)/shard_map/ppermute | solution.py:47
  186.7 8.2 %project.2.refs_9_ = bf16[2,4,2,16,2048]{4,3,2,1,0:T(8,128)(2,1)} custom-call(s32[3]{0:T(128)S(1)} %pad_add_fusion.1.owners, bf16[32,4096]{1,0:T(8,128)(2,1)S(1)} %attend.2.refs_0_, bf16[32,4096]{1,0:T(8,128)(2,1)S(1)} %collective-permute-done.26.refs_1_, bf16[32,4096]{1,0:T(8,128)(2,1)S(1)} %collective-permute-done.28.refs_2_, ...), custom_call_target="tpu_custom_call" | custom-call | flops 3221225472 | bytes 19136512 | tf_op jit(solution)/shard_map/project/pallas_call | solution.py:648
  195.6 8.8 %project.3 = bf16[2,4,2,16,2048]{4,3,2,1,0:T(8,128)(2,1)} custom-call(s32[4]{0:T(128)S(1)} %pad_add_fusion.owners, bf16[32,4096]{1,0:T(8,128)(2,1)S(1)} %collective-permute-done.27.refs_0_, bf16[32,4096]{1,0:T(8,128)(2,1)S(1)} %collective-permute-done.29.refs_1_, bf16[32,4096]{1,0:T(8,128)(2,1)S(1)} %collective-permute-done.30.refs_2_, ...), custom_call_target="tpu_custom_call" | custom-call | flops 2147483648 | bytes 18350080 | tf_op jit(solution)/shard_map/project/pallas_call | solution.py:648
  (159 shorter events, 71.5 us)
Async XLA Ops:
  8.6 24.5 %collective-permute-start.8 = (bf16[256,2048]{1,0:T(8,128)(2,1)S(1)}, bf16[256,2048]{1,0:T(8,128)(2,1)}, u32[]{:S(2)}, u32[]{:S(2)}) collective-permute-start(bf16[256,2048]{1,0:T(8,128)(2,1)S(1)} %bitcast.54), channel_id=1, source_target_pairs={{0,8},{4,12},{8,0},{12,4},{1,9},{5,13},{9,1},{13,5},{2,10},{6,14},... | collective-permute-start | bytes 3145736 | tf_op jit(solution)/shard_map/ppermute | solution.py:34
  12.7 22.3 %collective-permute-start.4 = (bf16[256,2048]{1,0:T(8,128)(2,1)S(1)}, bf16[256,2048]{1,0:T(8,128)(2,1)}, u32[]{:S(2)}, u32[]{:S(2)}) collective-permute-start(bf16[256,2048]{1,0:T(8,128)(2,1)S(1)} %bitcast.55), channel_id=1, source_target_pairs={{0,1},{1,2},{2,3},{4,5},{5,6},{6,7},{8,9},{9,10},{10,11},{12,13},{... | collective-permute-start | bytes 3145736 | tf_op jit(solution)/shard_map/ppermute | solution.py:46
  15.0 25.1 %collective-permute-start.5 = (bf16[256,2048]{1,0:T(8,128)(2,1)S(1)}, bf16[256,2048]{1,0:T(8,128)(2,1)S(1)}, u32[]{:S(2)}, u32[]{:S(2)}) collective-permute-start(bf16[256,2048]{1,0:T(8,128)(2,1)S(1)} %bitcast.56), channel_id=1, source_target_pairs={{3,2},{2,1},{1,0},{7,6},{6,5},{5,4},{11,10},{10,9},{9,8},{15,14},{... | collective-permute-start | bytes 3145736 | tf_op jit(solution)/shard_map/ppermute | solution.py:47
  16.6 16.5 %collective-permute-start.3 = (f32[1,272]{1,0:T(1,128)S(1)}, f32[1,272]{1,0:T(1,128)S(1)}, u32[]{:S(2)}, u32[]{:S(2)}) collective-permute-start(f32[1,272]{1,0:T(1,128)S(1)} %reshape.106), channel_id=1, source_target_pairs={{0,8},{4,12},{8,0},{12,4},{1,9},{5,13},{9,1},{13,5},{2,10},{6,14},... | collective-permute-start | bytes 3272 | tf_op jit(solution)/shard_map/ppermute | solution.py:34
  18.2 26.9 %collective-permute-start.7 = (bf16[256,2048]{1,0:T(8,128)(2,1)S(1)}, bf16[256,2048]{1,0:T(8,128)(2,1)}, u32[]{:S(2)}, u32[]{:S(2)}) collective-permute-start(bf16[256,2048]{1,0:T(8,128)(2,1)S(1)} %bitcast.57), channel_id=1, source_target_pairs={{0,4},{4,0},{8,12},{12,8},{1,5},{5,1},{9,13},{13,9},{2,6},{6,2},{1... | collective-permute-start | bytes 3145736 | tf_op jit(solution)/shard_map/ppermute | solution.py:34
  41.0 33.7 %collective-permute-start.13 = (bf16[256,2048]{1,0:T(8,128)(2,1)}, bf16[256,2048]{1,0:T(8,128)(2,1)S(1)}, u32[]{:S(2)}, u32[]{:S(2)}) collective-permute-start(bf16[256,2048]{1,0:T(8,128)(2,1)} %collective-permute-done.4.refs_1_), channel_id=1, source_target_pairs={{1,2},{2,3},{5,6},{6,7},{9,10},{10,11},{13,14},{14,15},{17,18},{18... | collective-permute-start | bytes 3145736 | tf_op jit(solution)/shard_map/ppermute | solution.py:46
  41.8 32.9 %collective-permute-start.14 = (bf16[256,2048]{1,0:T(8,128)(2,1)}, bf16[256,2048]{1,0:T(8,128)(2,1)S(1)}, u32[]{:S(2)}, u32[]{:S(2)}) collective-permute-start(bf16[256,2048]{1,0:T(8,128)(2,1)} %copy-done.3), channel_id=1, source_target_pairs={{2,1},{1,0},{6,5},{5,4},{10,9},{9,8},{14,13},{13,12},{18,17},{17,1... | collective-permute-start | bytes 3145736 | tf_op jit(solution)/shard_map/ppermute | solution.py:47
  60.0 13.8 %collective-permute-start.12 = (f32[128,128]{1,0:T(8,128)}, f32[128,128]{1,0:T(8,128)}, u32[]{:S(2)}, u32[]{:S(2)}) collective-permute-start(f32[128,128]{1,0:T(8,128)} %fusion.8), channel_id=1, source_target_pairs={{0,1},{1,0},{2,3},{3,2},{4,5},{5,4},{6,7},{7,6},{8,9},{9,8},{10,11... | collective-permute-start | bytes 196616 | tf_op jit(solution)/shard_map/ppermute | solution.py:34
  81.3 15.3 %collective-permute-start.18 = (bf16[128,2048]{1,0:T(8,128)(2,1)}, bf16[128,2048]{1,0:T(8,128)(2,1)}, u32[]{:S(2)}, u32[]{:S(2)}) collective-permute-start(bf16[128,2048]{1,0:T(8,128)(2,1)} %get-tuple-element.54), channel_id=1, source_target_pairs={{2,3},{6,7},{10,11},{14,15},{18,19},{22,23},{26,27},{30,31}} | collective-permute-start | bytes 1572872 | tf_op jit(solution)/shard_map/ppermute | solution.py:46
  82.7 15.1 %collective-permute-start.19 = (bf16[128,2048]{1,0:T(8,128)(2,1)}, bf16[128,2048]{1,0:T(8,128)(2,1)}, u32[]{:S(2)}, u32[]{:S(2)}) collective-permute-start(bf16[128,2048]{1,0:T(8,128)(2,1)} %get-tuple-element.55), channel_id=1, source_target_pairs={{1,0},{5,4},{9,8},{13,12},{17,16},{21,20},{25,24},{29,28}} | collective-permute-start | bytes 1572872 | tf_op jit(solution)/shard_map/ppermute | solution.py:47
  99.7 15.3 %collective-permute-start.21 = (f32[256,1280]{1,0:T(8,128)}, f32[256,1280]{1,0:T(8,128)}, u32[]{:S(2)}, u32[]{:S(2)}) collective-permute-start(f32[256,1280]{1,0:T(8,128)} %get-tuple-element.62), channel_id=1, source_target_pairs={{0,4},{4,0},{8,12},{12,8},{1,5},{5,1},{9,13},{13,9},{2,6},{6,2},{1... | collective-permute-start | bytes 3932168 | tf_op jit(solution)/shard_map/ppermute | solution.py:34
  101.3 23.5 %collective-permute-start.23 = (bf16[128,2048]{1,0:T(8,128)(2,1)}, bf16[128,2048]{1,0:T(8,128)(2,1)}, u32[]{:S(2)}, u32[]{:S(2)}) collective-permute-start(bf16[128,2048]{1,0:T(8,128)(2,1)} %get-tuple-element.64), channel_id=1, source_target_pairs={{2,3},{6,7},{10,11},{14,15},{18,19},{22,23},{26,27},{30,31}} | collective-permute-start | bytes 1572872 | tf_op jit(solution)/shard_map/ppermute | solution.py:46
  102.7 22.0 %collective-permute-start.24 = (bf16[128,2048]{1,0:T(8,128)(2,1)}, bf16[128,2048]{1,0:T(8,128)(2,1)}, u32[]{:S(2)}, u32[]{:S(2)}) collective-permute-start(bf16[128,2048]{1,0:T(8,128)(2,1)} %get-tuple-element.65), channel_id=1, source_target_pairs={{1,0},{5,4},{9,8},{13,12},{17,16},{21,20},{25,24},{29,28}} | collective-permute-start | bytes 1572872 | tf_op jit(solution)/shard_map/ppermute | solution.py:47
  108.0 22.3 %collective-permute-start.25 = (f16[128,1280]{1,0:T(8,128)(2,1)}, f16[128,1280]{1,0:T(8,128)(2,1)}, u32[]{:S(2)}, u32[]{:S(2)}) collective-permute-start(f16[128,1280]{1,0:T(8,128)(2,1)} %get-tuple-element.69), channel_id=1, source_target_pairs={{0,8},{4,12},{8,0},{12,4},{1,9},{5,13},{9,1},{13,5},{2,10},{6,14},... | collective-permute-start | bytes 983048 | tf_op jit(solution)/shard_map/ppermute | solution.py:34
  119.3 14.2 %all-to-all-start = ((bf16[4,32,1280]{2,1,0:T(8,128)(2,1)}), bf16[4,32,1280]{2,1,0:T(8,128)(2,1)S(1)}, u32[]{:S(2)}, u32[]{:S(2)}) async-start(bf16[4,32,1280]{2,1,0:T(8,128)(2,1)} %bitcast.66), calls=%async_computation | async-start | bytes 655360 | tf_op jit(solution)/shard_map/all_to_all | solution.py:812
  133.5 17.7 %all-to-all-start.1 = ((bf16[4,32,1280]{2,1,0:T(8,128)(2,1)}), bf16[4,32,1280]{2,1,0:T(8,128)(2,1)S(1)}, u32[]{:S(2)}, u32[]{:S(2)}) async-start(bf16[4,32,1280]{2,1,0:T(8,128)(2,1)} %bitcast.33), calls=%async_computation.1 | async-start | bytes 655360 | tf_op jit(solution)/shard_map/all_to_all | solution.py:812
  145.7 18.1 %collective-permute-start.26 = (bf16[32,4096]{1,0:T(8,128)(2,1)S(1)}, bf16[32,4096]{1,0:T(8,128)(2,1)S(1)}, u32[]{:S(2)}, u32[]{:S(2)}) collective-permute-start(bf16[32,4096]{1,0:T(8,128)(2,1)S(1)} %attend.2.refs_0_), channel_id=1, source_target_pairs={{0,1},{1,2},{2,3},{4,5},{5,6},{6,7},{8,9},{9,10},{10,11},{12,13},{... | collective-permute-start | bytes 786440 | tf_op jit(solution)/shard_map/ppermute | solution.py:46
  149.6 14.8 %collective-permute-start.28 = (bf16[32,4096]{1,0:T(8,128)(2,1)S(1)}, bf16[32,4096]{1,0:T(8,128)(2,1)S(1)}, u32[]{:S(2)}, u32[]{:S(2)}) collective-permute-start(bf16[32,4096]{1,0:T(8,128)(2,1)S(1)} %attend.2.refs_0_), channel_id=1, source_target_pairs={{3,2},{2,1},{1,0},{7,6},{6,5},{5,4},{11,10},{10,9},{9,8},{15,14},{... | collective-permute-start | bytes 786440 | tf_op jit(solution)/shard_map/ppermute | solution.py:47
  164.5 14.9 %collective-permute-start.29 = (bf16[32,4096]{1,0:T(8,128)(2,1)S(1)}, bf16[32,4096]{1,0:T(8,128)(2,1)S(1)}, u32[]{:S(2)}, u32[]{:S(2)}) collective-permute-start(bf16[32,4096]{1,0:T(8,128)(2,1)S(1)} %collective-permute-done.28.refs_2_), channel_id=1, source_target_pairs={{2,1},{1,0},{6,5},{5,4},{10,9},{9,8},{14,13},{13,12},{18,17},{17,1... | collective-permute-start | bytes 786440 | tf_op jit(solution)/shard_map/ppermute | solution.py:47
  166.3 14.4 %collective-permute-start.33 = (bf16[32,4096]{1,0:T(8,128)(2,1)S(1)}, bf16[32,4096]{1,0:T(8,128)(2,1)S(1)}, u32[]{:S(2)}, u32[]{:S(2)}) collective-permute-start(bf16[32,4096]{1,0:T(8,128)(2,1)S(1)} %collective-permute-done.32.refs_4_), channel_id=1, source_target_pairs={{1,2},{2,3},{5,6},{6,7},{9,10},{10,11},{13,14},{14,15},{17,18},{18... | collective-permute-start | bytes 786440 | tf_op jit(solution)/shard_map/ppermute | solution.py:46
  173.2 12.2 %collective-permute-start.35 = (bf16[32,4096]{1,0:T(8,128)(2,1)S(1)}, bf16[32,4096]{1,0:T(8,128)(2,1)S(1)}, u32[]{:S(2)}, u32[]{:S(2)}) collective-permute-start(bf16[32,4096]{1,0:T(8,128)(2,1)S(1)} %collective-permute-done.34.refs_5_), channel_id=1, source_target_pairs={{2,1},{1,0},{6,5},{5,4},{10,9},{9,8},{14,13},{13,12},{18,17},{17,1... | collective-permute-start | bytes 786440 | tf_op jit(solution)/shard_map/ppermute | solution.py:47
  174.5 20.3 %collective-permute-start.30 = (bf16[32,4096]{1,0:T(8,128)(2,1)S(1)}, bf16[32,4096]{1,0:T(8,128)(2,1)S(1)}, u32[]{:S(2)}, u32[]{:S(2)}) collective-permute-start(bf16[32,4096]{1,0:T(8,128)(2,1)S(1)} %collective-permute-done.27.refs_0_), channel_id=1, source_target_pairs={{2,3},{6,7},{10,11},{14,15},{18,19},{22,23},{26,27},{30,31}} | collective-permute-start | bytes 786440 | tf_op jit(solution)/shard_map/ppermute | solution.py:46
  179.4 15.4 %collective-permute-start.31 = (bf16[32,4096]{1,0:T(8,128)(2,1)S(1)}, bf16[32,4096]{1,0:T(8,128)(2,1)S(1)}, u32[]{:S(2)}, u32[]{:S(2)}) collective-permute-start(bf16[32,4096]{1,0:T(8,128)(2,1)S(1)} %collective-permute-done.29.refs_1_), channel_id=1, source_target_pairs={{1,0},{5,4},{9,8},{13,12},{17,16},{21,20},{25,24},{29,28}} | collective-permute-start | bytes 786440 | tf_op jit(solution)/shard_map/ppermute | solution.py:47
  180.7 14.2 %collective-permute-start.36 = (bf16[32,4096]{1,0:T(8,128)(2,1)S(1)}, bf16[32,4096]{1,0:T(8,128)(2,1)S(1)}, u32[]{:S(2)}, u32[]{:S(2)}) collective-permute-start(bf16[32,4096]{1,0:T(8,128)(2,1)S(1)} %collective-permute-done.33.refs_4_), channel_id=1, source_target_pairs={{2,3},{6,7},{10,11},{14,15},{18,19},{22,23},{26,27},{30,31}} | collective-permute-start | bytes 786440 | tf_op jit(solution)/shard_map/ppermute | solution.py:46
  (35 other events, 278.9 us)

commit v9 on v8

--- a/solution.py
+++ b/solution.py
@@ -27,6 +27,7 @@
 VMEM = pl.BlockSpec(memory_space=pltpu.VMEM)
 SMEM = pl.BlockSpec(memory_space=pltpu.SMEM)
 HBM = pl.BlockSpec(memory_space=pltpu.HBM)
+ANY = pl.BlockSpec(memory_space=pl.ANY)
 
 
 def swap(values, axis, distance):
@@ -120,7 +121,7 @@
     return pl.pallas_call(
         functools.partial(block_kernel, first_rows, total is not None),
         out_shape=jax.ShapeDtypeStruct((rows, columns), F32),
-        in_specs=[SMEM] + [HBM] * count + [VMEM] * 2 + [HBM] + [VMEM] * len(more),
+        in_specs=[SMEM] + [ANY] * count + [VMEM] * 2 + [HBM] + [VMEM] * len(more),
         out_specs=VMEM,
         scratch_shapes=[
             pltpu.VMEM((present, rows, depth), BF16),
@@ -130,8 +131,8 @@
         ],
         compiler_params=pltpu.CompilerParams(vmem_limit_bytes=46 * MIB),
         cost_estimate=pl.CostEstimate(
-            flops=rows * columns,
-            bytes_accessed=rows * columns,
+            flops=2 * present * rows * depth * columns,
+            bytes_accessed=2 * present * depth * (rows + columns) + 4 * rows * columns,
             transcendentals=0,
         ),
         name="base_block",
@@ -299,7 +300,7 @@
     return pl.pallas_call(
         shrink_kernel,
         out_shape=[jax.ShapeDtypeStruct((2, rows // 2, 2 * rank), F32)] * 2,
-        in_specs=[SMEM] * 2 + [HBM] * 4 + [VMEM] * 2 + [HBM],
+        in_specs=[SMEM] * 2 + [ANY] * 4 + [VMEM] * 2 + [HBM],
         out_specs=[VMEM] * 2,
         scratch_shapes=[
             pltpu.SMEM((4 * runs,), jnp.int32),
@@ -573,7 +574,7 @@
             pltpu.VMEM((rows, kv_heads, cached, width), BF16),
             pltpu.SemaphoreType.DMA((rows, 2)),
         ],
-        compiler_params=pltpu.CompilerParams(vmem_limit_bytes=48 * MIB),
+        compiler_params=pltpu.CompilerParams(vmem_limit_bytes=28 * MIB),
         cost_estimate=pl.CostEstimate(
             flops=4 * local * HEADS * HD * cached,
             bytes_accessed=2 * rows * kv_heads * cached * width,
@@ -586,17 +587,21 @@
 def out_kernel(count, has_earlier, owners, *refs):
     blocks = refs[:count]
     w_ref = refs[count]
-    out_ref, lhs, total, held, sems = refs[-5:]
-    local = blocks[0].shape[0]
+    if has_earlier:
+        out_ref, lhs, total = refs[-3:]
+    else:
+        out_ref, lhs, total, held, sems = refs[-5:]
+        tiles, tile, _ = held.shape
+        copies = [
+            pltpu.make_async_copy(w_ref.at[pl.ds(k * tile, tile), :], held.at[k], sems.at[k])
+            for k in range(tiles)
+        ]
+        for copy in copies:
+            copy.start()
+    local, depth = blocks[0].shape
     rows = local // STEPS
-    tiles, depth, columns = held.shape
+    columns = w_ref.shape[1]
     halves = out_ref.shape[2]
-    copies = [
-        pltpu.make_async_copy(w_ref.at[pl.ds(k * depth, depth), :], held.at[k], sems.at[k])
-        for k in range(tiles)
-    ]
-    for copy in copies:
-        copy.start()
     slots = count // halves
 
     def place(j):
@@ -615,16 +620,17 @@
     if has_earlier:
         out_ref[...] = refs[count + 1][...]
     width = min(512, columns)
-    for k, copy in enumerate(copies):
-        copy.wait()
-        for j in range(columns // width):
-            span = slice(j * width, (j + 1) * width)
-            product = jnp.dot(
-                lhs[:, k * depth : (k + 1) * depth], held[k, :, span], preferred_element_type=F32
-            )
-            if k > 0:
-                product = total[:, span] + product
-            total[:, span] = product
+    spans = [slice(j * width, (j + 1) * width) for j in range(columns // width)]
+    if has_earlier:
+        for span in spans:
+            total[:, span] = jnp.dot(lhs[...], w_ref[:, span], preferred_element_type=F32)
+    else:
+        for k, copy in enumerate(copies):
+            copy.wait()
+            part = lhs[:, k * tile : (k + 1) * tile]
+            for span in spans:
+                product = jnp.dot(part, held[k, :, span], preferred_element_type=F32)
+                total[:, span] = product if k == 0 else total[:, span] + product
     for j in range(count):
 
         @pl.when(owners[j % slots] >= 0)
@@ -641,22 +647,25 @@
     flat = [block for part in blocks for block in part]
     local, depth = flat[0].shape
     columns = weight.shape[1]
-    tile = min(512, depth)
     rows = local // STEPS
     count = len(flat)
     more = [] if earlier is None else [earlier]
+    tile = min(512, depth)
+    streamed = [
+        pltpu.VMEM((depth // tile, tile, columns), BF16),
+        pltpu.SemaphoreType.DMA((depth // tile,)),
+    ]
     return pl.pallas_call(
         functools.partial(out_kernel, count, earlier is not None),
         out_shape=jax.ShapeDtypeStruct((STEPS, 4, halves, rows, columns), BF16),
-        in_specs=[SMEM] + [VMEM] * count + [HBM] + [VMEM] * len(more),
+        in_specs=[SMEM] + [VMEM] * count + [VMEM if more else HBM] + [VMEM] * len(more),
         out_specs=VMEM,
         scratch_shapes=[
             pltpu.VMEM((present * halves * local, depth), BF16),
             pltpu.VMEM((present * halves * local, columns), F32),
-            pltpu.VMEM((depth // tile, tile, columns), BF16),
-            pltpu.SemaphoreType.DMA((depth // tile,)),
-        ],
-        compiler_params=pltpu.CompilerParams(vmem_limit_bytes=52 * MIB),
+        ]
+        + ([] if more else streamed),
+        compiler_params=pltpu.CompilerParams(vmem_limit_bytes=(24 if more else 28) * MIB),
         cost_estimate=pl.CostEstimate(
             flops=2 * present * halves * local * depth * columns,
             bytes_accessed=2 * depth * columns + 4 * present * local * (depth + columns),
@@ -734,9 +743,11 @@
         own_runs = own_runs.reshape(tensor_count, halves, -1).swapaxes(0, 1).reshape(-1)
     told = jnp.concatenate([squares, own_runs.astype(F32)]).reshape(1, -1)
     told = jnp.concatenate([told, swap(told, "store", 2)], axis=0)
+    beside = swap(raw, "store", 1)
     if line:
-        told, hop1 = lax.optimization_barrier((told, hop1))
-        hop2 = line_hop(*hop1, "tensor", 2)
+        told, hop1, beside = lax.optimization_barrier((told, hop1, beside))
+        sent = [(hop1[0][part], hop1[1][part]) for part in parts]
+        hop2 = [line_hop(*sent[0], "tensor", 2)]
     told = jnp.concatenate([told, swap(told, "store", 1)], axis=0)
     told = jnp.stack([told[d] for d in (0, 2, 1, 3)])
     told = jnp.stack([jnp.stack([told[p ^ q] for q in range(4)]) for p in range(4)])
@@ -753,7 +764,6 @@
     own_scale = lax.dynamic_index_in_dim(scales, store_pos, 0, keepdims=False)
 
     across = swap(raw, "store", 2)
-    beside = swap(raw, "store", 1)
     diagonal = swap(across, "store", 1)
     mine = slots.reshape(-1)
     down = jnp.swapaxes(adapter_down_weight, 1, 2)
@@ -761,15 +771,12 @@
     kept = kept + swap(passed, "store", 1)
     shrunk = kept[0] + swap(kept[1], "store", 2)
     if line:
-        shrunk, early = lax.optimization_barrier((shrunk, (raw,) + hop1))
-        near = jnp.concatenate(owners[:2])
-        total = base_block(early, own_scale, gains, query_key_value_weight, near, (0,) * 3, 3)
+        shrunk, hop2[0] = lax.optimization_barrier((shrunk, hop2[0]))
         shrunk = shrunk + swap(shrunk, "tensor", 1)
-        shrunk, total, hop2 = lax.optimization_barrier((shrunk, total, hop2))
-        sent = [(hop2[0][part], hop2[1][part]) for part in parts]
         shrunk = shrunk + swap(shrunk, "tensor", 2)
-        shrunk, sent = lax.optimization_barrier((shrunk, sent))
-        hop3 = [line_hop(up, down, "tensor", 3) for up, down in sent]
+        shrunk, sent[1], hop2[0] = lax.optimization_barrier((shrunk, sent[1], hop2[0]))
+        hop3 = [line_hop(*hop2[0], "tensor", 3)]
+        hop2.append(line_hop(*sent[1], "tensor", 2))
     else:
         shrunk = summed_over(shrunk, "tensor")
     shrunk = shrunk.astype(BF16)
@@ -781,18 +788,23 @@
     passed = [swap(piece, "store", 1) for piece in passed]
     leaving = [(kept[1, part] + passed[1][part]).astype(F16) for part in parts]
     arrived = [swap(piece, "store", 2).astype(F32) for piece in leaving]
+    if line:
+        arrived[0], hop2[1] = lax.optimization_barrier((arrived[0], hop2[1]))
+        hop3.append(line_hop(*hop2[1], "tensor", 3))
     deltas = [(kept[0, p] + passed[0][p]) + far for p, far in zip(parts, arrived)]
 
     weight = query_key_value_weight
     mixed = []
     if line:
-        total, leaving = lax.optimization_barrier((total, leaving))
+        early, leaving = lax.optimization_barrier(((raw,) + hop1, leaving))
+        near = jnp.concatenate(owners[:2])
+        total = base_block(early, own_scale, gains, weight, near, (0,) * 3, 3)
         far = jnp.concatenate(owners[2:])
         for h, part in enumerate(parts):
             if mixed:
                 far, mixed[-1] = lax.optimization_barrier((far, mixed[-1]))
-            blocks = hop2 + hop3[h]
-            first_rows = (h * count, h * count, 0, 0)
+            blocks = hop2[h] + hop3[h]
+            first_rows = (0,) * 4
             sums = base_block(
                 blocks, own_scale[part], gains, weight, far, first_rows, 2, total[part]
             )

time: 205 us -> 218 us (1.063)
  waiting for transfers between devices: 50.8 us -> 80.6 us
  local copies, waits for them, and re-layouts: 13.3 us -> 6.98 us
  Pallas kernels: 60.7 us -> 56 us
  other arithmetic: 14.1 us -> 10.6 us
  starting transfers between devices: 64.8 us -> 61.3 us
    ppermute x10 -> x11, waiting for transfers between devices: 20.9 us -> 44.5 us  [line_hop(): down = lax.ppermute(down, axis, [(i, i - 1) for i in range(4 - hop, 0, -1)])]
    ppermute x18, starting transfers between devices: 23.7 us -> 15.7 us  [swap(): return lax.ppermute(values, axis, [(i, i ^ distance) for i in range(count)])]
    ppermute x18, waiting for transfers between devices: 26.7 us -> 34.2 us  [swap(): return lax.ppermute(values, axis, [(i, i ^ distance) for i in range(count)])]
    pallas_call x2, Pallas kernels: 17 us -> 10.2 us  [project(): pl.pallas_call(functools.partial(out_kernel, count, earlier is not None),...]
    unnamed x38 -> x30, local copies, waits for them, and re-layouts: 5.55 us -> 0.69 us
    all_to_all x2, starting transfers between devices: 10.3 us -> 14 us  [on_device(): exchanged.append(lax.all_to_all(qkv, 'tensor', 0, 0, tiled=True))]
    ppermute x10 -> x11, starting transfers between devices: 13.1 us -> 14.4 us  [line_hop(): down = lax.ppermute(down, axis, [(i, i - 1) for i in range(4 - hop, 0, -1)])]
    ppermute x10 -> x11, starting transfers between devices: 17.8 us -> 17.3 us  [line_hop(): up = lax.ppermute(up, axis, [(i, i + 1) for i in range(hop - 1, 3)])]
  transfers between devices with their start and end apart: 40 -> 42, of which waited for: 16 -> 17; matrix products, arithmetic and copies ran while one was open for 10% -> 7% of each run, Pallas kernels for 25% -> 24%
where the time goes in v9:
time: 218 us; the launch traced here: 216 us
  waiting for transfers between devices  80.6 us (37%)
  starting transfers between devices  61.3 us (28%)
  Pallas kernels  56 us (26%)
  other arithmetic  10.6 us (5%)
  local copies, waits for them, and re-layouts  6.98 us (3%)
    ppermute x11, waiting for transfers between devices, line_hop(): down = lax.ppermute(down, axis, [(i, i - 1) for i in range(4 - hop, 0, -1)])  44.5 us
    ppermute x18, waiting for transfers between devices, swap(): return lax.ppermute(values, axis, [(i, i ^ distance) for i in range(count)])  34.2 us
    pallas_call x3, Pallas kernels, base_block(): pl.pallas_call(functools.partial(block_kernel, first_rows, total is not N...  18.2 us
    ppermute x11, starting transfers between devices, line_hop(): up = lax.ppermute(up, axis, [(i, i + 1) for i in range(hop - 1, 3)])  17.3 us
    ppermute x18, starting transfers between devices, swap(): return lax.ppermute(values, axis, [(i, i ^ distance) for i in range(count)])  15.7 us
    ppermute x11, starting transfers between devices, line_hop(): down = lax.ppermute(down, axis, [(i, i - 1) for i in range(4 - hop, 0, -1)])  14.4 us
    all_to_all x2, starting transfers between devices, on_device(): exchanged.append(lax.all_to_all(qkv, 'tensor', 0, 0, tiled=True))  14 us
    pallas_call x2, Pallas kernels, attend(): pl.pallas_call(functools.partial(attend_kernel, unit, first_row), out_sha...  13.6 us
  transfers between devices with their start and end apart: 42, of which 17 were waited for; matrix products, arithmetic and copies ran while one was open for 7% of the time, Pallas kernels for 24%

profile of v9, /device:TPU:0, one launch (start us, length us, event | category | flops | bytes accessed | tf_op | source)
XLA Modules:
  0.0 216.2 jit_solution(15299925967476915415)
XLA Ops:
  1.7 3.1 %collective-permute-start = (f32[256]{0:T(256)S(1)}, f32[256]{0:T(256)S(1)}, u32[]{:S(2)}, u32[]{:S(2)}) collective-permute-start(f32[256]{0:T(256)S(1)} %reduce_sum.59), channel_id=1, source_target_pairs={{0,1},{1,0},{2,3},{3,2},{4,5},{5,4},{6,7},{7,6},{8,9},{9,8},{10,11... | collective-permute-start | bytes 3080 | tf_op jit(solution)/shard_map/ppermute | solution.py:35
  17.8 16.6 %collective-permute-done.3 = f32[1,272]{1,0:T(1,128)S(1)} collective-permute-done((f32[1,272]{1,0:T(1,128)S(1)}, f32[1,272]{1,0:T(1,128)S(1)}, u32[]{:S(2)}, u32[]{:S(2)}) %collective-permute-start.3) | collective-permute-done | bytes 1120 | tf_op jit(solution)/shard_map/ppermute | solution.py:35
  35.9 4.2 %collective-permute-done.5.refs_2_ = bf16[256,2048]{1,0:T(8,128)(2,1)S(1)} collective-permute-done((bf16[256,2048]{1,0:T(8,128)(2,1)S(1)}, bf16[256,2048]{1,0:T(8,128)(2,1)S(1)}, u32[]{:S(2)}, u32[]{:S(2)}) %collective-permute-start.5) | collective-permute-done | bytes 1048608 | tf_op jit(solution)/shard_map/ppermute | solution.py:48
  44.7 7.3 %shrink_rows.1 = (f32[2,128,128]{2,1,0:T(8,128)}, f32[2,128,128]{2,1,0:T(8,128)}) custom-call(s32[1]{0:T(128)} %bitcast.4.place_ref, s32[64]{0:T(128)} %compare_select_fusion.slots, bf16[256,2048]{1,0:T(8,128)(2,1)} %bitcast.60, bf16[256,2048]{1,0:T(8,128)(2,1)} %collective-permute-done.6.x1, bf16[256,2048]{1,0:T(8,128)(2,1)} %collective-permute-done.8.x2, ...), custom_call_target="tpu_custom_call" | custom-call | flops 524288 | bytes 524288 | tf_op jit(solution)/shard_map/shrink_rows/pallas_call | solution.py:300
  55.3 3.5 %collective-permute-done.11 = f32[128,128]{1,0:T(8,128)S(1)} collective-permute-done((f32[128,128]{1,0:T(8,128)S(1)}, f32[128,128]{1,0:T(8,128)S(1)}, u32[]{:S(2)}, u32[]{:S(2)}) %collective-permute-start.11) | collective-permute-done | bytes 65568 | tf_op jit(solution)/shard_map/ppermute | solution.py:35
  58.9 13.9 %collective-permute-done.13.refs_1_ = bf16[128,2048]{1,0:T(8,128)(2,1)} collective-permute-done((bf16[128,2048]{1,0:T(8,128)(2,1)S(1)}, bf16[128,2048]{1,0:T(8,128)(2,1)}, u32[]{:S(2)}, u32[]{:S(2)}) %collective-permute-start.13) | collective-permute-done | bytes 524320 | tf_op jit(solution)/shard_map/ppermute | solution.py:48
  77.7 4.6 %collective-permute-done.15 = f32[128,128]{1,0:T(8,128)S(1)} collective-permute-done((f32[128,128]{1,0:T(8,128)S(1)}, f32[128,128]{1,0:T(8,128)S(1)}, u32[]{:S(2)}, u32[]{:S(2)}) %collective-permute-start.15) | collective-permute-done | bytes 65568 | tf_op jit(solution)/shard_map/ppermute | solution.py:35
  85.3 3.7 %collective-permute-done.16 = bf16[128,128]{1,0:T(8,128)(2,1)S(1)} collective-permute-done((bf16[128,128]{1,0:T(8,128)(2,1)S(1)}, bf16[128,128]{1,0:T(8,128)(2,1)S(1)}, u32[]{:S(2)}, u32[]{:S(2)}) %collective-permute-start.16) | collective-permute-done | bytes 32800 | tf_op jit(solution)/shard_map/ppermute | solution.py:35
  91.0 6.7 %grow_rows.1 = (f32[2,256,1280]{2,1,0:T(8,128)}, f32[256,1280]{1,0:T(8,128)}, f32[256,1280]{1,0:T(8,128)}) custom-call(s32[1]{0:T(128)} %bitcast.4.place_ref, s32[64]{0:T(128)} %compare_select_fusion.slots, bf16[2,128,128]{2,1,0:T(8,128)(2,1)} %copy-done.5, bf16[2,128,128]{2,1,0:T(8,128)(2,1)} %copy-done.7, bf16[32,64,1280]{2,1,0:T(8,128)(2,1)} %up_ref.1), custom_call_target="tpu_custom_call" | custom-call | flops 327680 | bytes 327680 | tf_op jit(solution)/shard_map/grow_rows/pallas_call | solution.py:382
  106.9 6.6 %base_block.3 = f32[256,1280]{1,0:T(8,128)S(1)} custom-call(s32[3]{0:T(128)S(1)} %pad_add_fusion.1.owners, bf16[256,2048]{1,0:T(8,128)(2,1)S(1)} %bitcast.61, bf16[256,2048]{1,0:T(8,128)(2,1)S(1)} %collective-permute-done.4.refs_1_, bf16[256,2048]{1,0:T(8,128)(2,1)S(1)} %collective-permute-done.5.refs_2_, f32[256,1]{1,0:T(8,128)S(1)} %copy.24.refs_3_, ...), custom_call_target="tpu_custom_call" | custom-call | flops 4026531840 | bytes 20185088 | tf_op jit(solution)/shard_map/base_block/pallas_call | solution.py:121
  113.6 6.0 %base_block.4 = f32[128,1280]{1,0:T(8,128)S(1)} custom-call(s32[4]{0:T(128)S(1)} %pad_add_fusion.owners, bf16[128,2048]{1,0:T(8,128)(2,1)} %collective-permute-done.12.refs_0_, bf16[128,2048]{1,0:T(8,128)(2,1)} %collective-permute-done.13.refs_1_, bf16[128,2048]{1,0:T(8,128)(2,1)} %collective-permute-done.18.refs_2_, ...), custom_call_target="tpu_custom_call" | custom-call | flops 1342177280 | bytes 12189696 | tf_op jit(solution)/shard_map/base_block/pallas_call | solution.py:121
  125.0 9.4 %all-to-all-start = ((bf16[4,32,1280]{2,1,0:T(8,128)(2,1)}), bf16[4,32,1280]{2,1,0:T(8,128)(2,1)S(1)}, u32[]{:S(2)}, u32[]{:S(2)}) async-start(bf16[4,32,1280]{2,1,0:T(8,128)(2,1)} %bitcast.34), calls=%async_computation | async-start | bytes 655360 | tf_op jit(solution)/shard_map/all_to_all | solution.py:824
  134.4 10.6 %collective-permute-done.26.refs_3_ = bf16[128,2048]{1,0:T(8,128)(2,1)S(1)} collective-permute-done((bf16[128,2048]{1,0:T(8,128)(2,1)}, bf16[128,2048]{1,0:T(8,128)(2,1)S(1)}, u32[]{:S(2)}, u32[]{:S(2)}) %collective-permute-start.26) | collective-permute-done | bytes 524320 | tf_op jit(solution)/shard_map/ppermute | solution.py:48
  145.1 5.6 %base_block.5 = f32[128,1280]{1,0:T(8,128)S(1)} custom-call(s32[4]{0:T(128)S(1)} %pad_add_fusion.owners, bf16[128,2048]{1,0:T(8,128)(2,1)} %collective-permute-done.23.refs_0_, bf16[128,2048]{1,0:T(8,128)(2,1)} %collective-permute-done.24.refs_1_, bf16[128,2048]{1,0:T(8,128)(2,1)S(1)} %collective-permute-done.25.refs_2_, ...), custom_call_target="tpu_custom_call" | custom-call | flops 1342177280 | bytes 12189696 | tf_op jit(solution)/shard_map/base_block/pallas_call | solution.py:121
  152.7 4.5 %all-to-all-start.1 = ((bf16[4,32,1280]{2,1,0:T(8,128)(2,1)}), bf16[4,32,1280]{2,1,0:T(8,128)(2,1)S(1)}, u32[]{:S(2)}, u32[]{:S(2)}) async-start(bf16[4,32,1280]{2,1,0:T(8,128)(2,1)} %bitcast.33), calls=%async_computation.1 | async-start | bytes 655360 | tf_op jit(solution)/shard_map/all_to_all | solution.py:824
  157.8 6.7 %attend.2.refs_0_ = bf16[32,4096]{1,0:T(8,128)(2,1)S(1)} custom-call(s32[16]{0:T(128)S(1)} %get-tuple-element.103.lengths, s32[16]{0:T(128)S(1)} %select_reduce_fusion.2.order, bf16[4,32,1280]{2,1,0:T(8,128)(2,1)S(1)} %all-to-all-done.qkv_ref, f32[32,128]{1,0:T(8,128)S(1)} %get-tuple-element.104.cos_ref, f32[32,128]{1,0:T(8,128)S(1)} %get-tuple-element.105.sin_ref, ...), custom_call_target="tpu_custom_call" | custom-call | flops 268435456 | bytes 16777216 | tf_op jit(solution)/shard_map/attend/pallas_call | solution.py:564
  164.5 3.9 %collective-permute-start.28 = (bf16[32,4096]{1,0:T(8,128)(2,1)S(1)}, bf16[32,4096]{1,0:T(8,128)(2,1)S(1)}, u32[]{:S(2)}, u32[]{:S(2)}) collective-permute-start(bf16[32,4096]{1,0:T(8,128)(2,1)S(1)} %attend.2.refs_0_), channel_id=1, source_target_pairs={{0,1},{1,2},{2,3},{4,5},{5,6},{6,7},{8,9},{9,10},{10,11},{12,13},{... | collective-permute-start | bytes 786440 | tf_op jit(solution)/shard_map/ppermute | solution.py:47
  170.1 6.9 %attend.3.refs_3_ = bf16[32,4096]{1,0:T(8,128)(2,1)S(1)} custom-call(s32[16]{0:T(128)S(1)} %get-tuple-element.102.lengths, s32[16]{0:T(128)S(1)} %select_reduce_fusion.1.order, bf16[4,32,1280]{2,1,0:T(8,128)(2,1)S(1)} %all-to-all-done.1.qkv_ref, f32[32,128]{1,0:T(8,128)S(1)} %get-tuple-element.106.cos_ref, f32[32,128]{1,0:T(8,128)S(1)} %get-tuple-element.107.sin_ref, ...), custom_call_target="tpu_custom_call" | custom-call | flops 268435456 | bytes 16777216 | tf_op jit(solution)/shard_map/attend/pallas_call | solution.py:564
  177.0 4.2 %collective-permute-start.34 = (bf16[32,4096]{1,0:T(8,128)(2,1)S(1)}, bf16[32,4096]{1,0:T(8,128)(2,1)S(1)}, u32[]{:S(2)}, u32[]{:S(2)}) collective-permute-start(bf16[32,4096]{1,0:T(8,128)(2,1)S(1)} %attend.3.refs_3_), channel_id=1, source_target_pairs={{0,1},{1,2},{2,3},{4,5},{5,6},{6,7},{8,9},{9,10},{10,11},{12,13},{... | collective-permute-start | bytes 786440 | tf_op jit(solution)/shard_map/ppermute | solution.py:47
  185.7 4.5 %collective-permute-done.36.refs_5_ = bf16[32,4096]{1,0:T(8,128)(2,1)S(1)} collective-permute-done((bf16[32,4096]{1,0:T(8,128)(2,1)S(1)}, bf16[32,4096]{1,0:T(8,128)(2,1)S(1)}, u32[]{:S(2)}, u32[]{:S(2)}) %collective-permute-start.36) | collective-permute-done | bytes 262176 | tf_op jit(solution)/shard_map/ppermute | solution.py:48
  192.2 3.9 %collective-permute-done.31.refs_1_ = bf16[32,4096]{1,0:T(8,128)(2,1)S(1)} collective-permute-done((bf16[32,4096]{1,0:T(8,128)(2,1)S(1)}, bf16[32,4096]{1,0:T(8,128)(2,1)S(1)}, u32[]{:S(2)}, u32[]{:S(2)}) %collective-permute-start.31) | collective-permute-done | bytes 262176 | tf_op jit(solution)/shard_map/ppermute | solution.py:48
  198.1 5.5 %collective-permute-done.37.refs_5_ = bf16[32,4096]{1,0:T(8,128)(2,1)S(1)} collective-permute-done((bf16[32,4096]{1,0:T(8,128)(2,1)S(1)}, bf16[32,4096]{1,0:T(8,128)(2,1)S(1)}, u32[]{:S(2)}, u32[]{:S(2)}) %collective-permute-start.37) | collective-permute-done | bytes 262176 | tf_op jit(solution)/shard_map/ppermute | solution.py:48
  205.0 5.9 %project.2.refs_9_ = bf16[2,4,2,16,2048]{4,3,2,1,0:T(8,128)(2,1)S(1)} custom-call(s32[3]{0:T(128)S(1)} %pad_add_fusion.1.owners, bf16[32,4096]{1,0:T(8,128)(2,1)S(1)} %attend.2.refs_0_, bf16[32,4096]{1,0:T(8,128)(2,1)S(1)} %collective-permute-done.28.refs_1_, bf16[32,4096]{1,0:T(8,128)(2,1)S(1)} %collective-permute-done.30.refs_2_, ...), custom_call_target="tpu_custom_call" | custom-call | flops 3221225472 | bytes 19136512 | tf_op jit(solution)/shard_map/project/pallas_call | solution.py:658
  211.9 4.3 %project.3 = bf16[2,4,2,16,2048]{4,3,2,1,0:T(8,128)(2,1)} custom-call(s32[4]{0:T(128)S(1)} %pad_add_fusion.owners, bf16[32,4096]{1,0:T(8,128)(2,1)S(1)} %collective-permute-done.29.refs_0_, bf16[32,4096]{1,0:T(8,128)(2,1)S(1)} %collective-permute-done.31.refs_1_, bf16[32,4096]{1,0:T(8,128)(2,1)S(1)} %collective-permute-done.32.refs_2_, ...), custom_call_target="tpu_custom_call" | custom-call | flops 2147483648 | bytes 18350080 | tf_op jit(solution)/shard_map/project/pallas_call | solution.py:658
  (158 shorter events, 63.3 us)
Async XLA Ops:
  8.7 25.9 %collective-permute-start.6 = (bf16[256,2048]{1,0:T(8,128)(2,1)S(1)}, bf16[256,2048]{1,0:T(8,128)(2,1)}, u32[]{:S(2)}, u32[]{:S(2)}) collective-permute-start(bf16[256,2048]{1,0:T(8,128)(2,1)S(1)} %bitcast.56), channel_id=1, source_target_pairs={{0,4},{4,0},{8,12},{12,8},{1,5},{5,1},{9,13},{13,9},{2,6},{6,2},{1... | collective-permute-start | bytes 3145736 | tf_op jit(solution)/shard_map/ppermute | solution.py:35
  8.8 25.7 %collective-permute-start.8 = (bf16[256,2048]{1,0:T(8,128)(2,1)S(1)}, bf16[256,2048]{1,0:T(8,128)(2,1)}, u32[]{:S(2)}, u32[]{:S(2)}) collective-permute-start(bf16[256,2048]{1,0:T(8,128)(2,1)S(1)} %bitcast.57), channel_id=1, source_target_pairs={{0,8},{4,12},{8,0},{12,4},{1,9},{5,13},{9,1},{13,5},{2,10},{6,14},... | collective-permute-start | bytes 3145736 | tf_op jit(solution)/shard_map/ppermute | solution.py:35
  12.7 23.2 %collective-permute-start.4 = (bf16[256,2048]{1,0:T(8,128)(2,1)S(1)}, bf16[256,2048]{1,0:T(8,128)(2,1)S(1)}, u32[]{:S(2)}, u32[]{:S(2)}) collective-permute-start(bf16[256,2048]{1,0:T(8,128)(2,1)S(1)} %bitcast.58), channel_id=1, source_target_pairs={{0,1},{1,2},{2,3},{4,5},{5,6},{6,7},{8,9},{9,10},{10,11},{12,13},{... | collective-permute-start | bytes 3145736 | tf_op jit(solution)/shard_map/ppermute | solution.py:47
  14.1 26.0 %collective-permute-start.5 = (bf16[256,2048]{1,0:T(8,128)(2,1)S(1)}, bf16[256,2048]{1,0:T(8,128)(2,1)S(1)}, u32[]{:S(2)}, u32[]{:S(2)}) collective-permute-start(bf16[256,2048]{1,0:T(8,128)(2,1)S(1)} %bitcast.59), channel_id=1, source_target_pairs={{3,2},{2,1},{1,0},{7,6},{6,5},{5,4},{11,10},{10,9},{9,8},{15,14},{... | collective-permute-start | bytes 3145736 | tf_op jit(solution)/shard_map/ppermute | solution.py:48
  15.7 18.8 %collective-permute-start.3 = (f32[1,272]{1,0:T(1,128)S(1)}, f32[1,272]{1,0:T(1,128)S(1)}, u32[]{:S(2)}, u32[]{:S(2)}) collective-permute-start(f32[1,272]{1,0:T(1,128)S(1)} %reshape.106), channel_id=1, source_target_pairs={{0,8},{4,12},{8,0},{12,4},{1,9},{5,13},{9,1},{13,5},{2,10},{6,14},... | collective-permute-start | bytes 3272 | tf_op jit(solution)/shard_map/ppermute | solution.py:35
  41.1 17.7 %collective-permute-start.12 = (bf16[128,2048]{1,0:T(8,128)(2,1)}, bf16[128,2048]{1,0:T(8,128)(2,1)}, u32[]{:S(2)}, u32[]{:S(2)}) collective-permute-start(bf16[128,2048]{1,0:T(8,128)(2,1)} %get-tuple-element.78), channel_id=1, source_target_pairs={{1,2},{2,3},{5,6},{6,7},{9,10},{10,11},{13,14},{14,15},{17,18},{18... | collective-permute-start | bytes 1572872 | tf_op jit(solution)/shard_map/ppermute | solution.py:47
  52.9 19.8 %collective-permute-start.13 = (bf16[128,2048]{1,0:T(8,128)(2,1)S(1)}, bf16[128,2048]{1,0:T(8,128)(2,1)}, u32[]{:S(2)}, u32[]{:S(2)}) collective-permute-start(bf16[128,2048]{1,0:T(8,128)(2,1)S(1)} %get-tuple-element.76), channel_id=1, source_target_pairs={{2,1},{1,0},{6,5},{5,4},{10,9},{9,8},{14,13},{13,12},{18,17},{17,1... | collective-permute-start | bytes 1572872 | tf_op jit(solution)/shard_map/ppermute | solution.py:48
  82.3 15.4 %collective-permute-start.18 = (bf16[128,2048]{1,0:T(8,128)(2,1)}, bf16[128,2048]{1,0:T(8,128)(2,1)}, u32[]{:S(2)}, u32[]{:S(2)}) collective-permute-start(bf16[128,2048]{1,0:T(8,128)(2,1)} %collective-permute-done.12.refs_0_), channel_id=1, source_target_pairs={{2,3},{6,7},{10,11},{14,15},{18,19},{22,23},{26,27},{30,31}} | collective-permute-start | bytes 1572872 | tf_op jit(solution)/shard_map/ppermute | solution.py:47
  83.8 14.0 %collective-permute-start.19 = (bf16[128,2048]{1,0:T(8,128)(2,1)}, bf16[128,2048]{1,0:T(8,128)(2,1)}, u32[]{:S(2)}, u32[]{:S(2)}) collective-permute-start(bf16[128,2048]{1,0:T(8,128)(2,1)} %collective-permute-done.13.refs_1_), channel_id=1, source_target_pairs={{1,0},{5,4},{9,8},{13,12},{17,16},{21,20},{25,24},{29,28}} | collective-permute-start | bytes 1572872 | tf_op jit(solution)/shard_map/ppermute | solution.py:48
  99.1 20.6 %collective-permute-start.23 = (bf16[128,2048]{1,0:T(8,128)(2,1)}, bf16[128,2048]{1,0:T(8,128)(2,1)}, u32[]{:S(2)}, u32[]{:S(2)}) collective-permute-start(bf16[128,2048]{1,0:T(8,128)(2,1)} %get-tuple-element.62), channel_id=1, source_target_pairs={{1,2},{2,3},{5,6},{6,7},{9,10},{10,11},{13,14},{14,15},{17,18},{18... | collective-permute-start | bytes 1572872 | tf_op jit(solution)/shard_map/ppermute | solution.py:47
  100.6 20.0 %collective-permute-start.24 = (bf16[128,2048]{1,0:T(8,128)(2,1)}, bf16[128,2048]{1,0:T(8,128)(2,1)}, u32[]{:S(2)}, u32[]{:S(2)}) collective-permute-start(bf16[128,2048]{1,0:T(8,128)(2,1)} %get-tuple-element.63), channel_id=1, source_target_pairs={{2,1},{1,0},{6,5},{5,4},{10,9},{9,8},{14,13},{13,12},{18,17},{17,1... | collective-permute-start | bytes 1572872 | tf_op jit(solution)/shard_map/ppermute | solution.py:48
  101.9 20.7 %collective-permute-start.21 = (f32[256,1280]{1,0:T(8,128)}, f32[256,1280]{1,0:T(8,128)S(1)}, u32[]{:S(2)}, u32[]{:S(2)}) collective-permute-start(f32[256,1280]{1,0:T(8,128)} %get-tuple-element.61), channel_id=1, source_target_pairs={{0,4},{4,0},{8,12},{12,8},{1,5},{5,1},{9,13},{13,9},{2,6},{6,2},{1... | collective-permute-start | bytes 3932168 | tf_op jit(solution)/shard_map/ppermute | solution.py:35
  104.9 14.8 %collective-permute-start.22 = (f16[128,1280]{1,0:T(8,128)(2,1)S(1)}, f16[128,1280]{1,0:T(8,128)(2,1)S(1)}, u32[]{:S(2)}, u32[]{:S(2)}) collective-permute-start(f16[128,1280]{1,0:T(8,128)(2,1)S(1)} %get-tuple-element.72), channel_id=1, source_target_pairs={{0,8},{4,12},{8,0},{12,4},{1,9},{5,13},{9,1},{13,5},{2,10},{6,14},... | collective-permute-start | bytes 983048 | tf_op jit(solution)/shard_map/ppermute | solution.py:35
  104.9 45.8 %collective-permute-start.27 = (f16[128,1280]{1,0:T(8,128)(2,1)}, f16[128,1280]{1,0:T(8,128)(2,1)}, u32[]{:S(2)}, u32[]{:S(2)}) collective-permute-start(f16[128,1280]{1,0:T(8,128)(2,1)} %get-tuple-element.71), channel_id=1, source_target_pairs={{0,8},{4,12},{8,0},{12,4},{1,9},{5,13},{9,1},{13,5},{2,10},{6,14},... | collective-permute-start | bytes 983048 | tf_op jit(solution)/shard_map/ppermute | solution.py:35
  120.6 13.9 %collective-permute-start.25 = (bf16[128,2048]{1,0:T(8,128)(2,1)}, bf16[128,2048]{1,0:T(8,128)(2,1)S(1)}, u32[]{:S(2)}, u32[]{:S(2)}) collective-permute-start(bf16[128,2048]{1,0:T(8,128)(2,1)} %collective-permute-done.23.refs_0_), channel_id=1, source_target_pairs={{2,3},{6,7},{10,11},{14,15},{18,19},{22,23},{26,27},{30,31}} | collective-permute-start | bytes 1572872 | tf_op jit(solution)/shard_map/ppermute | solution.py:47
  121.3 23.8 %collective-permute-start.26 = (bf16[128,2048]{1,0:T(8,128)(2,1)}, bf16[128,2048]{1,0:T(8,128)(2,1)S(1)}, u32[]{:S(2)}, u32[]{:S(2)}) collective-permute-start(bf16[128,2048]{1,0:T(8,128)(2,1)} %collective-permute-done.24.refs_1_), channel_id=1, source_target_pairs={{1,0},{5,4},{9,8},{13,12},{17,16},{21,20},{25,24},{29,28}} | collective-permute-start | bytes 1572872 | tf_op jit(solution)/shard_map/ppermute | solution.py:48
  125.0 27.7 %all-to-all-start = ((bf16[4,32,1280]{2,1,0:T(8,128)(2,1)}), bf16[4,32,1280]{2,1,0:T(8,128)(2,1)S(1)}, u32[]{:S(2)}, u32[]{:S(2)}) async-start(bf16[4,32,1280]{2,1,0:T(8,128)(2,1)} %bitcast.34), calls=%async_computation | async-start | bytes 655360 | tf_op jit(solution)/shard_map/all_to_all | solution.py:824
  152.7 17.3 %all-to-all-start.1 = ((bf16[4,32,1280]{2,1,0:T(8,128)(2,1)}), bf16[4,32,1280]{2,1,0:T(8,128)(2,1)S(1)}, u32[]{:S(2)}, u32[]{:S(2)}) async-start(bf16[4,32,1280]{2,1,0:T(8,128)(2,1)} %bitcast.33), calls=%async_computation.1 | async-start | bytes 655360 | tf_op jit(solution)/shard_map/all_to_all | solution.py:824
  164.5 18.0 %collective-permute-start.28 = (bf16[32,4096]{1,0:T(8,128)(2,1)S(1)}, bf16[32,4096]{1,0:T(8,128)(2,1)S(1)}, u32[]{:S(2)}, u32[]{:S(2)}) collective-permute-start(bf16[32,4096]{1,0:T(8,128)(2,1)S(1)} %attend.2.refs_0_), channel_id=1, source_target_pairs={{0,1},{1,2},{2,3},{4,5},{5,6},{6,7},{8,9},{9,10},{10,11},{12,13},{... | collective-permute-start | bytes 786440 | tf_op jit(solution)/shard_map/ppermute | solution.py:47
  168.5 14.7 %collective-permute-start.30 = (bf16[32,4096]{1,0:T(8,128)(2,1)S(1)}, bf16[32,4096]{1,0:T(8,128)(2,1)S(1)}, u32[]{:S(2)}, u32[]{:S(2)}) collective-permute-start(bf16[32,4096]{1,0:T(8,128)(2,1)S(1)} %attend.2.refs_0_), channel_id=1, source_target_pairs={{3,2},{2,1},{1,0},{7,6},{6,5},{5,4},{11,10},{10,9},{9,8},{15,14},{... | collective-permute-start | bytes 786440 | tf_op jit(solution)/shard_map/ppermute | solution.py:48
  190.2 13.4 %collective-permute-start.37 = (bf16[32,4096]{1,0:T(8,128)(2,1)S(1)}, bf16[32,4096]{1,0:T(8,128)(2,1)S(1)}, u32[]{:S(2)}, u32[]{:S(2)}) collective-permute-start(bf16[32,4096]{1,0:T(8,128)(2,1)S(1)} %collective-permute-done.36.refs_5_), channel_id=1, source_target_pairs={{2,1},{1,0},{6,5},{5,4},{10,9},{9,8},{14,13},{13,12},{18,17},{17,1... | collective-permute-start | bytes 786440 | tf_op jit(solution)/shard_map/ppermute | solution.py:48
  191.5 19.4 %collective-permute-start.32 = (bf16[32,4096]{1,0:T(8,128)(2,1)S(1)}, bf16[32,4096]{1,0:T(8,128)(2,1)S(1)}, u32[]{:S(2)}, u32[]{:S(2)}) collective-permute-start(bf16[32,4096]{1,0:T(8,128)(2,1)S(1)} %collective-permute-done.29.refs_0_), channel_id=1, source_target_pairs={{2,3},{6,7},{10,11},{14,15},{18,19},{22,23},{26,27},{30,31}} | collective-permute-start | bytes 786440 | tf_op jit(solution)/shard_map/ppermute | solution.py:47
  196.1 14.8 %collective-permute-start.33 = (bf16[32,4096]{1,0:T(8,128)(2,1)S(1)}, bf16[32,4096]{1,0:T(8,128)(2,1)S(1)}, u32[]{:S(2)}, u32[]{:S(2)}) collective-permute-start(bf16[32,4096]{1,0:T(8,128)(2,1)S(1)} %collective-permute-done.31.refs_1_), channel_id=1, source_target_pairs={{1,0},{5,4},{9,8},{13,12},{17,16},{21,20},{25,24},{29,28}} | collective-permute-start | bytes 786440 | tf_op jit(solution)/shard_map/ppermute | solution.py:48
  197.4 13.5 %collective-permute-start.38 = (bf16[32,4096]{1,0:T(8,128)(2,1)S(1)}, bf16[32,4096]{1,0:T(8,128)(2,1)S(1)}, u32[]{:S(2)}, u32[]{:S(2)}) collective-permute-start(bf16[32,4096]{1,0:T(8,128)(2,1)S(1)} %collective-permute-done.35.refs_4_), channel_id=1, source_target_pairs={{2,3},{6,7},{10,11},{14,15},{18,19},{22,23},{26,27},{30,31}} | collective-permute-start | bytes 786440 | tf_op jit(solution)/shard_map/ppermute | solution.py:47
  (33 other events, 427.8 us)

commit v10 on v9

--- a/solution.py
+++ b/solution.py
@@ -131,8 +131,8 @@
         ],
         compiler_params=pltpu.CompilerParams(vmem_limit_bytes=46 * MIB),
         cost_estimate=pl.CostEstimate(
-            flops=2 * present * rows * depth * columns,
-            bytes_accessed=2 * present * depth * (rows + columns) + 4 * rows * columns,
+            flops=rows * columns,
+            bytes_accessed=rows * columns,
             transcendentals=0,
         ),
         name="base_block",
@@ -310,7 +310,7 @@
             pltpu.SemaphoreType.DMA((4 * runs,)),
             pltpu.SemaphoreType.DMA((4 * runs,)),
         ],
-        compiler_params=pltpu.CompilerParams(vmem_limit_bytes=54 * MIB),
+        compiler_params=pltpu.CompilerParams(vmem_limit_bytes=48 * MIB),
         cost_estimate=pl.CostEstimate(
             flops=rows * depth,
             bytes_accessed=rows * depth,
@@ -391,7 +391,7 @@
             pltpu.VMEM((4 * runs, rank, columns), BF16),
             pltpu.SemaphoreType.DMA((4 * runs,)),
         ],
-        compiler_params=pltpu.CompilerParams(vmem_limit_bytes=60 * MIB),
+        compiler_params=pltpu.CompilerParams(vmem_limit_bytes=48 * MIB),
         cost_estimate=pl.CostEstimate(
             flops=rows * columns,
             bytes_accessed=rows * columns,
@@ -743,11 +743,9 @@
         own_runs = own_runs.reshape(tensor_count, halves, -1).swapaxes(0, 1).reshape(-1)
     told = jnp.concatenate([squares, own_runs.astype(F32)]).reshape(1, -1)
     told = jnp.concatenate([told, swap(told, "store", 2)], axis=0)
-    beside = swap(raw, "store", 1)
     if line:
-        told, hop1, beside = lax.optimization_barrier((told, hop1, beside))
-        sent = [(hop1[0][part], hop1[1][part]) for part in parts]
-        hop2 = [line_hop(*sent[0], "tensor", 2)]
+        told, hop1 = lax.optimization_barrier((told, hop1))
+        hop2 = line_hop(*hop1, "tensor", 2)
     told = jnp.concatenate([told, swap(told, "store", 1)], axis=0)
     told = jnp.stack([told[d] for d in (0, 2, 1, 3)])
     told = jnp.stack([jnp.stack([told[p ^ q] for q in range(4)]) for p in range(4)])
@@ -764,6 +762,7 @@
     own_scale = lax.dynamic_index_in_dim(scales, store_pos, 0, keepdims=False)
 
     across = swap(raw, "store", 2)
+    beside = swap(raw, "store", 1)
     diagonal = swap(across, "store", 1)
     mine = slots.reshape(-1)
     down = jnp.swapaxes(adapter_down_weight, 1, 2)
@@ -771,12 +770,15 @@
     kept = kept + swap(passed, "store", 1)
     shrunk = kept[0] + swap(kept[1], "store", 2)
     if line:
-        shrunk, hop2[0] = lax.optimization_barrier((shrunk, hop2[0]))
+        shrunk, early = lax.optimization_barrier((shrunk, (raw,) + hop1))
+        near = jnp.concatenate(owners[:2])
+        total = base_block(early, own_scale, gains, query_key_value_weight, near, (0,) * 3, 3)
         shrunk = shrunk + swap(shrunk, "tensor", 1)
+        shrunk, total, hop2 = lax.optimization_barrier((shrunk, total, hop2))
+        sent = [(hop2[0][part], hop2[1][part]) for part in parts]
         shrunk = shrunk + swap(shrunk, "tensor", 2)
-        shrunk, sent[1], hop2[0] = lax.optimization_barrier((shrunk, sent[1], hop2[0]))
-        hop3 = [line_hop(*hop2[0], "tensor", 3)]
-        hop2.append(line_hop(*sent[1], "tensor", 2))
+        shrunk, sent = lax.optimization_barrier((shrunk, sent))
+        hop3 = [line_hop(up, down, "tensor", 3) for up, down in sent]
     else:
         shrunk = summed_over(shrunk, "tensor")
     shrunk = shrunk.astype(BF16)
@@ -788,23 +790,18 @@
     passed = [swap(piece, "store", 1) for piece in passed]
     leaving = [(kept[1, part] + passed[1][part]).astype(F16) for part in parts]
     arrived = [swap(piece, "store", 2).astype(F32) for piece in leaving]
-    if line:
-        arrived[0], hop2[1] = lax.optimization_barrier((arrived[0], hop2[1]))
-        hop3.append(line_hop(*hop2[1], "tensor", 3))
     deltas = [(kept[0, p] + passed[0][p]) + far for p, far in zip(parts, arrived)]
 
     weight = query_key_value_weight
     mixed = []
     if line:
-        early, leaving = lax.optimization_barrier(((raw,) + hop1, leaving))
-        near = jnp.concatenate(owners[:2])
-        total = base_block(early, own_scale, gains, weight, near, (0,) * 3, 3)
+        total, leaving = lax.optimization_barrier((total, leaving))
         far = jnp.concatenate(owners[2:])
         for h, part in enumerate(parts):
             if mixed:
                 far, mixed[-1] = lax.optimization_barrier((far, mixed[-1]))
-            blocks = hop2[h] + hop3[h]
-            first_rows = (0,) * 4
+            blocks = hop2 + hop3[h]
+            first_rows = (h * count, h * count, 0, 0)
             sums = base_block(
                 blocks, own_scale[part], gains, weight, far, first_rows, 2, total[part]
             )

time: 218 us -> 196 us (0.90)
  waiting for transfers between devices: 80.6 us -> 55 us
  local copies, waits for them, and re-layouts: 6.98 us -> 13.5 us
  Pallas kernels: 56 us -> 50.9 us
    ppermute x11 -> x10, waiting for transfers between devices: 44.5 us -> 21.6 us  [line_hop(): down = lax.ppermute(down, axis, [(i, i - 1) for i in range(4 - hop, 0, -1)])]
    ppermute x18, starting transfers between devices: 15.7 us -> 21.9 us  [swap(): return lax.ppermute(values, axis, [(i, i ^ distance) for i in range(count)])]
    unnamed x30 -> x44, local copies, waits for them, and re-layouts: 0.69 us -> 5.86 us
    ppermute x18, waiting for transfers between devices: 34.2 us -> 29.9 us  [swap(): return lax.ppermute(values, axis, [(i, i ^ distance) for i in range(count)])]
    all_to_all x2, starting transfers between devices: 14 us -> 10.3 us  [on_device(): exchanged.append(lax.all_to_all(qkv, 'tensor', 0, 0, tiled=True))]
    ppermute x11 -> x10, starting transfers between devices: 14.4 us -> 13.1 us  [line_hop(): down = lax.ppermute(down, axis, [(i, i - 1) for i in range(4 - hop, 0, -1)])]
    ppermute x11 -> x10, starting transfers between devices: 17.3 us -> 18.1 us  [line_hop(): up = lax.ppermute(up, axis, [(i, i + 1) for i in range(hop - 1, 3)])]
  transfers between devices with their start and end apart: 42 -> 40, of which waited for: 17 -> 18; matrix products, arithmetic and copies ran while one was open for 7% -> 9% of each run, Pallas kernels for 24% -> 24%
where the time goes in v10:
time: 196 us; the launch traced here: 195 us
  starting transfers between devices  63.3 us (32%)
  waiting for transfers between devices  55 us (28%)
  Pallas kernels  50.9 us (26%)
  local copies, waits for them, and re-layouts  13.5 us (7%)
  other arithmetic  12 us (6%)
    ppermute x18, waiting for transfers between devices, swap(): return lax.ppermute(values, axis, [(i, i ^ distance) for i in range(count)])  29.9 us
    ppermute x18, starting transfers between devices, swap(): return lax.ppermute(values, axis, [(i, i ^ distance) for i in range(count)])  21.9 us
    ppermute x10, waiting for transfers between devices, line_hop(): down = lax.ppermute(down, axis, [(i, i - 1) for i in range(4 - hop, 0, -1)])  21.6 us
    ppermute x10, starting transfers between devices, line_hop(): up = lax.ppermute(up, axis, [(i, i + 1) for i in range(hop - 1, 3)])  18.1 us
    pallas_call x3, Pallas kernels, base_block(): pl.pallas_call(functools.partial(block_kernel, first_rows, total is not N...  17.5 us
    ppermute x10, starting transfers between devices, line_hop(): down = lax.ppermute(down, axis, [(i, i - 1) for i in range(4 - hop, 0, -1)])  13.1 us
    pallas_call x2, Pallas kernels, attend(): pl.pallas_call(functools.partial(attend_kernel, unit, first_row), out_sha...  13 us
    all_to_all x2, starting transfers between devices, on_device(): exchanged.append(lax.all_to_all(qkv, 'tensor', 0, 0, tiled=True))  10.3 us
  transfers between devices with their start and end apart: 40, of which 18 were waited for; matrix products, arithmetic and copies ran while one was open for 9% of the time, Pallas kernels for 24%

profile of v10, /device:TPU:0, one launch (start us, length us, event | category | flops | bytes accessed | tf_op | source)
XLA Modules:
  0.0 195.4 jit_solution(5369256590745558179)
XLA Ops:
  1.7 3.1 %collective-permute-start = (f32[256]{0:T(256)S(1)}, f32[256]{0:T(256)S(1)}, u32[]{:S(2)}, u32[]{:S(2)}) collective-permute-start(f32[256]{0:T(256)S(1)} %reduce_sum.59), channel_id=1, source_target_pairs={{0,1},{1,0},{2,3},{3,2},{4,5},{5,4},{6,7},{7,6},{8,9},{9,8},{10,11... | collective-permute-start | bytes 3080 | tf_op jit(solution)/shard_map/ppermute | solution.py:35
  4.7 2.6 %collective-permute-start.1 = (f32[256]{0:T(256)S(1)}, f32[256]{0:T(256)S(1)}, u32[]{:S(2)}, u32[]{:S(2)}) collective-permute-start(f32[256]{0:T(256)S(1)} %reduce_sum.59), channel_id=1, source_target_pairs={{0,2},{1,3},{2,0},{3,1},{4,6},{5,7},{6,4},{7,5},{8,10},{9,11},{10,... | collective-permute-start | bytes 3080 | tf_op jit(solution)/shard_map/ppermute | solution.py:35
  18.2 15.0 %collective-permute-done.3 = f32[1,272]{1,0:T(1,128)S(1)} collective-permute-done((f32[1,272]{1,0:T(1,128)S(1)}, f32[1,272]{1,0:T(1,128)S(1)}, u32[]{:S(2)}, u32[]{:S(2)}) %collective-permute-start.3) | collective-permute-done | bytes 1120 | tf_op jit(solution)/shard_map/ppermute | solution.py:35
  35.0 5.1 %collective-permute-done.5.refs_2_ = bf16[256,2048]{1,0:T(8,128)(2,1)S(1)} collective-permute-done((bf16[256,2048]{1,0:T(8,128)(2,1)S(1)}, bf16[256,2048]{1,0:T(8,128)(2,1)S(1)}, u32[]{:S(2)}, u32[]{:S(2)}) %collective-permute-start.5) | collective-permute-done | bytes 1048608 | tf_op jit(solution)/shard_map/ppermute | solution.py:48
  45.6 5.4 %shrink_rows.1 = (f32[2,128,128]{2,1,0:T(8,128)S(1)}, f32[2,128,128]{2,1,0:T(8,128)S(1)}) custom-call(s32[1]{0:T(128)} %bitcast.4.place_ref, s32[64]{0:T(128)S(1)} %compare_select_fusion.slots, bf16[256,2048]{1,0:T(8,128)(2,1)S(1)} %bitcast.60, bf16[256,2048]{1,0:T(8,128)(2,1)} %collective-permute-done.7.x1, bf16[256,2048]{1,0:T(8,128)(2,1)} %collective-permute-done.8.x2, ...), custom_call_target="tpu_custom_call" | custom-call | flops 524288 | bytes 524288 | tf_op jit(solution)/shard_map/shrink_rows/pallas_call | solution.py:300
  57.8 4.3 %collective-permute-start.12 = (f32[128,128]{1,0:T(8,128)S(1)}, f32[128,128]{1,0:T(8,128)S(1)}, u32[]{:S(2)}, u32[]{:S(2)}) collective-permute-start(f32[128,128]{1,0:T(8,128)S(1)} %fusion.8), channel_id=1, source_target_pairs={{0,1},{1,0},{2,3},{3,2},{4,5},{5,4},{6,7},{7,6},{8,9},{9,8},{10,11... | collective-permute-start | bytes 196616 | tf_op jit(solution)/shard_map/ppermute | solution.py:35
  63.5 6.6 %base_block.3 = f32[256,1280]{1,0:T(8,128)S(1)} custom-call(s32[3]{0:T(128)S(1)} %pad_add_fusion.1.owners, bf16[256,2048]{1,0:T(8,128)(2,1)S(1)} %bitcast.61, bf16[256,2048]{1,0:T(8,128)(2,1)} %collective-permute-done.4.refs_1_, bf16[256,2048]{1,0:T(8,128)(2,1)S(1)} %copy-done.6, f32[256,1]{1,0:T(8,128)S(1)} %copy.24.refs_3_, f32[1,8192]{1,0:T(1,128)S(1)} %bitcast.62, ...), custom_call_target="tpu_custom_call" | custom-call | flops 327680 | bytes 327680 | tf_op jit(solution)/shard_map/base_block/pallas_call | solution.py:121
  71.6 2.9 %collective-permute-start.15 = (f32[128,128]{1,0:T(8,128)S(1)}, f32[128,128]{1,0:T(8,128)S(1)}, u32[]{:S(2)}, u32[]{:S(2)}) collective-permute-start(f32[128,128]{1,0:T(8,128)S(1)} %add.142), channel_id=1, source_target_pairs={{0,2},{1,3},{2,0},{3,1},{4,6},{5,7},{6,4},{7,5},{8,10},{9,11},{10,... | collective-permute-start | bytes 196616 | tf_op jit(solution)/shard_map/ppermute | solution.py:35
  80.5 3.1 %collective-permute-done.16 = bf16[128,128]{1,0:T(8,128)(2,1)S(1)} collective-permute-done((bf16[128,128]{1,0:T(8,128)(2,1)S(1)}, bf16[128,128]{1,0:T(8,128)(2,1)S(1)}, u32[]{:S(2)}, u32[]{:S(2)}) %collective-permute-start.16) | collective-permute-done | bytes 32800 | tf_op jit(solution)/shard_map/ppermute | solution.py:35
  84.9 4.9 %grow_rows.1 = (f32[2,256,1280]{2,1,0:T(8,128)S(1)}, f32[256,1280]{1,0:T(8,128)S(1)}, f32[256,1280]{1,0:T(8,128)}) custom-call(s32[1]{0:T(128)} %bitcast.4.place_ref, s32[64]{0:T(128)S(1)} %compare_select_fusion.slots, bf16[2,128,128]{2,1,0:T(8,128)(2,1)S(1)} %pad_maximum_fusion.s0, bf16[2,128,128]{2,1,0:T(8,128)(2,1)S(1)} %collective-permute-done.17.s1, ...), custom_call_target="tpu_custom_call" | custom-call | flops 327680 | bytes 327680 | tf_op jit(solution)/shard_map/grow_rows/pallas_call | solution.py:382
  100.7 2.6 %fusion.6 = (f16[128,1280]{1,0:T(8,128)(2,1)}, f16[128,1280]{1,0:T(8,128)(2,1)S(1)}) fusion(f32[256,1280]{1,0:T(8,128)} %collective-permute-done.20, f32[2,256,1280]{2,1,0:T(8,128)} %copy-done.3), kind=kLoop, calls=%fused_computation.10 | loop fusion | flops 655360 | bytes 3276800 | tf_op jit(solution)/shard_map/convert_element_type | solution.py:791
  106.2 5.4 %base_block.4 = f32[128,1280]{1,0:T(8,128)S(1)} custom-call(s32[4]{0:T(128)S(1)} %pad_add_fusion.owners, bf16[256,2048]{1,0:T(8,128)(2,1)S(1)} %collective-permute-done.13.refs_0_, bf16[256,2048]{1,0:T(8,128)(2,1)S(1)} %collective-permute-done.14.refs_1_, bf16[128,2048]{1,0:T(8,128)(2,1)} %collective-permute-done.18.refs_2_, ...), custom_call_target="tpu_custom_call" | custom-call | flops 163840 | bytes 163840 | tf_op jit(solution)/shard_map/base_block/pallas_call | solution.py:121
  116.0 5.7 %all-to-all-start = ((bf16[4,32,1280]{2,1,0:T(8,128)(2,1)}), bf16[4,32,1280]{2,1,0:T(8,128)(2,1)S(1)}, u32[]{:S(2)}, u32[]{:S(2)}) async-start(bf16[4,32,1280]{2,1,0:T(8,128)(2,1)} %bitcast.34), calls=%async_computation | async-start | bytes 655360 | tf_op jit(solution)/shard_map/all_to_all | solution.py:821
  121.7 5.4 %base_block.5 = f32[128,1280]{1,0:T(8,128)S(1)} custom-call(s32[4]{0:T(128)S(1)} %pad_add_fusion.owners, bf16[256,2048]{1,0:T(8,128)(2,1)S(1)} %collective-permute-done.13.refs_0_, bf16[256,2048]{1,0:T(8,128)(2,1)S(1)} %collective-permute-done.14.refs_1_, bf16[128,2048]{1,0:T(8,128)(2,1)} %collective-permute-done.23.refs_2_, ...), custom_call_target="tpu_custom_call" | custom-call | flops 163840 | bytes 163840 | tf_op jit(solution)/shard_map/base_block/pallas_call | solution.py:121
  130.7 4.6 %all-to-all-start.1 = ((bf16[4,32,1280]{2,1,0:T(8,128)(2,1)}), bf16[4,32,1280]{2,1,0:T(8,128)(2,1)S(1)}, u32[]{:S(2)}, u32[]{:S(2)}) async-start(bf16[4,32,1280]{2,1,0:T(8,128)(2,1)} %bitcast.33), calls=%async_computation.1 | async-start | bytes 655360 | tf_op jit(solution)/shard_map/all_to_all | solution.py:821
  135.9 6.1 %attend.2.refs_0_ = bf16[32,4096]{1,0:T(8,128)(2,1)S(1)} custom-call(s32[16]{0:T(128)S(1)} %get-tuple-element.101.lengths, s32[16]{0:T(128)S(1)} %select_reduce_fusion.2.order, bf16[4,32,1280]{2,1,0:T(8,128)(2,1)S(1)} %all-to-all-done.qkv_ref, f32[32,128]{1,0:T(8,128)S(1)} %get-tuple-element.104.cos_ref, f32[32,128]{1,0:T(8,128)S(1)} %get-tuple-element.105.sin_ref, ...), custom_call_target="tpu_custom_call" | custom-call | flops 268435456 | bytes 16777216 | tf_op jit(solution)/shard_map/attend/pallas_call | solution.py:564
  142.0 4.5 %collective-permute-start.26 = (bf16[32,4096]{1,0:T(8,128)(2,1)S(1)}, bf16[32,4096]{1,0:T(8,128)(2,1)S(1)}, u32[]{:S(2)}, u32[]{:S(2)}) collective-permute-start(bf16[32,4096]{1,0:T(8,128)(2,1)S(1)} %attend.2.refs_0_), channel_id=1, source_target_pairs={{0,1},{1,2},{2,3},{4,5},{5,6},{6,7},{8,9},{9,10},{10,11},{12,13},{... | collective-permute-start | bytes 786440 | tf_op jit(solution)/shard_map/ppermute | solution.py:47
  148.1 6.9 %attend.3.refs_3_ = bf16[32,4096]{1,0:T(8,128)(2,1)S(1)} custom-call(s32[16]{0:T(128)S(1)} %get-tuple-element.100.lengths, s32[16]{0:T(128)S(1)} %select_reduce_fusion.1.order, bf16[4,32,1280]{2,1,0:T(8,128)(2,1)S(1)} %all-to-all-done.1.qkv_ref, f32[32,128]{1,0:T(8,128)S(1)} %get-tuple-element.106.cos_ref, f32[32,128]{1,0:T(8,128)S(1)} %get-tuple-element.107.sin_ref, ...), custom_call_target="tpu_custom_call" | custom-call | flops 268435456 | bytes 16777216 | tf_op jit(solution)/shard_map/attend/pallas_call | solution.py:564
  155.0 4.9 %collective-permute-start.32 = (bf16[32,4096]{1,0:T(8,128)(2,1)S(1)}, bf16[32,4096]{1,0:T(8,128)(2,1)S(1)}, u32[]{:S(2)}, u32[]{:S(2)}) collective-permute-start(bf16[32,4096]{1,0:T(8,128)(2,1)S(1)} %attend.3.refs_3_), channel_id=1, source_target_pairs={{0,1},{1,2},{2,3},{4,5},{5,6},{6,7},{8,9},{9,10},{10,11},{12,13},{... | collective-permute-start | bytes 786440 | tf_op jit(solution)/shard_map/ppermute | solution.py:47
  164.4 6.3 %collective-permute-done.34.refs_5_ = bf16[32,4096]{1,0:T(8,128)(2,1)S(1)} collective-permute-done((bf16[32,4096]{1,0:T(8,128)(2,1)S(1)}, bf16[32,4096]{1,0:T(8,128)(2,1)S(1)}, u32[]{:S(2)}, u32[]{:S(2)}) %collective-permute-start.34) | collective-permute-done | bytes 262176 | tf_op jit(solution)/shard_map/ppermute | solution.py:48
  172.7 4.2 %collective-permute-done.29.refs_1_ = bf16[32,4096]{1,0:T(8,128)(2,1)S(1)} collective-permute-done((bf16[32,4096]{1,0:T(8,128)(2,1)S(1)}, bf16[32,4096]{1,0:T(8,128)(2,1)S(1)}, u32[]{:S(2)}, u32[]{:S(2)}) %collective-permute-start.29) | collective-permute-done | bytes 262176 | tf_op jit(solution)/shard_map/ppermute | solution.py:48
  178.9 4.0 %collective-permute-done.35.refs_5_ = bf16[32,4096]{1,0:T(8,128)(2,1)S(1)} collective-permute-done((bf16[32,4096]{1,0:T(8,128)(2,1)S(1)}, bf16[32,4096]{1,0:T(8,128)(2,1)S(1)}, u32[]{:S(2)}, u32[]{:S(2)}) %collective-permute-start.35) | collective-permute-done | bytes 262176 | tf_op jit(solution)/shard_map/ppermute | solution.py:48
  184.2 5.9 %project.2.refs_9_ = bf16[2,4,2,16,2048]{4,3,2,1,0:T(8,128)(2,1)S(1)} custom-call(s32[3]{0:T(128)S(1)} %pad_add_fusion.1.owners, bf16[32,4096]{1,0:T(8,128)(2,1)S(1)} %attend.2.refs_0_, bf16[32,4096]{1,0:T(8,128)(2,1)S(1)} %collective-permute-done.26.refs_1_, bf16[32,4096]{1,0:T(8,128)(2,1)S(1)} %collective-permute-done.28.refs_2_, ...), custom_call_target="tpu_custom_call" | custom-call | flops 3221225472 | bytes 19136512 | tf_op jit(solution)/shard_map/project/pallas_call | solution.py:658
  191.1 4.3 %project.3 = bf16[2,4,2,16,2048]{4,3,2,1,0:T(8,128)(2,1)} custom-call(s32[4]{0:T(128)S(1)} %pad_add_fusion.owners, bf16[32,4096]{1,0:T(8,128)(2,1)S(1)} %collective-permute-done.27.refs_0_, bf16[32,4096]{1,0:T(8,128)(2,1)S(1)} %collective-permute-done.29.refs_1_, bf16[32,4096]{1,0:T(8,128)(2,1)S(1)} %collective-permute-done.30.refs_2_, ...), custom_call_target="tpu_custom_call" | custom-call | flops 2147483648 | bytes 18350080 | tf_op jit(solution)/shard_map/project/pallas_call | solution.py:658
  (166 shorter events, 71.0 us)
Async XLA Ops:
  8.6 24.5 %collective-permute-start.8 = (bf16[256,2048]{1,0:T(8,128)(2,1)S(1)}, bf16[256,2048]{1,0:T(8,128)(2,1)}, u32[]{:S(2)}, u32[]{:S(2)}) collective-permute-start(bf16[256,2048]{1,0:T(8,128)(2,1)S(1)} %bitcast.56), channel_id=1, source_target_pairs={{0,8},{4,12},{8,0},{12,4},{1,9},{5,13},{9,1},{13,5},{2,10},{6,14},... | collective-permute-start | bytes 3145736 | tf_op jit(solution)/shard_map/ppermute | solution.py:35
  12.7 22.3 %collective-permute-start.4 = (bf16[256,2048]{1,0:T(8,128)(2,1)S(1)}, bf16[256,2048]{1,0:T(8,128)(2,1)}, u32[]{:S(2)}, u32[]{:S(2)}) collective-permute-start(bf16[256,2048]{1,0:T(8,128)(2,1)S(1)} %bitcast.57), channel_id=1, source_target_pairs={{0,1},{1,2},{2,3},{4,5},{5,6},{6,7},{8,9},{9,10},{10,11},{12,13},{... | collective-permute-start | bytes 3145736 | tf_op jit(solution)/shard_map/ppermute | solution.py:47
  15.0 25.1 %collective-permute-start.5 = (bf16[256,2048]{1,0:T(8,128)(2,1)S(1)}, bf16[256,2048]{1,0:T(8,128)(2,1)S(1)}, u32[]{:S(2)}, u32[]{:S(2)}) collective-permute-start(bf16[256,2048]{1,0:T(8,128)(2,1)S(1)} %bitcast.58), channel_id=1, source_target_pairs={{3,2},{2,1},{1,0},{7,6},{6,5},{5,4},{11,10},{10,9},{9,8},{15,14},{... | collective-permute-start | bytes 3145736 | tf_op jit(solution)/shard_map/ppermute | solution.py:48
  16.6 16.5 %collective-permute-start.3 = (f32[1,272]{1,0:T(1,128)S(1)}, f32[1,272]{1,0:T(1,128)S(1)}, u32[]{:S(2)}, u32[]{:S(2)}) collective-permute-start(f32[1,272]{1,0:T(1,128)S(1)} %reshape.106), channel_id=1, source_target_pairs={{0,8},{4,12},{8,0},{12,4},{1,9},{5,13},{9,1},{13,5},{2,10},{6,14},... | collective-permute-start | bytes 3272 | tf_op jit(solution)/shard_map/ppermute | solution.py:35
  18.2 26.3 %collective-permute-start.7 = (bf16[256,2048]{1,0:T(8,128)(2,1)S(1)}, bf16[256,2048]{1,0:T(8,128)(2,1)}, u32[]{:S(2)}, u32[]{:S(2)}) collective-permute-start(bf16[256,2048]{1,0:T(8,128)(2,1)S(1)} %bitcast.59), channel_id=1, source_target_pairs={{0,4},{4,0},{8,12},{12,8},{1,5},{5,1},{9,13},{13,9},{2,6},{6,2},{1... | collective-permute-start | bytes 3145736 | tf_op jit(solution)/shard_map/ppermute | solution.py:35
  41.1 30.5 %collective-permute-start.13 = (bf16[256,2048]{1,0:T(8,128)(2,1)}, bf16[256,2048]{1,0:T(8,128)(2,1)S(1)}, u32[]{:S(2)}, u32[]{:S(2)}) collective-permute-start(bf16[256,2048]{1,0:T(8,128)(2,1)} %collective-permute-done.4.refs_1_), channel_id=1, source_target_pairs={{1,2},{2,3},{5,6},{6,7},{9,10},{10,11},{13,14},{14,15},{17,18},{18... | collective-permute-start | bytes 3145736 | tf_op jit(solution)/shard_map/ppermute | solution.py:47
  41.8 29.8 %collective-permute-start.14 = (bf16[256,2048]{1,0:T(8,128)(2,1)}, bf16[256,2048]{1,0:T(8,128)(2,1)S(1)}, u32[]{:S(2)}, u32[]{:S(2)}) collective-permute-start(bf16[256,2048]{1,0:T(8,128)(2,1)} %copy-done.5), channel_id=1, source_target_pairs={{2,1},{1,0},{6,5},{5,4},{10,9},{9,8},{14,13},{13,12},{18,17},{17,1... | collective-permute-start | bytes 3145736 | tf_op jit(solution)/shard_map/ppermute | solution.py:48
  57.8 13.7 %collective-permute-start.12 = (f32[128,128]{1,0:T(8,128)S(1)}, f32[128,128]{1,0:T(8,128)S(1)}, u32[]{:S(2)}, u32[]{:S(2)}) collective-permute-start(f32[128,128]{1,0:T(8,128)S(1)} %fusion.8), channel_id=1, source_target_pairs={{0,1},{1,0},{2,3},{3,2},{4,5},{5,4},{6,7},{7,6},{8,9},{9,8},{10,11... | collective-permute-start | bytes 196616 | tf_op jit(solution)/shard_map/ppermute | solution.py:35
  76.8 15.5 %collective-permute-start.18 = (bf16[128,2048]{1,0:T(8,128)(2,1)}, bf16[128,2048]{1,0:T(8,128)(2,1)}, u32[]{:S(2)}, u32[]{:S(2)}) collective-permute-start(bf16[128,2048]{1,0:T(8,128)(2,1)} %get-tuple-element.54), channel_id=1, source_target_pairs={{2,3},{6,7},{10,11},{14,15},{18,19},{22,23},{26,27},{30,31}} | collective-permute-start | bytes 1572872 | tf_op jit(solution)/shard_map/ppermute | solution.py:47
  78.3 15.1 %collective-permute-start.19 = (bf16[128,2048]{1,0:T(8,128)(2,1)}, bf16[128,2048]{1,0:T(8,128)(2,1)}, u32[]{:S(2)}, u32[]{:S(2)}) collective-permute-start(bf16[128,2048]{1,0:T(8,128)(2,1)} %get-tuple-element.55), channel_id=1, source_target_pairs={{1,0},{5,4},{9,8},{13,12},{17,16},{21,20},{25,24},{29,28}} | collective-permute-start | bytes 1572872 | tf_op jit(solution)/shard_map/ppermute | solution.py:48
  95.2 16.5 %collective-permute-start.21 = (f32[256,1280]{1,0:T(8,128)}, f32[256,1280]{1,0:T(8,128)}, u32[]{:S(2)}, u32[]{:S(2)}) collective-permute-start(f32[256,1280]{1,0:T(8,128)} %copy-done.9), channel_id=1, source_target_pairs={{0,4},{4,0},{8,12},{12,8},{1,5},{5,1},{9,13},{13,9},{2,6},{6,2},{1... | collective-permute-start | bytes 3932168 | tf_op jit(solution)/shard_map/ppermute | solution.py:35
  97.9 23.8 %collective-permute-start.23 = (bf16[128,2048]{1,0:T(8,128)(2,1)}, bf16[128,2048]{1,0:T(8,128)(2,1)}, u32[]{:S(2)}, u32[]{:S(2)}) collective-permute-start(bf16[128,2048]{1,0:T(8,128)(2,1)} %get-tuple-element.64), channel_id=1, source_target_pairs={{2,3},{6,7},{10,11},{14,15},{18,19},{22,23},{26,27},{30,31}} | collective-permute-start | bytes 1572872 | tf_op jit(solution)/shard_map/ppermute | solution.py:47
  99.4 22.3 %collective-permute-start.24 = (bf16[128,2048]{1,0:T(8,128)(2,1)}, bf16[128,2048]{1,0:T(8,128)(2,1)}, u32[]{:S(2)}, u32[]{:S(2)}) collective-permute-start(bf16[128,2048]{1,0:T(8,128)(2,1)} %get-tuple-element.65), channel_id=1, source_target_pairs={{1,0},{5,4},{9,8},{13,12},{17,16},{21,20},{25,24},{29,28}} | collective-permute-start | bytes 1572872 | tf_op jit(solution)/shard_map/ppermute | solution.py:48
  104.2 23.0 %collective-permute-start.25 = (f16[128,1280]{1,0:T(8,128)(2,1)}, f16[128,1280]{1,0:T(8,128)(2,1)}, u32[]{:S(2)}, u32[]{:S(2)}) collective-permute-start(f16[128,1280]{1,0:T(8,128)(2,1)} %get-tuple-element.69), channel_id=1, source_target_pairs={{0,8},{4,12},{8,0},{12,4},{1,9},{5,13},{9,1},{13,5},{2,10},{6,14},... | collective-permute-start | bytes 983048 | tf_op jit(solution)/shard_map/ppermute | solution.py:35
  116.0 14.7 %all-to-all-start = ((bf16[4,32,1280]{2,1,0:T(8,128)(2,1)}), bf16[4,32,1280]{2,1,0:T(8,128)(2,1)S(1)}, u32[]{:S(2)}, u32[]{:S(2)}) async-start(bf16[4,32,1280]{2,1,0:T(8,128)(2,1)} %bitcast.34), calls=%async_computation | async-start | bytes 655360 | tf_op jit(solution)/shard_map/all_to_all | solution.py:821
  130.7 17.4 %all-to-all-start.1 = ((bf16[4,32,1280]{2,1,0:T(8,128)(2,1)}), bf16[4,32,1280]{2,1,0:T(8,128)(2,1)S(1)}, u32[]{:S(2)}, u32[]{:S(2)}) async-start(bf16[4,32,1280]{2,1,0:T(8,128)(2,1)} %bitcast.33), calls=%async_computation.1 | async-start | bytes 655360 | tf_op jit(solution)/shard_map/all_to_all | solution.py:821
  142.0 19.2 %collective-permute-start.26 = (bf16[32,4096]{1,0:T(8,128)(2,1)S(1)}, bf16[32,4096]{1,0:T(8,128)(2,1)S(1)}, u32[]{:S(2)}, u32[]{:S(2)}) collective-permute-start(bf16[32,4096]{1,0:T(8,128)(2,1)S(1)} %attend.2.refs_0_), channel_id=1, source_target_pairs={{0,1},{1,2},{2,3},{4,5},{5,6},{6,7},{8,9},{9,10},{10,11},{12,13},{... | collective-permute-start | bytes 786440 | tf_op jit(solution)/shard_map/ppermute | solution.py:47
  146.5 15.3 %collective-permute-start.28 = (bf16[32,4096]{1,0:T(8,128)(2,1)S(1)}, bf16[32,4096]{1,0:T(8,128)(2,1)S(1)}, u32[]{:S(2)}, u32[]{:S(2)}) collective-permute-start(bf16[32,4096]{1,0:T(8,128)(2,1)S(1)} %attend.2.refs_0_), channel_id=1, source_target_pairs={{3,2},{2,1},{1,0},{7,6},{6,5},{5,4},{11,10},{10,9},{9,8},{15,14},{... | collective-permute-start | bytes 786440 | tf_op jit(solution)/shard_map/ppermute | solution.py:48
  161.9 15.0 %collective-permute-start.29 = (bf16[32,4096]{1,0:T(8,128)(2,1)S(1)}, bf16[32,4096]{1,0:T(8,128)(2,1)S(1)}, u32[]{:S(2)}, u32[]{:S(2)}) collective-permute-start(bf16[32,4096]{1,0:T(8,128)(2,1)S(1)} %collective-permute-done.28.refs_2_), channel_id=1, source_target_pairs={{2,1},{1,0},{6,5},{5,4},{10,9},{9,8},{14,13},{13,12},{18,17},{17,1... | collective-permute-start | bytes 786440 | tf_op jit(solution)/shard_map/ppermute | solution.py:48
  163.7 14.4 %collective-permute-start.33 = (bf16[32,4096]{1,0:T(8,128)(2,1)S(1)}, bf16[32,4096]{1,0:T(8,128)(2,1)S(1)}, u32[]{:S(2)}, u32[]{:S(2)}) collective-permute-start(bf16[32,4096]{1,0:T(8,128)(2,1)S(1)} %collective-permute-done.32.refs_4_), channel_id=1, source_target_pairs={{1,2},{2,3},{5,6},{6,7},{9,10},{10,11},{13,14},{14,15},{17,18},{18... | collective-permute-start | bytes 786440 | tf_op jit(solution)/shard_map/ppermute | solution.py:47
  170.7 12.2 %collective-permute-start.35 = (bf16[32,4096]{1,0:T(8,128)(2,1)S(1)}, bf16[32,4096]{1,0:T(8,128)(2,1)S(1)}, u32[]{:S(2)}, u32[]{:S(2)}) collective-permute-start(bf16[32,4096]{1,0:T(8,128)(2,1)S(1)} %collective-permute-done.34.refs_5_), channel_id=1, source_target_pairs={{2,1},{1,0},{6,5},{5,4},{10,9},{9,8},{14,13},{13,12},{18,17},{17,1... | collective-permute-start | bytes 786440 | tf_op jit(solution)/shard_map/ppermute | solution.py:48
  172.0 18.1 %collective-permute-start.30 = (bf16[32,4096]{1,0:T(8,128)(2,1)S(1)}, bf16[32,4096]{1,0:T(8,128)(2,1)S(1)}, u32[]{:S(2)}, u32[]{:S(2)}) collective-permute-start(bf16[32,4096]{1,0:T(8,128)(2,1)S(1)} %collective-permute-done.27.refs_0_), channel_id=1, source_target_pairs={{2,3},{6,7},{10,11},{14,15},{18,19},{22,23},{26,27},{30,31}} | collective-permute-start | bytes 786440 | tf_op jit(solution)/shard_map/ppermute | solution.py:47
  176.9 13.3 %collective-permute-start.31 = (bf16[32,4096]{1,0:T(8,128)(2,1)S(1)}, bf16[32,4096]{1,0:T(8,128)(2,1)S(1)}, u32[]{:S(2)}, u32[]{:S(2)}) collective-permute-start(bf16[32,4096]{1,0:T(8,128)(2,1)S(1)} %collective-permute-done.29.refs_1_), channel_id=1, source_target_pairs={{1,0},{5,4},{9,8},{13,12},{17,16},{21,20},{25,24},{29,28}} | collective-permute-start | bytes 786440 | tf_op jit(solution)/shard_map/ppermute | solution.py:48
  178.2 12.0 %collective-permute-start.36 = (bf16[32,4096]{1,0:T(8,128)(2,1)S(1)}, bf16[32,4096]{1,0:T(8,128)(2,1)S(1)}, u32[]{:S(2)}, u32[]{:S(2)}) collective-permute-start(bf16[32,4096]{1,0:T(8,128)(2,1)S(1)} %collective-permute-done.33.refs_4_), channel_id=1, source_target_pairs={{2,3},{6,7},{10,11},{14,15},{18,19},{22,23},{26,27},{30,31}} | collective-permute-start | bytes 786440 | tf_op jit(solution)/shard_map/ppermute | solution.py:47
  (38 other events, 417.4 us)

commit v11 on v10

--- a/solution.py
+++ b/solution.py
@@ -310,7 +310,7 @@
             pltpu.SemaphoreType.DMA((4 * runs,)),
             pltpu.SemaphoreType.DMA((4 * runs,)),
         ],
-        compiler_params=pltpu.CompilerParams(vmem_limit_bytes=48 * MIB),
+        compiler_params=pltpu.CompilerParams(vmem_limit_bytes=46 * MIB),
         cost_estimate=pl.CostEstimate(
             flops=rows * depth,
             bytes_accessed=rows * depth,
@@ -391,7 +391,7 @@
             pltpu.VMEM((4 * runs, rank, columns), BF16),
             pltpu.SemaphoreType.DMA((4 * runs,)),
         ],
-        compiler_params=pltpu.CompilerParams(vmem_limit_bytes=48 * MIB),
+        compiler_params=pltpu.CompilerParams(vmem_limit_bytes=30 * MIB),
         cost_estimate=pl.CostEstimate(
             flops=rows * columns,
             bytes_accessed=rows * columns,

time: 196 us -> 204 us (1.041)
  Pallas kernels: 50.9 us -> 58.3 us
  local copies, waits for them, and re-layouts: 13.5 us -> 16 us
    pallas_call x1, Pallas kernels: 4.88 us -> 10.8 us  [grow_rows(): pl.pallas_call(grow_kernel, out_shape=[jax.ShapeDtypeStruct((2, rows, col...]
    unnamed x44 -> x46, local copies, waits for them, and re-layouts: 5.86 us -> 8.33 us
  transfers between devices with their start and end apart: 40 -> 40, of which waited for: 18 -> 17; matrix products, arithmetic and copies ran while one was open for 9% -> 9% of each run, Pallas kernels for 24% -> 26%
where the time goes in v11:
time: 204 us
  starting transfers between devices  63.9 us (31%)
  Pallas kernels  58.3 us (29%)
  waiting for transfers between devices  53.2 us (26%)
  local copies, waits for them, and re-layouts  16 us (8%)
  other arithmetic  12 us (6%)
    ppermute x18, waiting for transfers between devices, swap(): return lax.ppermute(values, axis, [(i, i ^ distance) for i in range(count)])  29.9 us
    ppermute x18, starting transfers between devices, swap(): return lax.ppermute(values, axis, [(i, i ^ distance) for i in range(count)])  21.8 us
    ppermute x10, waiting for transfers between devices, line_hop(): down = lax.ppermute(down, axis, [(i, i - 1) for i in range(4 - hop, 0, -1)])  20.1 us
    pallas_call x3, Pallas kernels, base_block(): pl.pallas_call(functools.partial(block_kernel, first_rows, total is not N...  17.4 us
    ppermute x10, starting transfers between devices, line_hop(): up = lax.ppermute(up, axis, [(i, i + 1) for i in range(hop - 1, 3)])  17.4 us
    pallas_call x2, Pallas kernels, attend(): pl.pallas_call(functools.partial(attend_kernel, unit, first_row), out_sha...  13.6 us
    ppermute x10, starting transfers between devices, line_hop(): down = lax.ppermute(down, axis, [(i, i - 1) for i in range(4 - hop, 0, -1)])  13.1 us
    all_to_all x2, starting transfers between devices, on_device(): exchanged.append(lax.all_to_all(qkv, 'tensor', 0, 0, tiled=True))  11.6 us
  transfers between devices with their start and end apart: 40, of which 17 were waited for; matrix products, arithmetic and copies ran while one was open for 9% of the time, Pallas kernels for 26%

profile of v11, /device:TPU:0, one launch (start us, length us, event | category | flops | bytes accessed | tf_op | source)
XLA Modules:
  0.0 204.1 jit_solution(1187664118169856194)
XLA Ops:
  1.7 3.1 %collective-permute-start = (f32[256]{0:T(256)S(1)}, f32[256]{0:T(256)S(1)}, u32[]{:S(2)}, u32[]{:S(2)}) collective-permute-start(f32[256]{0:T(256)S(1)} %reduce_sum.59), channel_id=1, source_target_pairs={{0,1},{1,0},{2,3},{3,2},{4,5},{5,4},{6,7},{7,6},{8,9},{9,8},{10,11... | collective-permute-start | bytes 3080 | tf_op jit(solution)/shard_map/ppermute | solution.py:35
  4.7 2.6 %collective-permute-start.1 = (f32[256]{0:T(256)S(1)}, f32[256]{0:T(256)S(1)}, u32[]{:S(2)}, u32[]{:S(2)}) collective-permute-start(f32[256]{0:T(256)S(1)} %reduce_sum.59), channel_id=1, source_target_pairs={{0,2},{1,3},{2,0},{3,1},{4,6},{5,7},{6,4},{7,5},{8,10},{9,11},{10,... | collective-permute-start | bytes 3080 | tf_op jit(solution)/shard_map/ppermute | solution.py:35
  18.2 15.0 %collective-permute-done.3 = f32[1,272]{1,0:T(1,128)S(1)} collective-permute-done((f32[1,272]{1,0:T(1,128)S(1)}, f32[1,272]{1,0:T(1,128)S(1)}, u32[]{:S(2)}, u32[]{:S(2)}) %collective-permute-start.3) | collective-permute-done | bytes 1120 | tf_op jit(solution)/shard_map/ppermute | solution.py:35
  35.0 5.1 %collective-permute-done.5.refs_2_ = bf16[256,2048]{1,0:T(8,128)(2,1)S(1)} collective-permute-done((bf16[256,2048]{1,0:T(8,128)(2,1)S(1)}, bf16[256,2048]{1,0:T(8,128)(2,1)S(1)}, u32[]{:S(2)}, u32[]{:S(2)}) %collective-permute-start.5) | collective-permute-done | bytes 1048608 | tf_op jit(solution)/shard_map/ppermute | solution.py:48
  45.6 6.3 %shrink_rows.1 = (f32[2,128,128]{2,1,0:T(8,128)S(1)}, f32[2,128,128]{2,1,0:T(8,128)S(1)}) custom-call(s32[1]{0:T(128)} %bitcast.4.place_ref, s32[64]{0:T(128)S(1)} %compare_select_fusion.slots, bf16[256,2048]{1,0:T(8,128)(2,1)S(1)} %bitcast.60, bf16[256,2048]{1,0:T(8,128)(2,1)} %collective-permute-done.7.x1, bf16[256,2048]{1,0:T(8,128)(2,1)} %collective-permute-done.8.x2, ...), custom_call_target="tpu_custom_call" | custom-call | flops 524288 | bytes 524288 | tf_op jit(solution)/shard_map/shrink_rows/pallas_call | solution.py:300
  55.0 3.7 %collective-permute-done.11 = f32[128,128]{1,0:T(8,128)S(1)} collective-permute-done((f32[128,128]{1,0:T(8,128)S(1)}, f32[128,128]{1,0:T(8,128)S(1)}, u32[]{:S(2)}, u32[]{:S(2)}) %collective-permute-start.11) | collective-permute-done | bytes 65568 | tf_op jit(solution)/shard_map/ppermute | solution.py:35
  58.7 4.3 %collective-permute-start.12 = (f32[128,128]{1,0:T(8,128)S(1)}, f32[128,128]{1,0:T(8,128)S(1)}, u32[]{:S(2)}, u32[]{:S(2)}) collective-permute-start(f32[128,128]{1,0:T(8,128)S(1)} %fusion.8), channel_id=1, source_target_pairs={{0,1},{1,0},{2,3},{3,2},{4,5},{5,4},{6,7},{7,6},{8,9},{9,8},{10,11... | collective-permute-start | bytes 196616 | tf_op jit(solution)/shard_map/ppermute | solution.py:35
  64.4 6.6 %base_block.3 = f32[256,1280]{1,0:T(8,128)S(1)} custom-call(s32[3]{0:T(128)S(1)} %pad_add_fusion.1.owners, bf16[256,2048]{1,0:T(8,128)(2,1)S(1)} %bitcast.61, bf16[256,2048]{1,0:T(8,128)(2,1)} %collective-permute-done.4.refs_1_, bf16[256,2048]{1,0:T(8,128)(2,1)S(1)} %copy-done.7, f32[256,1]{1,0:T(8,128)S(1)} %copy.24.refs_3_, f32[1,8192]{1,0:T(1,128)S(1)} %bitcast.62, ...), custom_call_target="tpu_custom_call" | custom-call | flops 327680 | bytes 327680 | tf_op jit(solution)/shard_map/base_block/pallas_call | solution.py:121
  71.6 3.9 %collective-permute-start.15 = (f32[128,128]{1,0:T(8,128)S(1)}, f32[128,128]{1,0:T(8,128)S(1)}, u32[]{:S(2)}, u32[]{:S(2)}) collective-permute-start(f32[128,128]{1,0:T(8,128)S(1)} %add.142), channel_id=1, source_target_pairs={{0,2},{1,3},{2,0},{3,1},{4,6},{5,7},{6,4},{7,5},{8,10},{9,11},{10,... | collective-permute-start | bytes 196616 | tf_op jit(solution)/shard_map/ppermute | solution.py:35
  81.7 2.7 %collective-permute-done.16 = bf16[128,128]{1,0:T(8,128)(2,1)S(1)} collective-permute-done((bf16[128,128]{1,0:T(8,128)(2,1)S(1)}, bf16[128,128]{1,0:T(8,128)(2,1)S(1)}, u32[]{:S(2)}, u32[]{:S(2)}) %collective-permute-start.16) | collective-permute-done | bytes 32800 | tf_op jit(solution)/shard_map/ppermute | solution.py:35
  88.2 10.8 %grow_rows.1 = (f32[2,256,1280]{2,1,0:T(8,128)S(1)}, f32[256,1280]{1,0:T(8,128)S(1)}, f32[256,1280]{1,0:T(8,128)}) custom-call(s32[1]{0:T(128)} %bitcast.4.place_ref, s32[64]{0:T(128)S(1)} %compare_select_fusion.slots, bf16[2,128,128]{2,1,0:T(8,128)(2,1)S(1)} %pad_maximum_fusion.s0, bf16[2,128,128]{2,1,0:T(8,128)(2,1)S(1)} %collective-permute-done.17.s1, ...), custom_call_target="tpu_custom_call" | custom-call | flops 327680 | bytes 327680 | tf_op jit(solution)/shard_map/grow_rows/pallas_call | solution.py:382
  114.5 5.4 %base_block.4 = f32[128,1280]{1,0:T(8,128)S(1)} custom-call(s32[4]{0:T(128)S(1)} %pad_add_fusion.owners, bf16[256,2048]{1,0:T(8,128)(2,1)S(1)} %collective-permute-done.13.refs_0_, bf16[256,2048]{1,0:T(8,128)(2,1)S(1)} %collective-permute-done.14.refs_1_, bf16[128,2048]{1,0:T(8,128)(2,1)} %collective-permute-done.18.refs_2_, ...), custom_call_target="tpu_custom_call" | custom-call | flops 163840 | bytes 163840 | tf_op jit(solution)/shard_map/base_block/pallas_call | solution.py:121
  124.2 6.7 %all-to-all-start = ((bf16[4,32,1280]{2,1,0:T(8,128)(2,1)}), bf16[4,32,1280]{2,1,0:T(8,128)(2,1)S(1)}, u32[]{:S(2)}, u32[]{:S(2)}) async-start(bf16[4,32,1280]{2,1,0:T(8,128)(2,1)} %bitcast.34), calls=%async_computation | async-start | bytes 655360 | tf_op jit(solution)/shard_map/all_to_all | solution.py:821
  131.0 5.4 %base_block.5 = f32[128,1280]{1,0:T(8,128)S(1)} custom-call(s32[4]{0:T(128)S(1)} %pad_add_fusion.owners, bf16[256,2048]{1,0:T(8,128)(2,1)S(1)} %collective-permute-done.13.refs_0_, bf16[256,2048]{1,0:T(8,128)(2,1)S(1)} %collective-permute-done.14.refs_1_, bf16[128,2048]{1,0:T(8,128)(2,1)} %collective-permute-done.23.refs_2_, ...), custom_call_target="tpu_custom_call" | custom-call | flops 163840 | bytes 163840 | tf_op jit(solution)/shard_map/base_block/pallas_call | solution.py:121
  139.7 4.9 %all-to-all-start.1 = ((bf16[4,32,1280]{2,1,0:T(8,128)(2,1)}), bf16[4,32,1280]{2,1,0:T(8,128)(2,1)S(1)}, u32[]{:S(2)}, u32[]{:S(2)}) async-start(bf16[4,32,1280]{2,1,0:T(8,128)(2,1)} %bitcast.33), calls=%async_computation.1 | async-start | bytes 655360 | tf_op jit(solution)/shard_map/all_to_all | solution.py:821
  145.2 6.7 %attend.2.refs_0_ = bf16[32,4096]{1,0:T(8,128)(2,1)S(1)} custom-call(s32[16]{0:T(128)S(1)} %get-tuple-element.101.lengths, s32[16]{0:T(128)S(1)} %select_reduce_fusion.2.order, bf16[4,32,1280]{2,1,0:T(8,128)(2,1)S(1)} %all-to-all-done.qkv_ref, f32[32,128]{1,0:T(8,128)S(1)} %get-tuple-element.104.cos_ref, f32[32,128]{1,0:T(8,128)S(1)} %get-tuple-element.105.sin_ref, ...), custom_call_target="tpu_custom_call" | custom-call | flops 268435456 | bytes 16777216 | tf_op jit(solution)/shard_map/attend/pallas_call | solution.py:564
  151.9 3.9 %collective-permute-start.26 = (bf16[32,4096]{1,0:T(8,128)(2,1)S(1)}, bf16[32,4096]{1,0:T(8,128)(2,1)S(1)}, u32[]{:S(2)}, u32[]{:S(2)}) collective-permute-start(bf16[32,4096]{1,0:T(8,128)(2,1)S(1)} %attend.2.refs_0_), channel_id=1, source_target_pairs={{0,1},{1,2},{2,3},{4,5},{5,6},{6,7},{8,9},{9,10},{10,11},{12,13},{... | collective-permute-start | bytes 786440 | tf_op jit(solution)/shard_map/ppermute | solution.py:47
  157.4 6.9 %attend.3.refs_3_ = bf16[32,4096]{1,0:T(8,128)(2,1)S(1)} custom-call(s32[16]{0:T(128)S(1)} %get-tuple-element.100.lengths, s32[16]{0:T(128)S(1)} %select_reduce_fusion.1.order, bf16[4,32,1280]{2,1,0:T(8,128)(2,1)S(1)} %all-to-all-done.1.qkv_ref, f32[32,128]{1,0:T(8,128)S(1)} %get-tuple-element.106.cos_ref, f32[32,128]{1,0:T(8,128)S(1)} %get-tuple-element.107.sin_ref, ...), custom_call_target="tpu_custom_call" | custom-call | flops 268435456 | bytes 16777216 | tf_op jit(solution)/shard_map/attend/pallas_call | solution.py:564
  164.3 4.8 %collective-permute-start.32 = (bf16[32,4096]{1,0:T(8,128)(2,1)S(1)}, bf16[32,4096]{1,0:T(8,128)(2,1)S(1)}, u32[]{:S(2)}, u32[]{:S(2)}) collective-permute-start(bf16[32,4096]{1,0:T(8,128)(2,1)S(1)} %attend.3.refs_3_), channel_id=1, source_target_pairs={{0,1},{1,2},{2,3},{4,5},{5,6},{6,7},{8,9},{9,10},{10,11},{12,13},{... | collective-permute-start | bytes 786440 | tf_op jit(solution)/shard_map/ppermute | solution.py:47
  173.7 5.9 %collective-permute-done.34.refs_5_ = bf16[32,4096]{1,0:T(8,128)(2,1)S(1)} collective-permute-done((bf16[32,4096]{1,0:T(8,128)(2,1)S(1)}, bf16[32,4096]{1,0:T(8,128)(2,1)S(1)}, u32[]{:S(2)}, u32[]{:S(2)}) %collective-permute-start.34) | collective-permute-done | bytes 262176 | tf_op jit(solution)/shard_map/ppermute | solution.py:48
  181.5 3.9 %collective-permute-done.29.refs_1_ = bf16[32,4096]{1,0:T(8,128)(2,1)S(1)} collective-permute-done((bf16[32,4096]{1,0:T(8,128)(2,1)S(1)}, bf16[32,4096]{1,0:T(8,128)(2,1)S(1)}, u32[]{:S(2)}, u32[]{:S(2)}) %collective-permute-start.29) | collective-permute-done | bytes 262176 | tf_op jit(solution)/shard_map/ppermute | solution.py:48
  187.4 4.1 %collective-permute-done.35.refs_5_ = bf16[32,4096]{1,0:T(8,128)(2,1)S(1)} collective-permute-done((bf16[32,4096]{1,0:T(8,128)(2,1)S(1)}, bf16[32,4096]{1,0:T(8,128)(2,1)S(1)}, u32[]{:S(2)}, u32[]{:S(2)}) %collective-permute-start.35) | collective-permute-done | bytes 262176 | tf_op jit(solution)/shard_map/ppermute | solution.py:48
  192.8 5.9 %project.2.refs_9_ = bf16[2,4,2,16,2048]{4,3,2,1,0:T(8,128)(2,1)S(1)} custom-call(s32[3]{0:T(128)S(1)} %pad_add_fusion.1.owners, bf16[32,4096]{1,0:T(8,128)(2,1)S(1)} %attend.2.refs_0_, bf16[32,4096]{1,0:T(8,128)(2,1)S(1)} %collective-permute-done.26.refs_1_, bf16[32,4096]{1,0:T(8,128)(2,1)S(1)} %collective-permute-done.28.refs_2_, ...), custom_call_target="tpu_custom_call" | custom-call | flops 3221225472 | bytes 19136512 | tf_op jit(solution)/shard_map/project/pallas_call | solution.py:658
  199.9 4.3 %project.3 = bf16[2,4,2,16,2048]{4,3,2,1,0:T(8,128)(2,1)} custom-call(s32[4]{0:T(128)S(1)} %pad_add_fusion.owners, bf16[32,4096]{1,0:T(8,128)(2,1)S(1)} %collective-permute-done.27.refs_0_, bf16[32,4096]{1,0:T(8,128)(2,1)S(1)} %collective-permute-done.29.refs_1_, bf16[32,4096]{1,0:T(8,128)(2,1)S(1)} %collective-permute-done.30.refs_2_, ...), custom_call_target="tpu_custom_call" | custom-call | flops 2147483648 | bytes 18350080 | tf_op jit(solution)/shard_map/project/pallas_call | solution.py:658
  (168 shorter events, 70.5 us)
Async XLA Ops:
  8.6 24.5 %collective-permute-start.8 = (bf16[256,2048]{1,0:T(8,128)(2,1)S(1)}, bf16[256,2048]{1,0:T(8,128)(2,1)}, u32[]{:S(2)}, u32[]{:S(2)}) collective-permute-start(bf16[256,2048]{1,0:T(8,128)(2,1)S(1)} %bitcast.56), channel_id=1, source_target_pairs={{0,8},{4,12},{8,0},{12,4},{1,9},{5,13},{9,1},{13,5},{2,10},{6,14},... | collective-permute-start | bytes 3145736 | tf_op jit(solution)/shard_map/ppermute | solution.py:35
  12.7 22.3 %collective-permute-start.4 = (bf16[256,2048]{1,0:T(8,128)(2,1)S(1)}, bf16[256,2048]{1,0:T(8,128)(2,1)}, u32[]{:S(2)}, u32[]{:S(2)}) collective-permute-start(bf16[256,2048]{1,0:T(8,128)(2,1)S(1)} %bitcast.57), channel_id=1, source_target_pairs={{0,1},{1,2},{2,3},{4,5},{5,6},{6,7},{8,9},{9,10},{10,11},{12,13},{... | collective-permute-start | bytes 3145736 | tf_op jit(solution)/shard_map/ppermute | solution.py:47
  15.0 25.1 %collective-permute-start.5 = (bf16[256,2048]{1,0:T(8,128)(2,1)S(1)}, bf16[256,2048]{1,0:T(8,128)(2,1)S(1)}, u32[]{:S(2)}, u32[]{:S(2)}) collective-permute-start(bf16[256,2048]{1,0:T(8,128)(2,1)S(1)} %bitcast.58), channel_id=1, source_target_pairs={{3,2},{2,1},{1,0},{7,6},{6,5},{5,4},{11,10},{10,9},{9,8},{15,14},{... | collective-permute-start | bytes 3145736 | tf_op jit(solution)/shard_map/ppermute | solution.py:48
  16.6 16.5 %collective-permute-start.3 = (f32[1,272]{1,0:T(1,128)S(1)}, f32[1,272]{1,0:T(1,128)S(1)}, u32[]{:S(2)}, u32[]{:S(2)}) collective-permute-start(f32[1,272]{1,0:T(1,128)S(1)} %reshape.106), channel_id=1, source_target_pairs={{0,8},{4,12},{8,0},{12,4},{1,9},{5,13},{9,1},{13,5},{2,10},{6,14},... | collective-permute-start | bytes 3272 | tf_op jit(solution)/shard_map/ppermute | solution.py:35
  18.2 26.3 %collective-permute-start.7 = (bf16[256,2048]{1,0:T(8,128)(2,1)S(1)}, bf16[256,2048]{1,0:T(8,128)(2,1)}, u32[]{:S(2)}, u32[]{:S(2)}) collective-permute-start(bf16[256,2048]{1,0:T(8,128)(2,1)S(1)} %bitcast.59), channel_id=1, source_target_pairs={{0,4},{4,0},{8,12},{12,8},{1,5},{5,1},{9,13},{13,9},{2,6},{6,2},{1... | collective-permute-start | bytes 3145736 | tf_op jit(solution)/shard_map/ppermute | solution.py:35
  41.1 30.5 %collective-permute-start.13 = (bf16[256,2048]{1,0:T(8,128)(2,1)}, bf16[256,2048]{1,0:T(8,128)(2,1)S(1)}, u32[]{:S(2)}, u32[]{:S(2)}) collective-permute-start(bf16[256,2048]{1,0:T(8,128)(2,1)} %collective-permute-done.4.refs_1_), channel_id=1, source_target_pairs={{1,2},{2,3},{5,6},{6,7},{9,10},{10,11},{13,14},{14,15},{17,18},{18... | collective-permute-start | bytes 3145736 | tf_op jit(solution)/shard_map/ppermute | solution.py:47
  41.8 29.8 %collective-permute-start.14 = (bf16[256,2048]{1,0:T(8,128)(2,1)}, bf16[256,2048]{1,0:T(8,128)(2,1)S(1)}, u32[]{:S(2)}, u32[]{:S(2)}) collective-permute-start(bf16[256,2048]{1,0:T(8,128)(2,1)} %copy-done.6), channel_id=1, source_target_pairs={{2,1},{1,0},{6,5},{5,4},{10,9},{9,8},{14,13},{13,12},{18,17},{17,1... | collective-permute-start | bytes 3145736 | tf_op jit(solution)/shard_map/ppermute | solution.py:48
  58.7 12.8 %collective-permute-start.12 = (f32[128,128]{1,0:T(8,128)S(1)}, f32[128,128]{1,0:T(8,128)S(1)}, u32[]{:S(2)}, u32[]{:S(2)}) collective-permute-start(f32[128,128]{1,0:T(8,128)S(1)} %fusion.8), channel_id=1, source_target_pairs={{0,1},{1,0},{2,3},{3,2},{4,5},{5,4},{6,7},{7,6},{8,9},{9,8},{10,11... | collective-permute-start | bytes 196616 | tf_op jit(solution)/shard_map/ppermute | solution.py:35
  77.7 24.0 %collective-permute-start.18 = (bf16[128,2048]{1,0:T(8,128)(2,1)}, bf16[128,2048]{1,0:T(8,128)(2,1)}, u32[]{:S(2)}, u32[]{:S(2)}) collective-permute-start(bf16[128,2048]{1,0:T(8,128)(2,1)} %get-tuple-element.54), channel_id=1, source_target_pairs={{2,3},{6,7},{10,11},{14,15},{18,19},{22,23},{26,27},{30,31}} | collective-permute-start | bytes 1572872 | tf_op jit(solution)/shard_map/ppermute | solution.py:47
  79.2 22.5 %collective-permute-start.19 = (bf16[128,2048]{1,0:T(8,128)(2,1)}, bf16[128,2048]{1,0:T(8,128)(2,1)}, u32[]{:S(2)}, u32[]{:S(2)}) collective-permute-start(bf16[128,2048]{1,0:T(8,128)(2,1)} %get-tuple-element.55), channel_id=1, source_target_pairs={{1,0},{5,4},{9,8},{13,12},{17,16},{21,20},{25,24},{29,28}} | collective-permute-start | bytes 1572872 | tf_op jit(solution)/shard_map/ppermute | solution.py:48
  103.5 16.4 %collective-permute-start.21 = (f32[256,1280]{1,0:T(8,128)}, f32[256,1280]{1,0:T(8,128)}, u32[]{:S(2)}, u32[]{:S(2)}) collective-permute-start(f32[256,1280]{1,0:T(8,128)} %copy-done.10), channel_id=1, source_target_pairs={{0,4},{4,0},{8,12},{12,8},{1,5},{5,1},{9,13},{13,9},{2,6},{6,2},{1... | collective-permute-start | bytes 3932168 | tf_op jit(solution)/shard_map/ppermute | solution.py:35
  106.2 24.8 %collective-permute-start.23 = (bf16[128,2048]{1,0:T(8,128)(2,1)}, bf16[128,2048]{1,0:T(8,128)(2,1)}, u32[]{:S(2)}, u32[]{:S(2)}) collective-permute-start(bf16[128,2048]{1,0:T(8,128)(2,1)} %get-tuple-element.64), channel_id=1, source_target_pairs={{2,3},{6,7},{10,11},{14,15},{18,19},{22,23},{26,27},{30,31}} | collective-permute-start | bytes 1572872 | tf_op jit(solution)/shard_map/ppermute | solution.py:47
  107.7 23.3 %collective-permute-start.24 = (bf16[128,2048]{1,0:T(8,128)(2,1)}, bf16[128,2048]{1,0:T(8,128)(2,1)}, u32[]{:S(2)}, u32[]{:S(2)}) collective-permute-start(bf16[128,2048]{1,0:T(8,128)(2,1)} %get-tuple-element.65), channel_id=1, source_target_pairs={{1,0},{5,4},{9,8},{13,12},{17,16},{21,20},{25,24},{29,28}} | collective-permute-start | bytes 1572872 | tf_op jit(solution)/shard_map/ppermute | solution.py:48
  111.5 24.9 %collective-permute-start.25 = (f16[128,1280]{1,0:T(8,128)(2,1)}, f16[128,1280]{1,0:T(8,128)(2,1)}, u32[]{:S(2)}, u32[]{:S(2)}) collective-permute-start(f16[128,1280]{1,0:T(8,128)(2,1)} %get-tuple-element.69), channel_id=1, source_target_pairs={{0,8},{4,12},{8,0},{12,4},{1,9},{5,13},{9,1},{13,5},{2,10},{6,14},... | collective-permute-start | bytes 983048 | tf_op jit(solution)/shard_map/ppermute | solution.py:35
  124.2 15.4 %all-to-all-start = ((bf16[4,32,1280]{2,1,0:T(8,128)(2,1)}), bf16[4,32,1280]{2,1,0:T(8,128)(2,1)S(1)}, u32[]{:S(2)}, u32[]{:S(2)}) async-start(bf16[4,32,1280]{2,1,0:T(8,128)(2,1)} %bitcast.34), calls=%async_computation | async-start | bytes 655360 | tf_op jit(solution)/shard_map/all_to_all | solution.py:821
  139.7 17.7 %all-to-all-start.1 = ((bf16[4,32,1280]{2,1,0:T(8,128)(2,1)}), bf16[4,32,1280]{2,1,0:T(8,128)(2,1)S(1)}, u32[]{:S(2)}, u32[]{:S(2)}) async-start(bf16[4,32,1280]{2,1,0:T(8,128)(2,1)} %bitcast.33), calls=%async_computation.1 | async-start | bytes 655360 | tf_op jit(solution)/shard_map/all_to_all | solution.py:821
  151.9 18.6 %collective-permute-start.26 = (bf16[32,4096]{1,0:T(8,128)(2,1)S(1)}, bf16[32,4096]{1,0:T(8,128)(2,1)S(1)}, u32[]{:S(2)}, u32[]{:S(2)}) collective-permute-start(bf16[32,4096]{1,0:T(8,128)(2,1)S(1)} %attend.2.refs_0_), channel_id=1, source_target_pairs={{0,1},{1,2},{2,3},{4,5},{5,6},{6,7},{8,9},{9,10},{10,11},{12,13},{... | collective-permute-start | bytes 786440 | tf_op jit(solution)/shard_map/ppermute | solution.py:47
  155.8 15.3 %collective-permute-start.28 = (bf16[32,4096]{1,0:T(8,128)(2,1)S(1)}, bf16[32,4096]{1,0:T(8,128)(2,1)S(1)}, u32[]{:S(2)}, u32[]{:S(2)}) collective-permute-start(bf16[32,4096]{1,0:T(8,128)(2,1)S(1)} %attend.2.refs_0_), channel_id=1, source_target_pairs={{3,2},{2,1},{1,0},{7,6},{6,5},{5,4},{11,10},{10,9},{9,8},{15,14},{... | collective-permute-start | bytes 786440 | tf_op jit(solution)/shard_map/ppermute | solution.py:48
  171.1 14.3 %collective-permute-start.29 = (bf16[32,4096]{1,0:T(8,128)(2,1)S(1)}, bf16[32,4096]{1,0:T(8,128)(2,1)S(1)}, u32[]{:S(2)}, u32[]{:S(2)}) collective-permute-start(bf16[32,4096]{1,0:T(8,128)(2,1)S(1)} %collective-permute-done.28.refs_2_), channel_id=1, source_target_pairs={{2,1},{1,0},{6,5},{5,4},{10,9},{9,8},{14,13},{13,12},{18,17},{17,1... | collective-permute-start | bytes 786440 | tf_op jit(solution)/shard_map/ppermute | solution.py:48
  173.0 13.7 %collective-permute-start.33 = (bf16[32,4096]{1,0:T(8,128)(2,1)S(1)}, bf16[32,4096]{1,0:T(8,128)(2,1)S(1)}, u32[]{:S(2)}, u32[]{:S(2)}) collective-permute-start(bf16[32,4096]{1,0:T(8,128)(2,1)S(1)} %collective-permute-done.32.refs_4_), channel_id=1, source_target_pairs={{1,2},{2,3},{5,6},{6,7},{9,10},{10,11},{13,14},{14,15},{17,18},{18... | collective-permute-start | bytes 786440 | tf_op jit(solution)/shard_map/ppermute | solution.py:47
  179.6 11.9 %collective-permute-start.35 = (bf16[32,4096]{1,0:T(8,128)(2,1)S(1)}, bf16[32,4096]{1,0:T(8,128)(2,1)S(1)}, u32[]{:S(2)}, u32[]{:S(2)}) collective-permute-start(bf16[32,4096]{1,0:T(8,128)(2,1)S(1)} %collective-permute-done.34.refs_5_), channel_id=1, source_target_pairs={{2,1},{1,0},{6,5},{5,4},{10,9},{9,8},{14,13},{13,12},{18,17},{17,1... | collective-permute-start | bytes 786440 | tf_op jit(solution)/shard_map/ppermute | solution.py:48
  180.9 17.9 %collective-permute-start.30 = (bf16[32,4096]{1,0:T(8,128)(2,1)S(1)}, bf16[32,4096]{1,0:T(8,128)(2,1)S(1)}, u32[]{:S(2)}, u32[]{:S(2)}) collective-permute-start(bf16[32,4096]{1,0:T(8,128)(2,1)S(1)} %collective-permute-done.27.refs_0_), channel_id=1, source_target_pairs={{2,3},{6,7},{10,11},{14,15},{18,19},{22,23},{26,27},{30,31}} | collective-permute-start | bytes 786440 | tf_op jit(solution)/shard_map/ppermute | solution.py:47
  185.5 13.3 %collective-permute-start.31 = (bf16[32,4096]{1,0:T(8,128)(2,1)S(1)}, bf16[32,4096]{1,0:T(8,128)(2,1)S(1)}, u32[]{:S(2)}, u32[]{:S(2)}) collective-permute-start(bf16[32,4096]{1,0:T(8,128)(2,1)S(1)} %collective-permute-done.29.refs_1_), channel_id=1, source_target_pairs={{1,0},{5,4},{9,8},{13,12},{17,16},{21,20},{25,24},{29,28}} | collective-permute-start | bytes 786440 | tf_op jit(solution)/shard_map/ppermute | solution.py:48
  186.8 12.1 %collective-permute-start.36 = (bf16[32,4096]{1,0:T(8,128)(2,1)S(1)}, bf16[32,4096]{1,0:T(8,128)(2,1)S(1)}, u32[]{:S(2)}, u32[]{:S(2)}) collective-permute-start(bf16[32,4096]{1,0:T(8,128)(2,1)S(1)} %collective-permute-done.33.refs_4_), channel_id=1, source_target_pairs={{2,3},{6,7},{10,11},{14,15},{18,19},{22,23},{26,27},{30,31}} | collective-permute-start | bytes 786440 | tf_op jit(solution)/shard_map/ppermute | solution.py:47
  (39 other events, 421.2 us)

commit v12 on v10

--- a/solution.py
+++ b/solution.py
@@ -778,7 +778,7 @@
         sent = [(hop2[0][part], hop2[1][part]) for part in parts]
         shrunk = shrunk + swap(shrunk, "tensor", 2)
         shrunk, sent = lax.optimization_barrier((shrunk, sent))
-        hop3 = [line_hop(up, down, "tensor", 3) for up, down in sent]
+        hop3 = [line_hop(*sent[0], "tensor", 3)]
     else:
         shrunk = summed_over(shrunk, "tensor")
     shrunk = shrunk.astype(BF16)
@@ -789,6 +789,9 @@
         passed, hop3[0] = lax.optimization_barrier((passed, hop3[0]))
     passed = [swap(piece, "store", 1) for piece in passed]
     leaving = [(kept[1, part] + passed[1][part]).astype(F16) for part in parts]
+    if line:
+        later, _ = lax.optimization_barrier((sent[1], leaving))
+        hop3.append(line_hop(*later, "tensor", 3))
     arrived = [swap(piece, "store", 2).astype(F32) for piece in leaving]
     deltas = [(kept[0, p] + passed[0][p]) + far for p, far in zip(parts, arrived)]
 

time: 196 us -> 192 us (0.980)
  starting transfers between devices: 63.3 us -> 59.2 us
    all_to_all x2, starting transfers between devices: 10.3 us -> 7.86 us  [on_device(): exchanged.append(lax.all_to_all(qkv, 'tensor', 0, 0, tiled=True))]
  transfers between devices with their start and end apart: 40 -> 40, of which waited for: 18 -> 18; matrix products, arithmetic and copies ran while one was open for 9% -> 9% of each run, Pallas kernels for 24% -> 25%
where the time goes in v12:
time: 192 us; the launch traced here: 191 us
  starting transfers between devices  59.2 us (31%)
  waiting for transfers between devices  53.7 us (28%)
  Pallas kernels  51.9 us (27%)
  local copies, waits for them, and re-layouts  13.6 us (7%)
  other arithmetic  12.1 us (6%)
    ppermute x18, waiting for transfers between devices, swap(): return lax.ppermute(values, axis, [(i, i ^ distance) for i in range(count)])  28.1 us
    ppermute x10, waiting for transfers between devices, line_hop(): down = lax.ppermute(down, axis, [(i, i - 1) for i in range(4 - hop, 0, -1)])  22.9 us
    ppermute x18, starting transfers between devices, swap(): return lax.ppermute(values, axis, [(i, i ^ distance) for i in range(count)])  21.4 us
    pallas_call x3, Pallas kernels, base_block(): pl.pallas_call(functools.partial(block_kernel, first_rows, total is not N...  17.4 us
    ppermute x10, starting transfers between devices, line_hop(): up = lax.ppermute(up, axis, [(i, i + 1) for i in range(hop - 1, 3)])  16.9 us
    pallas_call x2, Pallas kernels, attend(): pl.pallas_call(functools.partial(attend_kernel, unit, first_row), out_sha...  14.2 us
    ppermute x10, starting transfers between devices, line_hop(): down = lax.ppermute(down, axis, [(i, i - 1) for i in range(4 - hop, 0, -1)])  13.1 us
    pallas_call x2, Pallas kernels, project(): pl.pallas_call(functools.partial(out_kernel, count, earlier is not None),...  10.2 us
  transfers between devices with their start and end apart: 40, of which 18 were waited for; matrix products, arithmetic and copies ran while one was open for 9% of the time, Pallas kernels for 25%

profile of v12, /device:TPU:0, one launch (start us, length us, event | category | flops | bytes accessed | tf_op | source)
XLA Modules:
  0.0 191.2 jit_solution(7939400201721149376)
XLA Ops:
  1.7 3.1 %collective-permute-start = (f32[256]{0:T(256)S(1)}, f32[256]{0:T(256)S(1)}, u32[]{:S(2)}, u32[]{:S(2)}) collective-permute-start(f32[256]{0:T(256)S(1)} %reduce_sum.59), channel_id=1, source_target_pairs={{0,1},{1,0},{2,3},{3,2},{4,5},{5,4},{6,7},{7,6},{8,9},{9,8},{10,11... | collective-permute-start | bytes 3080 | tf_op jit(solution)/shard_map/ppermute | solution.py:35
  4.7 2.6 %collective-permute-start.1 = (f32[256]{0:T(256)S(1)}, f32[256]{0:T(256)S(1)}, u32[]{:S(2)}, u32[]{:S(2)}) collective-permute-start(f32[256]{0:T(256)S(1)} %reduce_sum.59), channel_id=1, source_target_pairs={{0,2},{1,3},{2,0},{3,1},{4,6},{5,7},{6,4},{7,5},{8,10},{9,11},{10,... | collective-permute-start | bytes 3080 | tf_op jit(solution)/shard_map/ppermute | solution.py:35
  18.2 15.0 %collective-permute-done.3 = f32[1,272]{1,0:T(1,128)S(1)} collective-permute-done((f32[1,272]{1,0:T(1,128)S(1)}, f32[1,272]{1,0:T(1,128)S(1)}, u32[]{:S(2)}, u32[]{:S(2)}) %collective-permute-start.3) | collective-permute-done | bytes 1120 | tf_op jit(solution)/shard_map/ppermute | solution.py:35
  35.0 5.1 %collective-permute-done.5.refs_2_ = bf16[256,2048]{1,0:T(8,128)(2,1)S(1)} collective-permute-done((bf16[256,2048]{1,0:T(8,128)(2,1)S(1)}, bf16[256,2048]{1,0:T(8,128)(2,1)S(1)}, u32[]{:S(2)}, u32[]{:S(2)}) %collective-permute-start.5) | collective-permute-done | bytes 1048608 | tf_op jit(solution)/shard_map/ppermute | solution.py:48
  45.6 5.4 %shrink_rows.1 = (f32[2,128,128]{2,1,0:T(8,128)S(1)}, f32[2,128,128]{2,1,0:T(8,128)S(1)}) custom-call(s32[1]{0:T(128)} %bitcast.4.place_ref, s32[64]{0:T(128)S(1)} %compare_select_fusion.slots, bf16[256,2048]{1,0:T(8,128)(2,1)S(1)} %bitcast.60, bf16[256,2048]{1,0:T(8,128)(2,1)} %collective-permute-done.7.x1, bf16[256,2048]{1,0:T(8,128)(2,1)} %collective-permute-done.8.x2, ...), custom_call_target="tpu_custom_call" | custom-call | flops 524288 | bytes 524288 | tf_op jit(solution)/shard_map/shrink_rows/pallas_call | solution.py:300
  57.9 4.3 %collective-permute-start.12 = (f32[128,128]{1,0:T(8,128)S(1)}, f32[128,128]{1,0:T(8,128)S(1)}, u32[]{:S(2)}, u32[]{:S(2)}) collective-permute-start(f32[128,128]{1,0:T(8,128)S(1)} %fusion.8), channel_id=1, source_target_pairs={{0,1},{1,0},{2,3},{3,2},{4,5},{5,4},{6,7},{7,6},{8,9},{9,8},{10,11... | collective-permute-start | bytes 196616 | tf_op jit(solution)/shard_map/ppermute | solution.py:35
  63.5 6.6 %base_block.3 = f32[256,1280]{1,0:T(8,128)S(1)} custom-call(s32[3]{0:T(128)S(1)} %pad_add_fusion.1.owners, bf16[256,2048]{1,0:T(8,128)(2,1)S(1)} %bitcast.61, bf16[256,2048]{1,0:T(8,128)(2,1)} %collective-permute-done.4.refs_1_, bf16[256,2048]{1,0:T(8,128)(2,1)S(1)} %copy-done.6, f32[256,1]{1,0:T(8,128)S(1)} %copy.24.refs_3_, f32[1,8192]{1,0:T(1,128)S(1)} %bitcast.62, ...), custom_call_target="tpu_custom_call" | custom-call | flops 327680 | bytes 327680 | tf_op jit(solution)/shard_map/base_block/pallas_call | solution.py:121
  71.6 2.9 %collective-permute-start.15 = (f32[128,128]{1,0:T(8,128)S(1)}, f32[128,128]{1,0:T(8,128)S(1)}, u32[]{:S(2)}, u32[]{:S(2)}) collective-permute-start(f32[128,128]{1,0:T(8,128)S(1)} %add.142), channel_id=1, source_target_pairs={{0,2},{1,3},{2,0},{3,1},{4,6},{5,7},{6,4},{7,5},{8,10},{9,11},{10,... | collective-permute-start | bytes 196616 | tf_op jit(solution)/shard_map/ppermute | solution.py:35
  80.2 3.4 %collective-permute-done.16 = bf16[128,128]{1,0:T(8,128)(2,1)S(1)} collective-permute-done((bf16[128,128]{1,0:T(8,128)(2,1)S(1)}, bf16[128,128]{1,0:T(8,128)(2,1)S(1)}, u32[]{:S(2)}, u32[]{:S(2)}) %collective-permute-start.16) | collective-permute-done | bytes 32800 | tf_op jit(solution)/shard_map/ppermute | solution.py:35
  84.9 4.7 %grow_rows.1 = (f32[2,256,1280]{2,1,0:T(8,128)S(1)}, f32[256,1280]{1,0:T(8,128)S(1)}, f32[256,1280]{1,0:T(8,128)}) custom-call(s32[1]{0:T(128)} %bitcast.4.place_ref, s32[64]{0:T(128)S(1)} %compare_select_fusion.slots, bf16[2,128,128]{2,1,0:T(8,128)(2,1)S(1)} %pad_maximum_fusion.s0, bf16[2,128,128]{2,1,0:T(8,128)(2,1)S(1)} %collective-permute-done.17.s1, ...), custom_call_target="tpu_custom_call" | custom-call | flops 327680 | bytes 327680 | tf_op jit(solution)/shard_map/grow_rows/pallas_call | solution.py:382
  98.0 2.6 %fusion.6 = (f16[128,1280]{1,0:T(8,128)(2,1)}, f16[128,1280]{1,0:T(8,128)(2,1)S(1)}) fusion(f32[256,1280]{1,0:T(8,128)} %collective-permute-done.20, f32[2,256,1280]{2,1,0:T(8,128)} %copy-done.3), kind=kLoop, calls=%fused_computation.10 | loop fusion | flops 655360 | bytes 3276800 | tf_op jit(solution)/shard_map/convert_element_type | solution.py:791
  106.3 5.4 %base_block.4 = f32[128,1280]{1,0:T(8,128)S(1)} custom-call(s32[4]{0:T(128)S(1)} %pad_add_fusion.owners, bf16[256,2048]{1,0:T(8,128)(2,1)S(1)} %collective-permute-done.13.refs_0_, bf16[256,2048]{1,0:T(8,128)(2,1)S(1)} %collective-permute-done.14.refs_1_, bf16[128,2048]{1,0:T(8,128)(2,1)} %collective-permute-done.18.refs_2_, ...), custom_call_target="tpu_custom_call" | custom-call | flops 163840 | bytes 163840 | tf_op jit(solution)/shard_map/base_block/pallas_call | solution.py:121
  113.9 4.1 %all-to-all-start = ((bf16[4,32,1280]{2,1,0:T(8,128)(2,1)}), bf16[4,32,1280]{2,1,0:T(8,128)(2,1)S(1)}, u32[]{:S(2)}, u32[]{:S(2)}) async-start(bf16[4,32,1280]{2,1,0:T(8,128)(2,1)} %bitcast.34), calls=%async_computation | async-start | bytes 655360 | tf_op jit(solution)/shard_map/all_to_all | solution.py:824
  119.7 5.4 %base_block.5 = f32[128,1280]{1,0:T(8,128)S(1)} custom-call(s32[4]{0:T(128)S(1)} %pad_add_fusion.owners, bf16[256,2048]{1,0:T(8,128)(2,1)S(1)} %collective-permute-done.13.refs_0_, bf16[256,2048]{1,0:T(8,128)(2,1)S(1)} %collective-permute-done.14.refs_1_, bf16[128,2048]{1,0:T(8,128)(2,1)} %collective-permute-done.23.refs_2_, ...), custom_call_target="tpu_custom_call" | custom-call | flops 163840 | bytes 163840 | tf_op jit(solution)/shard_map/base_block/pallas_call | solution.py:121
  127.8 3.8 %all-to-all-start.1 = ((bf16[4,32,1280]{2,1,0:T(8,128)(2,1)}), bf16[4,32,1280]{2,1,0:T(8,128)(2,1)S(1)}, u32[]{:S(2)}, u32[]{:S(2)}) async-start(bf16[4,32,1280]{2,1,0:T(8,128)(2,1)} %bitcast.33), calls=%async_computation.1 | async-start | bytes 655360 | tf_op jit(solution)/shard_map/all_to_all | solution.py:824
  132.2 6.7 %attend.2.refs_0_ = bf16[32,4096]{1,0:T(8,128)(2,1)S(1)} custom-call(s32[16]{0:T(128)S(1)} %get-tuple-element.105.lengths, s32[16]{0:T(128)S(1)} %select_reduce_fusion.2.order, bf16[4,32,1280]{2,1,0:T(8,128)(2,1)S(1)} %all-to-all-done.qkv_ref, f32[32,128]{1,0:T(8,128)S(1)} %get-tuple-element.108.cos_ref, f32[32,128]{1,0:T(8,128)S(1)} %get-tuple-element.109.sin_ref, ...), custom_call_target="tpu_custom_call" | custom-call | flops 268435456 | bytes 16777216 | tf_op jit(solution)/shard_map/attend/pallas_call | solution.py:564
  138.9 4.0 %collective-permute-start.26 = (bf16[32,4096]{1,0:T(8,128)(2,1)S(1)}, bf16[32,4096]{1,0:T(8,128)(2,1)S(1)}, u32[]{:S(2)}, u32[]{:S(2)}) collective-permute-start(bf16[32,4096]{1,0:T(8,128)(2,1)S(1)} %attend.2.refs_0_), channel_id=1, source_target_pairs={{0,1},{1,2},{2,3},{4,5},{5,6},{6,7},{8,9},{9,10},{10,11},{12,13},{... | collective-permute-start | bytes 786440 | tf_op jit(solution)/shard_map/ppermute | solution.py:47
  144.4 7.5 %attend.3.refs_3_ = bf16[32,4096]{1,0:T(8,128)(2,1)S(1)} custom-call(s32[16]{0:T(128)S(1)} %get-tuple-element.104.lengths, s32[16]{0:T(128)S(1)} %select_reduce_fusion.1.order, bf16[4,32,1280]{2,1,0:T(8,128)(2,1)S(1)} %all-to-all-done.1.qkv_ref, f32[32,128]{1,0:T(8,128)S(1)} %get-tuple-element.110.cos_ref, f32[32,128]{1,0:T(8,128)S(1)} %get-tuple-element.111.sin_ref, ...), custom_call_target="tpu_custom_call" | custom-call | flops 268435456 | bytes 16777216 | tf_op jit(solution)/shard_map/attend/pallas_call | solution.py:564
  151.9 4.2 %collective-permute-start.32 = (bf16[32,4096]{1,0:T(8,128)(2,1)S(1)}, bf16[32,4096]{1,0:T(8,128)(2,1)S(1)}, u32[]{:S(2)}, u32[]{:S(2)}) collective-permute-start(bf16[32,4096]{1,0:T(8,128)(2,1)S(1)} %attend.3.refs_3_), channel_id=1, source_target_pairs={{0,1},{1,2},{2,3},{4,5},{5,6},{6,7},{8,9},{9,10},{10,11},{12,13},{... | collective-permute-start | bytes 786440 | tf_op jit(solution)/shard_map/ppermute | solution.py:47
  160.7 5.3 %collective-permute-done.34.refs_5_ = bf16[32,4096]{1,0:T(8,128)(2,1)S(1)} collective-permute-done((bf16[32,4096]{1,0:T(8,128)(2,1)S(1)}, bf16[32,4096]{1,0:T(8,128)(2,1)S(1)}, u32[]{:S(2)}, u32[]{:S(2)}) %collective-permute-start.34) | collective-permute-done | bytes 262176 | tf_op jit(solution)/shard_map/ppermute | solution.py:48
  168.0 3.9 %collective-permute-done.29.refs_1_ = bf16[32,4096]{1,0:T(8,128)(2,1)S(1)} collective-permute-done((bf16[32,4096]{1,0:T(8,128)(2,1)S(1)}, bf16[32,4096]{1,0:T(8,128)(2,1)S(1)}, u32[]{:S(2)}, u32[]{:S(2)}) %collective-permute-start.29) | collective-permute-done | bytes 262176 | tf_op jit(solution)/shard_map/ppermute | solution.py:48
  173.9 4.6 %collective-permute-done.35.refs_5_ = bf16[32,4096]{1,0:T(8,128)(2,1)S(1)} collective-permute-done((bf16[32,4096]{1,0:T(8,128)(2,1)S(1)}, bf16[32,4096]{1,0:T(8,128)(2,1)S(1)}, u32[]{:S(2)}, u32[]{:S(2)}) %collective-permute-start.35) | collective-permute-done | bytes 262176 | tf_op jit(solution)/shard_map/ppermute | solution.py:48
  179.9 5.9 %project.2.refs_9_ = bf16[2,4,2,16,2048]{4,3,2,1,0:T(8,128)(2,1)S(1)} custom-call(s32[3]{0:T(128)S(1)} %pad_add_fusion.1.owners, bf16[32,4096]{1,0:T(8,128)(2,1)S(1)} %attend.2.refs_0_, bf16[32,4096]{1,0:T(8,128)(2,1)S(1)} %collective-permute-done.26.refs_1_, bf16[32,4096]{1,0:T(8,128)(2,1)S(1)} %collective-permute-done.28.refs_2_, ...), custom_call_target="tpu_custom_call" | custom-call | flops 3221225472 | bytes 19136512 | tf_op jit(solution)/shard_map/project/pallas_call | solution.py:658
  186.9 4.3 %project.3 = bf16[2,4,2,16,2048]{4,3,2,1,0:T(8,128)(2,1)} custom-call(s32[4]{0:T(128)S(1)} %pad_add_fusion.owners, bf16[32,4096]{1,0:T(8,128)(2,1)S(1)} %collective-permute-done.27.refs_0_, bf16[32,4096]{1,0:T(8,128)(2,1)S(1)} %collective-permute-done.29.refs_1_, bf16[32,4096]{1,0:T(8,128)(2,1)S(1)} %collective-permute-done.30.refs_2_, ...), custom_call_target="tpu_custom_call" | custom-call | flops 2147483648 | bytes 18350080 | tf_op jit(solution)/shard_map/project/pallas_call | solution.py:658
  (166 shorter events, 69.8 us)
Async XLA Ops:
  8.6 24.5 %collective-permute-start.8 = (bf16[256,2048]{1,0:T(8,128)(2,1)S(1)}, bf16[256,2048]{1,0:T(8,128)(2,1)}, u32[]{:S(2)}, u32[]{:S(2)}) collective-permute-start(bf16[256,2048]{1,0:T(8,128)(2,1)S(1)} %bitcast.56), channel_id=1, source_target_pairs={{0,8},{4,12},{8,0},{12,4},{1,9},{5,13},{9,1},{13,5},{2,10},{6,14},... | collective-permute-start | bytes 3145736 | tf_op jit(solution)/shard_map/ppermute | solution.py:35
  12.7 22.3 %collective-permute-start.4 = (bf16[256,2048]{1,0:T(8,128)(2,1)S(1)}, bf16[256,2048]{1,0:T(8,128)(2,1)}, u32[]{:S(2)}, u32[]{:S(2)}) collective-permute-start(bf16[256,2048]{1,0:T(8,128)(2,1)S(1)} %bitcast.57), channel_id=1, source_target_pairs={{0,1},{1,2},{2,3},{4,5},{5,6},{6,7},{8,9},{9,10},{10,11},{12,13},{... | collective-permute-start | bytes 3145736 | tf_op jit(solution)/shard_map/ppermute | solution.py:47
  15.0 25.1 %collective-permute-start.5 = (bf16[256,2048]{1,0:T(8,128)(2,1)S(1)}, bf16[256,2048]{1,0:T(8,128)(2,1)S(1)}, u32[]{:S(2)}, u32[]{:S(2)}) collective-permute-start(bf16[256,2048]{1,0:T(8,128)(2,1)S(1)} %bitcast.58), channel_id=1, source_target_pairs={{3,2},{2,1},{1,0},{7,6},{6,5},{5,4},{11,10},{10,9},{9,8},{15,14},{... | collective-permute-start | bytes 3145736 | tf_op jit(solution)/shard_map/ppermute | solution.py:48
  16.6 16.5 %collective-permute-start.3 = (f32[1,272]{1,0:T(1,128)S(1)}, f32[1,272]{1,0:T(1,128)S(1)}, u32[]{:S(2)}, u32[]{:S(2)}) collective-permute-start(f32[1,272]{1,0:T(1,128)S(1)} %reshape.106), channel_id=1, source_target_pairs={{0,8},{4,12},{8,0},{12,4},{1,9},{5,13},{9,1},{13,5},{2,10},{6,14},... | collective-permute-start | bytes 3272 | tf_op jit(solution)/shard_map/ppermute | solution.py:35
  18.2 26.4 %collective-permute-start.7 = (bf16[256,2048]{1,0:T(8,128)(2,1)S(1)}, bf16[256,2048]{1,0:T(8,128)(2,1)}, u32[]{:S(2)}, u32[]{:S(2)}) collective-permute-start(bf16[256,2048]{1,0:T(8,128)(2,1)S(1)} %bitcast.59), channel_id=1, source_target_pairs={{0,4},{4,0},{8,12},{12,8},{1,5},{5,1},{9,13},{13,9},{2,6},{6,2},{1... | collective-permute-start | bytes 3145736 | tf_op jit(solution)/shard_map/ppermute | solution.py:35
  41.1 30.5 %collective-permute-start.13 = (bf16[256,2048]{1,0:T(8,128)(2,1)}, bf16[256,2048]{1,0:T(8,128)(2,1)S(1)}, u32[]{:S(2)}, u32[]{:S(2)}) collective-permute-start(bf16[256,2048]{1,0:T(8,128)(2,1)} %collective-permute-done.4.refs_1_), channel_id=1, source_target_pairs={{1,2},{2,3},{5,6},{6,7},{9,10},{10,11},{13,14},{14,15},{17,18},{18... | collective-permute-start | bytes 3145736 | tf_op jit(solution)/shard_map/ppermute | solution.py:47
  41.8 29.8 %collective-permute-start.14 = (bf16[256,2048]{1,0:T(8,128)(2,1)}, bf16[256,2048]{1,0:T(8,128)(2,1)S(1)}, u32[]{:S(2)}, u32[]{:S(2)}) collective-permute-start(bf16[256,2048]{1,0:T(8,128)(2,1)} %copy-done.5), channel_id=1, source_target_pairs={{2,1},{1,0},{6,5},{5,4},{10,9},{9,8},{14,13},{13,12},{18,17},{17,1... | collective-permute-start | bytes 3145736 | tf_op jit(solution)/shard_map/ppermute | solution.py:48
  57.9 13.7 %collective-permute-start.12 = (f32[128,128]{1,0:T(8,128)S(1)}, f32[128,128]{1,0:T(8,128)S(1)}, u32[]{:S(2)}, u32[]{:S(2)}) collective-permute-start(f32[128,128]{1,0:T(8,128)S(1)} %fusion.8), channel_id=1, source_target_pairs={{0,1},{1,0},{2,3},{3,2},{4,5},{5,4},{6,7},{7,6},{8,9},{9,8},{10,11... | collective-permute-start | bytes 196616 | tf_op jit(solution)/shard_map/ppermute | solution.py:35
  76.8 15.4 %collective-permute-start.18 = (bf16[128,2048]{1,0:T(8,128)(2,1)}, bf16[128,2048]{1,0:T(8,128)(2,1)}, u32[]{:S(2)}, u32[]{:S(2)}) collective-permute-start(bf16[128,2048]{1,0:T(8,128)(2,1)} %get-tuple-element.56), channel_id=1, source_target_pairs={{2,3},{6,7},{10,11},{14,15},{18,19},{22,23},{26,27},{30,31}} | collective-permute-start | bytes 1572872 | tf_op jit(solution)/shard_map/ppermute | solution.py:47
  78.3 15.1 %collective-permute-start.19 = (bf16[128,2048]{1,0:T(8,128)(2,1)}, bf16[128,2048]{1,0:T(8,128)(2,1)}, u32[]{:S(2)}, u32[]{:S(2)}) collective-permute-start(bf16[128,2048]{1,0:T(8,128)(2,1)} %get-tuple-element.57), channel_id=1, source_target_pairs={{1,0},{5,4},{9,8},{13,12},{17,16},{21,20},{25,24},{29,28}} | collective-permute-start | bytes 1572872 | tf_op jit(solution)/shard_map/ppermute | solution.py:48
  95.2 16.5 %collective-permute-start.21 = (f32[256,1280]{1,0:T(8,128)}, f32[256,1280]{1,0:T(8,128)}, u32[]{:S(2)}, u32[]{:S(2)}) collective-permute-start(f32[256,1280]{1,0:T(8,128)} %copy-done.9), channel_id=1, source_target_pairs={{0,4},{4,0},{8,12},{12,8},{1,5},{5,1},{9,13},{13,9},{2,6},{6,2},{1... | collective-permute-start | bytes 3932168 | tf_op jit(solution)/shard_map/ppermute | solution.py:35
  100.5 24.6 %collective-permute-start.25 = (f16[128,1280]{1,0:T(8,128)(2,1)}, f16[128,1280]{1,0:T(8,128)(2,1)}, u32[]{:S(2)}, u32[]{:S(2)}) collective-permute-start(f16[128,1280]{1,0:T(8,128)(2,1)} %get-tuple-element.73), channel_id=1, source_target_pairs={{0,8},{4,12},{8,0},{12,4},{1,9},{5,13},{9,1},{13,5},{2,10},{6,14},... | collective-permute-start | bytes 983048 | tf_op jit(solution)/shard_map/ppermute | solution.py:35
  102.6 15.4 %collective-permute-start.23 = (bf16[128,2048]{1,0:T(8,128)(2,1)}, bf16[128,2048]{1,0:T(8,128)(2,1)}, u32[]{:S(2)}, u32[]{:S(2)}) collective-permute-start(bf16[128,2048]{1,0:T(8,128)(2,1)} %get-tuple-element.68), channel_id=1, source_target_pairs={{2,3},{6,7},{10,11},{14,15},{18,19},{22,23},{26,27},{30,31}} | collective-permute-start | bytes 1572872 | tf_op jit(solution)/shard_map/ppermute | solution.py:47
  104.1 15.6 %collective-permute-start.24 = (bf16[128,2048]{1,0:T(8,128)(2,1)}, bf16[128,2048]{1,0:T(8,128)(2,1)}, u32[]{:S(2)}, u32[]{:S(2)}) collective-permute-start(bf16[128,2048]{1,0:T(8,128)(2,1)} %get-tuple-element.69), channel_id=1, source_target_pairs={{1,0},{5,4},{9,8},{13,12},{17,16},{21,20},{25,24},{29,28}} | collective-permute-start | bytes 1572872 | tf_op jit(solution)/shard_map/ppermute | solution.py:48
  113.9 13.9 %all-to-all-start = ((bf16[4,32,1280]{2,1,0:T(8,128)(2,1)}), bf16[4,32,1280]{2,1,0:T(8,128)(2,1)S(1)}, u32[]{:S(2)}, u32[]{:S(2)}) async-start(bf16[4,32,1280]{2,1,0:T(8,128)(2,1)} %bitcast.34), calls=%async_computation | async-start | bytes 655360 | tf_op jit(solution)/shard_map/all_to_all | solution.py:824
  127.8 16.6 %all-to-all-start.1 = ((bf16[4,32,1280]{2,1,0:T(8,128)(2,1)}), bf16[4,32,1280]{2,1,0:T(8,128)(2,1)S(1)}, u32[]{:S(2)}, u32[]{:S(2)}) async-start(bf16[4,32,1280]{2,1,0:T(8,128)(2,1)} %bitcast.33), calls=%async_computation.1 | async-start | bytes 655360 | tf_op jit(solution)/shard_map/all_to_all | solution.py:824
  138.9 18.6 %collective-permute-start.26 = (bf16[32,4096]{1,0:T(8,128)(2,1)S(1)}, bf16[32,4096]{1,0:T(8,128)(2,1)S(1)}, u32[]{:S(2)}, u32[]{:S(2)}) collective-permute-start(bf16[32,4096]{1,0:T(8,128)(2,1)S(1)} %attend.2.refs_0_), channel_id=1, source_target_pairs={{0,1},{1,2},{2,3},{4,5},{5,6},{6,7},{8,9},{9,10},{10,11},{12,13},{... | collective-permute-start | bytes 786440 | tf_op jit(solution)/shard_map/ppermute | solution.py:47
  142.9 15.3 %collective-permute-start.28 = (bf16[32,4096]{1,0:T(8,128)(2,1)S(1)}, bf16[32,4096]{1,0:T(8,128)(2,1)S(1)}, u32[]{:S(2)}, u32[]{:S(2)}) collective-permute-start(bf16[32,4096]{1,0:T(8,128)(2,1)S(1)} %attend.2.refs_0_), channel_id=1, source_target_pairs={{3,2},{2,1},{1,0},{7,6},{6,5},{5,4},{11,10},{10,9},{9,8},{15,14},{... | collective-permute-start | bytes 786440 | tf_op jit(solution)/shard_map/ppermute | solution.py:48
  158.2 13.7 %collective-permute-start.29 = (bf16[32,4096]{1,0:T(8,128)(2,1)S(1)}, bf16[32,4096]{1,0:T(8,128)(2,1)S(1)}, u32[]{:S(2)}, u32[]{:S(2)}) collective-permute-start(bf16[32,4096]{1,0:T(8,128)(2,1)S(1)} %collective-permute-done.28.refs_2_), channel_id=1, source_target_pairs={{2,1},{1,0},{6,5},{5,4},{10,9},{9,8},{14,13},{13,12},{18,17},{17,1... | collective-permute-start | bytes 786440 | tf_op jit(solution)/shard_map/ppermute | solution.py:48
  160.0 13.2 %collective-permute-start.33 = (bf16[32,4096]{1,0:T(8,128)(2,1)S(1)}, bf16[32,4096]{1,0:T(8,128)(2,1)S(1)}, u32[]{:S(2)}, u32[]{:S(2)}) collective-permute-start(bf16[32,4096]{1,0:T(8,128)(2,1)S(1)} %collective-permute-done.32.refs_4_), channel_id=1, source_target_pairs={{1,2},{2,3},{5,6},{6,7},{9,10},{10,11},{13,14},{14,15},{17,18},{18... | collective-permute-start | bytes 786440 | tf_op jit(solution)/shard_map/ppermute | solution.py:47
  166.0 12.5 %collective-permute-start.35 = (bf16[32,4096]{1,0:T(8,128)(2,1)S(1)}, bf16[32,4096]{1,0:T(8,128)(2,1)S(1)}, u32[]{:S(2)}, u32[]{:S(2)}) collective-permute-start(bf16[32,4096]{1,0:T(8,128)(2,1)S(1)} %collective-permute-done.34.refs_5_), channel_id=1, source_target_pairs={{2,1},{1,0},{6,5},{5,4},{10,9},{9,8},{14,13},{13,12},{18,17},{17,1... | collective-permute-start | bytes 786440 | tf_op jit(solution)/shard_map/ppermute | solution.py:48
  167.3 18.5 %collective-permute-start.30 = (bf16[32,4096]{1,0:T(8,128)(2,1)S(1)}, bf16[32,4096]{1,0:T(8,128)(2,1)S(1)}, u32[]{:S(2)}, u32[]{:S(2)}) collective-permute-start(bf16[32,4096]{1,0:T(8,128)(2,1)S(1)} %collective-permute-done.27.refs_0_), channel_id=1, source_target_pairs={{2,3},{6,7},{10,11},{14,15},{18,19},{22,23},{26,27},{30,31}} | collective-permute-start | bytes 786440 | tf_op jit(solution)/shard_map/ppermute | solution.py:47
  171.9 13.9 %collective-permute-start.31 = (bf16[32,4096]{1,0:T(8,128)(2,1)S(1)}, bf16[32,4096]{1,0:T(8,128)(2,1)S(1)}, u32[]{:S(2)}, u32[]{:S(2)}) collective-permute-start(bf16[32,4096]{1,0:T(8,128)(2,1)S(1)} %collective-permute-done.29.refs_1_), channel_id=1, source_target_pairs={{1,0},{5,4},{9,8},{13,12},{17,16},{21,20},{25,24},{29,28}} | collective-permute-start | bytes 786440 | tf_op jit(solution)/shard_map/ppermute | solution.py:48
  173.2 12.6 %collective-permute-start.36 = (bf16[32,4096]{1,0:T(8,128)(2,1)S(1)}, bf16[32,4096]{1,0:T(8,128)(2,1)S(1)}, u32[]{:S(2)}, u32[]{:S(2)}) collective-permute-start(bf16[32,4096]{1,0:T(8,128)(2,1)S(1)} %collective-permute-done.33.refs_4_), channel_id=1, source_target_pairs={{2,3},{6,7},{10,11},{14,15},{18,19},{22,23},{26,27},{30,31}} | collective-permute-start | bytes 786440 | tf_op jit(solution)/shard_map/ppermute | solution.py:47
  (38 other events, 403.0 us)
